TPU v7x, 32 devices: a whole 2x2x4 slice. The times are simulated.
32 devices in a mesh: dp: 4 (over y, x), expert: 8 (over z, core).
Axes of the slice: x: 2, y: 2, z: 4, core: 2. Of those that a mesh axis runs over, the one named last changes fastest.
Arguments:
- cotangent: bfloat16 [4096, 4096], P(('dp', 'expert')), may hold values from -6 to 6
- hidden: bfloat16 [4, 8, 128, 768], P('dp', 'expert'), may hold values from -6 to 6
- down_matrix: bfloat16 [8, 4096, 768], P('expert'), may hold values from -0.21875 to 0.21875
- adapter_in: bfloat16 [2, 128, 768], replicated, may hold values from -0.21875 to 0.21875
- adapter_out: bfloat16 [2, 4096, 128], replicated, may hold values from -0.5 to 0.5
- probs: bfloat16 [4096, 8], P(('dp', 'expert')), may hold values from 0.019897461 to 0.5
- routes: int32 [4096, 8], P(('dp', 'expert')), may hold values from 0 to 127, as said below
- token_loop: int32 [4096], P(('dp', 'expert')), may hold values from 0 to 1
Outputs:
- hidden_gradient: bfloat16 [4, 8, 128, 768], P('dp', 'expert')
- down_matrix_gradient: float32 [8, 4096, 768], P('expert', 'dp')
- combine_weight_gradient: float32 [4096, 8], P(('dp', 'expert'))
- adapter_in_gradient: float32 [2, 128, 768], P(None, 'expert', 'dp')
- adapter_out_gradient: float32 [2, 4096, 128], P(None, 'dp', 'expert')
Inputs may be any that keep to these rules, and one draw needn't show every extreme that they name: `routes`: each row names 8 different experts. In the 128 rows of one device every expert below 8 is named by 4 to 16 rows, and within each index of dp one such expert is named by exactly 16 rows of every device.
All inputs are finite; a program needn't handle non-finite values.
Results may differ from a plain program's by a relative error of at most 0.0049.
Values may be sent and summed in bfloat16 or wider, within the bound.
No kernel may reach another device: no remote copies, remote signals or barrier semaphores. Data moves between devices by JAX's collectives and lax.ppermute only.
A program may use at most 128 MiB of HBM per device.

v0:
```python
import jax
import jax.numpy as jnp
from jax import lax
from jax.sharding import PartitionSpec as P


def route_slots(routes, owner_devices, slot_capacity):
    experts = jnp.arange(owner_devices, dtype=jnp.int32)
    named_count = jnp.sum((routes[:, :, None] == experts[None, None, :]).astype(jnp.int32), axis=1)
    before = jnp.cumsum(named_count, axis=0) - named_count
    in_window = routes < owner_devices
    target = jnp.where(in_window, routes, 0)
    column = jnp.take_along_axis(before, target, axis=1)
    slot_index = jnp.where(
        in_window, target * slot_capacity + column, owner_devices * slot_capacity
    )
    return (in_window, slot_index)


def on_device(cotangent, hidden, down_matrix, adapter_in, adapter_out, probs, routes, token_loop):
    owner_devices = lax.axis_size("expert")
    dp_size = lax.axis_size("dp")
    tok_count, model_width = cotangent.shape
    loop_number, adapter_rank_size, hidden_unit_count = adapter_in.shape
    route_count = routes.shape[1]
    slot_capacity = hidden.shape[2] // owner_devices
    slot_count = owner_devices * slot_capacity
    in_window, slot_index = route_slots(routes, owner_devices, slot_capacity)
    token_index = jnp.broadcast_to(
        jnp.arange(tok_count, dtype=jnp.int32)[:, None], slot_index.shape
    )
    slot_token = (
        jnp.full((slot_count,), tok_count, jnp.int32)
        .at[slot_index.reshape(-1)]
        .set(token_index.reshape(-1), mode="drop")
    )
    slot_weight = (
        jnp.zeros((slot_count,), jnp.float32)
        .at[slot_index.reshape(-1)]
        .set(probs.astype(jnp.float32).reshape(-1), mode="drop")
    )
    loop_mask = (token_loop[:, None] == jnp.arange(loop_number, dtype=jnp.int32)[None, :]).astype(
        jnp.float32
    )
    padded_dy = jnp.concatenate([cotangent, jnp.zeros((1, model_width), jnp.bfloat16)], axis=0)
    padded_mask = jnp.concatenate([loop_mask, jnp.zeros((1, loop_number), jnp.float32)], axis=0)
    send_dy = padded_dy[slot_token].reshape(owner_devices, slot_capacity, model_width)
    send_mix = (
        (slot_weight[:, None] * padded_mask[slot_token])
        .astype(jnp.bfloat16)
        .reshape(owner_devices, slot_capacity, loop_number)
    )
    got_dy, got_mix = (
        lax.all_to_all(send_dy, "expert", split_axis=0, concat_axis=0, tiled=True),
        lax.all_to_all(send_mix, "expert", split_axis=0, concat_axis=0, tiled=True),
    )
    received_output_gradient = got_dy.reshape(slot_count, model_width)
    weight_mix = got_mix.reshape(slot_count, loop_number).astype(jnp.float32)
    arrived_mask = (weight_mix > 0.0).astype(jnp.float32)
    every_loop = jnp.einsum(
        "ct,jtg->cjg", received_output_gradient, adapter_out, preferred_element_type=jnp.float32
    )
    projected = jnp.sum(every_loop * arrived_mask[:, :, None], axis=1).astype(jnp.bfloat16)
    weight_slot = jnp.sum(weight_mix, axis=1)
    hidden_row_block = hidden.reshape(slot_count, hidden_unit_count)
    adapter_flattened = adapter_in.reshape(loop_number * adapter_rank_size, hidden_unit_count)
    masked_projection = (
        (projected[:, None, :].astype(jnp.float32) * arrived_mask[:, :, None])
        .astype(jnp.bfloat16)
        .reshape(slot_count, loop_number * adapter_rank_size)
    )
    input_gradient = jnp.dot(
        received_output_gradient, down_matrix[0], preferred_element_type=jnp.float32
    ) + jnp.dot(masked_projection, adapter_flattened, preferred_element_type=jnp.float32)
    hidden_gradient = (weight_slot[:, None] * input_gradient).astype(jnp.bfloat16)
    grad_mix = jnp.sum(hidden_row_block.astype(jnp.float32) * input_gradient, axis=1)
    scaled = (weight_slot[:, None] * received_output_gradient.astype(jnp.float32)).astype(
        jnp.bfloat16
    )
    weighted_proj = (weight_slot[:, None] * projected.astype(jnp.float32)).astype(jnp.bfloat16)
    masked_weighted = (
        (weighted_proj[:, None, :].astype(jnp.float32) * arrived_mask[:, :, None])
        .astype(jnp.bfloat16)
        .reshape(slot_count, loop_number * adapter_rank_size)
    )
    grad_a = lax.dot_general(
        masked_weighted,
        hidden_row_block,
        (((0,), (0,)), ((), ())),
        preferred_element_type=jnp.float32,
    ).reshape(loop_number, adapter_rank_size, hidden_unit_count)
    down_rank = lax.dot_general(
        hidden_row_block,
        adapter_flattened,
        (((1,), (1,)), ((), ())),
        preferred_element_type=jnp.float32,
    ).reshape(slot_count, loop_number, adapter_rank_size)
    weighted_down = weight_slot[:, None] * jnp.sum(down_rank * arrived_mask[:, :, None], axis=1)
    back_mix, back_down = (
        lax.all_to_all(
            grad_mix.reshape(owner_devices, slot_capacity),
            "expert",
            split_axis=0,
            concat_axis=0,
            tiled=True,
        ),
        lax.all_to_all(
            weighted_down.reshape(owner_devices, slot_capacity, adapter_rank_size),
            "expert",
            split_axis=0,
            concat_axis=0,
            tiled=True,
        ),
    )
    position = jnp.minimum(slot_index, slot_count - 1)
    combine_weight_gradient = jnp.where(in_window, back_mix.reshape(slot_count)[position], 0.0)
    pulled = back_down.reshape(slot_count, adapter_rank_size)[position.reshape(-1)].reshape(
        tok_count, route_count, adapter_rank_size
    )
    summed = jnp.sum(jnp.where(in_window[:, :, None], pulled, 0.0), axis=1).astype(jnp.bfloat16)
    masked_sum = (summed[:, None, :].astype(jnp.float32) * loop_mask[:, :, None]).astype(
        jnp.bfloat16
    )
    grad_b = jnp.einsum("td,tlk->ldk", cotangent, masked_sum, preferred_element_type=jnp.float32)
    part_rows = model_width // dp_size
    columns = lax.all_to_all(scaled, "dp", split_axis=1, concat_axis=0, tiled=True)
    down_matrix_gradient = lax.dot_general(
        columns,
        lax.all_gather(hidden_row_block, "dp", axis=0, tiled=True),
        (((0,), (0,)), ((), ())),
        preferred_element_type=jnp.float32,
    )
    part_a, part_b = (
        lax.psum_scatter(grad_a, "dp", scatter_dimension=2, tiled=True),
        lax.psum_scatter(grad_b, "dp", scatter_dimension=1, tiled=True),
    )
    done_a, done_b = (
        lax.psum_scatter(part_a, "expert", scatter_dimension=1, tiled=True),
        lax.psum_scatter(part_b, "expert", scatter_dimension=2, tiled=True),
    )
    return (
        hidden_gradient.reshape(hidden.shape),
        down_matrix_gradient.reshape(1, part_rows, hidden_unit_count),
        combine_weight_gradient,
        done_a,
        done_b,
    )


def solution(mesh):
    return jax.shard_map(
        on_device,
        mesh=mesh,
        in_specs=(
            P(("dp", "expert"), None),
            P("dp", "expert", None, None),
            P("expert", None, None),
            P(),
            P(),
            P(("dp", "expert"), None),
            P(("dp", "expert"), None),
            P(("dp", "expert")),
        ),
        out_specs=(
            P("dp", "expert", None, None),
            P("expert", "dp", None),
            P(("dp", "expert"), None),
            P(None, "expert", "dp"),
            P(None, "dp", "expert"),
        ),
        check_vma=False,
    )
```

profile of v0, /device:TPU:0, one launch (start us, length us, event | category | flops | bytes accessed | tf_op | source)
XLA Modules:
  0.0 253.3 jit_solution(7802427964385131495)
XLA Ops:
  9.3 7.1 %gather_fusion.4 = s32[1024]{0:T(1024)S(1)} fusion(s32[128,8]{1,0:T(8,128)S(1)} %sub.3, s32[1024]{0:T(1024)S(1)} %reshape.276), kind=kCustom, calls=%fused_computation.4 | custom fusion | bytes 16384 | tf_op jit(solution)/shard_map/jit(take_along_axis)/gather | solution.py:13
  17.3 4.3 %scatter_custom_fusion.1 = s32[128]{0:T(128)S(1)} fusion(s32[1024]{0:T(1024)S(1)} %bitcast.75, s32[1024]{0:T(1024)S(1)} %reshape.294, s32[]{:T(128)} %constant.16.clone.1), kind=kCustom, calls=%fused_computation.62 | custom fusion | bytes 516 | tf_op jit(solution)/shard_map/scatter | solution.py:35
  22.8 4.3 %scatter_custom_fusion = f32[128]{0:T(128)S(1)} fusion(s32[1024]{0:T(1024)S(1)} %bitcast.76, f32[1024]{0:T(1024)S(1)} %reshape.286, f32[]{:T(128)} %constant.10.clone.1), kind=kCustom, calls=%fused_computation.64 | custom fusion | bytes 516 | tf_op jit(solution)/shard_map/scatter | solution.py:40
  27.8 6.3 %all-to-all-start = ((bf16[8,16,2]{1,2,0:T(2,128)(2,1)}), bf16[8,16,2]{1,2,0:T(2,128)(2,1)S(1)}, u32[]{:S(2)}, u32[]{:S(2)}) async-start(bf16[8,16,2]{1,2,0:T(2,128)(2,1)} %copy.92), calls=%async_computation | async-start | bytes 8192 | tf_op jit(solution)/shard_map/all_to_all | solution.py:55
  34.1 1.3 concatenate.7
  35.4 2.2 gather_fusion.1
  37.6 2.0 all-to-all-done
  39.6 3.6 %all-to-all-start.1 = ((bf16[8,16,4096]{2,1,0:T(8,128)(2,1)}), bf16[8,16,4096]{2,1,0:T(8,128)(2,1)S(1)}, u32[]{:S(2)}, u32[]{:S(2)}) async-start(bf16[8,16,4096]{2,1,0:T(8,128)(2,1)} %bitcast.70), calls=%async_computation.1 | async-start | bytes 2097152 | tf_op jit(solution)/shard_map/all_to_all | solution.py:54
  43.4 26.3 %all-to-all-done.1 = bf16[8,16,4096]{2,1,0:T(8,128)(2,1)S(1)} async-done(((bf16[8,16,4096]{2,1,0:T(8,128)(2,1)}), bf16[8,16,4096]{2,1,0:T(8,128)(2,1)S(1)}, u32[]{:S(2)}, u32[]{:S(2)}) %all-to-all-start.1) | async-done | bytes 1048608 | tf_op jit(solution)/shard_map/all_to_all | solution.py:54
  71.0 1.6 copy.96
  72.5 2.0 fusion.10
  74.7 1.3 fusion.4
  76.7 3.4 %all-to-all-start.4 = ((f32[8,16,128]{2,1,0:T(8,128)}), f32[8,16,128]{2,1,0:T(8,128)S(1)}, u32[]{:S(2)}, u32[]{:S(2)}) async-start(f32[8,16,128]{2,1,0:T(8,128)} %broadcast_multiply_fusion), calls=%async_computation.5 | async-start | bytes 131072 | tf_op jit(solution)/shard_map/all_to_all | solution.py:107
  80.1 5.8 %all-to-all-done.4 = f32[8,16,128]{2,1,0:T(8,128)S(1)} async-done(((f32[8,16,128]{2,1,0:T(8,128)}), f32[8,16,128]{2,1,0:T(8,128)S(1)}, u32[]{:S(2)}, u32[]{:S(2)}) %all-to-all-start.4) | async-done | bytes 65568 | tf_op jit(solution)/shard_map/all_to_all | solution.py:107
  85.9 4.0 %gather_fusion.3 = f32[1024,128]{1,0:T(8,128)} fusion(f32[128,128]{1,0:T(8,128)S(1)} %bitcast.67, s32[1024]{0:T(1024)S(1)} %broadcast_clamp_fusion), kind=kCustom, calls=%fused_computation.3 | custom fusion | bytes 1052672 | tf_op jit(solution)/shard_map/gather | solution.py:117
  89.9 1.3 fusion.7
  91.3 3.9 %convolution_bitcast_fusion = f32[2,4096,128]{1,2,0:T(8,128)} fusion(bf16[128,4096]{1,0:T(8,128)(2,1)} %param.8, f32[128,2]{0,1:T(2,128)} %copy-done.6, f32[128,128]{0,1:T(8,128)S(1)} %copy.99), kind=kOutput, calls=%fused_computation.9 | convolution fusion | flops 268500992 | bytes 5309440 | tf_op jit(solution)/shard_map/td,tlk->ldk/dot_general | solution.py:124
  95.2 4.5 %reduce-scatter.4.cloned.1.call-done = f32[2,128,192]{1,2,0:T(8,128)} async-done(((f32[2,128,768]{1,2,0:T(8,128)}), f32[2,128,192]{1,2,0:T(8,128)}) %reduce-scatter.4.cloned.1.call-update) | async-done | bytes 196624 | tf_op jit(solution)/shard_map/reduce_scatter | solution.py:134
  99.7 1.8 copy.98
  101.6 53.8 %reduce-scatter.6.cloned.1.call-done = f32[2,1024,128]{1,2,0:T(8,128)} async-done(((f32[2,4096,128]{1,2,0:T(8,128)}), f32[2,1024,128]{1,2,0:T(8,128)}) %reduce-scatter.6.cloned.1.call-update) | async-done | bytes 1048592 | tf_op jit(solution)/shard_map/reduce_scatter | solution.py:135
  155.5 3.8 %fusion = f32[128,768]{1,0:T(8,128)S(1)} fusion(bf16[128,4096]{1,0:T(8,128)(2,1)S(1)} %bitcast.69, bf16[1,4096,768]{2,1,0:T(8,128)(2,1)} %param.10), kind=kOutput, calls=%fused_computation.7 | convolution fusion | flops 805306368 | bytes 7733248 | tf_op jit(solution)/shard_map/dot_general | solution.py:72
  159.3 0.9 multiply_reduce_fusion
  160.9 4.6 %all-to-all-start.3 = ((f32[8,1,16]{2,1,0:T(1,128)}), f32[8,1,16]{2,1,0:T(1,128)S(1)}, u32[]{:S(2)}, u32[]{:S(2)}) async-start(f32[8,1,16]{2,1,0:T(1,128)} %bitcast.14), calls=%async_computation.3 | async-start | bytes 8192 | tf_op jit(solution)/shard_map/all_to_all | solution.py:100
  165.6 2.7 %reshape.243 = f32[128,4,1024]{2,1,0:T(4,128)} reshape(bf16[8,16,4096]{2,1,0:T(8,128)(2,1)S(1)} %all-to-all-done.1) | data formatting | bytes 3145728 | tf_op jit(solution)/shard_map/convert_element_type | solution.py:77
  168.2 2.0 multiply_convert_fusion
  170.3 1.3 copy.94
  171.6 3.5 %all-to-all-start.2 = ((bf16[128,4,1024]{2,0,1:T(8,128)(2,1)}), bf16[128,4,1024]{2,0,1:T(8,128)(2,1)S(1)}, u32[]{:S(2)}, u32[]{:S(2)}) async-start(bf16[128,4,1024]{2,0,1:T(8,128)(2,1)} %copy.94), calls=%async_computation.2 | async-start | bytes 2097152 | tf_op jit(solution)/shard_map/all_to_all | solution.py:126
  177.9 20.5 %all-gather = bf16[1,1,512,768]{3,2,1,0:T(8,128)(2,1)} all-gather(bf16[1,1,128,768]{3,2,1,0:T(8,128)(2,1)S(1)} %copy-done.1), channel_id=2, replica_groups=mesh['dp'=4,'expert'=8] {'dp'}, dimensions={2}, use_global_device_ids=true | all-gather | bytes 983040 | tf_op jit(solution)/shard_map/all_gather | solution.py:129
  199.7 6.6 %gather_fusion.2 = f32[1024]{0:T(1024)S(1)} fusion(f32[128]{0:T(128)S(1)} %reshape.236, s32[1024]{0:T(1024)S(1)} %broadcast_clamp_fusion.1), kind=kCustom, calls=%fused_computation.2 | custom fusion | bytes 12288 | tf_op jit(solution)/shard_map/gather | solution.py:116
  207.0 3.8 %convolution_bitcast_fusion.1 = f32[1,1024,768]{2,1,0:T(8,128)} fusion(bf16[512,1024]{1,0:T(8,128)(2,1)S(1)} %bitcast.71, bf16[1,1,512,768]{3,2,1,0:T(8,128)(2,1)} %all-gather), kind=kOutput, calls=%fused_computation.11 | convolution fusion | flops 805306368 | bytes 4980736 | tf_op jit(solution)/shard_map/dot_general | solution.py:127
  210.8 2.0 all-reduce.5.cloned.1.call-done
  214.2 32.5 %reduce-scatter.8.cloned.1.call-done = f32[2,1024,16]{1,2,0:T(8,128)} async-done(((f32[2,1024,128]{1,2,0:T(8,128)}), f32[2,1024,16]{1,2,0:T(8,128)}) %reduce-scatter.8.cloned.1.call-update) | async-done | bytes 131088 | tf_op jit(solution)/shard_map/reduce_scatter | solution.py:139
  (85 shorter events, 13.7 us)
Async XLA Ops:
  7.2 62.5 %copy-start = (bf16[2,4096,128]{2,1,0:T(8,128)(2,1)S(1)}, bf16[2,4096,128]{2,1,0:T(8,128)(2,1)}, u32[]{:S(2)}) copy-start(bf16[2,4096,128]{2,1,0:T(8,128)(2,1)} %param.12) | copy-start | bytes 6291460
  9.2 12.4 %copy-start.10 = (s32[128]{0:T(128)S(1)}, s32[128]{0:T(128)}, u32[]{:S(2)}) copy-start(s32[128]{0:T(128)} %param.15) | copy-start | bytes 1540
  9.2 13.3 %copy-start.9 = (bf16[128,8]{0,1:T(8,128)(2,1)S(1)}, bf16[128,8]{0,1:T(8,128)(2,1)}, u32[]{:S(2)}) copy-start(bf16[128,8]{0,1:T(8,128)(2,1)} %param.13) | copy-start | bytes 6148
  21.7 0.8 copy-start.6
  27.8 11.8 %all-to-all-start = ((bf16[8,16,2]{1,2,0:T(2,128)(2,1)}), bf16[8,16,2]{1,2,0:T(2,128)(2,1)S(1)}, u32[]{:S(2)}, u32[]{:S(2)}) async-start(bf16[8,16,2]{1,2,0:T(2,128)(2,1)} %copy.92), calls=%async_computation | async-start | bytes 8192 | tf_op jit(solution)/shard_map/all_to_all | solution.py:55
  39.6 30.1 %all-to-all-start.1 = ((bf16[8,16,4096]{2,1,0:T(8,128)(2,1)}), bf16[8,16,4096]{2,1,0:T(8,128)(2,1)S(1)}, u32[]{:S(2)}, u32[]{:S(2)}) async-start(bf16[8,16,4096]{2,1,0:T(8,128)(2,1)} %bitcast.70), calls=%async_computation.1 | async-start | bytes 2097152 | tf_op jit(solution)/shard_map/all_to_all | solution.py:54
  43.2 29.4 %copy-start.1 = (bf16[1,1,128,768]{3,2,1,0:T(8,128)(2,1)S(1)}, bf16[1,1,128,768]{3,2,1,0:T(8,128)(2,1)}, u32[]{:S(2)}) copy-start(bf16[1,1,128,768]{3,2,1,0:T(8,128)(2,1)} %param.9) | copy-start | bytes 589828
  43.2 56.5 %reduce-scatter.4.cloned.1.call-start = ((), (), s32[]{:S(2)}) async-start(), calls=%async_computation.8 | async-start | bytes 983040 | tf_op jit(solution)/shard_map/reduce_scatter | solution.py:134
  43.3 31.4 %copy-start.4 = (f32[128,2]{0,1:T(2,128)}, f32[128,2]{0,1:T(2,128)S(1)}, u32[]{:S(2)}) copy-start(f32[128,2]{0,1:T(2,128)S(1)} %reshape.242) | copy-start | bytes 3076
  43.4 31.1 %copy-start.7 = (f32[128]{0:T(128)}, f32[128]{0:T(128)S(1)}, u32[]{:S(2)}) copy-start(f32[128]{0:T(128)S(1)} %mul.116) | copy-start | bytes 1540
  69.7 4.9 %copy-start.3 = (s32[128,8]{1,0:T(8,128)S(1)}, s32[128,8]{1,0:T(8,128)}, u32[]{:S(2)}) copy-start(s32[128,8]{1,0:T(8,128)} %get-tuple-element.40) | copy-start | bytes 12292
  76.7 9.2 %all-to-all-start.4 = ((f32[8,16,128]{2,1,0:T(8,128)}), f32[8,16,128]{2,1,0:T(8,128)S(1)}, u32[]{:S(2)}, u32[]{:S(2)}) async-start(f32[8,16,128]{2,1,0:T(8,128)} %broadcast_multiply_fusion), calls=%async_computation.5 | async-start | bytes 131072 | tf_op jit(solution)/shard_map/all_to_all | solution.py:107
  80.1 75.3 %reduce-scatter.6.cloned.1.call-start = ((), (), s32[]{:S(2)}) async-start(), calls=%async_computation.9 | async-start | bytes 5242880 | tf_op jit(solution)/shard_map/reduce_scatter | solution.py:135
  95.2 117.6 %all-reduce.5.cloned.1.call-start = ((), (), s32[]{:S(2)}) async-start(), calls=%async_computation.11 | async-start | bytes 524288
  101.5 145.2 %reduce-scatter.8.cloned.1.call-start = ((), (), s32[]{:S(2)}) async-start(), calls=%async_computation.10 | async-start | bytes 1179648 | tf_op jit(solution)/shard_map/reduce_scatter | solution.py:139
  155.4 3.9 %copy-start.2 = (bf16[2,128,768]{2,1,0:T(8,128)(2,1)S(1)}, bf16[2,128,768]{2,1,0:T(8,128)(2,1)}, u32[]{:S(2)}) copy-start(bf16[2,128,768]{2,1,0:T(8,128)(2,1)} %param.11) | copy-start | bytes 1179652
  155.4 3.9 %copy-start.5 = (f32[128,2]{0,1:T(2,128)S(1)}, f32[128,2]{0,1:T(2,128)}, u32[]{:S(2)}) copy-start(f32[128,2]{0,1:T(2,128)} %copy-done.4) | copy-start | bytes 3076
  155.5 3.9 %copy-start.8 = (f32[128]{0:T(128)S(1)}, f32[128]{0:T(128)}, u32[]{:S(2)}) copy-start(f32[128]{0:T(128)} %copy-done.7) | copy-start | bytes 1540
  160.9 10.6 %all-to-all-start.3 = ((f32[8,1,16]{2,1,0:T(1,128)}), f32[8,1,16]{2,1,0:T(1,128)S(1)}, u32[]{:S(2)}, u32[]{:S(2)}) async-start(f32[8,1,16]{2,1,0:T(1,128)} %bitcast.14), calls=%async_computation.3 | async-start | bytes 8192 | tf_op jit(solution)/shard_map/all_to_all | solution.py:100
  170.3 6.4 %copy-start.11 = (u32[32]{0:T(128)S(1)}, u32[32]{0:T(128)}, u32[]{:S(2)}) copy-start(u32[32]{0:T(128)} %constant.63) | copy-start | bytes 388
  171.6 35.5 %all-to-all-start.2 = ((bf16[128,4,1024]{2,0,1:T(8,128)(2,1)}), bf16[128,4,1024]{2,0,1:T(8,128)(2,1)S(1)}, u32[]{:S(2)}, u32[]{:S(2)}) async-start(bf16[128,4,1024]{2,0,1:T(8,128)(2,1)} %copy.94), calls=%async_computation.2 | async-start | bytes 2097152 | tf_op jit(solution)/shard_map/all_to_all | solution.py:126
Sparse Core Ops, SparseCore 0:
  74.7 24.9 reduce-scatter.3
  102.7 52.6 reduce-scatter.5
  157.8 54.9 all-reduce.4
  215.5 31.1 reduce-scatter.7
where the time goes:
time: 254 us; the launch traced here: 253 us
  waiting for transfers between devices  127 us (50%)
  local copies, waits for them, and re-layouts  45.3 us (18%)
  starting transfers between devices  21.5 us (8%)
  blocking collectives  20.5 us (8%)
  matrix products  16.2 us (6%)
  between operations  14.8 us (6%)
  other arithmetic  7.94 us (3%)
    reduce_scatter x1, waiting for transfers between devices, on_device(): lax.psum_scatter(grad_b, 'dp', scatter_dimension=1, tiled=True)  53.8 us
    reduce_scatter x1, waiting for transfers between devices, on_device(): lax.psum_scatter(part_b, 'expert', scatter_dimension=2, tiled=True)  32.5 us
    all_to_all x1, waiting for transfers between devices, on_device(): lax.all_to_all(send_dy, 'expert', split_axis=0, concat_axis=0, tiled=True)  26.3 us
    all_gather x1, blocking collectives, on_device(): lax.all_gather(hidden_row_block, 'dp', axis=0, tiled=True)  20.5 us
    gather x3, local copies, waits for them, and re-layouts, route_slots(): column = jnp.take_along_axis(before, target, axis=1)  7.24 us
    gather x2, local copies, waits for them, and re-layouts, on_device(): back_mix.reshape(slot_count)[position]  6.65 us
    all_to_all x1, starting transfers between devices, on_device(): lax.all_to_all(send_mix, 'expert', split_axis=0, concat_axis=0, tiled=True)  6.33 us
    all_to_all x1, waiting for transfers between devices, on_device(): lax.all_to_all(weighted_down.reshape(owner_devices, slot_capacity, adapte...  5.79 us
  transfers between devices with their start and end apart: 9, of which 7 were waited for; matrix products, arithmetic and copies ran while one was open for 17% of the time, Pallas kernels for 0%

commit v1 on v0

v1 whole, which is shorter than its diff:
```python
import functools

import jax
import jax.numpy as jnp
from jax import lax
from jax.experimental import pallas as pl
from jax.experimental.pallas import tpu as pltpu
from jax.sharding import PartitionSpec as P

bf16 = jnp.bfloat16
f32 = jnp.float32
LANES = 128
MIB = 1 << 20


def dot(a, b, dims):
    return lax.dot_general(a, b, (dims, ((), ())), preferred_element_type=f32)


def nn(a, b):
    return dot(a, b, ((1,), (0,)))


def nt(a, b):
    return dot(a, b, ((1,), (1,)))


def tn(a, b):
    return dot(a, b, ((0,), (0,)))


def swap(x, axis, size, mask):
    return lax.ppermute(x, axis, [(i, i ^ mask) for i in range(size)])


def call(body, out_shape, ins, scratch=(), limit=24 * MIB, cost=None):
    specs = [pl.BlockSpec(memory_space=s) for s in ins]
    outs = jax.tree.map(lambda _: pl.BlockSpec(memory_space=pltpu.VMEM), out_shape)
    return pl.pallas_call(
        body,
        out_shape=out_shape,
        in_specs=specs,
        out_specs=outs,
        scratch_shapes=list(scratch),
        cost_estimate=cost,
        compiler_params=pltpu.CompilerParams(vmem_limit_bytes=limit),
    )


def cost(flops, nbytes):
    return pl.CostEstimate(flops=int(flops), bytes_accessed=int(nbytes), transcendentals=0)


def owner_column(place, chips, experts):
    j = lax.broadcasted_iota(jnp.int32, (experts, 1), 0)
    half, hop = j // chips, j % chips
    return ((place // 2) ^ hop) * 2 + ((place % 2) ^ half)


def route_body(chips, cap, place, routes, probs, loops, cot, keep, give, picks, mixed):
    experts = 2 * chips
    ways, toks = routes.shape
    width = cot.shape[1]
    owner = owner_column(place[0], chips, experts)
    named = jnp.zeros((experts, toks), f32)
    weight = jnp.zeros((experts, toks), f32)
    for k in range(ways):
        hit = routes[k : k + 1, :] == owner
        named = named + jnp.where(hit, 1.0, 0.0)
        weight = weight + jnp.where(hit, probs[k : k + 1, :].astype(f32), 0.0)
    earlier = lax.broadcasted_iota(jnp.int32, (toks, toks), 0) < lax.broadcasted_iota(
        jnp.int32, (toks, toks), 1
    )
    before = nn(named.astype(bf16), jnp.where(earlier, 1.0, 0.0).astype(bf16))
    spot = jnp.where(named > 0.0, before, -1.0)
    slot = lax.broadcasted_iota(jnp.int32, (cap, toks), 0).astype(f32)
    for j in range(experts):
        hit = spot[j : j + 1, :] == slot
        rows = slice(j * cap, (j + 1) * cap)
        picks[rows, :] = jnp.where(hit, 1.0, 0.0).astype(bf16)
        mixed[rows, :] = jnp.where(hit, weight[j : j + 1, :], 0.0).astype(bf16)
    loop_rows = lax.broadcasted_iota(jnp.int32, (LANES, toks), 0) == loops[...]
    mix = nt(mixed[...], jnp.where(loop_rows, 1.0, 0.0).astype(bf16)).astype(bf16)
    half = chips * cap
    keep[:, :, width:] = mix[:half].reshape(chips, cap, LANES)
    give[:, :, width:] = mix[half:].reshape(chips, cap, LANES)
    step = min(width, 512)
    for at in range(0, width, step):
        got = nn(picks[...], cot[:, at : at + step]).astype(bf16)
        keep[:, :, at : at + step] = got[:half].reshape(chips, cap, step)
        give[:, :, at : at + step] = got[half:].reshape(chips, cap, step)


def arrive_body(groups, cap, n_far, place, adapter_out, near, sib, *refs):
    far, outs = refs[:n_far], refs[n_far:]
    rows_out, masked_out, parts = outs[0], outs[1], outs[2:]
    loops, width, rank = adapter_out.shape
    e, i = place[0], place[1]
    z, c = e // 2, e % 2
    blocks = [(z * 2 + c, near[0]), (z * 2 + (1 - c), sib[0])]
    for hop in range(1, n_far + 1):
        pair = far[hop - 1]
        blocks += [((z ^ hop) * 2 + c, pair[0]), ((z ^ hop) * 2 + (1 - c), pair[1])]
    for source, block in blocks:
        rows_out[pl.ds(pl.multiple_of(source * cap, cap), cap), :] = block
    mix = rows_out[:, width:].astype(f32)
    weight = jnp.sum(mix, axis=1, keepdims=True)
    part = width // groups
    for hop in range(groups):
        at = pl.multiple_of((i ^ hop) * part, part)
        piece = rows_out[:, pl.ds(at, part)].astype(f32)
        parts[hop][:, :part] = (weight * piece).astype(bf16)
    proj = jnp.zeros((rows_out.shape[0], rank), f32)
    rows = rows_out[:, :width]
    masks = []
    for l in range(loops):
        mask = mix[:, l : l + 1] > 0.0
        masks.append(mask)
        proj = proj + jnp.where(mask, nn(rows, adapter_out[l]), 0.0)
    proj = proj.astype(bf16).astype(f32)
    for l in range(loops):
        masked_out[:, l * rank : (l + 1) * rank] = jnp.where(masks[l], proj, 0.0).astype(bf16)
    weighted = (weight * proj).astype(bf16)
    mix_block = mix.astype(bf16)
    for hop in range(groups):
        parts[hop][:, part : part + rank] = weighted
        parts[hop][:, part + rank :] = mix_block


def inner_body(steps, rows, down, masked, adapter_in, hidden, grad_out, mix_out, total):
    step = pl.program_id(0)
    width = rows.shape[1] - LANES
    part = width // steps
    at = pl.multiple_of(step * part, part)
    term = nn(rows[:, pl.ds(at, part)], down[...])

    @pl.when(step == 0)
    def _():
        total[...] = term + nn(masked[...], adapter_in[...])

    @pl.when(step > 0)
    def _():
        total[...] += term

    @pl.when(step == steps - 1)
    def _():
        grad = total[...]
        weight = jnp.sum(rows[:, width:].astype(f32), axis=1, keepdims=True)
        grad_out[...] = (weight * grad).astype(bf16)
        mix_out[...] = jnp.broadcast_to(
            jnp.sum(hidden[...].astype(f32) * grad, axis=1, keepdims=True), mix_out.shape
        )


def adapter_body(groups, loops, chips, part, cols, place, adapter_in, *refs):
    rows = refs[:groups]
    hids = refs[groups : 2 * groups]
    keep, give, sums, narrow = refs[2 * groups :]
    rank = adapter_in.shape[0] // loops
    share = rank // (2 * chips)
    hid_width = hids[0].shape[1]
    wide = keep.shape[2] - part
    e, i = place[0], place[1]
    pick = lax.broadcasted_iota(jnp.int32, (hid_width, wide), 0)
    lane = lax.broadcasted_iota(jnp.int32, (hid_width, wide), 1)
    pick = jnp.where((pick == lane + i * cols) & (lane < cols), 1.0, 0.0).astype(bf16)
    out = jnp.zeros((loops * rank, part), f32)
    inn = jnp.zeros((loops * rank, wide), f32)
    for g in range(groups):
        hid = hids[g][...]
        down = nt(hid, adapter_in[...])
        mix = rows[g][:, part + rank :].astype(f32)
        weighted = rows[g][:, part : part + rank].astype(f32)
        picked = nn(hid, pick).astype(bf16)
        masks = [mix[:, l : l + 1] > 0.0 for l in range(loops)]
        lefts = [
            jnp.where(masks[l], down[:, l * rank : (l + 1) * rank], 0.0) for l in range(loops)
        ]
        out = out + tn(jnp.concatenate(lefts, axis=1).astype(bf16), rows[g][:, :part])
        lefts = [jnp.where(masks[l], weighted, 0.0) for l in range(loops)]
        inn = inn + tn(jnp.concatenate(lefts, axis=1).astype(bf16), picked)
    sums[...] = out
    narrow[...] = inn
    z, c = e // 2, e % 2
    for hop in range(chips):
        for half, target in ((0, keep), (1, give)):
            owner = (z ^ hop) * 2 + (c ^ half)
            for l in range(loops):
                src = pl.ds(pl.multiple_of(l * rank + owner * share, share), share)
                dst = slice(l * share, (l + 1) * share)
                target[hop, dst, :part] = sums[src, :]
                target[hop, dst, part:] = narrow[src, :]


def pair_body(chips, cap, part, cols, place, keep, got, mix, got_mix, *outs):
    e = place[0]
    z, c = e // 2, e % 2
    wide = keep.shape[2] - part
    lane = lax.broadcasted_iota(jnp.int32, (cap, wide), 1)
    for hop in range(chips):
        total = keep[hop] + got[hop]
        outs[hop][:, :part] = total[:, :part].astype(bf16)
        own = mix[pl.ds(pl.multiple_of(((z ^ hop) * 2 + c) * cap, cap), cap), :]
        sib = got_mix[pl.ds(pl.multiple_of(((z ^ hop) * 2 + c) * cap, cap), cap), :]
        tail = total[:, part:]
        words = []
        for value in (own, sib):
            value = value[:, :1]
            high = value.astype(bf16).astype(f32)
            words += [high, value - high]
        first = tail[:cap]
        for n, word in enumerate(words):
            first = jnp.where(lane == cols + n, word, first)
        outs[hop][:cap, part:] = first.astype(bf16)
        if tail.shape[0] > cap:
            outs[hop][cap:, part:] = tail[cap:].astype(bf16)


def final_body(chips, cap, part, cols, loops, place, routes, picks, *refs):
    blocks, (out_grad, in_grad, combine) = refs[:chips], refs[chips:]
    experts = 2 * chips
    share = out_grad.shape[1]
    total = blocks[0][:, :part].astype(f32)
    tail = blocks[0][:, part:].astype(f32)
    for hop in range(1, chips):
        total = total + blocks[hop][:, :part].astype(f32)
        tail = tail + blocks[hop][:, part:].astype(f32)
    for l in range(loops):
        out_grad[l] = total[l * share : (l + 1) * share]
        in_grad[l] = tail[l * share : (l + 1) * share, :cols]
    owner = owner_column(place[0], chips, experts)
    ways, toks = routes.shape
    sums = jnp.zeros((ways, toks), f32)
    for j in range(experts):
        half, hop = j // chips, j % chips
        words = blocks[hop][:cap, part:].astype(f32)
        at = cols + 2 * half
        value = words[:, at : at + 1] + words[:, at + 1 : at + 2]
        pick = picks[j * cap : (j + 1) * cap, :].astype(f32)
        by_token = jnp.sum(pick * value, axis=0, keepdims=True)
        sums = sums + jnp.where(routes[...] == owner[j : j + 1, :], by_token, 0.0)
    combine[...] = sums


def product_body(groups, part, *refs):
    rows, hids, out = refs[:groups], refs[groups : 2 * groups], refs[2 * groups]
    step = min(part, 256)
    lefts = jnp.concatenate([r[:, :part] for r in rows], axis=0)
    rights = jnp.concatenate([h[...] for h in hids], axis=0)
    for at in range(0, part, step):
        out[0, at : at + step, :] = tn(lefts[:, at : at + step], rights)


def on_device(cotangent, hidden, down_matrix, adapter_in, adapter_out, probs, routes, token_loop):
    experts = lax.axis_size("expert")
    groups = lax.axis_size("dp")
    chips = experts // 2
    toks, width = cotangent.shape
    loops, rank, hid_width = adapter_in.shape
    ways = routes.shape[1]
    slots = hidden.shape[2]
    cap = slots // experts
    part = width // groups
    cols = hid_width // groups
    share = rank // experts
    packed = width + LANES
    S, V = pltpu.SMEM, pltpu.VMEM
    place = jnp.stack([lax.axis_index("expert"), lax.axis_index("dp")]).astype(jnp.int32)
    routes_t = routes.T
    hid = hidden.reshape(slots, hid_width)
    flat_in = adapter_in.reshape(loops * rank, hid_width)

    def shape(dims, kind):
        return jax.ShapeDtypeStruct(dims, kind)

    with jax.named_scope("route"):
        keep, give, picks = call(
            functools.partial(route_body, chips, cap),
            (
                shape((chips, cap, packed), bf16),
                shape((chips, cap, packed), bf16),
                shape((slots, toks), bf16),
            ),
            (S, V, V, V, V),
            scratch=(pltpu.VMEM((slots, toks), bf16),),
            cost=cost(2 * slots * toks * width, 4 * toks * width),
        )(place, routes_t, probs.T, token_loop.reshape(1, toks), cotangent)
    with jax.named_scope("dispatch"):
        sib = swap(give, "expert", experts, 1)
        far = [
            swap(jnp.stack([keep[hop], sib[hop]]), "expert", experts, 2 * hop)
            for hop in range(1, chips)
        ]
        hids = [hid] + [swap(hid, "dp", groups, hop) for hop in range(1, groups)]
    with jax.named_scope("arrive"):
        got = call(
            functools.partial(arrive_body, groups, cap, chips - 1),
            (shape((slots, packed), bf16), shape((slots, loops * rank), bf16))
            + tuple(shape((slots, part + rank + LANES), bf16) for _ in range(groups)),
            (S,) + (V,) * (chips + 2),
            cost=cost(2 * slots * width * loops * rank, 6 * slots * width),
        )(place, adapter_out, keep, sib, *far)
        rows, masked, parts = got[0], got[1], got[2:]
    with jax.named_scope("columns"):
        pieces = [parts[0]] + [swap(parts[hop], "dp", groups, hop) for hop in range(1, groups)]
    with jax.named_scope("inner"):
        steps = max(1, width // 1024)
        grad, mix = pl.pallas_call(
            functools.partial(inner_body, steps),
            grid=(steps,),
            out_shape=(shape((slots, hid_width), bf16), shape((slots, LANES), f32)),
            in_specs=[
                pl.BlockSpec((slots, packed), lambda s: (0, 0)),
                pl.BlockSpec((width // steps, hid_width), lambda s: (s, 0)),
                pl.BlockSpec((slots, loops * rank), lambda s: (0, 0)),
                pl.BlockSpec((loops * rank, hid_width), lambda s: (0, 0)),
                pl.BlockSpec((slots, hid_width), lambda s: (0, 0)),
            ],
            out_specs=(
                pl.BlockSpec((slots, hid_width), lambda s: (0, 0)),
                pl.BlockSpec((slots, LANES), lambda s: (0, 0)),
            ),
            scratch_shapes=[pltpu.VMEM((slots, hid_width), f32)],
            cost_estimate=cost(
                2 * slots * width * hid_width, 2 * (width * hid_width + slots * width)
            ),
            compiler_params=pltpu.CompilerParams(vmem_limit_bytes=24 * MIB),
        )(rows, down_matrix[0], masked, flat_in, hid)
    with jax.named_scope("adapters"):
        wide = -(-(cols + 4) // LANES) * LANES
        block = (chips, loops * share, part + wide)
        keep3, give3 = call(
            functools.partial(adapter_body, groups, loops, chips, part, cols),
            (shape(block, f32), shape(block, f32)),
            (S,) + (V,) * (1 + 2 * groups),
            scratch=(
                pltpu.VMEM((loops * rank, part), f32),
                pltpu.VMEM((loops * rank, wide), f32),
            ),
            limit=40 * MIB,
            cost=cost(4 * groups * slots * loops * rank * part, 4 * groups * slots * part),
        )(place, flat_in, *pieces, *hids)
        got3 = swap(give3, "expert", experts, 1)
        got_mix = swap(mix, "expert", experts, 1)
        ready = call(
            functools.partial(pair_body, chips, cap, part, cols),
            tuple(shape(block[1:], bf16) for _ in range(chips)),
            (S, V, V, V, V),
            cost=cost(1e6, 2e6),
        )(place, keep3, got3, mix, got_mix)
        blocks = [ready[0]] + [
            swap(ready[hop], "expert", experts, 2 * hop) for hop in range(1, chips)
        ]
    with jax.named_scope("product"):
        product = call(
            functools.partial(product_body, groups, part),
            shape((1, part, hid_width), f32),
            (V,) * (2 * groups),
            limit=40 * MIB,
            cost=cost(2 * groups * slots * part * hid_width, 4 * groups * slots * part),
        )(*pieces, *hids)
    with jax.named_scope("final"):
        out_grad, in_grad, combine = call(
            functools.partial(final_body, chips, cap, part, cols, loops),
            (
                shape((loops, share, part), f32),
                shape((loops, share, cols), f32),
                shape((ways, toks), f32),
            ),
            (S, V, V) + (V,) * chips,
            cost=cost(1e6, 2e6),
        )(place, routes_t, picks, *blocks)
    return (
        grad.reshape(hidden.shape),
        product,
        combine.T,
        in_grad,
        jnp.swapaxes(out_grad, 1, 2),
    )


def solution(mesh):
    return jax.shard_map(
        on_device,
        mesh=mesh,
        in_specs=(
            P(("dp", "expert"), None),
            P("dp", "expert", None, None),
            P("expert", None, None),
            P(),
            P(),
            P(("dp", "expert"), None),
            P(("dp", "expert"), None),
            P(("dp", "expert")),
        ),
        out_specs=(
            P("dp", "expert", None, None),
            P("expert", "dp", None),
            P(("dp", "expert"), None),
            P(None, "expert", "dp"),
            P(None, "dp", "expert"),
        ),
        check_vma=False,
    )
```

time: 254 us -> 78.9 us (0.31)
  waiting for transfers between devices: 127 us -> 36.7 us
  local copies, waits for them, and re-layouts: 45.3 us -> 3.48 us
  blocking collectives: 20.5 us -> 0 us
  matrix products: 16.2 us -> 0 us
  between operations: 14.8 us -> 0.79 us
  Pallas kernels: 0 us -> 12.6 us
  other arithmetic: 7.94 us -> 0.17 us
  starting transfers between devices: 21.5 us -> 24.9 us
    reduce_scatter x3 -> x0, waiting for transfers between devices: 90.8 us -> none  [the longest x1 53.8 us: on_device(): lax.psum_scatter(grad_b, 'dp', scatter_dimension=1, tiled=True)]
    ppermute x0 -> x15, waiting for transfers between devices: none -> 36.7 us  [swap(): return lax.ppermute(x, axis, [(i, i ^ mask) for i in range(size)])]
    all_to_all x5 -> x0, waiting for transfers between devices: 34 us -> none  [the longest x1 26.3 us: on_device(): lax.all_to_all(send_dy, 'expert', split_axis=0, concat_axis=0, tiled=True)]
    ppermute x0 -> x15, starting transfers between devices: none -> 24.9 us  [swap(): return lax.ppermute(x, axis, [(i, i ^ mask) for i in range(size)])]
    all_to_all x5 -> x0, starting transfers between devices: 21.4 us -> none  [the longest x1 6.33 us: on_device(): lax.all_to_all(send_mix, 'expert', split_axis=0, concat_axis=0, tiled=True)]
    gather x9 -> x0, local copies, waits for them, and re-layouts: 20.8 us -> none  [the longest x3 7.24 us: route_slots(): column = jnp.take_along_axis(before, target, axis=1)]
    all_gather x1 -> x0, blocking collectives: 20.5 us -> none  [on_device(): lax.all_gather(hidden_row_block, 'dp', axis=0, tiled=True)]
    dot_general x7 -> x0, matrix products: 16.2 us -> none  [the longest x1 3.87 us: on_device(): jnp.einsum('td,tlk->ldk', cotangent, masked_sum, preferred_element_type=j...]
  transfers between devices with their start and end apart: 9 -> 15, of which waited for: 7 -> 6; matrix products, arithmetic and copies ran while one was open for 17% -> 0% of each run, Pallas kernels for 0% -> 9%
where the time goes in v1:
time: 78.9 us; the launch traced here: 78.7 us
  waiting for transfers between devices  36.7 us (47%)
  starting transfers between devices  24.9 us (32%)
  Pallas kernels  12.6 us (16%)
  local copies, waits for them, and re-layouts  3.48 us (4%)
  between operations  0.79 us (1%)
    ppermute x15, waiting for transfers between devices, swap(): return lax.ppermute(x, axis, [(i, i ^ mask) for i in range(size)])  36.7 us
    ppermute x15, starting transfers between devices, swap(): return lax.ppermute(x, axis, [(i, i ^ mask) for i in range(size)])  24.9 us
    unnamed x18, local copies, waits for them, and re-layouts  3.42 us
    pallas_call x1, Pallas kernels, on_device(): pl.pallas_call(functools.partial(inner_body, steps), grid=(steps,), out_s...  2.69 us
    pallas_call x1, Pallas kernels, on_device(): call(functools.partial(product_body, groups, part), shape((1, part, hid_w...  2.68 us
    pallas_call x1, Pallas kernels, on_device(): call(functools.partial(adapter_body, groups, loops, chips, part, cols), (...  2.61 us
  transfers between devices with their start and end apart: 15, of which 6 were waited for; matrix products, arithmetic and copies ran while one was open for 0% of the time, Pallas kernels for 9%

profile of v1, /device:TPU:0, one launch (start us, length us, event | category | flops | bytes accessed | tf_op | source)
XLA Modules:
  0.0 78.7 jit_solution(10297776298837368189)
XLA Ops:
  0.7 0.1 pad_add_fusion.place
  0.7 1.4 %copy-done.4 = bf16[128,4096]{1,0:T(8,128)(2,1)S(1)} copy-done((bf16[128,4096]{1,0:T(8,128)(2,1)S(1)}, bf16[128,4096]{1,0:T(8,128)(2,1)}, u32[]{:S(2)}) %copy-start.4) | copy-done | bytes 1048600
  2.1 0.7 copy-done.5
  2.8 0.7 copy-done.7
  3.5 0.7 copy-done.8
  4.1 1.1 %route.1 = (bf16[4,16,4224]{2,1,0:T(8,128)(2,1)S(1)}, bf16[4,16,4224]{2,1,0:T(8,128)(2,1)S(1)}, bf16[128,128]{1,0:T(8,128)(2,1)S(1)}) custom-call(s32[2]{0:T(128)S(1)} %pad_add_fusion.place, s32[8,128]{1,0:T(8,128)S(1)} %bitcast.20, bf16[8,128]{1,0:T(8,128)(2,1)S(1)} %bitcast.22, s32[1,128]{1,0:T(1,128)S(1)} %bitcast.23, bf16[128,4096]{1,0:T(8,128)(2,1)S(1)} %copy-done.4), custom_call_target="tpu_custom_call" | custom-call | flops 134217728 | bytes 2097152 | tf_op jit(solution)/shard_map/route/pallas_call | solution.py:277
  5.2 0.5 collective-permute-start
  5.8 1.5 %collective-permute-done.sib = bf16[4,16,4224]{2,1,0:T(8,128)(2,1)S(1)} collective-permute-done((bf16[4,16,4224]{2,1,0:T(8,128)(2,1)S(1)}, bf16[4,16,4224]{2,1,0:T(8,128)(2,1)S(1)}, u32[]{:S(2)}, u32[]{:S(2)}) %collective-permute-start) | collective-permute-done | bytes 540704 | tf_op jit(solution)/shard_map/dispatch/ppermute | solution.py:33
  7.4 3.0 %collective-permute-start.1 = (bf16[2,16,4224]{2,1,0:T(8,128)(2,1)S(1)}, bf16[2,16,4224]{2,1,0:T(8,128)(2,1)S(1)}, u32[]{:S(2)}, u32[]{:S(2)}) collective-permute-start(bf16[2,16,4224]{2,1,0:T(8,128)(2,1)S(1)} %pad_maximum_fusion), channel_id=1, source_target_pairs={{0,2},{1,3},{2,0},{3,1},{4,6},{5,7},{6,4},{7,5},{8,10},{9,11},{10,... | collective-permute-start | bytes 811016 | tf_op jit(solution)/shard_map/dispatch/ppermute | solution.py:33
  10.4 2.7 %collective-permute-start.2 = (bf16[2,16,4224]{2,1,0:T(8,128)(2,1)S(1)}, bf16[2,16,4224]{2,1,0:T(8,128)(2,1)S(1)}, u32[]{:S(2)}, u32[]{:S(2)}) collective-permute-start(bf16[2,16,4224]{2,1,0:T(8,128)(2,1)S(1)} %pad_maximum_fusion.1), channel_id=1, source_target_pairs={{0,4},{1,5},{2,6},{3,7},{4,0},{5,1},{6,2},{7,3},{8,12},{9,13},{10,... | collective-permute-start | bytes 811016 | tf_op jit(solution)/shard_map/dispatch/ppermute | solution.py:33
  13.2 2.6 %collective-permute-start.9 = (bf16[128,768]{1,0:T(8,128)(2,1)S(1)}, bf16[128,768]{1,0:T(8,128)(2,1)S(1)}, u32[]{:S(2)}, u32[]{:S(2)}) collective-permute-start(bf16[128,768]{1,0:T(8,128)(2,1)S(1)} %bitcast.12), channel_id=1, source_target_pairs={{0,24},{8,16},{16,8},{24,0},{1,25},{9,17},{17,9},{25,1},{2,26},{10... | collective-permute-start | bytes 589832 | tf_op jit(solution)/shard_map/dispatch/ppermute | solution.py:33
  15.9 6.5 %collective-permute-done.1.refs_0_ = bf16[2,16,4224]{2,1,0:T(8,128)(2,1)S(1)} collective-permute-done((bf16[2,16,4224]{2,1,0:T(8,128)(2,1)S(1)}, bf16[2,16,4224]{2,1,0:T(8,128)(2,1)S(1)}, u32[]{:S(2)}, u32[]{:S(2)}) %collective-permute-start.1) | collective-permute-done | bytes 270368 | tf_op jit(solution)/shard_map/dispatch/ppermute | solution.py:33
  22.3 10.0 %collective-permute-done.2.refs_1_ = bf16[2,16,4224]{2,1,0:T(8,128)(2,1)S(1)} collective-permute-done((bf16[2,16,4224]{2,1,0:T(8,128)(2,1)S(1)}, bf16[2,16,4224]{2,1,0:T(8,128)(2,1)S(1)}, u32[]{:S(2)}, u32[]{:S(2)}) %collective-permute-start.2) | collective-permute-done | bytes 270368 | tf_op jit(solution)/shard_map/dispatch/ppermute | solution.py:33
  32.4 1.5 %arrive.1 = (bf16[128,4224]{1,0:T(8,128)(2,1)S(1)}, bf16[128,256]{1,0:T(8,128)(2,1)S(1)}, bf16[128,1280]{1,0:T(8,128)(2,1)S(1)}, bf16[128,1280]{1,0:T(8,128)(2,1...) custom-call(s32[2]{0:T(128)S(1)} %pad_add_fusion.place, bf16[2,4096,128]{2,1,0:T(8,128)(2,1)S(1)} %copy-done.1, ...), custom_call_target="tpu_custom_call" | custom-call | flops 268435456 | bytes 3145728 | tf_op jit(solution)/shard_map/arrive/pallas_call | solution.py:296
  33.9 1.6 %collective-permute-start.4 = (bf16[128,1280]{1,0:T(8,128)(2,1)S(1)}, bf16[128,1280]{1,0:T(8,128)(2,1)S(1)}, u32[]{:S(2)}, u32[]{:S(2)}) collective-permute-start(bf16[128,1280]{1,0:T(8,128)(2,1)S(1)} %get-tuple-element.31), channel_id=1, source_target_pairs={{0,8},{8,0},{16,24},{24,16},{1,9},{9,1},{17,25},{25,17},{2,10},{10... | collective-permute-start | bytes 983048 | tf_op jit(solution)/shard_map/columns/ppermute | solution.py:33
  35.5 1.5 %collective-permute-start.5 = (bf16[128,1280]{1,0:T(8,128)(2,1)S(1)}, bf16[128,1280]{1,0:T(8,128)(2,1)S(1)}, u32[]{:S(2)}, u32[]{:S(2)}) collective-permute-start(bf16[128,1280]{1,0:T(8,128)(2,1)S(1)} %get-tuple-element.32), channel_id=1, source_target_pairs={{0,16},{8,24},{16,0},{24,8},{1,17},{9,25},{17,1},{25,9},{2,18},{10... | collective-permute-start | bytes 983048 | tf_op jit(solution)/shard_map/columns/ppermute | solution.py:33
  37.0 0.5 collective-permute-start.6
  37.5 1.5 %collective-permute-start.8 = (bf16[128,768]{1,0:T(8,128)(2,1)S(1)}, bf16[128,768]{1,0:T(8,128)(2,1)S(1)}, u32[]{:S(2)}, u32[]{:S(2)}) collective-permute-start(bf16[128,768]{1,0:T(8,128)(2,1)S(1)} %bitcast.13), channel_id=1, source_target_pairs={{0,16},{8,24},{16,0},{24,8},{1,17},{9,25},{17,1},{25,9},{2,18},{10... | collective-permute-start | bytes 589832 | tf_op jit(solution)/shard_map/dispatch/ppermute | solution.py:33
  39.0 1.5 %collective-permute-start.7 = (bf16[128,768]{1,0:T(8,128)(2,1)S(1)}, bf16[128,768]{1,0:T(8,128)(2,1)S(1)}, u32[]{:S(2)}, u32[]{:S(2)}) collective-permute-start(bf16[128,768]{1,0:T(8,128)(2,1)S(1)} %bitcast.14), channel_id=1, source_target_pairs={{0,8},{8,0},{16,24},{24,16},{1,9},{9,1},{17,25},{25,17},{2,10},{10... | collective-permute-start | bytes 589832 | tf_op jit(solution)/shard_map/dispatch/ppermute | solution.py:33
  40.5 13.5 %collective-permute-done.8.refs_6_ = bf16[128,768]{1,0:T(8,128)(2,1)S(1)} collective-permute-done((bf16[128,768]{1,0:T(8,128)(2,1)S(1)}, bf16[128,768]{1,0:T(8,128)(2,1)S(1)}, u32[]{:S(2)}, u32[]{:S(2)}) %collective-permute-start.8) | collective-permute-done | bytes 196640 | tf_op jit(solution)/shard_map/dispatch/ppermute | solution.py:33
  54.0 2.6 %adapters.2 = (f32[4,32,1280]{2,1,0:T(8,128)S(1)}, f32[4,32,1280]{2,1,0:T(8,128)S(1)}) custom-call(s32[2]{0:T(128)S(1)} %pad_add_fusion.place, bf16[256,768]{1,0:T(8,128)(2,1)S(1)} %bitcast.18, bf16[128,1280]{1,0:T(8,128)(2,1)S(1)} %get-tuple-element.30.refs_0_, bf16[128,1280]{1,0:T(8,128)(2,1)S(1)} %collective-permute-done.4.refs_1_, ...), custom_call_target="tpu_custom_call" | custom-call | flops 536870912 | bytes 2097152 | tf_op jit(solution)/shard_map/adapters/pallas_call | solution.py:332
  56.7 0.1 collective-permute-start.10
  56.7 2.7 %inner.1 = (bf16[128,768]{1,0:T(8,128)(2,1)}, f32[128,128]{1,0:T(8,128)S(1)}) custom-call(bf16[128,4224]{1,0:T(8,128)(2,1)S(1)} %get-tuple-element.27.rows, bf16[4096,768]{1,0:T(8,128)(2,1)S(1)} %bitcast.11, bf16[128,256]{1,0:T(8,128)(2,1)S(1)} %get-tuple-element.28.masked, bf16[256,768]{1,0:T(8,128)(2,1)S(1)} %bitcast.19, bf16[128,768]{1,0:T(8,128)(2,1)S(1)} %bitcast.16), custom_call_target="tpu_custom_call" | custom-call | flops 805306368 | bytes 7340032 | tf_op jit(solution)/shard_map/inner/pallas_call | solution.py:308
  59.4 0.5 collective-permute-start.11
  59.9 0.9 %collective-permute-done.11.got_mix = f32[128,128]{1,0:T(8,128)S(1)} collective-permute-done((f32[128,128]{1,0:T(8,128)S(1)}, f32[128,128]{1,0:T(8,128)S(1)}, u32[]{:S(2)}, u32[]{:S(2)}) %collective-permute-start.11) | collective-permute-done | bytes 65568 | tf_op jit(solution)/shard_map/adapters/ppermute | solution.py:33
  60.8 0.6 adapters.3
  61.5 6.4 %collective-permute-start.12 = (bf16[32,1280]{1,0:T(8,128)(2,1)S(1)}, bf16[32,1280]{1,0:T(8,128)(2,1)S(1)}, u32[]{:S(2)}, u32[]{:S(2)}) collective-permute-start(bf16[32,1280]{1,0:T(8,128)(2,1)S(1)} %get-tuple-element.39), channel_id=1, source_target_pairs={{0,2},{1,3},{2,0},{3,1},{4,6},{5,7},{6,4},{7,5},{8,10},{9,11},{10,... | collective-permute-start | bytes 245768 | tf_op jit(solution)/shard_map/adapters/ppermute | solution.py:33
  67.9 1.1 %collective-permute-start.13 = (bf16[32,1280]{1,0:T(8,128)(2,1)S(1)}, bf16[32,1280]{1,0:T(8,128)(2,1)S(1)}, u32[]{:S(2)}, u32[]{:S(2)}) collective-permute-start(bf16[32,1280]{1,0:T(8,128)(2,1)S(1)} %get-tuple-element.40), channel_id=1, source_target_pairs={{0,4},{1,5},{2,6},{3,7},{4,0},{5,1},{6,2},{7,3},{8,12},{9,13},{10,... | collective-permute-start | bytes 245768 | tf_op jit(solution)/shard_map/adapters/ppermute | solution.py:33
  69.0 1.4 %collective-permute-start.14 = (bf16[32,1280]{1,0:T(8,128)(2,1)S(1)}, bf16[32,1280]{1,0:T(8,128)(2,1)S(1)}, u32[]{:S(2)}, u32[]{:S(2)}) collective-permute-start(bf16[32,1280]{1,0:T(8,128)(2,1)S(1)} %get-tuple-element.41), channel_id=1, source_target_pairs={{0,6},{1,7},{2,4},{3,5},{4,2},{5,3},{6,0},{7,1},{8,14},{9,15},{10,... | collective-permute-start | bytes 245768 | tf_op jit(solution)/shard_map/adapters/ppermute | solution.py:33
  70.3 2.7 %product.1 = f32[1,1024,768]{2,1,0:T(8,128)} custom-call(bf16[128,1280]{1,0:T(8,128)(2,1)S(1)} %get-tuple-element.30.refs_0_, bf16[128,1280]{1,0:T(8,128)(2,1)S(1)} %collective-permute-done.4.refs_1_, bf16[128,1280]{1,0:T(8,128)(2,1)S(1)} %collective-permute-done.5.refs_2_, bf16[128,1280]{1,0:T(8,128)(2,1)S(1)} %collective-permute-done.6.refs_3_, ...), custom_call_target="tpu_custom_call" | custom-call | flops 805306368 | bytes 2097152 | tf_op jit(solution)/shard_map/product/pallas_call | solution.py:355
  73.0 4.3 %collective-permute-done.13.refs_2_ = bf16[32,1280]{1,0:T(8,128)(2,1)S(1)} collective-permute-done((bf16[32,1280]{1,0:T(8,128)(2,1)S(1)}, bf16[32,1280]{1,0:T(8,128)(2,1)S(1)}, u32[]{:S(2)}, u32[]{:S(2)}) %collective-permute-start.13) | collective-permute-done | bytes 81952 | tf_op jit(solution)/shard_map/adapters/ppermute | solution.py:33
  77.3 1.3 %final.1 = (f32[2,16,1024]{2,1,0:T(8,128)}, f32[2,16,192]{2,1,0:T(8,128)}, f32[8,128]{1,0:T(8,128)}) custom-call(s32[2]{0:T(128)S(1)} %pad_add_fusion.place, s32[8,128]{1,0:T(8,128)S(1)} %bitcast.21, bf16[128,128]{1,0:T(8,128)(2,1)S(1)} %get-tuple-element.34.picks, bf16[32,1280]{1,0:T(8,128)(2,1)S(1)} %get-tuple-element.38.refs_0_, ...), custom_call_target="tpu_custom_call" | custom-call | flops 1000000 | bytes 2000000 | tf_op jit(solution)/shard_map/final/pallas_call | solution.py:363
  (29 shorter events, 0.3 us)
Async XLA Ops:
  0.6 12.6 %copy-start.2 = (bf16[1,1,128,768]{3,2,1,0:T(8,128)(2,1)S(1)}, bf16[1,1,128,768]{3,2,1,0:T(8,128)(2,1)}, u32[]{:S(2)}) copy-start(bf16[1,1,128,768]{3,2,1,0:T(8,128)(2,1)} %param.9) | copy-start | bytes 589828
  0.6 31.7 %copy-start.1 = (bf16[2,4096,128]{2,1,0:T(8,128)(2,1)S(1)}, bf16[2,4096,128]{2,1,0:T(8,128)(2,1)}, u32[]{:S(2)}) copy-start(bf16[2,4096,128]{2,1,0:T(8,128)(2,1)} %adapter_out.1) | copy-start | bytes 6291460
  0.7 1.4 %copy-start.4 = (bf16[128,4096]{1,0:T(8,128)(2,1)S(1)}, bf16[128,4096]{1,0:T(8,128)(2,1)}, u32[]{:S(2)}) copy-start(bf16[128,4096]{1,0:T(8,128)(2,1)} %cot.1) | copy-start | bytes 3145732
  2.1 0.7 copy-start.5
  2.8 0.7 copy-start.7
  3.5 0.7 copy-start.8
  5.2 2.1 %collective-permute-start = (bf16[4,16,4224]{2,1,0:T(8,128)(2,1)S(1)}, bf16[4,16,4224]{2,1,0:T(8,128)(2,1)S(1)}, u32[]{:S(2)}, u32[]{:S(2)}) collective-permute-start(bf16[4,16,4224]{2,1,0:T(8,128)(2,1)S(1)} %get-tuple-element.26), channel_id=1, source_target_pairs={{0,1},{1,0},{2,3},{3,2},{4,5},{5,4},{6,7},{7,6},{8,9},{9,8},{10,11... | collective-permute-start | bytes 1622024 | tf_op jit(solution)/shard_map/dispatch/ppermute | solution.py:33
  5.8 48.2 %copy-start.3 = (bf16[2,128,768]{2,1,0:T(8,128)(2,1)S(1)}, bf16[2,128,768]{2,1,0:T(8,128)(2,1)}, u32[]{:S(2)}) copy-start(bf16[2,128,768]{2,1,0:T(8,128)(2,1)} %param.11) | copy-start | bytes 1179652
  7.4 14.9 %collective-permute-start.1 = (bf16[2,16,4224]{2,1,0:T(8,128)(2,1)S(1)}, bf16[2,16,4224]{2,1,0:T(8,128)(2,1)S(1)}, u32[]{:S(2)}, u32[]{:S(2)}) collective-permute-start(bf16[2,16,4224]{2,1,0:T(8,128)(2,1)S(1)} %pad_maximum_fusion), channel_id=1, source_target_pairs={{0,2},{1,3},{2,0},{3,1},{4,6},{5,7},{6,4},{7,5},{8,10},{9,11},{10,... | collective-permute-start | bytes 811016 | tf_op jit(solution)/shard_map/dispatch/ppermute | solution.py:33
  10.4 21.9 %collective-permute-start.2 = (bf16[2,16,4224]{2,1,0:T(8,128)(2,1)S(1)}, bf16[2,16,4224]{2,1,0:T(8,128)(2,1)S(1)}, u32[]{:S(2)}, u32[]{:S(2)}) collective-permute-start(bf16[2,16,4224]{2,1,0:T(8,128)(2,1)S(1)} %pad_maximum_fusion.1), channel_id=1, source_target_pairs={{0,4},{1,5},{2,6},{3,7},{4,0},{5,1},{6,2},{7,3},{8,12},{9,13},{10,... | collective-permute-start | bytes 811016 | tf_op jit(solution)/shard_map/dispatch/ppermute | solution.py:33
  13.1 19.2 %collective-permute-start.3 = (bf16[2,16,4224]{2,1,0:T(8,128)(2,1)S(1)}, bf16[2,16,4224]{2,1,0:T(8,128)(2,1)S(1)}, u32[]{:S(2)}, u32[]{:S(2)}) collective-permute-start(bf16[2,16,4224]{2,1,0:T(8,128)(2,1)S(1)} %pad_maximum_fusion.2), channel_id=1, source_target_pairs={{0,6},{1,7},{2,4},{3,5},{4,2},{5,3},{6,0},{7,1},{8,14},{9,15},{10,... | collective-permute-start | bytes 811016 | tf_op jit(solution)/shard_map/dispatch/ppermute | solution.py:33
  13.2 43.5 %copy-start = (bf16[1,4096,768]{2,1,0:T(8,128)(2,1)S(1)}, bf16[1,4096,768]{2,1,0:T(8,128)(2,1)}, u32[]{:S(2)}) copy-start(bf16[1,4096,768]{2,1,0:T(8,128)(2,1)} %param.10) | copy-start | bytes 18874372
  13.2 25.8 %collective-permute-start.9 = (bf16[128,768]{1,0:T(8,128)(2,1)S(1)}, bf16[128,768]{1,0:T(8,128)(2,1)S(1)}, u32[]{:S(2)}, u32[]{:S(2)}) collective-permute-start(bf16[128,768]{1,0:T(8,128)(2,1)S(1)} %bitcast.12), channel_id=1, source_target_pairs={{0,24},{8,16},{16,8},{24,0},{1,25},{9,17},{17,9},{25,1},{2,26},{10... | collective-permute-start | bytes 589832 | tf_op jit(solution)/shard_map/dispatch/ppermute | solution.py:33
  33.9 20.1 %collective-permute-start.4 = (bf16[128,1280]{1,0:T(8,128)(2,1)S(1)}, bf16[128,1280]{1,0:T(8,128)(2,1)S(1)}, u32[]{:S(2)}, u32[]{:S(2)}) collective-permute-start(bf16[128,1280]{1,0:T(8,128)(2,1)S(1)} %get-tuple-element.31), channel_id=1, source_target_pairs={{0,8},{8,0},{16,24},{24,16},{1,9},{9,1},{17,25},{25,17},{2,10},{10... | collective-permute-start | bytes 983048 | tf_op jit(solution)/shard_map/columns/ppermute | solution.py:33
  35.5 18.5 %collective-permute-start.5 = (bf16[128,1280]{1,0:T(8,128)(2,1)S(1)}, bf16[128,1280]{1,0:T(8,128)(2,1)S(1)}, u32[]{:S(2)}, u32[]{:S(2)}) collective-permute-start(bf16[128,1280]{1,0:T(8,128)(2,1)S(1)} %get-tuple-element.32), channel_id=1, source_target_pairs={{0,16},{8,24},{16,0},{24,8},{1,17},{9,25},{17,1},{25,9},{2,18},{10... | collective-permute-start | bytes 983048 | tf_op jit(solution)/shard_map/columns/ppermute | solution.py:33
  37.0 17.0 %collective-permute-start.6 = (bf16[128,1280]{1,0:T(8,128)(2,1)S(1)}, bf16[128,1280]{1,0:T(8,128)(2,1)S(1)}, u32[]{:S(2)}, u32[]{:S(2)}) collective-permute-start(bf16[128,1280]{1,0:T(8,128)(2,1)S(1)} %get-tuple-element.33), channel_id=1, source_target_pairs={{0,24},{8,16},{16,8},{24,0},{1,25},{9,17},{17,9},{25,1},{2,26},{10... | collective-permute-start | bytes 983048 | tf_op jit(solution)/shard_map/columns/ppermute | solution.py:33
  37.5 16.5 %collective-permute-start.8 = (bf16[128,768]{1,0:T(8,128)(2,1)S(1)}, bf16[128,768]{1,0:T(8,128)(2,1)S(1)}, u32[]{:S(2)}, u32[]{:S(2)}) collective-permute-start(bf16[128,768]{1,0:T(8,128)(2,1)S(1)} %bitcast.13), channel_id=1, source_target_pairs={{0,16},{8,24},{16,0},{24,8},{1,17},{9,25},{17,1},{25,9},{2,18},{10... | collective-permute-start | bytes 589832 | tf_op jit(solution)/shard_map/dispatch/ppermute | solution.py:33
  39.0 15.0 %collective-permute-start.7 = (bf16[128,768]{1,0:T(8,128)(2,1)S(1)}, bf16[128,768]{1,0:T(8,128)(2,1)S(1)}, u32[]{:S(2)}, u32[]{:S(2)}) collective-permute-start(bf16[128,768]{1,0:T(8,128)(2,1)S(1)} %bitcast.14), channel_id=1, source_target_pairs={{0,8},{8,0},{16,24},{24,16},{1,9},{9,1},{17,25},{25,17},{2,10},{10... | collective-permute-start | bytes 589832 | tf_op jit(solution)/shard_map/dispatch/ppermute | solution.py:33
  56.7 4.2 %collective-permute-start.10 = (f32[4,32,1280]{2,1,0:T(8,128)S(1)}, f32[4,32,1280]{2,1,0:T(8,128)S(1)}, u32[]{:S(2)}, u32[]{:S(2)}) collective-permute-start(f32[4,32,1280]{2,1,0:T(8,128)S(1)} %get-tuple-element.36), channel_id=1, source_target_pairs={{0,1},{1,0},{2,3},{3,2},{4,5},{5,4},{6,7},{7,6},{8,9},{9,8},{10,11... | collective-permute-start | bytes 1966088 | tf_op jit(solution)/shard_map/adapters/ppermute | solution.py:33
  59.4 1.4 %collective-permute-start.11 = (f32[128,128]{1,0:T(8,128)S(1)}, f32[128,128]{1,0:T(8,128)S(1)}, u32[]{:S(2)}, u32[]{:S(2)}) collective-permute-start(f32[128,128]{1,0:T(8,128)S(1)} %get-tuple-element.37.mix), channel_id=1, source_target_pairs={{0,1},{1,0},{2,3},{3,2},{4,5},{5,4},{6,7},{7,6},{8,9},{9,8},{10,11... | collective-permute-start | bytes 196616 | tf_op jit(solution)/shard_map/adapters/ppermute | solution.py:33
  60.8 16.5 %copy-start.6 = (s32[128,8]{0,1:T(8,128)S(1)}, s32[128,8]{0,1:T(8,128)}, u32[]{:S(2)}) copy-start(s32[128,8]{0,1:T(8,128)} %param.14) | copy-start | bytes 12292
  61.5 11.6 %collective-permute-start.12 = (bf16[32,1280]{1,0:T(8,128)(2,1)S(1)}, bf16[32,1280]{1,0:T(8,128)(2,1)S(1)}, u32[]{:S(2)}, u32[]{:S(2)}) collective-permute-start(bf16[32,1280]{1,0:T(8,128)(2,1)S(1)} %get-tuple-element.39), channel_id=1, source_target_pairs={{0,2},{1,3},{2,0},{3,1},{4,6},{5,7},{6,4},{7,5},{8,10},{9,11},{10,... | collective-permute-start | bytes 245768 | tf_op jit(solution)/shard_map/adapters/ppermute | solution.py:33
  67.9 9.5 %collective-permute-start.13 = (bf16[32,1280]{1,0:T(8,128)(2,1)S(1)}, bf16[32,1280]{1,0:T(8,128)(2,1)S(1)}, u32[]{:S(2)}, u32[]{:S(2)}) collective-permute-start(bf16[32,1280]{1,0:T(8,128)(2,1)S(1)} %get-tuple-element.40), channel_id=1, source_target_pairs={{0,4},{1,5},{2,6},{3,7},{4,0},{5,1},{6,2},{7,3},{8,12},{9,13},{10,... | collective-permute-start | bytes 245768 | tf_op jit(solution)/shard_map/adapters/ppermute | solution.py:33
  69.0 8.4 %collective-permute-start.14 = (bf16[32,1280]{1,0:T(8,128)(2,1)S(1)}, bf16[32,1280]{1,0:T(8,128)(2,1)S(1)}, u32[]{:S(2)}, u32[]{:S(2)}) collective-permute-start(bf16[32,1280]{1,0:T(8,128)(2,1)S(1)} %get-tuple-element.41), channel_id=1, source_target_pairs={{0,6},{1,7},{2,4},{3,5},{4,2},{5,3},{6,0},{7,1},{8,14},{9,15},{10,... | collective-permute-start | bytes 245768 | tf_op jit(solution)/shard_map/adapters/ppermute | solution.py:33

commit v2 on v1

v2 whole, which is shorter than its diff:
```python
import functools

import jax
import jax.numpy as jnp
from jax import lax
from jax.experimental import pallas as pl
from jax.experimental.pallas import tpu as pltpu
from jax.sharding import PartitionSpec as P

bf16 = jnp.bfloat16
f32 = jnp.float32
LANES = 128
MIB = 1 << 20
V, A = pltpu.VMEM, pl.ANY


def dot(a, b, dims):
    return lax.dot_general(a, b, (dims, ((), ())), preferred_element_type=f32)


def nn(a, b):
    return dot(a, b, ((1,), (0,)))


def nt(a, b):
    return dot(a, b, ((1,), (1,)))


def tn(a, b):
    return dot(a, b, ((0,), (0,)))


def swap(x, axis, size, mask):
    return lax.ppermute(x, axis, [(i, i ^ mask) for i in range(size)])


def shape(dims, kind):
    return jax.ShapeDtypeStruct(dims, kind)


def here():
    return lax.axis_index("expert"), lax.axis_index("dp")


def call(body, out_shape, ins, scratch=(), limit=24, flops=0, nbytes=0):
    return pl.pallas_call(
        body,
        out_shape=out_shape,
        in_specs=[pl.BlockSpec(memory_space=s) for s in ins],
        out_specs=jax.tree.map(lambda _: pl.BlockSpec(memory_space=V), out_shape),
        scratch_shapes=list(scratch),
        cost_estimate=pl.CostEstimate(
            flops=int(flops), bytes_accessed=int(nbytes), transcendentals=0
        ),
        compiler_params=pltpu.CompilerParams(vmem_limit_bytes=limit * MIB),
    )


def owner_column(place, chips, experts):
    j = lax.broadcasted_iota(jnp.int32, (experts, 1), 0)
    half, hop = j // chips, j % chips
    return ((place[0] // 2) ^ hop) * 2 + ((place[0] % 2) ^ half)


def route_body(chips, cap, ways, small, cot, keep, give, picks, mixed):
    experts = 2 * chips
    toks, width = cot.shape
    owner = owner_column(here(), chips, experts).astype(f32)
    named = jnp.zeros((experts, toks), f32)
    weight = jnp.zeros((experts, toks), f32)
    for k in range(ways):
        hit = small[k : k + 1, :] == owner
        named = named + jnp.where(hit, 1.0, 0.0)
        weight = weight + jnp.where(hit, small[ways + k : ways + k + 1, :], 0.0)
    earlier = lax.broadcasted_iota(jnp.int32, (toks, toks), 0) < lax.broadcasted_iota(
        jnp.int32, (toks, toks), 1
    )
    before = nn(named.astype(bf16), jnp.where(earlier, 1.0, 0.0).astype(bf16))
    spot = jnp.where(named > 0.0, before, -1.0)
    slot = lax.broadcasted_iota(jnp.int32, (cap, toks), 0).astype(f32)
    for j in range(experts):
        hit = spot[j : j + 1, :] == slot
        rows = slice(j * cap, (j + 1) * cap)
        picks[rows, :] = jnp.where(hit, 1.0, 0.0).astype(bf16)
        mixed[rows, :] = jnp.where(hit, weight[j : j + 1, :], 0.0).astype(bf16)
    loop_rows = lax.broadcasted_iota(jnp.int32, (LANES, toks), 0).astype(f32)
    loop_rows = jnp.where(loop_rows == small[2 * ways : 2 * ways + 1, :], 1.0, 0.0).astype(bf16)
    mix = nt(mixed[...], loop_rows).astype(bf16)
    half = chips * cap
    keep[:, :, width:] = mix[:half].reshape(chips, cap, LANES)
    give[:, :, width:] = mix[half:].reshape(chips, cap, LANES)
    step = 1024 if width % 1024 == 0 else width
    for n in range(0, width, step):
        at = slice(n, n + step)
        got = nn(picks[...], cot[:, at]).astype(bf16)
        keep[:, :, at] = got[:half].reshape(chips, cap, step)
        give[:, :, at] = got[half:].reshape(chips, cap, step)


def sources(place, chips):
    z, c = place[0] // 2, place[0] % 2
    return [(z ^ hop) * 2 + (c ^ half) for hop in range(chips) for half in range(2)]


def pack_far_body(chips, keep, sib, *far):
    for n, block in enumerate(far):
        hop = chips - len(far) + n
        block[0] = keep[hop]
        block[1] = sib[hop]


def pack_near_body(chips, cap, keep, sib, hidden, _, ordered, *near):
    for n, block in enumerate(near):
        block[0] = keep[1 + n]
        block[1] = sib[1 + n]
    for n, source in enumerate(sources(here(), chips)):
        rows = pl.ds(pl.multiple_of(source * cap, cap), cap)
        ordered[n * cap : (n + 1) * cap, :] = hidden[rows, :]


def arrive_body(groups, near, adapter_out, *refs):
    blocks = refs[: -2 - groups]
    rows, masked, parts = refs[-2 - groups], refs[-1 - groups], refs[-groups:]
    loops, width, rank = adapter_out.shape
    part = width // groups
    at = 0
    for n, block in enumerate(blocks):
        halves = (block[0],) if near and n < 2 else (block[0], block[1])
        for piece in halves:
            rows[at : at + piece.shape[0], :] = piece
            at += piece.shape[0]
    mix_block = rows[:, width:]
    mix = mix_block.astype(f32)
    weight = jnp.sum(mix, axis=1, keepdims=True)
    for hop in range(groups):
        start = pl.multiple_of((here()[1] ^ hop) * part, part)
        parts[hop][:, :part] = (weight * rows[:, pl.ds(start, part)].astype(f32)).astype(bf16)
    masks = [mix[:, l : l + 1] > 0.0 for l in range(loops)]
    proj = jnp.zeros((rows.shape[0], rank), f32)
    for l in range(loops):
        proj = proj + jnp.where(masks[l], nn(rows[:, :width], adapter_out[l]), 0.0)
    proj = proj.astype(bf16).astype(f32)
    for l in range(loops):
        masked[:, l * rank : (l + 1) * rank] = jnp.where(masks[l], proj, 0.0).astype(bf16)
    weighted = (weight * proj).astype(bf16)
    for hop in range(groups):
        parts[hop][:, part : part + rank] = weighted
        parts[hop][:, part + rank :] = mix_block


def inner_body(chips, cap, early, late, down, masked1, masked2, adapter_in, hidden, *refs):
    grad_out, mix_out = refs
    width, hid_width = down.shape
    step = 256 if hid_width % 256 == 0 else hid_width
    rows = jnp.concatenate([early[...], late[...]], axis=0)
    masked = jnp.concatenate([masked1[...], masked2[...]], axis=0)
    weight = jnp.sum(rows[:, width:].astype(f32), axis=1, keepdims=True)
    sums = jnp.zeros((mix_out.shape[0], 1), f32)
    order = sources(here(), chips)
    for at in range(0, hid_width, step):
        cols = slice(at, at + step)
        grad = nn(masked, adapter_in[:, cols]) + nn(rows[:, :width], down[:, cols])
        sums = sums + jnp.sum(hidden[: mix_out.shape[0], cols].astype(f32) * grad, axis=1, keepdims=True)
        scaled = (weight * grad).astype(bf16)
        for n, source in enumerate(order):
            spot = pl.ds(pl.multiple_of(source * cap, cap), cap)
            grad_out[spot, cols] = scaled[n * cap : (n + 1) * cap]
    mix_out[...] = jnp.broadcast_to(sums, mix_out.shape)


def adapter_sums(groups, loops, cols, start, adapter_in, rows, hids):
    slots = rows[0].shape[0]
    rank = adapter_in.shape[0] // loops
    hid_width = adapter_in.shape[1]
    part = rows[0].shape[1] - rank - LANES
    wide = wide_of(cols)
    row = lax.broadcasted_iota(jnp.int32, (hid_width, wide), 0)
    lane = lax.broadcasted_iota(jnp.int32, (hid_width, wide), 1)
    pick = (row == lane + here()[1] * cols) & (lane < cols)
    pick = jnp.where(pick, 1.0, 0.0).astype(bf16)
    total = hids.shape[0] // groups
    hid = jnp.concatenate(
        [hids[g * total + start : g * total + start + slots, :] for g in range(groups)], axis=0
    )
    tail = jnp.concatenate([r[:, part:] for r in rows], axis=0).astype(f32)
    body = jnp.concatenate([r[:, :part] for r in rows], axis=0)
    down = nt(hid, adapter_in[...])
    picked = nn(hid, pick).astype(bf16)
    masks = [tail[:, rank + l : rank + l + 1] > 0.0 for l in range(loops)]
    left = [jnp.where(masks[l], down[:, l * rank : (l + 1) * rank], 0.0) for l in range(loops)]
    out = tn(jnp.concatenate(left, axis=1).astype(bf16), body)
    left = [jnp.where(masks[l], tail[:, :rank], 0.0) for l in range(loops)]
    return out, tn(jnp.concatenate(left, axis=1).astype(bf16), picked)


def wide_of(cols):
    return -(-(cols + 4) // LANES) * LANES


def adapter_first_body(groups, loops, cols, adapter_in, hids, *refs):
    rows, (out, inn) = refs[:groups], refs[groups:]
    out[...], inn[...] = adapter_sums(groups, loops, cols, 0, adapter_in, rows, hids)


def adapter_last_body(groups, loops, chips, cap, cols, adapter_in, out, inn, mix, hids, *refs):
    rows, (keep, give, sums, narrow) = refs[:groups], refs[groups:]
    slots = rows[0].shape[0]
    rank = adapter_in.shape[0] // loops
    part = out.shape[1]
    share = rank // (2 * chips)
    start = mix.shape[0] - slots
    more = adapter_sums(groups, loops, cols, start, adapter_in, rows, hids)
    sums[...] = out[...] + more[0]
    narrow[...] = inn[...] + more[1]
    owners = sources(here(), chips)
    lane = lax.broadcasted_iota(jnp.int32, (cap, narrow.shape[1]), 1)
    for n, owner in enumerate(owners):
        hop, target = n // 2, (keep, give)[n % 2]
        for l in range(loops):
            src = pl.ds(pl.multiple_of(l * rank + owner * share, share), share)
            dst = slice(l * share, (l + 1) * share)
            target[hop, dst, :part] = sums[src, :]
            target[hop, dst, part:] = narrow[src, :]
        value = mix[n * cap : (n + 1) * cap, :1]
        target[hop, :cap, part:] = jnp.where(lane == cols, value, target[hop, :cap, part:])


def pair_body(chips, cap, part, cols, keep, got, *outs):
    wide = keep.shape[2] - part
    lane = lax.broadcasted_iota(jnp.int32, (cap, wide), 1)
    for hop in range(chips):
        outs[hop][...] = (keep[hop] + got[hop]).astype(bf16)
        tail = keep[hop, :cap, part:] + got[hop, :cap, part:]
        for n, block in enumerate((keep, got)):
            value = block[hop, :cap, part + cols : part + cols + 1]
            high = value.astype(bf16).astype(f32)
            tail = jnp.where(lane == cols + 2 * n, high, tail)
            tail = jnp.where(lane == cols + 2 * n + 1, value - high, tail)
        outs[hop][:cap, part:] = tail.astype(bf16)


def final_body(chips, cap, cols, small, picks, *refs):
    blocks = refs[:chips]
    out_grad, in_grad, combine = refs[chips:]
    loops, share, part = out_grad.shape
    total = blocks[0][...].astype(f32)
    for hop in range(1, chips):
        total = total + blocks[hop][...].astype(f32)
    for l in range(loops):
        rows = slice(l * share, (l + 1) * share)
        out_grad[l] = total[rows, :part]
        in_grad[l] = total[rows, part : part + cols]
    experts = 2 * chips
    owner = owner_column(here(), chips, experts).astype(f32)
    routes = small[: combine.shape[0], :]
    sums = jnp.zeros(combine.shape, f32)
    for j in range(experts):
        half, hop = j // chips, j % chips
        words = blocks[hop][:cap, part:].astype(f32)
        at = cols + 2 * half
        value = words[:, at : at + 1] + words[:, at + 1 : at + 2]
        pick = picks[j * cap : (j + 1) * cap, :].astype(f32)
        by_token = jnp.sum(pick * value, axis=0, keepdims=True)
        sums = sums + jnp.where(routes == owner[j : j + 1, :], by_token, 0.0)
    combine[...] = sums


def product_body(groups, *refs):
    early, late = refs[:groups], refs[groups : 2 * groups]
    hids, out = refs[2 * groups :]
    part = out.shape[1]
    rights = hids[...]
    step = 256 if part % 256 == 0 else LANES
    for at in range(0, part, step):
        left = [p[:, at : at + step] for pair in zip(early, late) for p in pair]
        out[0, at : at + step, :] = tn(jnp.concatenate(left, axis=0), rights)


def on_device(cotangent, hidden, down_matrix, adapter_in, adapter_out, probs, routes, token_loop):
    experts = lax.axis_size("expert")
    groups = lax.axis_size("dp")
    chips = experts // 2
    toks, width = cotangent.shape
    loops, rank, hid_width = adapter_in.shape
    ways = routes.shape[1]
    slots = hidden.shape[2]
    cap = slots // experts
    part = width // groups
    cols = hid_width // groups
    wide = wide_of(cols)
    share = rank // experts
    half = slots // 2
    flat_in = adapter_in.reshape(loops * rank, hid_width)
    small = jnp.concatenate(
        [routes.T.astype(f32), probs.T.astype(f32), token_loop.astype(f32).reshape(1, toks)]
    )

    with jax.named_scope("route"):
        packed = shape((chips, cap, width + LANES), bf16)
        keep, give, picks = call(
            functools.partial(route_body, chips, cap, ways),
            (packed, packed, shape((slots, toks), bf16)),
            (V, V),
            scratch=(pltpu.VMEM((slots, toks), bf16),),
            flops=2 * slots * toks * width,
            nbytes=6 * toks * width,
        )(small, cotangent)
        sib = swap(give, "expert", experts, 1)
    with jax.named_scope("dispatch"):
        pair = shape((2, cap, width + LANES), bf16)
        middle = chips // 2
        packs = call(
            functools.partial(pack_far_body, chips),
            (pair,) * (chips - middle),
            (V, V),
            nbytes=2 * slots * width,
        )(keep, sib)
        far = [swap(x, "expert", experts, 2 * (middle + n)) for n, x in enumerate(packs)]
        got = call(
            functools.partial(pack_near_body, chips, cap),
            (shape((slots, hid_width), bf16),) + (pair,) * (middle - 1),
            (V, V, V, A),
            nbytes=2 * slots * width,
        )(keep, sib, hidden.reshape(slots, hid_width), packs[0])
        near = [swap(x, "expert", experts, 2 * (1 + n)) for n, x in enumerate(got[1:])]
        hids, hop = got[0], 1
        while hop < groups:
            hids = jnp.concatenate([hids, swap(hids, "dp", groups, hop)])
            hop *= 2
    with jax.named_scope("arrive"):
        rows, masked, parts = [], [], []
        for own, blocks in ((True, [keep, sib] + near), (False, far)):
            got = call(
                functools.partial(arrive_body, groups, own),
                (shape((half, width + LANES), bf16), shape((half, loops * rank), bf16))
                + (shape((half, part + rank + LANES), bf16),) * groups,
                (V,) * (1 + len(blocks)),
                flops=2 * half * width * loops * rank,
                nbytes=4 * half * width,
            )(adapter_out, *blocks)
            rows.append(got[0])
            masked.append(got[1])
            parts.append(
                [got[2]] + [swap(got[2 + hop], "dp", groups, hop) for hop in range(1, groups)]
            )
    with jax.named_scope("inner"):
        grad, mix = call(
            functools.partial(inner_body, chips, cap),
            (shape((slots, hid_width), bf16), shape((slots, LANES), f32)),
            (V,) * 7,
            flops=2 * slots * width * hid_width,
            nbytes=2 * width * hid_width,
        )(*rows, down_matrix[0], *masked, flat_in, hids)
    with jax.named_scope("adapters"):
        work = 2 * groups * half * loops * rank * (part + hid_width + wide)
        sums = (shape((loops * rank, part), f32), shape((loops * rank, wide), f32))
        out, inn = call(
            functools.partial(adapter_first_body, groups, loops, cols),
            sums,
            (V,) * (2 + groups),
            flops=work,
            nbytes=2 * groups * half * part,
        )(flat_in, hids, *parts[0])
        block = (chips, loops * share, part + wide)
        keep3, give3 = call(
            functools.partial(adapter_last_body, groups, loops, chips, cap, cols),
            (shape(block, f32), shape(block, f32)),
            (V,) * (5 + groups),
            scratch=[pltpu.VMEM(s.shape, f32) for s in sums],
            flops=work,
            nbytes=2 * groups * half * part,
        )(flat_in, out, inn, mix, hids, *parts[1])
        got3 = swap(give3, "expert", experts, 1)
        ready = call(
            functools.partial(pair_body, chips, cap, part, cols),
            (shape(block[1:], bf16),) * chips,
            (V, V),
            nbytes=1e6,
        )(keep3, got3)
        blocks = list(ready)
        for hop in reversed(range(1, chips)):
            blocks[hop] = swap(ready[hop], "expert", experts, 2 * hop)
    with jax.named_scope("product"):
        product = call(
            functools.partial(product_body, groups),
            shape((1, part, hid_width), f32),
            (V,) * (2 * groups + 1),
            limit=40,
            flops=2 * groups * slots * part * hid_width,
            nbytes=4 * groups * slots * part,
        )(*parts[0], *parts[1], hids)
    with jax.named_scope("final"):
        out_grad, in_grad, combine = call(
            functools.partial(final_body, chips, cap, cols),
            (
                shape((loops, share, part), f32),
                shape((loops, share, cols), f32),
                shape((ways, toks), f32),
            ),
            (V,) * (2 + chips),
            nbytes=1e6,
        )(small, picks, *blocks)
    return (
        grad.reshape(hidden.shape),
        product,
        combine.T,
        in_grad,
        jnp.swapaxes(out_grad, 1, 2),
    )


def solution(mesh):
    return jax.shard_map(
        on_device,
        mesh=mesh,
        in_specs=(
            P(("dp", "expert"), None),
            P("dp", "expert", None, None),
            P("expert", None, None),
            P(),
            P(),
            P(("dp", "expert"), None),
            P(("dp", "expert"), None),
            P(("dp", "expert")),
        ),
        out_specs=(
            P("dp", "expert", None, None),
            P("expert", "dp", None),
            P(("dp", "expert"), None),
            P(None, "expert", "dp"),
            P(None, "dp", "expert"),
        ),
        check_vma=False,
    )
```

time: 78.9 us -> 62.6 us (0.79)
  waiting for transfers between devices: 36.7 us -> 24.8 us
  Pallas kernels: 12.6 us -> 8.58 us
  other arithmetic: 0.17 us -> 2.21 us
  starting transfers between devices: 24.9 us -> 23.6 us
  local copies, waits for them, and re-layouts: 3.48 us -> 2.37 us
    ppermute x15 -> x16, waiting for transfers between devices: 36.7 us -> 24.8 us  [swap(): return lax.ppermute(x, axis, [(i, i ^ mask) for i in range(size)])]
    pallas_call x7 -> x11, Pallas kernels: 12.6 us -> 8.58 us  [the longest x1 2.67 us: on_device(): call(functools.partial(product_body, groups), shape((1, part, hid_width),...]
    convert_element_type x0 -> x2, other arithmetic: none -> 1.37 us  [the longest x1 0.69 us: on_device(): routes.T.astype(f32)]
    ppermute x15 -> x16, starting transfers between devices: 24.9 us -> 23.6 us  [swap(): return lax.ppermute(x, axis, [(i, i ^ mask) for i in range(size)])]
    unnamed x18 -> x14, local copies, waits for them, and re-layouts: 3.42 us -> 2.35 us
    reshape x0 -> x1, other arithmetic: none -> 0.81 us  [on_device(): token_loop.astype(f32).reshape(1, toks)]
  transfers between devices with their start and end apart: 15 -> 16, of which waited for: 6 -> 9; matrix products, arithmetic and copies ran while one was open for 0% -> 0% of each run, Pallas kernels for 9% -> 10%
where the time goes in v2:
time: 62.6 us; the launch traced here: 62.4 us
  waiting for transfers between devices  24.8 us (40%)
  starting transfers between devices  23.6 us (38%)
  Pallas kernels  8.58 us (14%)
  local copies, waits for them, and re-layouts  2.37 us (4%)
  other arithmetic  2.21 us (4%)
  between operations  0.8 us (1%)
    ppermute x16, waiting for transfers between devices, swap(): return lax.ppermute(x, axis, [(i, i ^ mask) for i in range(size)])  24.8 us
    ppermute x16, starting transfers between devices, swap(): return lax.ppermute(x, axis, [(i, i ^ mask) for i in range(size)])  23.6 us
    pallas_call x1, Pallas kernels, on_device(): call(functools.partial(product_body, groups), shape((1, part, hid_width),...  2.67 us
    unnamed x14, local copies, waits for them, and re-layouts  2.35 us
    pallas_call x1, Pallas kernels, on_device(): call(functools.partial(inner_body, chips, cap), (shape((slots, hid_width)...  1.73 us
  transfers between devices with their start and end apart: 16, of which 9 were waited for; matrix products, arithmetic and copies ran while one was open for 0% of the time, Pallas kernels for 10%

profile of v2, /device:TPU:0, one launch (start us, length us, event | category | flops | bytes accessed | tf_op | source)
XLA Modules:
  0.0 62.4 jit_solution(15685316285487380598)
XLA Ops:
  0.6 0.8 %convert_bitcast_fusion.2 = f32[1,128]{1,0:T(1,128)S(1)} fusion(s32[128]{0:T(128)} %param.15), kind=kLoop, calls=%fused_computation.7 | loop fusion | flops 128 | bytes 1024 | tf_op jit(solution)/shard_map/reshape | solution.py:295
  1.4 0.7 %convert_bitcast_fusion = f32[8,128]{1,0:T(8,128)S(1)} fusion(bf16[128,8]{0,1:T(8,128)(2,1)} %param.13), kind=kLoop, calls=%fused_computation.5 | loop fusion | flops 1024 | bytes 6144 | tf_op jit(solution)/shard_map/convert_element_type | solution.py:295
  2.1 0.7 %convert_bitcast_fusion.1 = f32[8,128]{1,0:T(8,128)S(1)} fusion(s32[128,8]{0,1:T(8,128)} %param.14), kind=kLoop, calls=%fused_computation.6 | loop fusion | flops 1024 | bytes 8192 | tf_op jit(solution)/shard_map/convert_element_type | solution.py:295
  2.8 1.2 %copy-done.2 = bf16[128,4096]{1,0:T(8,128)(2,1)S(1)} copy-done((bf16[128,4096]{1,0:T(8,128)(2,1)S(1)}, bf16[128,4096]{1,0:T(8,128)(2,1)}, u32[]{:S(2)}) %copy-start.2) | copy-done | bytes 1048600
  5.1 1.6 %collective-permute-done.sib.refs_1_ = bf16[4,16,4224]{2,1,0:T(8,128)(2,1)S(1)} collective-permute-done((bf16[4,16,4224]{2,1,0:T(8,128)(2,1)S(1)}, bf16[4,16,4224]{2,1,0:T(8,128)(2,1)S(1)}, u32[]{:S(2)}, u32[]{:S(2)}) %collective-permute-start) | collective-permute-done | bytes 540704 | tf_op jit(solution)/shard_map/route/ppermute | solution.py:34
  6.8 1.1 %copy-done.3 = bf16[1,1,128,768]{3,2,1,0:T(8,128)(2,1)S(1)} copy-done((bf16[1,1,128,768]{3,2,1,0:T(8,128)(2,1)S(1)}, bf16[1,1,128,768]{3,2,1,0:T(8,128)(2,1)}, u32[]{:S(2)}) %copy-start.3) | copy-done | bytes 196632
  7.9 2.9 %collective-permute-start.4 = (bf16[128,768]{1,0:T(8,128)(2,1)S(1)}, bf16[128,768]{1,0:T(8,128)(2,1)S(1)}, u32[]{:S(2)}, u32[]{:S(2)}) collective-permute-start(bf16[128,768]{1,0:T(8,128)(2,1)S(1)} %get-tuple-element.46), channel_id=1, source_target_pairs={{0,8},{8,0},{16,24},{24,16},{1,9},{9,1},{17,25},{25,17},{2,10},{10... | collective-permute-start | bytes 589832 | tf_op jit(solution)/shard_map/dispatch/ppermute | solution.py:34
  10.8 1.6 %collective-permute-start.1 = (bf16[2,16,4224]{2,1,0:T(8,128)(2,1)S(1)}, bf16[2,16,4224]{2,1,0:T(8,128)(2,1)S(1)}, u32[]{:S(2)}, u32[]{:S(2)}) collective-permute-start(bf16[2,16,4224]{2,1,0:T(8,128)(2,1)S(1)} %get-tuple-element.40), channel_id=1, source_target_pairs={{0,2},{1,3},{2,0},{3,1},{4,6},{5,7},{6,4},{7,5},{8,10},{9,11},{10,... | collective-permute-start | bytes 811016 | tf_op jit(solution)/shard_map/dispatch/ppermute | solution.py:34
  12.4 2.5 %collective-permute-start.3 = (bf16[2,16,4224]{2,1,0:T(8,128)(2,1)S(1)}, bf16[2,16,4224]{2,1,0:T(8,128)(2,1)S(1)}, u32[]{:S(2)}, u32[]{:S(2)}) collective-permute-start(bf16[2,16,4224]{2,1,0:T(8,128)(2,1)S(1)} %get-tuple-element.42), channel_id=1, source_target_pairs={{0,6},{1,7},{2,4},{3,5},{4,2},{5,3},{6,0},{7,1},{8,14},{9,15},{10,... | collective-permute-start | bytes 811016 | tf_op jit(solution)/shard_map/dispatch/ppermute | solution.py:34
  14.8 1.1 %collective-permute-done.4 = bf16[128,768]{1,0:T(8,128)(2,1)S(1)} collective-permute-done((bf16[128,768]{1,0:T(8,128)(2,1)S(1)}, bf16[128,768]{1,0:T(8,128)(2,1)S(1)}, u32[]{:S(2)}, u32[]{:S(2)}) %collective-permute-start.4) | collective-permute-done | bytes 196640 | tf_op jit(solution)/shard_map/dispatch/ppermute | solution.py:34
  16.0 1.8 %collective-permute-start.5 = (bf16[256,768]{1,0:T(8,128)(2,1)S(1)}, bf16[256,768]{1,0:T(8,128)(2,1)S(1)}, u32[]{:S(2)}, u32[]{:S(2)}) collective-permute-start(bf16[256,768]{1,0:T(8,128)(2,1)S(1)} %pad_maximum_fusion), channel_id=1, source_target_pairs={{0,16},{8,24},{16,0},{24,8},{1,17},{9,25},{17,1},{25,9},{2,18},{10... | collective-permute-start | bytes 1179656 | tf_op jit(solution)/shard_map/dispatch/ppermute | solution.py:34
  17.9 2.6 %collective-permute-start.2 = (bf16[2,16,4224]{2,1,0:T(8,128)(2,1)S(1)}, bf16[2,16,4224]{2,1,0:T(8,128)(2,1)S(1)}, u32[]{:S(2)}, u32[]{:S(2)}) collective-permute-start(bf16[2,16,4224]{2,1,0:T(8,128)(2,1)S(1)} %get-tuple-element.39._), channel_id=1, source_target_pairs={{0,4},{1,5},{2,6},{3,7},{4,0},{5,1},{6,2},{7,3},{8,12},{9,13},{10,... | collective-permute-start | bytes 811016 | tf_op jit(solution)/shard_map/dispatch/ppermute | solution.py:34
  21.0 1.6 %collective-permute-start.6 = (bf16[64,1280]{1,0:T(8,128)(2,1)S(1)}, bf16[64,1280]{1,0:T(8,128)(2,1)S(1)}, u32[]{:S(2)}, u32[]{:S(2)}) collective-permute-start(bf16[64,1280]{1,0:T(8,128)(2,1)S(1)} %get-tuple-element.49), channel_id=1, source_target_pairs={{0,8},{8,0},{16,24},{24,16},{1,9},{9,1},{17,25},{25,17},{2,10},{10... | collective-permute-start | bytes 491528 | tf_op jit(solution)/shard_map/arrive/ppermute | solution.py:34
  22.6 0.6 collective-permute-start.7
  23.2 4.9 %collective-permute-done.3.refs_1_ = bf16[2,16,4224]{2,1,0:T(8,128)(2,1)S(1)} collective-permute-done((bf16[2,16,4224]{2,1,0:T(8,128)(2,1)S(1)}, bf16[2,16,4224]{2,1,0:T(8,128)(2,1)S(1)}, u32[]{:S(2)}, u32[]{:S(2)}) %collective-permute-start.3) | collective-permute-done | bytes 270368 | tf_op jit(solution)/shard_map/dispatch/ppermute | solution.py:34
  28.1 1.5 %collective-permute-start.8 = (bf16[64,1280]{1,0:T(8,128)(2,1)S(1)}, bf16[64,1280]{1,0:T(8,128)(2,1)S(1)}, u32[]{:S(2)}, u32[]{:S(2)}) collective-permute-start(bf16[64,1280]{1,0:T(8,128)(2,1)S(1)} %get-tuple-element.51), channel_id=1, source_target_pairs={{0,24},{8,16},{16,8},{24,0},{1,25},{9,17},{17,9},{25,1},{2,26},{10... | collective-permute-start | bytes 491528 | tf_op jit(solution)/shard_map/arrive/ppermute | solution.py:34
  29.6 9.0 %collective-permute-done.2.refs_0_ = bf16[2,16,4224]{2,1,0:T(8,128)(2,1)S(1)} collective-permute-done((bf16[2,16,4224]{2,1,0:T(8,128)(2,1)S(1)}, bf16[2,16,4224]{2,1,0:T(8,128)(2,1)S(1)}, u32[]{:S(2)}, u32[]{:S(2)}) %collective-permute-start.2) | collective-permute-done | bytes 270368 | tf_op jit(solution)/shard_map/dispatch/ppermute | solution.py:34
  39.1 0.6 collective-permute-start.9
  39.7 1.5 %collective-permute-start.10 = (bf16[64,1280]{1,0:T(8,128)(2,1)S(1)}, bf16[64,1280]{1,0:T(8,128)(2,1)S(1)}, u32[]{:S(2)}, u32[]{:S(2)}) collective-permute-start(bf16[64,1280]{1,0:T(8,128)(2,1)S(1)} %get-tuple-element.54), channel_id=1, source_target_pairs={{0,16},{8,24},{16,0},{24,8},{1,17},{9,25},{17,1},{25,9},{2,18},{10... | collective-permute-start | bytes 491528 | tf_op jit(solution)/shard_map/arrive/ppermute | solution.py:34
  41.2 1.4 %collective-permute-start.11 = (bf16[64,1280]{1,0:T(8,128)(2,1)S(1)}, bf16[64,1280]{1,0:T(8,128)(2,1)S(1)}, u32[]{:S(2)}, u32[]{:S(2)}) collective-permute-start(bf16[64,1280]{1,0:T(8,128)(2,1)S(1)} %get-tuple-element.55), channel_id=1, source_target_pairs={{0,24},{8,16},{16,8},{24,0},{1,25},{9,17},{17,9},{25,1},{2,26},{10... | collective-permute-start | bytes 491528 | tf_op jit(solution)/shard_map/arrive/ppermute | solution.py:34
  42.7 0.8 %adapters.3 = (f32[256,1024]{1,0:T(8,128)S(1)}, f32[256,256]{1,0:T(8,128)S(1)}) custom-call(bf16[256,768]{1,0:T(8,128)(2,1)S(1)} %bitcast.15, bf16[512,768]{1,0:T(8,128)(2,1)S(1)} %constant_dynamic-update-slice_fusion.hidden.refs_8_.hids, bf16[64,1280]{1,0:T(8,128)(2,1)S(1)} %get-tuple-element.48.refs_0_, ...), custom_call_target="tpu_custom_call" | custom-call | flops 268435456 | bytes 524288 | tf_op jit(solution)/shard_map/adapters/pallas_call | solution.py:357
  43.5 1.7 %inner.1 = (bf16[128,768]{1,0:T(8,128)(2,1)}, f32[128,128]{1,0:T(8,128)S(1)}) custom-call(bf16[64,4224]{1,0:T(8,128)(2,1)S(1)} %get-tuple-element.41.early, bf16[64,4224]{1,0:T(8,128)(2,1)S(1)} %get-tuple-element.43.late, bf16[4096,768]{1,0:T(8,128)(2,1)S(1)} %bitcast.14, bf16[64,256]{1,0:T(8,128)(2,1)S(1)} %get-tuple-element.44.masked1, ...), custom_call_target="tpu_custom_call" | custom-call | flops 805306368 | bytes 6291456 | tf_op jit(solution)/shard_map/inner/pallas_call | solution.py:347
  45.3 0.9 %collective-permute-done.9.refs_5_.refs_1_ = bf16[64,1280]{1,0:T(8,128)(2,1)S(1)} collective-permute-done((bf16[64,1280]{1,0:T(8,128)(2,1)S(1)}, bf16[64,1280]{1,0:T(8,128)(2,1)S(1)}, u32[]{:S(2)}, u32[]{:S(2)}) %collective-permute-start.9) | collective-permute-done | bytes 163872 | tf_op jit(solution)/shard_map/arrive/ppermute | solution.py:34
  46.1 1.2 %collective-permute-done.10.refs_6_.refs_2_ = bf16[64,1280]{1,0:T(8,128)(2,1)S(1)} collective-permute-done((bf16[64,1280]{1,0:T(8,128)(2,1)S(1)}, bf16[64,1280]{1,0:T(8,128)(2,1)S(1)}, u32[]{:S(2)}, u32[]{:S(2)}) %collective-permute-start.10) | collective-permute-done | bytes 163872 | tf_op jit(solution)/shard_map/arrive/ppermute | solution.py:34
  47.4 1.4 %collective-permute-done.11.refs_7_.refs_3_ = bf16[64,1280]{1,0:T(8,128)(2,1)S(1)} collective-permute-done((bf16[64,1280]{1,0:T(8,128)(2,1)S(1)}, bf16[64,1280]{1,0:T(8,128)(2,1)S(1)}, u32[]{:S(2)}, u32[]{:S(2)}) %collective-permute-start.11) | collective-permute-done | bytes 163872 | tf_op jit(solution)/shard_map/arrive/ppermute | solution.py:34
  48.7 0.8 %adapters.4 = (f32[4,32,1280]{2,1,0:T(8,128)S(1)}, f32[4,32,1280]{2,1,0:T(8,128)S(1)}) custom-call(bf16[256,768]{1,0:T(8,128)(2,1)S(1)} %bitcast.17, f32[256,1024]{1,0:T(8,128)S(1)} %get-tuple-element.57.out, f32[256,256]{1,0:T(8,128)S(1)} %get-tuple-element.58.inn, f32[128,128]{1,0:T(8,128)S(1)} %get-tuple-element.59.mix, ...), custom_call_target="tpu_custom_call" | custom-call | flops 268435456 | bytes 524288 | tf_op jit(solution)/shard_map/adapters/pallas_call | solution.py:365
  49.6 2.1 %collective-permute-done.12.got = f32[4,32,1280]{2,1,0:T(8,128)S(1)} collective-permute-done((f32[4,32,1280]{2,1,0:T(8,128)S(1)}, f32[4,32,1280]{2,1,0:T(8,128)S(1)}, u32[]{:S(2)}, u32[]{:S(2)}) %collective-permute-start.12) | collective-permute-done | bytes 655392 | tf_op jit(solution)/shard_map/adapters/ppermute | solution.py:34
  51.9 2.9 %collective-permute-start.14 = (bf16[32,1280]{1,0:T(8,128)(2,1)S(1)}, bf16[32,1280]{1,0:T(8,128)(2,1)S(1)}, u32[]{:S(2)}, u32[]{:S(2)}) collective-permute-start(bf16[32,1280]{1,0:T(8,128)(2,1)S(1)} %get-tuple-element.64), channel_id=1, source_target_pairs={{0,4},{1,5},{2,6},{3,7},{4,0},{5,1},{6,2},{7,3},{8,12},{9,13},{10,... | collective-permute-start | bytes 245768 | tf_op jit(solution)/shard_map/adapters/ppermute | solution.py:34
  54.8 1.5 %collective-permute-start.15 = (bf16[32,1280]{1,0:T(8,128)(2,1)S(1)}, bf16[32,1280]{1,0:T(8,128)(2,1)S(1)}, u32[]{:S(2)}, u32[]{:S(2)}) collective-permute-start(bf16[32,1280]{1,0:T(8,128)(2,1)S(1)} %get-tuple-element.65), channel_id=1, source_target_pairs={{0,6},{1,7},{2,4},{3,5},{4,2},{5,3},{6,0},{7,1},{8,14},{9,15},{10,... | collective-permute-start | bytes 245768 | tf_op jit(solution)/shard_map/adapters/ppermute | solution.py:34
  56.3 2.7 %product.1 = f32[1,1024,768]{2,1,0:T(8,128)} custom-call(bf16[64,1280]{1,0:T(8,128)(2,1)S(1)} %get-tuple-element.48.refs_0_, bf16[64,1280]{1,0:T(8,128)(2,1)S(1)} %collective-permute-done.6.refs_1_, bf16[64,1280]{1,0:T(8,128)(2,1)S(1)} %collective-permute-done.7.refs_2_, bf16[64,1280]{1,0:T(8,128)(2,1)S(1)} %collective-permute-done.8.refs_3_, ...), custom_call_target="tpu_custom_call" | custom-call | flops 805306368 | bytes 2097152 | tf_op jit(solution)/shard_map/product/pallas_call | solution.py:384
  58.9 2.6 %collective-permute-done.14.refs_2_ = bf16[32,1280]{1,0:T(8,128)(2,1)S(1)} collective-permute-done((bf16[32,1280]{1,0:T(8,128)(2,1)S(1)}, bf16[32,1280]{1,0:T(8,128)(2,1)S(1)}, u32[]{:S(2)}, u32[]{:S(2)}) %collective-permute-start.14) | collective-permute-done | bytes 81952 | tf_op jit(solution)/shard_map/adapters/ppermute | solution.py:34
  61.6 0.8 %final.1 = (f32[2,16,1024]{2,1,0:T(8,128)}, f32[2,16,192]{2,1,0:T(8,128)}, f32[8,128]{1,0:T(8,128)}) custom-call(f32[17,128]{1,0:T(8,128)S(1)} %pad_maximum_fusion.1.small, bf16[128,128]{1,0:T(8,128)(2,1)S(1)} %get-tuple-element.56.picks, bf16[32,1280]{1,0:T(8,128)(2,1)S(1)} %get-tuple-element.62.refs_0_, ...), custom_call_target="tpu_custom_call" | custom-call | bytes 1000000 | tf_op jit(solution)/shard_map/final/pallas_call | solution.py:393
  (32 shorter events, 2.6 us)
Async XLA Ops:
  0.6 19.9 %copy-start = (bf16[2,4096,128]{2,1,0:T(8,128)(2,1)S(1)}, bf16[2,4096,128]{2,1,0:T(8,128)(2,1)}, u32[]{:S(2)}) copy-start(bf16[2,4096,128]{2,1,0:T(8,128)(2,1)} %adapter_out.3) | copy-start | bytes 6291460
  2.8 1.2 %copy-start.2 = (bf16[128,4096]{1,0:T(8,128)(2,1)S(1)}, bf16[128,4096]{1,0:T(8,128)(2,1)}, u32[]{:S(2)}) copy-start(bf16[128,4096]{1,0:T(8,128)(2,1)} %cot.1) | copy-start | bytes 3145732
  4.6 2.1 %collective-permute-start = (bf16[4,16,4224]{2,1,0:T(8,128)(2,1)S(1)}, bf16[4,16,4224]{2,1,0:T(8,128)(2,1)S(1)}, u32[]{:S(2)}, u32[]{:S(2)}) collective-permute-start(bf16[4,16,4224]{2,1,0:T(8,128)(2,1)S(1)} %get-tuple-element.38), channel_id=1, source_target_pairs={{0,1},{1,0},{2,3},{3,2},{4,5},{5,4},{6,7},{7,6},{8,9},{9,8},{10,11... | collective-permute-start | bytes 1622024 | tf_op jit(solution)/shard_map/route/ppermute | solution.py:34
  6.7 36.8 %slice-start = ((s8[6291456]{0:T(1024)(128)(4,1)}), s8[4194304]{0:T(1024)(128)(4,1)S(1)}, s32[]{:S(2)}) async-start(s8[6291456]{0:T(1024)(128)(4,1)} %bitcast.12), calls=%async_computation | async-start | bytes 8388608
  6.7 1.1 %copy-start.3 = (bf16[1,1,128,768]{3,2,1,0:T(8,128)(2,1)S(1)}, bf16[1,1,128,768]{3,2,1,0:T(8,128)(2,1)}, u32[]{:S(2)}) copy-start(bf16[1,1,128,768]{3,2,1,0:T(8,128)(2,1)} %param.9) | copy-start | bytes 589828
  7.9 8.1 %collective-permute-start.4 = (bf16[128,768]{1,0:T(8,128)(2,1)S(1)}, bf16[128,768]{1,0:T(8,128)(2,1)S(1)}, u32[]{:S(2)}, u32[]{:S(2)}) collective-permute-start(bf16[128,768]{1,0:T(8,128)(2,1)S(1)} %get-tuple-element.46), channel_id=1, source_target_pairs={{0,8},{8,0},{16,24},{24,16},{1,9},{9,1},{17,25},{25,17},{2,10},{10... | collective-permute-start | bytes 589832 | tf_op jit(solution)/shard_map/dispatch/ppermute | solution.py:34
  10.8 9.7 %collective-permute-start.1 = (bf16[2,16,4224]{2,1,0:T(8,128)(2,1)S(1)}, bf16[2,16,4224]{2,1,0:T(8,128)(2,1)S(1)}, u32[]{:S(2)}, u32[]{:S(2)}) collective-permute-start(bf16[2,16,4224]{2,1,0:T(8,128)(2,1)S(1)} %get-tuple-element.40), channel_id=1, source_target_pairs={{0,2},{1,3},{2,0},{3,1},{4,6},{5,7},{6,4},{7,5},{8,10},{9,11},{10,... | collective-permute-start | bytes 811016 | tf_op jit(solution)/shard_map/dispatch/ppermute | solution.py:34
  12.4 15.7 %collective-permute-start.3 = (bf16[2,16,4224]{2,1,0:T(8,128)(2,1)S(1)}, bf16[2,16,4224]{2,1,0:T(8,128)(2,1)S(1)}, u32[]{:S(2)}, u32[]{:S(2)}) collective-permute-start(bf16[2,16,4224]{2,1,0:T(8,128)(2,1)S(1)} %get-tuple-element.42), channel_id=1, source_target_pairs={{0,6},{1,7},{2,4},{3,5},{4,2},{5,3},{6,0},{7,1},{8,14},{9,15},{10,... | collective-permute-start | bytes 811016 | tf_op jit(solution)/shard_map/dispatch/ppermute | solution.py:34
  16.0 26.7 %copy-start.1 = (bf16[2,128,768]{2,1,0:T(8,128)(2,1)S(1)}, bf16[2,128,768]{2,1,0:T(8,128)(2,1)}, u32[]{:S(2)}) copy-start(bf16[2,128,768]{2,1,0:T(8,128)(2,1)} %param.11) | copy-start | bytes 1179652
  16.0 27.5 %slice-start.1 = ((s8[6291456]{0:T(1024)(128)(4,1)}), s8[2097152]{0:T(1024)(128)(4,1)S(1)}, s32[]{:S(2)}) async-start(s8[6291456]{0:T(1024)(128)(4,1)} %bitcast.12), calls=%async_computation.1 | async-start | bytes 4194304
  16.0 25.2 %collective-permute-start.5 = (bf16[256,768]{1,0:T(8,128)(2,1)S(1)}, bf16[256,768]{1,0:T(8,128)(2,1)S(1)}, u32[]{:S(2)}, u32[]{:S(2)}) collective-permute-start(bf16[256,768]{1,0:T(8,128)(2,1)S(1)} %pad_maximum_fusion), channel_id=1, source_target_pairs={{0,16},{8,24},{16,0},{24,8},{1,17},{9,25},{17,1},{25,9},{2,18},{10... | collective-permute-start | bytes 1179656 | tf_op jit(solution)/shard_map/dispatch/ppermute | solution.py:34
  17.9 20.7 %collective-permute-start.2 = (bf16[2,16,4224]{2,1,0:T(8,128)(2,1)S(1)}, bf16[2,16,4224]{2,1,0:T(8,128)(2,1)S(1)}, u32[]{:S(2)}, u32[]{:S(2)}) collective-permute-start(bf16[2,16,4224]{2,1,0:T(8,128)(2,1)S(1)} %get-tuple-element.39._), channel_id=1, source_target_pairs={{0,4},{1,5},{2,6},{3,7},{4,0},{5,1},{6,2},{7,3},{8,12},{9,13},{10,... | collective-permute-start | bytes 811016 | tf_op jit(solution)/shard_map/dispatch/ppermute | solution.py:34
  21.0 18.7 %collective-permute-start.6 = (bf16[64,1280]{1,0:T(8,128)(2,1)S(1)}, bf16[64,1280]{1,0:T(8,128)(2,1)S(1)}, u32[]{:S(2)}, u32[]{:S(2)}) collective-permute-start(bf16[64,1280]{1,0:T(8,128)(2,1)S(1)} %get-tuple-element.49), channel_id=1, source_target_pairs={{0,8},{8,0},{16,24},{24,16},{1,9},{9,1},{17,25},{25,17},{2,10},{10... | collective-permute-start | bytes 491528 | tf_op jit(solution)/shard_map/arrive/ppermute | solution.py:34
  22.6 20.1 %collective-permute-start.7 = (bf16[64,1280]{1,0:T(8,128)(2,1)S(1)}, bf16[64,1280]{1,0:T(8,128)(2,1)S(1)}, u32[]{:S(2)}, u32[]{:S(2)}) collective-permute-start(bf16[64,1280]{1,0:T(8,128)(2,1)S(1)} %get-tuple-element.50), channel_id=1, source_target_pairs={{0,16},{8,24},{16,0},{24,8},{1,17},{9,25},{17,1},{25,9},{2,18},{10... | collective-permute-start | bytes 491528 | tf_op jit(solution)/shard_map/arrive/ppermute | solution.py:34
  28.1 14.6 %collective-permute-start.8 = (bf16[64,1280]{1,0:T(8,128)(2,1)S(1)}, bf16[64,1280]{1,0:T(8,128)(2,1)S(1)}, u32[]{:S(2)}, u32[]{:S(2)}) collective-permute-start(bf16[64,1280]{1,0:T(8,128)(2,1)S(1)} %get-tuple-element.51), channel_id=1, source_target_pairs={{0,24},{8,16},{16,8},{24,0},{1,25},{9,17},{17,9},{25,1},{2,26},{10... | collective-permute-start | bytes 491528 | tf_op jit(solution)/shard_map/arrive/ppermute | solution.py:34
  39.1 7.0 %collective-permute-start.9 = (bf16[64,1280]{1,0:T(8,128)(2,1)S(1)}, bf16[64,1280]{1,0:T(8,128)(2,1)S(1)}, u32[]{:S(2)}, u32[]{:S(2)}) collective-permute-start(bf16[64,1280]{1,0:T(8,128)(2,1)S(1)} %get-tuple-element.53), channel_id=1, source_target_pairs={{0,8},{8,0},{16,24},{24,16},{1,9},{9,1},{17,25},{25,17},{2,10},{10... | collective-permute-start | bytes 491528 | tf_op jit(solution)/shard_map/arrive/ppermute | solution.py:34
  39.7 7.7 %collective-permute-start.10 = (bf16[64,1280]{1,0:T(8,128)(2,1)S(1)}, bf16[64,1280]{1,0:T(8,128)(2,1)S(1)}, u32[]{:S(2)}, u32[]{:S(2)}) collective-permute-start(bf16[64,1280]{1,0:T(8,128)(2,1)S(1)} %get-tuple-element.54), channel_id=1, source_target_pairs={{0,16},{8,24},{16,0},{24,8},{1,17},{9,25},{17,1},{25,9},{2,18},{10... | collective-permute-start | bytes 491528 | tf_op jit(solution)/shard_map/arrive/ppermute | solution.py:34
  41.2 7.5 %collective-permute-start.11 = (bf16[64,1280]{1,0:T(8,128)(2,1)S(1)}, bf16[64,1280]{1,0:T(8,128)(2,1)S(1)}, u32[]{:S(2)}, u32[]{:S(2)}) collective-permute-start(bf16[64,1280]{1,0:T(8,128)(2,1)S(1)} %get-tuple-element.55), channel_id=1, source_target_pairs={{0,24},{8,16},{16,8},{24,0},{1,25},{9,17},{17,9},{25,1},{2,26},{10... | collective-permute-start | bytes 491528 | tf_op jit(solution)/shard_map/arrive/ppermute | solution.py:34
  49.6 2.2 %collective-permute-start.12 = (f32[4,32,1280]{2,1,0:T(8,128)S(1)}, f32[4,32,1280]{2,1,0:T(8,128)S(1)}, u32[]{:S(2)}, u32[]{:S(2)}) collective-permute-start(f32[4,32,1280]{2,1,0:T(8,128)S(1)} %get-tuple-element.61), channel_id=1, source_target_pairs={{0,1},{1,0},{2,3},{3,2},{4,5},{5,4},{6,7},{7,6},{8,9},{9,8},{10,11... | collective-permute-start | bytes 1966088 | tf_op jit(solution)/shard_map/adapters/ppermute | solution.py:34
  51.8 7.1 %collective-permute-start.13 = (bf16[32,1280]{1,0:T(8,128)(2,1)S(1)}, bf16[32,1280]{1,0:T(8,128)(2,1)S(1)}, u32[]{:S(2)}, u32[]{:S(2)}) collective-permute-start(bf16[32,1280]{1,0:T(8,128)(2,1)S(1)} %get-tuple-element.63), channel_id=1, source_target_pairs={{0,2},{1,3},{2,0},{3,1},{4,6},{5,7},{6,4},{7,5},{8,10},{9,11},{10,... | collective-permute-start | bytes 245768 | tf_op jit(solution)/shard_map/adapters/ppermute | solution.py:34
  51.9 9.7 %collective-permute-start.14 = (bf16[32,1280]{1,0:T(8,128)(2,1)S(1)}, bf16[32,1280]{1,0:T(8,128)(2,1)S(1)}, u32[]{:S(2)}, u32[]{:S(2)}) collective-permute-start(bf16[32,1280]{1,0:T(8,128)(2,1)S(1)} %get-tuple-element.64), channel_id=1, source_target_pairs={{0,4},{1,5},{2,6},{3,7},{4,0},{5,1},{6,2},{7,3},{8,12},{9,13},{10,... | collective-permute-start | bytes 245768 | tf_op jit(solution)/shard_map/adapters/ppermute | solution.py:34
  54.8 6.8 %collective-permute-start.15 = (bf16[32,1280]{1,0:T(8,128)(2,1)S(1)}, bf16[32,1280]{1,0:T(8,128)(2,1)S(1)}, u32[]{:S(2)}, u32[]{:S(2)}) collective-permute-start(bf16[32,1280]{1,0:T(8,128)(2,1)S(1)} %get-tuple-element.65), channel_id=1, source_target_pairs={{0,6},{1,7},{2,4},{3,5},{4,2},{5,3},{6,0},{7,1},{8,14},{9,15},{10,... | collective-permute-start | bytes 245768 | tf_op jit(solution)/shard_map/adapters/ppermute | solution.py:34

commit v3 on v2

--- a/solution.py
+++ b/solution.py
@@ -62,16 +62,27 @@
     return ((place[0] // 2) ^ hop) * 2 + ((place[0] % 2) ^ half)
 
 
-def route_body(chips, cap, ways, small, cot, keep, give, picks, mixed):
+def decode(small, experts, loops):
+    loop = jnp.zeros_like(small)
+    for l in range(1, loops):
+        loop = loop + jnp.where(small >= l * (experts + 1.0), 1.0, 0.0)
+    rest = small - loop * (experts + 1.0)
+    route = jnp.floor(rest)
+    return route, rest - route, loop[:1]
+
+
+def route_body(chips, cap, loops, small, cot, keep, give, picks, mixed):
     experts = 2 * chips
+    ways = small.shape[0]
     toks, width = cot.shape
     owner = owner_column(here(), chips, experts).astype(f32)
+    route, chance, loop = decode(small[...], experts, loops)
     named = jnp.zeros((experts, toks), f32)
     weight = jnp.zeros((experts, toks), f32)
     for k in range(ways):
-        hit = small[k : k + 1, :] == owner
+        hit = route[k : k + 1, :] == owner
         named = named + jnp.where(hit, 1.0, 0.0)
-        weight = weight + jnp.where(hit, small[ways + k : ways + k + 1, :], 0.0)
+        weight = weight + jnp.where(hit, chance[k : k + 1, :], 0.0)
     earlier = lax.broadcasted_iota(jnp.int32, (toks, toks), 0) < lax.broadcasted_iota(
         jnp.int32, (toks, toks), 1
     )
@@ -84,7 +95,7 @@
         picks[rows, :] = jnp.where(hit, 1.0, 0.0).astype(bf16)
         mixed[rows, :] = jnp.where(hit, weight[j : j + 1, :], 0.0).astype(bf16)
     loop_rows = lax.broadcasted_iota(jnp.int32, (LANES, toks), 0).astype(f32)
-    loop_rows = jnp.where(loop_rows == small[2 * ways : 2 * ways + 1, :], 1.0, 0.0).astype(bf16)
+    loop_rows = jnp.where(loop_rows == loop, 1.0, 0.0).astype(bf16)
     mix = nt(mixed[...], loop_rows).astype(bf16)
     half = chips * cap
     keep[:, :, width:] = mix[:half].reshape(chips, cap, LANES)
@@ -102,27 +113,17 @@
     return [(z ^ hop) * 2 + (c ^ half) for hop in range(chips) for half in range(2)]
 
 
-def pack_far_body(chips, keep, sib, *far):
-    for n, block in enumerate(far):
-        hop = chips - len(far) + n
-        block[0] = keep[hop]
-        block[1] = sib[hop]
-
-
-def pack_near_body(chips, cap, keep, sib, hidden, _, ordered, *near):
-    for n, block in enumerate(near):
-        block[0] = keep[1 + n]
-        block[1] = sib[1 + n]
-    for n, source in enumerate(sources(here(), chips)):
-        rows = pl.ds(pl.multiple_of(source * cap, cap), cap)
-        ordered[n * cap : (n + 1) * cap, :] = hidden[rows, :]
+def pack_body(chips, keep, sib, *out):
+    for hop in range(1, chips):
+        out[hop - 1][0] = keep[hop]
+        out[hop - 1][1] = sib[hop]
 
 
 def arrive_body(groups, near, adapter_out, *refs):
-    blocks = refs[: -2 - groups]
-    rows, masked, parts = refs[-2 - groups], refs[-1 - groups], refs[-groups:]
     loops, width, rank = adapter_out.shape
     part = width // groups
+    parts = refs[-groups:]
+    blocks, (rows, masked) = refs[: -2 - groups - near], refs[-2 - groups : -groups]
     at = 0
     for n, block in enumerate(blocks):
         halves = (block[0],) if near and n < 2 else (block[0], block[1])
@@ -168,20 +169,19 @@
     mix_out[...] = jnp.broadcast_to(sums, mix_out.shape)
 
 
-def adapter_sums(groups, loops, cols, start, adapter_in, rows, hids):
-    slots = rows[0].shape[0]
+def adapter_sums(loops, cols, start, adapter_in, rows, hids):
     rank = adapter_in.shape[0] // loops
     hid_width = adapter_in.shape[1]
+    slots = rows[0].shape[0]
     part = rows[0].shape[1] - rank - LANES
     wide = wide_of(cols)
     row = lax.broadcasted_iota(jnp.int32, (hid_width, wide), 0)
     lane = lax.broadcasted_iota(jnp.int32, (hid_width, wide), 1)
     pick = (row == lane + here()[1] * cols) & (lane < cols)
     pick = jnp.where(pick, 1.0, 0.0).astype(bf16)
-    total = hids.shape[0] // groups
-    hid = jnp.concatenate(
-        [hids[g * total + start : g * total + start + slots, :] for g in range(groups)], axis=0
-    )
+    total = hids.shape[0] // len(rows)
+    starts = [g * total + start for g in range(len(rows))]
+    hid = jnp.concatenate([hids[at : at + slots, :] for at in starts], axis=0)
     tail = jnp.concatenate([r[:, part:] for r in rows], axis=0).astype(f32)
     body = jnp.concatenate([r[:, :part] for r in rows], axis=0)
     down = nt(hid, adapter_in[...])
@@ -197,19 +197,23 @@
     return -(-(cols + 4) // LANES) * LANES
 
 
-def adapter_first_body(groups, loops, cols, adapter_in, hids, *refs):
-    rows, (out, inn) = refs[:groups], refs[groups:]
-    out[...], inn[...] = adapter_sums(groups, loops, cols, 0, adapter_in, rows, hids)
-
-
-def adapter_last_body(groups, loops, chips, cap, cols, adapter_in, out, inn, mix, hids, *refs):
-    rows, (keep, give, sums, narrow) = refs[:groups], refs[groups:]
-    slots = rows[0].shape[0]
+def adapter_first_body(loops, chips, cap, cols, adapter_in, hids, *refs):
+    rows, (out, inn, ordered) = refs[:-3], refs[-3:]
+    total = hids.shape[0] // len(rows)
+    for g in range(len(rows)):
+        for n, source in enumerate(sources(here(), chips)):
+            spot = pl.ds(pl.multiple_of(g * total + source * cap, cap), cap)
+            ordered[g * total + n * cap : g * total + (n + 1) * cap, :] = hids[spot, :]
+    out[...], inn[...] = adapter_sums(loops, cols, 0, adapter_in, rows, ordered)
+
+
+def adapter_last_body(loops, chips, cap, cols, adapter_in, out, inn, mix, hids, *refs):
+    rows, (keep, give, sums, narrow) = refs[:-4], refs[-4:]
     rank = adapter_in.shape[0] // loops
     part = out.shape[1]
     share = rank // (2 * chips)
-    start = mix.shape[0] - slots
-    more = adapter_sums(groups, loops, cols, start, adapter_in, rows, hids)
+    start = mix.shape[0] - rows[0].shape[0]
+    more = adapter_sums(loops, cols, start, adapter_in, rows, hids)
     sums[...] = out[...] + more[0]
     narrow[...] = inn[...] + more[1]
     owners = sources(here(), chips)
@@ -219,28 +223,28 @@
         for l in range(loops):
             src = pl.ds(pl.multiple_of(l * rank + owner * share, share), share)
             dst = slice(l * share, (l + 1) * share)
-            target[hop, dst, :part] = sums[src, :]
-            target[hop, dst, part:] = narrow[src, :]
+            target[hop, dst, :part] = sums[src, :].astype(target.dtype)
+            target[hop, dst, part:] = narrow[src, :].astype(target.dtype)
         value = mix[n * cap : (n + 1) * cap, :1]
-        target[hop, :cap, part:] = jnp.where(lane == cols, value, target[hop, :cap, part:])
-
-
-def pair_body(chips, cap, part, cols, keep, got, *outs):
-    wide = keep.shape[2] - part
-    lane = lax.broadcasted_iota(jnp.int32, (cap, wide), 1)
+        high = value.astype(bf16).astype(f32)
+        tail = target[hop, :cap, part:].astype(f32)
+        tail = jnp.where(lane == cols + 2 * (n % 2), high, tail)
+        tail = jnp.where(lane == cols + 2 * (n % 2) + 1, value - high, tail)
+        target[hop, :cap, part:] = tail.astype(target.dtype)
+
+
+def pair_body(chips, keep, got, *outs):
     for hop in range(chips):
-        outs[hop][...] = (keep[hop] + got[hop]).astype(bf16)
-        tail = keep[hop, :cap, part:] + got[hop, :cap, part:]
-        for n, block in enumerate((keep, got)):
-            value = block[hop, :cap, part + cols : part + cols + 1]
-            high = value.astype(bf16).astype(f32)
-            tail = jnp.where(lane == cols + 2 * n, high, tail)
-            tail = jnp.where(lane == cols + 2 * n + 1, value - high, tail)
-        outs[hop][:cap, part:] = tail.astype(bf16)
+        outs[hop][...] = (keep[hop] + got[hop].astype(f32)).astype(bf16)
+
+
+def far_first(chips):
+    return [0] + list(range(chips // 2, chips)) + list(range(1, chips // 2))
 
 
 def final_body(chips, cap, cols, small, picks, *refs):
-    blocks = refs[:chips]
+    order = far_first(chips)
+    blocks = [refs[order.index(hop)] for hop in range(chips)]
     out_grad, in_grad, combine = refs[chips:]
     loops, share, part = out_grad.shape
     total = blocks[0][...].astype(f32)
@@ -252,7 +256,7 @@
         in_grad[l] = total[rows, part : part + cols]
     experts = 2 * chips
     owner = owner_column(here(), chips, experts).astype(f32)
-    routes = small[: combine.shape[0], :]
+    routes = decode(small[...], experts, loops)[0]
     sums = jnp.zeros(combine.shape, f32)
     for j in range(experts):
         half, hop = j // chips, j % chips
@@ -291,14 +295,16 @@
     share = rank // experts
     half = slots // 2
     flat_in = adapter_in.reshape(loops * rank, hid_width)
-    small = jnp.concatenate(
-        [routes.T.astype(f32), probs.T.astype(f32), token_loop.astype(f32).reshape(1, toks)]
-    )
-
+    small = token_loop.reshape(1, toks) * (experts + 1) + jnp.minimum(routes.T, experts)
+    small = small.astype(f32) + probs.T.astype(f32)
+
+    with jax.named_scope("hidden"):
+        natural = hidden.reshape(slots, hid_width)
+        pair = jnp.concatenate([natural] + [swap(natural, "dp", groups, hop) for hop in range(1, groups)])
     with jax.named_scope("route"):
         packed = shape((chips, cap, width + LANES), bf16)
         keep, give, picks = call(
-            functools.partial(route_body, chips, cap, ways),
+            functools.partial(route_body, chips, cap, loops),
             (packed, packed, shape((slots, toks), bf16)),
             (V, V),
             scratch=(pltpu.VMEM((slots, toks), bf16),),
@@ -307,42 +313,44 @@
         )(small, cotangent)
         sib = swap(give, "expert", experts, 1)
     with jax.named_scope("dispatch"):
-        pair = shape((2, cap, width + LANES), bf16)
-        middle = chips // 2
         packs = call(
-            functools.partial(pack_far_body, chips),
-            (pair,) * (chips - middle),
+            functools.partial(pack_body, chips),
+            (shape((2, cap, width + LANES), bf16),) * (chips - 1),
             (V, V),
-            nbytes=2 * slots * width,
+            nbytes=4 * slots * width,
         )(keep, sib)
-        far = [swap(x, "expert", experts, 2 * (middle + n)) for n, x in enumerate(packs)]
-        got = call(
-            functools.partial(pack_near_body, chips, cap),
-            (shape((slots, hid_width), bf16),) + (pair,) * (middle - 1),
-            (V, V, V, A),
-            nbytes=2 * slots * width,
-        )(keep, sib, hidden.reshape(slots, hid_width), packs[0])
-        near = [swap(x, "expert", experts, 2 * (1 + n)) for n, x in enumerate(got[1:])]
-        hids, hop = got[0], 1
-        while hop < groups:
-            hids = jnp.concatenate([hids, swap(hids, "dp", groups, hop)])
-            hop *= 2
+        far = [swap(x, "expert", experts, 2 * hop) for hop, x in enumerate(packs, 1)]
     with jax.named_scope("arrive"):
         rows, masked, parts = [], [], []
-        for own, blocks in ((True, [keep, sib] + near), (False, far)):
+        for near in (True, False):
+            blocks = [keep, sib] + far[: chips // 2 - 1] if near else far[chips // 2 - 1 :]
             got = call(
-                functools.partial(arrive_body, groups, own),
+                functools.partial(arrive_body, groups, near),
                 (shape((half, width + LANES), bf16), shape((half, loops * rank), bf16))
                 + (shape((half, part + rank + LANES), bf16),) * groups,
-                (V,) * (1 + len(blocks)),
+                (V,) * (1 + len(blocks)) + (A,) * near,
                 flops=2 * half * width * loops * rank,
                 nbytes=4 * half * width,
-            )(adapter_out, *blocks)
+            )(adapter_out, *blocks, *([pair] if near else []))
             rows.append(got[0])
             masked.append(got[1])
             parts.append(
                 [got[2]] + [swap(got[2 + hop], "dp", groups, hop) for hop in range(1, groups)]
             )
+        hids, hop = pair, groups
+        while hop < groups:
+            hids = jnp.concatenate([hids, swap(hids, "dp", groups, hop)])
+            hop *= 2
+    with jax.named_scope("adapters"):
+        work = 2 * groups * half * loops * rank * (part + hid_width + wide)
+        sums = (shape((loops * rank, part), f32), shape((loops * rank, wide), f32))
+        out, inn, ordered = call(
+            functools.partial(adapter_first_body, loops, chips, cap, cols),
+            sums + (shape((groups * slots, hid_width), bf16),),
+            (V,) * (2 + groups),
+            flops=work,
+            nbytes=2 * groups * half * part,
+        )(flat_in, hids, *parts[0])
     with jax.named_scope("inner"):
         grad, mix = call(
             functools.partial(inner_body, chips, cap),
@@ -350,35 +358,26 @@
             (V,) * 7,
             flops=2 * slots * width * hid_width,
             nbytes=2 * width * hid_width,
-        )(*rows, down_matrix[0], *masked, flat_in, hids)
+        )(*rows, down_matrix[0], *masked, flat_in, ordered)
     with jax.named_scope("adapters"):
-        work = 2 * groups * half * loops * rank * (part + hid_width + wide)
-        sums = (shape((loops * rank, part), f32), shape((loops * rank, wide), f32))
-        out, inn = call(
-            functools.partial(adapter_first_body, groups, loops, cols),
-            sums,
-            (V,) * (2 + groups),
-            flops=work,
-            nbytes=2 * groups * half * part,
-        )(flat_in, hids, *parts[0])
         block = (chips, loops * share, part + wide)
         keep3, give3 = call(
-            functools.partial(adapter_last_body, groups, loops, chips, cap, cols),
-            (shape(block, f32), shape(block, f32)),
+            functools.partial(adapter_last_body, loops, chips, cap, cols),
+            (shape(block, f32), shape(block, bf16)),
             (V,) * (5 + groups),
             scratch=[pltpu.VMEM(s.shape, f32) for s in sums],
             flops=work,
             nbytes=2 * groups * half * part,
-        )(flat_in, out, inn, mix, hids, *parts[1])
+        )(flat_in, out, inn, mix, ordered, *parts[1])
         got3 = swap(give3, "expert", experts, 1)
         ready = call(
-            functools.partial(pair_body, chips, cap, part, cols),
+            functools.partial(pair_body, chips),
             (shape(block[1:], bf16),) * chips,
             (V, V),
             nbytes=1e6,
         )(keep3, got3)
         blocks = list(ready)
-        for hop in reversed(range(1, chips)):
+        for hop in far_first(chips)[1:]:
             blocks[hop] = swap(ready[hop], "expert", experts, 2 * hop)
     with jax.named_scope("product"):
         product = call(
@@ -388,7 +387,7 @@
             limit=40,
             flops=2 * groups * slots * part * hid_width,
             nbytes=4 * groups * slots * part,
-        )(*parts[0], *parts[1], hids)
+        )(*parts[0], *parts[1], ordered)
     with jax.named_scope("final"):
         out_grad, in_grad, combine = call(
             functools.partial(final_body, chips, cap, cols),
@@ -399,7 +398,7 @@
             ),
             (V,) * (2 + chips),
             nbytes=1e6,
-        )(small, picks, *blocks)
+        )(small, picks, *(blocks[hop] for hop in far_first(chips)))
     return (
         grad.reshape(hidden.shape),
         product,

time: 62.6 us -> 60 us (0.958)
  waiting for transfers between devices: 24.8 us -> 19.6 us
  starting transfers between devices: 23.6 us -> 28.3 us
  local copies, waits for them, and re-layouts: 2.37 us -> 1.24 us
  other arithmetic: 2.21 us -> 1.42 us
    ppermute x16 -> x17, waiting for transfers between devices: 24.8 us -> 19.6 us  [swap(): return lax.ppermute(x, axis, [(i, i ^ mask) for i in range(size)])]
    ppermute x16 -> x17, starting transfers between devices: 23.6 us -> 28.3 us  [swap(): return lax.ppermute(x, axis, [(i, i ^ mask) for i in range(size)])]
    convert_element_type x2 -> x0, other arithmetic: 1.37 us -> none  [the longest x1 0.69 us: on_device(): routes.T.astype(f32)]
    unnamed x14 -> x10, local copies, waits for them, and re-layouts: 2.35 us -> 1.24 us
    reshape x1 -> x0, other arithmetic: 0.81 us -> none  [on_device(): token_loop.astype(f32).reshape(1, toks)]
    add x0 -> x1, other arithmetic: none -> 0.71 us  [on_device(): small = small.astype(f32) + probs.T.astype(f32)]
    mul x0 -> x1, other arithmetic: none -> 0.66 us  [on_device(): token_loop.reshape(1, toks) * (experts + 1) + jnp.minimum(routes.T, experts)]
    pallas_call x8 -> x7, Pallas kernels: 3.4 us -> 3.37 us  [the longest x2 1.12 us: on_device(): call(functools.partial(arrive_body, groups, near), (shape((half, width +...]
  transfers between devices with their start and end apart: 16 -> 17, of which waited for: 9 -> 10; matrix products, arithmetic and copies ran while one was open for 0% -> 0% of each run, Pallas kernels for 10% -> 11%
where the time goes in v3:
time: 60 us; the launch traced here: 59.8 us
  starting transfers between devices  28.3 us (47%)
  waiting for transfers between devices  19.6 us (33%)
  Pallas kernels  8.54 us (14%)
  other arithmetic  1.42 us (2%)
  local copies, waits for them, and re-layouts  1.24 us (2%)
  between operations  0.73 us (1%)
    ppermute x17, starting transfers between devices, swap(): return lax.ppermute(x, axis, [(i, i ^ mask) for i in range(size)])  28.3 us
    ppermute x17, waiting for transfers between devices, swap(): return lax.ppermute(x, axis, [(i, i ^ mask) for i in range(size)])  19.6 us
    pallas_call x1, Pallas kernels, on_device(): call(functools.partial(product_body, groups), shape((1, part, hid_width),...  2.67 us
    pallas_call x1, Pallas kernels, on_device(): call(functools.partial(inner_body, chips, cap), (shape((slots, hid_width)...  1.72 us
    unnamed x10, local copies, waits for them, and re-layouts  1.24 us
  transfers between devices with their start and end apart: 17, of which 10 were waited for; matrix products, arithmetic and copies ran while one was open for 0% of the time, Pallas kernels for 11%

profile of v3, /device:TPU:0, one launch (start us, length us, event | category | flops | bytes accessed | tf_op | source)
XLA Modules:
  0.0 59.8 jit_solution(12342870429740569111)
XLA Ops:
  0.6 0.7 %broadcast_multiply_fusion = s32[128]{0:T(128)S(1)} fusion(s32[128]{0:T(128)} %param.15), kind=kLoop, calls=%fused_computation.2 | loop fusion | flops 128 | bytes 1024 | tf_op jit(solution)/shard_map/mul | solution.py:298
  1.3 0.7 %add_bitcast_fusion.small = f32[8,128]{1,0:T(8,128)S(1)} fusion(bf16[128,8]{0,1:T(8,128)(2,1)} %param.13, s32[128,8]{0,1:T(8,128)} %param.14, s32[128]{0:T(128)S(1)} %broadcast_multiply_fusion), kind=kLoop, calls=%fused_computation.1 | loop fusion | flops 5120 | bytes 10752 | tf_op jit(solution)/shard_map/add | solution.py:299
  2.0 1.2 %copy-done.3 = bf16[128,4096]{1,0:T(8,128)(2,1)S(1)} copy-done((bf16[128,4096]{1,0:T(8,128)(2,1)S(1)}, bf16[128,4096]{1,0:T(8,128)(2,1)}, u32[]{:S(2)}) %copy-start.3) | copy-done | bytes 1048600
  3.2 0.6 route.1
  3.8 0.5 collective-permute-start
  4.3 3.5 %collective-permute-start.4 = (bf16[128,768]{1,0:T(8,128)(2,1)}, bf16[128,768]{1,0:T(8,128)(2,1)S(1)}, u32[]{:S(2)}, u32[]{:S(2)}) collective-permute-start(bf16[128,768]{1,0:T(8,128)(2,1)} %bitcast.12), channel_id=1, source_target_pairs={{0,24},{8,16},{16,8},{24,0},{1,25},{9,17},{17,9},{25,1},{2,26},{10... | collective-permute-start | bytes 589832 | tf_op jit(solution)/shard_map/hidden/ppermute | solution.py:34
  7.8 0.5 collective-permute-start.3
  8.6 2.0 %collective-permute-start.1 = (bf16[2,16,4224]{2,1,0:T(8,128)(2,1)S(1)}, bf16[2,16,4224]{2,1,0:T(8,128)(2,1)S(1)}, u32[]{:S(2)}, u32[]{:S(2)}) collective-permute-start(bf16[2,16,4224]{2,1,0:T(8,128)(2,1)S(1)} %get-tuple-element.39), channel_id=1, source_target_pairs={{0,2},{1,3},{2,0},{3,1},{4,6},{5,7},{6,4},{7,5},{8,10},{9,11},{10,... | collective-permute-start | bytes 811016 | tf_op jit(solution)/shard_map/dispatch/ppermute | solution.py:34
  10.6 2.6 %collective-permute-start.5 = (bf16[2,16,4224]{2,1,0:T(8,128)(2,1)S(1)}, bf16[2,16,4224]{2,1,0:T(8,128)(2,1)S(1)}, u32[]{:S(2)}, u32[]{:S(2)}) collective-permute-start(bf16[2,16,4224]{2,1,0:T(8,128)(2,1)S(1)} %get-tuple-element.41), channel_id=1, source_target_pairs={{0,4},{1,5},{2,6},{3,7},{4,0},{5,1},{6,2},{7,3},{8,12},{9,13},{10,... | collective-permute-start | bytes 811016 | tf_op jit(solution)/shard_map/dispatch/ppermute | solution.py:34
  13.2 0.7 %collective-permute-done.4 = bf16[128,768]{1,0:T(8,128)(2,1)S(1)} collective-permute-done((bf16[128,768]{1,0:T(8,128)(2,1)}, bf16[128,768]{1,0:T(8,128)(2,1)S(1)}, u32[]{:S(2)}, u32[]{:S(2)}) %collective-permute-start.4) | collective-permute-done | bytes 196640 | tf_op jit(solution)/shard_map/hidden/ppermute | solution.py:34
  13.9 4.0 %collective-permute-start.6 = (bf16[2,16,4224]{2,1,0:T(8,128)(2,1)S(1)}, bf16[2,16,4224]{2,1,0:T(8,128)(2,1)S(1)}, u32[]{:S(2)}, u32[]{:S(2)}) collective-permute-start(bf16[2,16,4224]{2,1,0:T(8,128)(2,1)S(1)} %get-tuple-element.42), channel_id=1, source_target_pairs={{0,6},{1,7},{2,4},{3,5},{4,2},{5,3},{6,0},{7,1},{8,14},{9,15},{10,... | collective-permute-start | bytes 811016 | tf_op jit(solution)/shard_map/dispatch/ppermute | solution.py:34
  18.1 3.6 %collective-permute-done.1.refs_2_ = bf16[2,16,4224]{2,1,0:T(8,128)(2,1)S(1)} collective-permute-done((bf16[2,16,4224]{2,1,0:T(8,128)(2,1)S(1)}, bf16[2,16,4224]{2,1,0:T(8,128)(2,1)S(1)}, u32[]{:S(2)}, u32[]{:S(2)}) %collective-permute-start.1) | collective-permute-done | bytes 270368 | tf_op jit(solution)/shard_map/dispatch/ppermute | solution.py:34
  21.8 0.6 arrive.2
  22.3 1.7 %collective-permute-start.7 = (bf16[64,1280]{1,0:T(8,128)(2,1)S(1)}, bf16[64,1280]{1,0:T(8,128)(2,1)S(1)}, u32[]{:S(2)}, u32[]{:S(2)}) collective-permute-start(bf16[64,1280]{1,0:T(8,128)(2,1)S(1)} %get-tuple-element.47), channel_id=1, source_target_pairs={{0,8},{8,0},{16,24},{24,16},{1,9},{9,1},{17,25},{25,17},{2,10},{10... | collective-permute-start | bytes 491528 | tf_op jit(solution)/shard_map/arrive/ppermute | solution.py:34
  24.1 1.5 %collective-permute-start.8 = (bf16[64,1280]{1,0:T(8,128)(2,1)S(1)}, bf16[64,1280]{1,0:T(8,128)(2,1)S(1)}, u32[]{:S(2)}, u32[]{:S(2)}) collective-permute-start(bf16[64,1280]{1,0:T(8,128)(2,1)S(1)} %get-tuple-element.48), channel_id=1, source_target_pairs={{0,16},{8,24},{16,0},{24,8},{1,17},{9,25},{17,1},{25,9},{2,18},{10... | collective-permute-start | bytes 491528 | tf_op jit(solution)/shard_map/arrive/ppermute | solution.py:34
  25.9 6.6 %collective-permute-done.5.refs_0_ = bf16[2,16,4224]{2,1,0:T(8,128)(2,1)S(1)} collective-permute-done((bf16[2,16,4224]{2,1,0:T(8,128)(2,1)S(1)}, bf16[2,16,4224]{2,1,0:T(8,128)(2,1)S(1)}, u32[]{:S(2)}, u32[]{:S(2)}) %collective-permute-start.5) | collective-permute-done | bytes 270368 | tf_op jit(solution)/shard_map/dispatch/ppermute | solution.py:34
  32.5 0.6 arrive.3
  33.1 1.6 %collective-permute-start.10 = (bf16[64,1280]{1,0:T(8,128)(2,1)S(1)}, bf16[64,1280]{1,0:T(8,128)(2,1)S(1)}, u32[]{:S(2)}, u32[]{:S(2)}) collective-permute-start(bf16[64,1280]{1,0:T(8,128)(2,1)S(1)} %get-tuple-element.53), channel_id=1, source_target_pairs={{0,8},{8,0},{16,24},{24,16},{1,9},{9,1},{17,25},{25,17},{2,10},{10... | collective-permute-start | bytes 491528 | tf_op jit(solution)/shard_map/arrive/ppermute | solution.py:34
  34.6 1.5 %collective-permute-start.11 = (bf16[64,1280]{1,0:T(8,128)(2,1)S(1)}, bf16[64,1280]{1,0:T(8,128)(2,1)S(1)}, u32[]{:S(2)}, u32[]{:S(2)}) collective-permute-start(bf16[64,1280]{1,0:T(8,128)(2,1)S(1)} %get-tuple-element.54), channel_id=1, source_target_pairs={{0,16},{8,24},{16,0},{24,8},{1,17},{9,25},{17,1},{25,9},{2,18},{10... | collective-permute-start | bytes 491528 | tf_op jit(solution)/shard_map/arrive/ppermute | solution.py:34
  36.6 0.8 %adapters.3 = (f32[256,1024]{1,0:T(8,128)S(1)}, f32[256,256]{1,0:T(8,128)S(1)}, bf16[512,768]{1,0:T(8,128)(2,1)S(1)}) custom-call(bf16[256,768]{1,0:T(8,128)(2,1)S(1)} %bitcast.9, bf16[512,768]{1,0:T(8,128)(2,1)S(1)} %pad_maximum_fusion.refs_3_.hids, bf16[64,1280]{1,0:T(8,128)(2,1)S(1)} %get-tuple-element.46.refs_0_, ...), custom_call_target="tpu_custom_call" | custom-call | flops 268435456 | bytes 524288 | tf_op jit(solution)/shard_map/adapters/pallas_call | solution.py:347
  37.4 1.7 %inner.1 = (bf16[128,768]{1,0:T(8,128)(2,1)}, f32[128,128]{1,0:T(8,128)S(1)}) custom-call(bf16[64,4224]{1,0:T(8,128)(2,1)S(1)} %get-tuple-element.40.early, bf16[64,4224]{1,0:T(8,128)(2,1)S(1)} %get-tuple-element.43.late, bf16[4096,768]{1,0:T(8,128)(2,1)S(1)} %bitcast.8, bf16[64,256]{1,0:T(8,128)(2,1)S(1)} %get-tuple-element.44.masked1, ...), custom_call_target="tpu_custom_call" | custom-call | flops 805306368 | bytes 6291456 | tf_op jit(solution)/shard_map/inner/pallas_call | solution.py:355
  39.1 1.6 %collective-permute-done.11.refs_6_.refs_2_ = bf16[64,1280]{1,0:T(8,128)(2,1)S(1)} collective-permute-done((bf16[64,1280]{1,0:T(8,128)(2,1)S(1)}, bf16[64,1280]{1,0:T(8,128)(2,1)S(1)}, u32[]{:S(2)}, u32[]{:S(2)}) %collective-permute-start.11) | collective-permute-done | bytes 163872 | tf_op jit(solution)/shard_map/arrive/ppermute | solution.py:34
  40.8 1.6 %collective-permute-done.12.refs_7_.refs_3_ = bf16[64,1280]{1,0:T(8,128)(2,1)S(1)} collective-permute-done((bf16[64,1280]{1,0:T(8,128)(2,1)S(1)}, bf16[64,1280]{1,0:T(8,128)(2,1)S(1)}, u32[]{:S(2)}, u32[]{:S(2)}) %collective-permute-start.12) | collective-permute-done | bytes 163872 | tf_op jit(solution)/shard_map/arrive/ppermute | solution.py:34
  42.4 0.8 %adapters.4 = (f32[4,32,1280]{2,1,0:T(8,128)S(1)}, bf16[4,32,1280]{2,1,0:T(8,128)(2,1)S(1)}) custom-call(bf16[256,768]{1,0:T(8,128)(2,1)S(1)} %bitcast.11, f32[256,1024]{1,0:T(8,128)S(1)} %get-tuple-element.57.out, f32[256,256]{1,0:T(8,128)S(1)} %get-tuple-element.58.inn, f32[128,128]{1,0:T(8,128)S(1)} %get-tuple-element.59.mix, ...), custom_call_target="tpu_custom_call" | custom-call | flops 268435456 | bytes 524288 | tf_op jit(solution)/shard_map/adapters/pallas_call | solution.py:364
  43.3 1.6 %collective-permute-done.13.got = bf16[4,32,1280]{2,1,0:T(8,128)(2,1)S(1)} collective-permute-done((bf16[4,32,1280]{2,1,0:T(8,128)(2,1)S(1)}, bf16[4,32,1280]{2,1,0:T(8,128)(2,1)S(1)}, u32[]{:S(2)}, u32[]{:S(2)}) %collective-permute-start.13) | collective-permute-done | bytes 327712 | tf_op jit(solution)/shard_map/adapters/ppermute | solution.py:34
  44.9 6.5 %collective-permute-start.14 = (bf16[32,1280]{1,0:T(8,128)(2,1)S(1)}, bf16[32,1280]{1,0:T(8,128)(2,1)S(1)}, u32[]{:S(2)}, u32[]{:S(2)}) collective-permute-start(bf16[32,1280]{1,0:T(8,128)(2,1)S(1)} %get-tuple-element.63), channel_id=1, source_target_pairs={{0,4},{1,5},{2,6},{3,7},{4,0},{5,1},{6,2},{7,3},{8,12},{9,13},{10,... | collective-permute-start | bytes 245768 | tf_op jit(solution)/shard_map/adapters/ppermute | solution.py:34
  51.4 1.4 %collective-permute-start.15 = (bf16[32,1280]{1,0:T(8,128)(2,1)S(1)}, bf16[32,1280]{1,0:T(8,128)(2,1)S(1)}, u32[]{:S(2)}, u32[]{:S(2)}) collective-permute-start(bf16[32,1280]{1,0:T(8,128)(2,1)S(1)} %get-tuple-element.64), channel_id=1, source_target_pairs={{0,6},{1,7},{2,4},{3,5},{4,2},{5,3},{6,0},{7,1},{8,14},{9,15},{10,... | collective-permute-start | bytes 245768 | tf_op jit(solution)/shard_map/adapters/ppermute | solution.py:34
  52.8 2.7 %product.1 = f32[1,1024,768]{2,1,0:T(8,128)} custom-call(bf16[64,1280]{1,0:T(8,128)(2,1)S(1)} %get-tuple-element.46.refs_0_, bf16[64,1280]{1,0:T(8,128)(2,1)S(1)} %collective-permute-done.7.refs_1_, bf16[64,1280]{1,0:T(8,128)(2,1)S(1)} %collective-permute-done.8.refs_2_, bf16[64,1280]{1,0:T(8,128)(2,1)S(1)} %collective-permute-done.9.refs_3_, ...), custom_call_target="tpu_custom_call" | custom-call | flops 805306368 | bytes 2097152 | tf_op jit(solution)/shard_map/product/pallas_call | solution.py:383
  55.4 2.3 %collective-permute-done.14.refs_1_ = bf16[32,1280]{1,0:T(8,128)(2,1)S(1)} collective-permute-done((bf16[32,1280]{1,0:T(8,128)(2,1)S(1)}, bf16[32,1280]{1,0:T(8,128)(2,1)S(1)}, u32[]{:S(2)}, u32[]{:S(2)}) %collective-permute-start.14) | collective-permute-done | bytes 81952 | tf_op jit(solution)/shard_map/adapters/ppermute | solution.py:34
  57.8 0.6 collective-permute-done.15.refs_2_
  58.3 0.7 %collective-permute-done.16.refs_3_ = bf16[32,1280]{1,0:T(8,128)(2,1)S(1)} collective-permute-done((bf16[32,1280]{1,0:T(8,128)(2,1)S(1)}, bf16[32,1280]{1,0:T(8,128)(2,1)S(1)}, u32[]{:S(2)}, u32[]{:S(2)}) %collective-permute-start.16) | collective-permute-done | bytes 81952 | tf_op jit(solution)/shard_map/adapters/ppermute | solution.py:34
  59.0 0.8 %final.1 = (f32[2,16,1024]{2,1,0:T(8,128)}, f32[2,16,192]{2,1,0:T(8,128)}, f32[8,128]{1,0:T(8,128)}) custom-call(f32[8,128]{1,0:T(8,128)S(1)} %add_bitcast_fusion.small, bf16[128,128]{1,0:T(8,128)(2,1)S(1)} %get-tuple-element.56.picks, bf16[32,1280]{1,0:T(8,128)(2,1)S(1)} %get-tuple-element.62.refs_0_, bf16[32,1280]{1,0:T(8,128)(2,1)S(1)} %collective-permute-done.14.refs_1_, ...), custom_call_target="tpu_custom_call" | custom-call | bytes 1000000 | tf_op jit(solution)/shard_map/final/pallas_call | solution.py:392
  (25 shorter events, 1.4 us)
Async XLA Ops:
  2.0 1.2 %copy-start.3 = (bf16[128,4096]{1,0:T(8,128)(2,1)S(1)}, bf16[128,4096]{1,0:T(8,128)(2,1)}, u32[]{:S(2)}) copy-start(bf16[128,4096]{1,0:T(8,128)(2,1)} %cot.1) | copy-start | bytes 3145732
  3.2 14.9 %copy-start.4 = (bf16[1,1,128,768]{3,2,1,0:T(8,128)(2,1)S(1)}, bf16[1,1,128,768]{3,2,1,0:T(8,128)(2,1)}, u32[]{:S(2)}) copy-start(bf16[1,1,128,768]{3,2,1,0:T(8,128)(2,1)} %param.9) | copy-start | bytes 589828
  3.8 18.0 %copy-start = (bf16[2,4096,128]{2,1,0:T(8,128)(2,1)S(1)}, bf16[2,4096,128]{2,1,0:T(8,128)(2,1)}, u32[]{:S(2)}) copy-start(bf16[2,4096,128]{2,1,0:T(8,128)(2,1)} %adapter_out.3) | copy-start | bytes 6291460
  3.8 4.7 %collective-permute-start = (bf16[4,16,4224]{2,1,0:T(8,128)(2,1)S(1)}, bf16[4,16,4224]{2,1,0:T(8,128)(2,1)S(1)}, u32[]{:S(2)}, u32[]{:S(2)}) collective-permute-start(bf16[4,16,4224]{2,1,0:T(8,128)(2,1)S(1)} %get-tuple-element.38), channel_id=1, source_target_pairs={{0,1},{1,0},{2,3},{3,2},{4,5},{5,4},{6,7},{7,6},{8,9},{9,8},{10,11... | collective-permute-start | bytes 1622024 | tf_op jit(solution)/shard_map/route/ppermute | solution.py:34
  4.3 9.5 %collective-permute-start.4 = (bf16[128,768]{1,0:T(8,128)(2,1)}, bf16[128,768]{1,0:T(8,128)(2,1)S(1)}, u32[]{:S(2)}, u32[]{:S(2)}) collective-permute-start(bf16[128,768]{1,0:T(8,128)(2,1)} %bitcast.12), channel_id=1, source_target_pairs={{0,24},{8,16},{16,8},{24,0},{1,25},{9,17},{17,9},{25,1},{2,26},{10... | collective-permute-start | bytes 589832 | tf_op jit(solution)/shard_map/hidden/ppermute | solution.py:34
  7.8 10.0 %collective-permute-start.3 = (bf16[128,768]{1,0:T(8,128)(2,1)}, bf16[128,768]{1,0:T(8,128)(2,1)S(1)}, u32[]{:S(2)}, u32[]{:S(2)}) collective-permute-start(bf16[128,768]{1,0:T(8,128)(2,1)} %bitcast.13), channel_id=1, source_target_pairs={{0,16},{8,24},{16,0},{24,8},{1,17},{9,25},{17,1},{25,9},{2,18},{10... | collective-permute-start | bytes 589832 | tf_op jit(solution)/shard_map/hidden/ppermute | solution.py:34
  8.4 9.7 %collective-permute-start.2 = (bf16[128,768]{1,0:T(8,128)(2,1)}, bf16[128,768]{1,0:T(8,128)(2,1)S(1)}, u32[]{:S(2)}, u32[]{:S(2)}) collective-permute-start(bf16[128,768]{1,0:T(8,128)(2,1)} %bitcast.14), channel_id=1, source_target_pairs={{0,8},{8,0},{16,24},{24,16},{1,9},{9,1},{17,25},{25,17},{2,10},{10... | collective-permute-start | bytes 589832 | tf_op jit(solution)/shard_map/hidden/ppermute | solution.py:34
  8.6 13.2 %collective-permute-start.1 = (bf16[2,16,4224]{2,1,0:T(8,128)(2,1)S(1)}, bf16[2,16,4224]{2,1,0:T(8,128)(2,1)S(1)}, u32[]{:S(2)}, u32[]{:S(2)}) collective-permute-start(bf16[2,16,4224]{2,1,0:T(8,128)(2,1)S(1)} %get-tuple-element.39), channel_id=1, source_target_pairs={{0,2},{1,3},{2,0},{3,1},{4,6},{5,7},{6,4},{7,5},{8,10},{9,11},{10,... | collective-permute-start | bytes 811016 | tf_op jit(solution)/shard_map/dispatch/ppermute | solution.py:34
  10.6 21.9 %collective-permute-start.5 = (bf16[2,16,4224]{2,1,0:T(8,128)(2,1)S(1)}, bf16[2,16,4224]{2,1,0:T(8,128)(2,1)S(1)}, u32[]{:S(2)}, u32[]{:S(2)}) collective-permute-start(bf16[2,16,4224]{2,1,0:T(8,128)(2,1)S(1)} %get-tuple-element.41), channel_id=1, source_target_pairs={{0,4},{1,5},{2,6},{3,7},{4,0},{5,1},{6,2},{7,3},{8,12},{9,13},{10,... | collective-permute-start | bytes 811016 | tf_op jit(solution)/shard_map/dispatch/ppermute | solution.py:34
  13.9 18.6 %collective-permute-start.6 = (bf16[2,16,4224]{2,1,0:T(8,128)(2,1)S(1)}, bf16[2,16,4224]{2,1,0:T(8,128)(2,1)S(1)}, u32[]{:S(2)}, u32[]{:S(2)}) collective-permute-start(bf16[2,16,4224]{2,1,0:T(8,128)(2,1)S(1)} %get-tuple-element.42), channel_id=1, source_target_pairs={{0,6},{1,7},{2,4},{3,5},{4,2},{5,3},{6,0},{7,1},{8,14},{9,15},{10,... | collective-permute-start | bytes 811016 | tf_op jit(solution)/shard_map/dispatch/ppermute | solution.py:34
  21.8 15.7 %copy-start.1 = (bf16[1,4096,768]{2,1,0:T(8,128)(2,1)S(1)}, bf16[1,4096,768]{2,1,0:T(8,128)(2,1)}, u32[]{:S(2)}) copy-start(bf16[1,4096,768]{2,1,0:T(8,128)(2,1)} %param.10) | copy-start | bytes 18874372
  22.3 14.3 %copy-start.2 = (bf16[2,128,768]{2,1,0:T(8,128)(2,1)S(1)}, bf16[2,128,768]{2,1,0:T(8,128)(2,1)}, u32[]{:S(2)}) copy-start(bf16[2,128,768]{2,1,0:T(8,128)(2,1)} %param.11) | copy-start | bytes 1179652
  22.3 13.8 %collective-permute-start.7 = (bf16[64,1280]{1,0:T(8,128)(2,1)S(1)}, bf16[64,1280]{1,0:T(8,128)(2,1)S(1)}, u32[]{:S(2)}, u32[]{:S(2)}) collective-permute-start(bf16[64,1280]{1,0:T(8,128)(2,1)S(1)} %get-tuple-element.47), channel_id=1, source_target_pairs={{0,8},{8,0},{16,24},{24,16},{1,9},{9,1},{17,25},{25,17},{2,10},{10... | collective-permute-start | bytes 491528 | tf_op jit(solution)/shard_map/arrive/ppermute | solution.py:34
  24.1 12.6 %collective-permute-start.8 = (bf16[64,1280]{1,0:T(8,128)(2,1)S(1)}, bf16[64,1280]{1,0:T(8,128)(2,1)S(1)}, u32[]{:S(2)}, u32[]{:S(2)}) collective-permute-start(bf16[64,1280]{1,0:T(8,128)(2,1)S(1)} %get-tuple-element.48), channel_id=1, source_target_pairs={{0,16},{8,24},{16,0},{24,8},{1,17},{9,25},{17,1},{25,9},{2,18},{10... | collective-permute-start | bytes 491528 | tf_op jit(solution)/shard_map/arrive/ppermute | solution.py:34
  25.6 11.1 %collective-permute-start.9 = (bf16[64,1280]{1,0:T(8,128)(2,1)S(1)}, bf16[64,1280]{1,0:T(8,128)(2,1)S(1)}, u32[]{:S(2)}, u32[]{:S(2)}) collective-permute-start(bf16[64,1280]{1,0:T(8,128)(2,1)S(1)} %get-tuple-element.49), channel_id=1, source_target_pairs={{0,24},{8,16},{16,8},{24,0},{1,25},{9,17},{17,9},{25,1},{2,26},{10... | collective-permute-start | bytes 491528 | tf_op jit(solution)/shard_map/arrive/ppermute | solution.py:34
  33.1 6.1 %collective-permute-start.10 = (bf16[64,1280]{1,0:T(8,128)(2,1)S(1)}, bf16[64,1280]{1,0:T(8,128)(2,1)S(1)}, u32[]{:S(2)}, u32[]{:S(2)}) collective-permute-start(bf16[64,1280]{1,0:T(8,128)(2,1)S(1)} %get-tuple-element.53), channel_id=1, source_target_pairs={{0,8},{8,0},{16,24},{24,16},{1,9},{9,1},{17,25},{25,17},{2,10},{10... | collective-permute-start | bytes 491528 | tf_op jit(solution)/shard_map/arrive/ppermute | solution.py:34
  34.6 6.1 %collective-permute-start.11 = (bf16[64,1280]{1,0:T(8,128)(2,1)S(1)}, bf16[64,1280]{1,0:T(8,128)(2,1)S(1)}, u32[]{:S(2)}, u32[]{:S(2)}) collective-permute-start(bf16[64,1280]{1,0:T(8,128)(2,1)S(1)} %get-tuple-element.54), channel_id=1, source_target_pairs={{0,16},{8,24},{16,0},{24,8},{1,17},{9,25},{17,1},{25,9},{2,18},{10... | collective-permute-start | bytes 491528 | tf_op jit(solution)/shard_map/arrive/ppermute | solution.py:34
  36.2 6.2 %collective-permute-start.12 = (bf16[64,1280]{1,0:T(8,128)(2,1)S(1)}, bf16[64,1280]{1,0:T(8,128)(2,1)S(1)}, u32[]{:S(2)}, u32[]{:S(2)}) collective-permute-start(bf16[64,1280]{1,0:T(8,128)(2,1)S(1)} %get-tuple-element.55), channel_id=1, source_target_pairs={{0,24},{8,16},{16,8},{24,0},{1,25},{9,17},{17,9},{25,1},{2,26},{10... | collective-permute-start | bytes 491528 | tf_op jit(solution)/shard_map/arrive/ppermute | solution.py:34
  43.2 1.7 %collective-permute-start.13 = (bf16[4,32,1280]{2,1,0:T(8,128)(2,1)S(1)}, bf16[4,32,1280]{2,1,0:T(8,128)(2,1)S(1)}, u32[]{:S(2)}, u32[]{:S(2)}) collective-permute-start(bf16[4,32,1280]{2,1,0:T(8,128)(2,1)S(1)} %get-tuple-element.61), channel_id=1, source_target_pairs={{0,1},{1,0},{2,3},{3,2},{4,5},{5,4},{6,7},{7,6},{8,9},{9,8},{10,11... | collective-permute-start | bytes 983048 | tf_op jit(solution)/shard_map/adapters/ppermute | solution.py:34
  44.9 12.8 %collective-permute-start.14 = (bf16[32,1280]{1,0:T(8,128)(2,1)S(1)}, bf16[32,1280]{1,0:T(8,128)(2,1)S(1)}, u32[]{:S(2)}, u32[]{:S(2)}) collective-permute-start(bf16[32,1280]{1,0:T(8,128)(2,1)S(1)} %get-tuple-element.63), channel_id=1, source_target_pairs={{0,4},{1,5},{2,6},{3,7},{4,0},{5,1},{6,2},{7,3},{8,12},{9,13},{10,... | collective-permute-start | bytes 245768 | tf_op jit(solution)/shard_map/adapters/ppermute | solution.py:34
  51.4 6.9 %collective-permute-start.15 = (bf16[32,1280]{1,0:T(8,128)(2,1)S(1)}, bf16[32,1280]{1,0:T(8,128)(2,1)S(1)}, u32[]{:S(2)}, u32[]{:S(2)}) collective-permute-start(bf16[32,1280]{1,0:T(8,128)(2,1)S(1)} %get-tuple-element.64), channel_id=1, source_target_pairs={{0,6},{1,7},{2,4},{3,5},{4,2},{5,3},{6,0},{7,1},{8,14},{9,15},{10,... | collective-permute-start | bytes 245768 | tf_op jit(solution)/shard_map/adapters/ppermute | solution.py:34
  52.8 6.3 %collective-permute-start.16 = (bf16[32,1280]{1,0:T(8,128)(2,1)S(1)}, bf16[32,1280]{1,0:T(8,128)(2,1)S(1)}, u32[]{:S(2)}, u32[]{:S(2)}) collective-permute-start(bf16[32,1280]{1,0:T(8,128)(2,1)S(1)} %get-tuple-element.65), channel_id=1, source_target_pairs={{0,2},{1,3},{2,0},{3,1},{4,6},{5,7},{6,4},{7,5},{8,10},{9,11},{10,... | collective-permute-start | bytes 245768 | tf_op jit(solution)/shard_map/adapters/ppermute | solution.py:34

commit v4 on v3

--- a/solution.py
+++ b/solution.py
@@ -113,20 +113,29 @@
     return [(z ^ hop) * 2 + (c ^ half) for hop in range(chips) for half in range(2)]
 
 
-def pack_body(chips, keep, sib, *out):
-    for hop in range(1, chips):
-        out[hop - 1][0] = keep[hop]
-        out[hop - 1][1] = sib[hop]
-
-
-def arrive_body(groups, near, adapter_out, *refs):
+def pack_body(hops, keep, sib, *refs):
+    for hop, out in zip(hops, refs[-len(hops) :]):
+        out[0] = keep[hop]
+        out[1] = sib[hop]
+
+
+def arrive_body(groups, chips, cap, own, extra, adapter_out, *refs):
     loops, width, rank = adapter_out.shape
     part = width // groups
+    side = part + rank + LANES
     parts = refs[-groups:]
-    blocks, (rows, masked) = refs[: -2 - groups - near], refs[-2 - groups : -groups]
+    blocks, (rows, masked) = refs[: -2 - groups - extra], refs[-2 - groups : -groups]
+    if own:
+        hidden, blocks = blocks[0], blocks[1:]
+        hid_width = hidden.shape[1]
+        for n, source in enumerate(sources(here(), chips)):
+            block = hidden[pl.ds(pl.multiple_of(source * cap, cap), cap), :]
+            start, at = side + (n // 2) * hid_width, (n % 2) * cap
+            for target in parts:
+                target[at : at + cap, start : start + hid_width] = block
     at = 0
-    for n, block in enumerate(blocks):
-        halves = (block[0],) if near and n < 2 else (block[0], block[1])
+    for block in blocks:
+        halves = (block[0],) if own else (block[0], block[1])
         for piece in halves:
             rows[at : at + piece.shape[0], :] = piece
             at += piece.shape[0]
@@ -146,43 +155,50 @@
     weighted = (weight * proj).astype(bf16)
     for hop in range(groups):
         parts[hop][:, part : part + rank] = weighted
-        parts[hop][:, part + rank :] = mix_block
-
-
-def inner_body(chips, cap, early, late, down, masked1, masked2, adapter_in, hidden, *refs):
-    grad_out, mix_out = refs
+        parts[hop][:, part + rank : side] = mix_block
+
+
+def inner_body(chips, cap, chunks, down, adapter_in, hidden, *refs):
+    grad_out, mix_out = refs[-2:]
     width, hid_width = down.shape
     step = 256 if hid_width % 256 == 0 else hid_width
-    rows = jnp.concatenate([early[...], late[...]], axis=0)
-    masked = jnp.concatenate([masked1[...], masked2[...]], axis=0)
+    rows = jnp.concatenate([r[...] for r in refs[:chunks]], axis=0)
+    masked = jnp.concatenate([r[...] for r in refs[chunks : 2 * chunks]], axis=0)
     weight = jnp.sum(rows[:, width:].astype(f32), axis=1, keepdims=True)
     sums = jnp.zeros((mix_out.shape[0], 1), f32)
     order = sources(here(), chips)
     for at in range(0, hid_width, step):
         cols = slice(at, at + step)
         grad = nn(masked, adapter_in[:, cols]) + nn(rows[:, :width], down[:, cols])
-        sums = sums + jnp.sum(hidden[: mix_out.shape[0], cols].astype(f32) * grad, axis=1, keepdims=True)
+        spots = [pl.ds(pl.multiple_of(source * cap, cap), cap) for source in order]
+        hid = jnp.concatenate([hidden[spot, cols] for spot in spots], axis=0)
+        sums = sums + jnp.sum(hid.astype(f32) * grad, axis=1, keepdims=True)
         scaled = (weight * grad).astype(bf16)
-        for n, source in enumerate(order):
-            spot = pl.ds(pl.multiple_of(source * cap, cap), cap)
+        for n, spot in enumerate(spots):
             grad_out[spot, cols] = scaled[n * cap : (n + 1) * cap]
     mix_out[...] = jnp.broadcast_to(sums, mix_out.shape)
 
 
-def adapter_sums(loops, cols, start, adapter_in, rows, hids):
+def hidden_rows(holder, hid_width, chips, start, stop):
+    size = holder.shape[0]
+    side = holder.shape[1] - chips * hid_width
+    blocks = [side + n * hid_width for n in range(start // size, stop // size)]
+    return [holder[:, at : at + hid_width] for at in blocks]
+
+
+def adapter_sums(loops, chips, cols, part, start, adapter_in, rows, holders):
     rank = adapter_in.shape[0] // loops
     hid_width = adapter_in.shape[1]
-    slots = rows[0].shape[0]
-    part = rows[0].shape[1] - rank - LANES
+    stop = start + rows[0].shape[0]
+    side = part + rank + LANES
     wide = wide_of(cols)
     row = lax.broadcasted_iota(jnp.int32, (hid_width, wide), 0)
     lane = lax.broadcasted_iota(jnp.int32, (hid_width, wide), 1)
     pick = (row == lane + here()[1] * cols) & (lane < cols)
     pick = jnp.where(pick, 1.0, 0.0).astype(bf16)
-    total = hids.shape[0] // len(rows)
-    starts = [g * total + start for g in range(len(rows))]
-    hid = jnp.concatenate([hids[at : at + slots, :] for at in starts], axis=0)
-    tail = jnp.concatenate([r[:, part:] for r in rows], axis=0).astype(f32)
+    hid = [x for h in holders for x in hidden_rows(h, hid_width, chips, start, stop)]
+    hid = jnp.concatenate(hid, axis=0)
+    tail = jnp.concatenate([r[:, part:side] for r in rows], axis=0).astype(f32)
     body = jnp.concatenate([r[:, :part] for r in rows], axis=0)
     down = nt(hid, adapter_in[...])
     picked = nn(hid, pick).astype(bf16)
@@ -197,23 +213,26 @@
     return -(-(cols + 4) // LANES) * LANES
 
 
-def adapter_first_body(loops, chips, cap, cols, adapter_in, hids, *refs):
-    rows, (out, inn, ordered) = refs[:-3], refs[-3:]
-    total = hids.shape[0] // len(rows)
-    for g in range(len(rows)):
-        for n, source in enumerate(sources(here(), chips)):
-            spot = pl.ds(pl.multiple_of(g * total + source * cap, cap), cap)
-            ordered[g * total + n * cap : g * total + (n + 1) * cap, :] = hids[spot, :]
-    out[...], inn[...] = adapter_sums(loops, cols, 0, adapter_in, rows, ordered)
-
-
-def adapter_last_body(loops, chips, cap, cols, adapter_in, out, inn, mix, hids, *refs):
-    rows, (keep, give, sums, narrow) = refs[:-4], refs[-4:]
+def adapter_first_body(loops, chips, cols, groups, adapter_in, _, *refs):
+    rows, (out, inn) = refs[:-2], refs[-2:]
+    start = 0
+    for at in range(0, len(rows), groups):
+        chunk = rows[at : at + groups]
+        terms = adapter_sums(
+            loops, chips, cols, out.shape[1], start, adapter_in, chunk, rows[:groups]
+        )
+        for target, term in zip((out, inn), terms):
+            target[...] = target[...] + term if start else term
+        start += chunk[0].shape[0]
+
+
+def adapter_last_body(loops, chips, cap, cols, groups, adapter_in, out, inn, mix, *refs):
+    holders, rows, (keep, give, sums, narrow) = refs[:groups], refs[groups:-4], refs[-4:]
     rank = adapter_in.shape[0] // loops
     part = out.shape[1]
     share = rank // (2 * chips)
     start = mix.shape[0] - rows[0].shape[0]
-    more = adapter_sums(loops, cols, start, adapter_in, rows, hids)
+    more = adapter_sums(loops, chips, cols, part, start, adapter_in, rows, holders)
     sums[...] = out[...] + more[0]
     narrow[...] = inn[...] + more[1]
     owners = sources(here(), chips)
@@ -269,14 +288,15 @@
     combine[...] = sums
 
 
-def product_body(groups, *refs):
-    early, late = refs[:groups], refs[groups : 2 * groups]
-    hids, out = refs[2 * groups :]
-    part = out.shape[1]
-    rights = hids[...]
+def product_body(groups, chips, *refs):
+    rows, out = refs[:-1], refs[-1]
+    _, part, hid_width = out.shape
+    slots = chips * rows[0].shape[0]
+    rights = [x for h in rows[:groups] for x in hidden_rows(h, hid_width, chips, 0, slots)]
+    rights = jnp.concatenate(rights, axis=0)
     step = 256 if part % 256 == 0 else LANES
     for at in range(0, part, step):
-        left = [p[:, at : at + step] for pair in zip(early, late) for p in pair]
+        left = [p[:, at : at + step] for g in range(groups) for p in rows[g::groups]]
         out[0, at : at + step, :] = tn(jnp.concatenate(left, axis=0), rights)
 
 
@@ -293,14 +313,15 @@
     cols = hid_width // groups
     wide = wide_of(cols)
     share = rank // experts
-    half = slots // 2
+    bounds = [0, 1, max(2, 3 * chips // 4), chips]
+    chunks = [range(a, b) for a, b in zip(bounds[:-1], bounds[1:])]
     flat_in = adapter_in.reshape(loops * rank, hid_width)
     small = token_loop.reshape(1, toks) * (experts + 1) + jnp.minimum(routes.T, experts)
     small = small.astype(f32) + probs.T.astype(f32)
 
-    with jax.named_scope("hidden"):
-        natural = hidden.reshape(slots, hid_width)
-        pair = jnp.concatenate([natural] + [swap(natural, "dp", groups, hop) for hop in range(1, groups)])
+    turns = range(groups - 1, 0, -1)
+    natural = hidden.reshape(slots, hid_width)
+
     with jax.named_scope("route"):
         packed = shape((chips, cap, width + LANES), bf16)
         keep, give, picks = call(
@@ -313,62 +334,60 @@
         )(small, cotangent)
         sib = swap(give, "expert", experts, 1)
     with jax.named_scope("dispatch"):
-        packs = call(
-            functools.partial(pack_body, chips),
-            (shape((2, cap, width + LANES), bf16),) * (chips - 1),
-            (V, V),
-            nbytes=4 * slots * width,
-        )(keep, sib)
-        far = [swap(x, "expert", experts, 2 * hop) for hop, x in enumerate(packs, 1)]
+        far = []
+        for hops in (range(1, bounds[-2]), chunks[-1]):
+            packs = call(
+                functools.partial(pack_body, hops),
+                (shape((2, cap, width + LANES), bf16),) * len(hops),
+                (V, V) + (A,) * len(far[-1:]),
+                nbytes=4 * slots * width,
+            )(keep, sib, *far[-1:])
+            far += [swap(x, "expert", experts, 2 * hop) for hop, x in zip(hops, packs)]
     with jax.named_scope("arrive"):
         rows, masked, parts = [], [], []
-        for near in (True, False):
-            blocks = [keep, sib] + far[: chips // 2 - 1] if near else far[chips // 2 - 1 :]
+        for hops in chunks:
+            own, half = hops[0] == 0, 2 * len(hops) * cap
+            blocks = [natural, keep, sib] if own else far[hops[0] - 1 : hops[-1]]
+            before = parts[0][1:] if len(parts) == 1 else []
+            sent = part + rank + LANES + chips * hid_width * own
             got = call(
-                functools.partial(arrive_body, groups, near),
+                functools.partial(arrive_body, groups, chips, cap, own, len(before)),
                 (shape((half, width + LANES), bf16), shape((half, loops * rank), bf16))
-                + (shape((half, part + rank + LANES), bf16),) * groups,
-                (V,) * (1 + len(blocks)) + (A,) * near,
+                + (shape((half, sent), bf16),) * groups,
+                (V,) * (1 + len(blocks)) + (A,) * len(before),
                 flops=2 * half * width * loops * rank,
                 nbytes=4 * half * width,
-            )(adapter_out, *blocks, *([pair] if near else []))
+            )(adapter_out, *blocks, *before)
             rows.append(got[0])
             masked.append(got[1])
-            parts.append(
-                [got[2]] + [swap(got[2 + hop], "dp", groups, hop) for hop in range(1, groups)]
-            )
-        hids, hop = pair, groups
-        while hop < groups:
-            hids = jnp.concatenate([hids, swap(hids, "dp", groups, hop)])
-            hop *= 2
-    with jax.named_scope("adapters"):
-        work = 2 * groups * half * loops * rank * (part + hid_width + wide)
-        sums = (shape((loops * rank, part), f32), shape((loops * rank, wide), f32))
-        out, inn, ordered = call(
-            functools.partial(adapter_first_body, loops, chips, cap, cols),
-            sums + (shape((groups * slots, hid_width), bf16),),
-            (V,) * (2 + groups),
-            flops=work,
-            nbytes=2 * groups * half * part,
-        )(flat_in, hids, *parts[0])
+            parts.append([got[2]] + [swap(got[2 + hop], "dp", groups, hop) for hop in turns])
     with jax.named_scope("inner"):
         grad, mix = call(
-            functools.partial(inner_body, chips, cap),
+            functools.partial(inner_body, chips, cap, len(chunks)),
             (shape((slots, hid_width), bf16), shape((slots, LANES), f32)),
-            (V,) * 7,
+            (V,) * (3 + 2 * len(chunks)),
             flops=2 * slots * width * hid_width,
             nbytes=2 * width * hid_width,
-        )(*rows, down_matrix[0], *masked, flat_in, ordered)
+        )(down_matrix[0], flat_in, natural, *rows, *masked)
     with jax.named_scope("adapters"):
+        work = groups * slots * loops * rank * (part + hid_width + wide)
+        sums = (shape((loops * rank, part), f32), shape((loops * rank, wide), f32))
+        out, inn = call(
+            functools.partial(adapter_first_body, loops, chips, cols, groups),
+            sums,
+            (V, A) + (V,) * (groups * (len(chunks) - 1)),
+            flops=work,
+            nbytes=groups * slots * part,
+        )(flat_in, mix, *(p for chunk in parts[:-1] for p in chunk))
         block = (chips, loops * share, part + wide)
         keep3, give3 = call(
-            functools.partial(adapter_last_body, loops, chips, cap, cols),
+            functools.partial(adapter_last_body, loops, chips, cap, cols, groups),
             (shape(block, f32), shape(block, bf16)),
-            (V,) * (5 + groups),
+            (V,) * (4 + 2 * groups),
             scratch=[pltpu.VMEM(s.shape, f32) for s in sums],
             flops=work,
-            nbytes=2 * groups * half * part,
-        )(flat_in, out, inn, mix, ordered, *parts[1])
+            nbytes=groups * slots * part,
+        )(flat_in, out, inn, mix, *parts[0], *parts[-1])
         got3 = swap(give3, "expert", experts, 1)
         ready = call(
             functools.partial(pair_body, chips),
@@ -381,13 +400,13 @@
             blocks[hop] = swap(ready[hop], "expert", experts, 2 * hop)
     with jax.named_scope("product"):
         product = call(
-            functools.partial(product_body, groups),
+            functools.partial(product_body, groups, chips),
             shape((1, part, hid_width), f32),
-            (V,) * (2 * groups + 1),
+            (V,) * (groups * len(chunks)),
             limit=40,
             flops=2 * groups * slots * part * hid_width,
             nbytes=4 * groups * slots * part,
-        )(*parts[0], *parts[1], ordered)
+        )(*(p for chunk in parts for p in chunk))
     with jax.named_scope("final"):
         out_grad, in_grad, combine = call(
             functools.partial(final_body, chips, cap, cols),

time: 60 us -> 57.2 us (0.953)
  waiting for transfers between devices: 19.6 us -> 15.9 us
  starting transfers between devices: 28.3 us -> 27.1 us
  Pallas kernels: 8.54 us -> 9.53 us
  local copies, waits for them, and re-layouts: 1.24 us -> 2.17 us
    ppermute x17, waiting for transfers between devices: 19.6 us -> 15.9 us  [swap(): return lax.ppermute(x, axis, [(i, i ^ mask) for i in range(size)])]
    ppermute x17, starting transfers between devices: 28.3 us -> 27.1 us  [swap(): return lax.ppermute(x, axis, [(i, i ^ mask) for i in range(size)])]
    pallas_call x7 -> x9, Pallas kernels: 7.14 us -> 8.13 us  [the longest x1 2.67 us: on_device(): call(functools.partial(product_body, groups, chips), shape((1, part, hid_...]
    unnamed x10 -> x12, local copies, waits for them, and re-layouts: 1.24 us -> 2.17 us
  transfers between devices with their start and end apart: 17 -> 17, of which waited for: 10 -> 12; matrix products, arithmetic and copies ran while one was open for 0% -> 0% of each run, Pallas kernels for 11% -> 13%
where the time goes in v4:
time: 57.2 us; the launch traced here: 56.9 us
  starting transfers between devices  27.1 us (47%)
  waiting for transfers between devices  15.9 us (28%)
  Pallas kernels  9.53 us (17%)
  local copies, waits for them, and re-layouts  2.17 us (4%)
  other arithmetic  1.51 us (3%)
  between operations  0.74 us (1%)
    ppermute x17, starting transfers between devices, swap(): return lax.ppermute(x, axis, [(i, i ^ mask) for i in range(size)])  27.1 us
    ppermute x17, waiting for transfers between devices, swap(): return lax.ppermute(x, axis, [(i, i ^ mask) for i in range(size)])  15.9 us
    pallas_call x1, Pallas kernels, on_device(): call(functools.partial(product_body, groups, chips), shape((1, part, hid_...  2.67 us
    unnamed x12, local copies, waits for them, and re-layouts  2.17 us
    pallas_call x1, Pallas kernels, on_device(): call(functools.partial(inner_body, chips, cap, len(chunks)), (shape((slot...  1.8 us
    pallas_call x3, Pallas kernels, on_device(): call(functools.partial(arrive_body, groups, chips, cap, own, len(before))...  1.47 us
    pallas_call x1, Pallas kernels, on_device(): call(functools.partial(adapter_first_body, loops, chips, cols, groups), s...  1.31 us
  transfers between devices with their start and end apart: 17, of which 12 were waited for; matrix products, arithmetic and copies ran while one was open for 0% of the time, Pallas kernels for 13%

profile of v4, /device:TPU:0, one launch (start us, length us, event | category | flops | bytes accessed | tf_op | source)
XLA Modules:
  0.0 56.9 jit_solution(1992804341586803262)
XLA Ops:
  0.6 0.8 %broadcast_multiply_fusion = s32[128]{0:T(128)S(1)} fusion(s32[128]{0:T(128)} %param.15), kind=kLoop, calls=%fused_computation.1 | loop fusion | flops 128 | bytes 1024 | tf_op jit(solution)/shard_map/mul | solution.py:319
  1.4 0.7 %add_bitcast_fusion.small = f32[8,128]{1,0:T(8,128)S(1)} fusion(bf16[128,8]{0,1:T(8,128)(2,1)} %param.13, s32[128,8]{0,1:T(8,128)} %param.14, s32[128]{0:T(128)S(1)} %broadcast_multiply_fusion), kind=kLoop, calls=%fused_computation | loop fusion | flops 5120 | bytes 10752 | tf_op jit(solution)/shard_map/add | solution.py:320
  2.2 1.2 %copy-done.3 = bf16[128,4096]{1,0:T(8,128)(2,1)S(1)} copy-done((bf16[128,4096]{1,0:T(8,128)(2,1)S(1)}, bf16[128,4096]{1,0:T(8,128)(2,1)}, u32[]{:S(2)}) %copy-start.3) | copy-done | bytes 1048600
  3.4 0.6 route.1
  4.0 0.5 collective-permute-start
  4.5 1.6 %collective-permute-done.refs_2_.sib = bf16[4,16,4224]{2,1,0:T(8,128)(2,1)S(1)} collective-permute-done((bf16[4,16,4224]{2,1,0:T(8,128)(2,1)S(1)}, bf16[4,16,4224]{2,1,0:T(8,128)(2,1)S(1)}, u32[]{:S(2)}, u32[]{:S(2)}) %collective-permute-start) | collective-permute-done | bytes 540704 | tf_op jit(solution)/shard_map/route/ppermute | solution.py:34
  6.1 4.0 %collective-permute-start.2 = (bf16[2,16,4224]{2,1,0:T(8,128)(2,1)S(1)}, bf16[2,16,4224]{2,1,0:T(8,128)(2,1)S(1)}, u32[]{:S(2)}, u32[]{:S(2)}) collective-permute-start(bf16[2,16,4224]{2,1,0:T(8,128)(2,1)S(1)} %get-tuple-element.45), channel_id=1, source_target_pairs={{0,4},{1,5},{2,6},{3,7},{4,0},{5,1},{6,2},{7,3},{8,12},{9,13},{10,... | collective-permute-start | bytes 811016 | tf_op jit(solution)/shard_map/dispatch/ppermute | solution.py:34
  10.1 0.9 %copy-done.4 = bf16[1,1,128,768]{3,2,1,0:T(8,128)(2,1)S(1)} copy-done((bf16[1,1,128,768]{3,2,1,0:T(8,128)(2,1)S(1)}, bf16[1,1,128,768]{3,2,1,0:T(8,128)(2,1)}, u32[]{:S(2)}) %copy-start.4) | copy-done | bytes 196632
  11.5 2.5 %collective-permute-start.3 = (bf16[32,4352]{1,0:T(8,128)(2,1)S(1)}, bf16[32,4352]{1,0:T(8,128)(2,1)S(1)}, u32[]{:S(2)}, u32[]{:S(2)}) collective-permute-start(bf16[32,4352]{1,0:T(8,128)(2,1)S(1)} %get-tuple-element.46), channel_id=1, source_target_pairs={{0,24},{8,16},{16,8},{24,0},{1,25},{9,17},{17,9},{25,1},{2,26},{10... | collective-permute-start | bytes 835592 | tf_op jit(solution)/shard_map/arrive/ppermute | solution.py:34
  14.0 0.5 collective-permute-start.4
  14.5 0.5 collective-permute-start.5
  15.1 1.6 %collective-permute-start.1 = (bf16[2,16,4224]{2,1,0:T(8,128)(2,1)S(1)}, bf16[2,16,4224]{2,1,0:T(8,128)(2,1)S(1)}, u32[]{:S(2)}, u32[]{:S(2)}) collective-permute-start(bf16[2,16,4224]{2,1,0:T(8,128)(2,1)S(1)} %get-tuple-element.44), channel_id=1, source_target_pairs={{0,2},{1,3},{2,0},{3,1},{4,6},{5,7},{6,4},{7,5},{8,10},{9,11},{10,... | collective-permute-start | bytes 811016 | tf_op jit(solution)/shard_map/dispatch/ppermute | solution.py:34
  16.6 6.1 %collective-permute-done.2.refs_1_.refs_0_ = bf16[2,16,4224]{2,1,0:T(8,128)(2,1)S(1)} collective-permute-done((bf16[2,16,4224]{2,1,0:T(8,128)(2,1)S(1)}, bf16[2,16,4224]{2,1,0:T(8,128)(2,1)S(1)}, u32[]{:S(2)}, u32[]{:S(2)}) %collective-permute-start.2) | collective-permute-done | bytes 270368 | tf_op jit(solution)/shard_map/dispatch/ppermute | solution.py:34
  22.8 3.6 %collective-permute-start.6 = (bf16[2,16,4224]{2,1,0:T(8,128)(2,1)S(1)}, bf16[2,16,4224]{2,1,0:T(8,128)(2,1)S(1)}, u32[]{:S(2)}, u32[]{:S(2)}) collective-permute-start(bf16[2,16,4224]{2,1,0:T(8,128)(2,1)S(1)} %dispatch.3), channel_id=1, source_target_pairs={{0,6},{1,7},{2,4},{3,5},{4,2},{5,3},{6,0},{7,1},{8,14},{9,15},{10,... | collective-permute-start | bytes 811016 | tf_op jit(solution)/shard_map/dispatch/ppermute | solution.py:34
  26.4 0.7 %collective-permute-done.1.refs_0_ = bf16[2,16,4224]{2,1,0:T(8,128)(2,1)S(1)} collective-permute-done((bf16[2,16,4224]{2,1,0:T(8,128)(2,1)S(1)}, bf16[2,16,4224]{2,1,0:T(8,128)(2,1)S(1)}, u32[]{:S(2)}, u32[]{:S(2)}) %collective-permute-start.1) | collective-permute-done | bytes 270368 | tf_op jit(solution)/shard_map/dispatch/ppermute | solution.py:34
  27.1 0.6 arrive.4
  27.7 2.6 %collective-permute-start.7 = (bf16[64,1280]{1,0:T(8,128)(2,1)S(1)}, bf16[64,1280]{1,0:T(8,128)(2,1)S(1)}, u32[]{:S(2)}, u32[]{:S(2)}) collective-permute-start(bf16[64,1280]{1,0:T(8,128)(2,1)S(1)} %get-tuple-element.57), channel_id=1, source_target_pairs={{0,24},{8,16},{16,8},{24,0},{1,25},{9,17},{17,9},{25,1},{2,26},{10... | collective-permute-start | bytes 491528 | tf_op jit(solution)/shard_map/arrive/ppermute | solution.py:34
  30.2 0.5 collective-permute-start.8
  31.2 1.9 %collective-permute-done.6.refs_0_ = bf16[2,16,4224]{2,1,0:T(8,128)(2,1)S(1)} collective-permute-done((bf16[2,16,4224]{2,1,0:T(8,128)(2,1)S(1)}, bf16[2,16,4224]{2,1,0:T(8,128)(2,1)S(1)}, u32[]{:S(2)}, u32[]{:S(2)}) %collective-permute-start.6) | collective-permute-done | bytes 270368 | tf_op jit(solution)/shard_map/dispatch/ppermute | solution.py:34
  33.6 2.5 %collective-permute-start.10 = (bf16[32,1280]{1,0:T(8,128)(2,1)S(1)}, bf16[32,1280]{1,0:T(8,128)(2,1)S(1)}, u32[]{:S(2)}, u32[]{:S(2)}) collective-permute-start(bf16[32,1280]{1,0:T(8,128)(2,1)S(1)} %get-tuple-element.61), channel_id=1, source_target_pairs={{0,24},{8,16},{16,8},{24,0},{1,25},{9,17},{17,9},{25,1},{2,26},{10... | collective-permute-start | bytes 245768 | tf_op jit(solution)/shard_map/arrive/ppermute | solution.py:34
  36.1 0.5 collective-permute-start.11
  36.6 0.7 %collective-permute-start.12 = (bf16[32,1280]{1,0:T(8,128)(2,1)S(1)}, bf16[32,1280]{1,0:T(8,128)(2,1)S(1)}, u32[]{:S(2)}, u32[]{:S(2)}) collective-permute-start(bf16[32,1280]{1,0:T(8,128)(2,1)S(1)} %get-tuple-element.63), channel_id=1, source_target_pairs={{0,8},{8,0},{16,24},{24,16},{1,9},{9,1},{17,25},{25,17},{2,10},{10... | collective-permute-start | bytes 245768 | tf_op jit(solution)/shard_map/arrive/ppermute | solution.py:34
  37.3 1.8 %inner.1 = (bf16[128,768]{1,0:T(8,128)(2,1)}, f32[128,128]{1,0:T(8,128)S(1)}) custom-call(bf16[4096,768]{1,0:T(8,128)(2,1)S(1)} %bitcast.8, bf16[256,768]{1,0:T(8,128)(2,1)S(1)} %bitcast.9, bf16[128,768]{1,0:T(8,128)(2,1)S(1)} %bitcast.13, bf16[32,4224]{1,0:T(8,128)(2,1)S(1)} %get-tuple-element.43.refs_0_, bf16[64,4224]{1,0:T(8,128)(2,1)S(1)} %get-tuple-element.49.refs_1_, ...), custom_call_target="tpu_custom_call" | custom-call | flops 805306368 | bytes 6291456 | tf_op jit(solution)/shard_map/inner/pallas_call | solution.py:365
  39.4 1.3 %adapters.3 = (f32[256,1024]{1,0:T(8,128)S(1)}, f32[256,256]{1,0:T(8,128)S(1)}) custom-call(bf16[256,768]{1,0:T(8,128)(2,1)S(1)} %bitcast.10, f32[128,128]{1,0:T(8,128)S(1)} %get-tuple-element.65._.mix, bf16[32,4352]{1,0:T(8,128)(2,1)S(1)} %get-tuple-element.55.refs_0_, bf16[32,4352]{1,0:T(8,128)(2,1)S(1)} %collective-permute-done.3.refs_2_.refs_1_, ...), custom_call_target="tpu_custom_call" | custom-call | flops 268435456 | bytes 524288 | tf_op jit(solution)/shard_map/adapters/pallas_call | solution.py:375
  40.8 0.7 %collective-permute-done.11.refs_10_.refs_6_ = bf16[32,1280]{1,0:T(8,128)(2,1)S(1)} collective-permute-done((bf16[32,1280]{1,0:T(8,128)(2,1)S(1)}, bf16[32,1280]{1,0:T(8,128)(2,1)S(1)}, u32[]{:S(2)}, u32[]{:S(2)}) %collective-permute-start.11) | collective-permute-done | bytes 81952 | tf_op jit(solution)/shard_map/arrive/ppermute | solution.py:34
  41.6 0.8 %adapters.4 = (f32[4,32,1280]{2,1,0:T(8,128)S(1)}, bf16[4,32,1280]{2,1,0:T(8,128)(2,1)S(1)}) custom-call(bf16[256,768]{1,0:T(8,128)(2,1)S(1)} %bitcast.11, f32[256,1024]{1,0:T(8,128)S(1)} %get-tuple-element.66.out, f32[256,256]{1,0:T(8,128)S(1)} %get-tuple-element.67.inn, f32[128,128]{1,0:T(8,128)S(1)} %get-tuple-element.65._.mix, ...), custom_call_target="tpu_custom_call" | custom-call | flops 268435456 | bytes 524288 | tf_op jit(solution)/shard_map/adapters/pallas_call | solution.py:383
  42.5 1.6 %collective-permute-done.13.got = bf16[4,32,1280]{2,1,0:T(8,128)(2,1)S(1)} collective-permute-done((bf16[4,32,1280]{2,1,0:T(8,128)(2,1)S(1)}, bf16[4,32,1280]{2,1,0:T(8,128)(2,1)S(1)}, u32[]{:S(2)}, u32[]{:S(2)}) %collective-permute-start.13) | collective-permute-done | bytes 327712 | tf_op jit(solution)/shard_map/adapters/ppermute | solution.py:34
  44.2 3.8 %collective-permute-start.14 = (bf16[32,1280]{1,0:T(8,128)(2,1)S(1)}, bf16[32,1280]{1,0:T(8,128)(2,1)S(1)}, u32[]{:S(2)}, u32[]{:S(2)}) collective-permute-start(bf16[32,1280]{1,0:T(8,128)(2,1)S(1)} %get-tuple-element.71), channel_id=1, source_target_pairs={{0,4},{1,5},{2,6},{3,7},{4,0},{5,1},{6,2},{7,3},{8,12},{9,13},{10,... | collective-permute-start | bytes 245768 | tf_op jit(solution)/shard_map/adapters/ppermute | solution.py:34
  48.1 2.6 %collective-permute-start.15 = (bf16[32,1280]{1,0:T(8,128)(2,1)S(1)}, bf16[32,1280]{1,0:T(8,128)(2,1)S(1)}, u32[]{:S(2)}, u32[]{:S(2)}) collective-permute-start(bf16[32,1280]{1,0:T(8,128)(2,1)S(1)} %get-tuple-element.72), channel_id=1, source_target_pairs={{0,6},{1,7},{2,4},{3,5},{4,2},{5,3},{6,0},{7,1},{8,14},{9,15},{10,... | collective-permute-start | bytes 245768 | tf_op jit(solution)/shard_map/adapters/ppermute | solution.py:34
  50.7 2.7 %product.1 = f32[1,1024,768]{2,1,0:T(8,128)} custom-call(bf16[32,4352]{1,0:T(8,128)(2,1)S(1)} %get-tuple-element.55.refs_0_, bf16[32,4352]{1,0:T(8,128)(2,1)S(1)} %collective-permute-done.3.refs_2_.refs_1_, bf16[32,4352]{1,0:T(8,128)(2,1)S(1)} %collective-permute-done.4.refs_3_.refs_2_, bf16[32,4352]{1,0:T(8,128)(2,1)S(1)} %collective-permute-done.5.refs_4_.refs_3_, ...), custom_call_target="tpu_custom_call" | custom-call | flops 805306368 | bytes 2097152 | tf_op jit(solution)/shard_map/product/pallas_call | solution.py:402
  53.4 2.4 %collective-permute-done.15.refs_2_ = bf16[32,1280]{1,0:T(8,128)(2,1)S(1)} collective-permute-done((bf16[32,1280]{1,0:T(8,128)(2,1)S(1)}, bf16[32,1280]{1,0:T(8,128)(2,1)S(1)}, u32[]{:S(2)}, u32[]{:S(2)}) %collective-permute-start.15) | collective-permute-done | bytes 81952 | tf_op jit(solution)/shard_map/adapters/ppermute | solution.py:34
  56.2 0.8 %final.1 = (f32[2,16,1024]{2,1,0:T(8,128)}, f32[2,16,192]{2,1,0:T(8,128)}, f32[8,128]{1,0:T(8,128)}) custom-call(f32[8,128]{1,0:T(8,128)S(1)} %add_bitcast_fusion.small, bf16[128,128]{1,0:T(8,128)(2,1)S(1)} %get-tuple-element.64.picks, bf16[32,1280]{1,0:T(8,128)(2,1)S(1)} %get-tuple-element.70.refs_0_, bf16[32,1280]{1,0:T(8,128)(2,1)S(1)} %collective-permute-done.14.refs_1_, ...), custom_call_target="tpu_custom_call" | custom-call | bytes 1000000 | tf_op jit(solution)/shard_map/final/pallas_call | solution.py:411
  (28 shorter events, 2.5 us)
Async XLA Ops:
  0.6 9.5 %copy-start = (bf16[2,4096,128]{2,1,0:T(8,128)(2,1)S(1)}, bf16[2,4096,128]{2,1,0:T(8,128)(2,1)}, u32[]{:S(2)}) copy-start(bf16[2,4096,128]{2,1,0:T(8,128)(2,1)} %adapter_out.5) | copy-start | bytes 6291460
  2.2 1.2 %copy-start.3 = (bf16[128,4096]{1,0:T(8,128)(2,1)S(1)}, bf16[128,4096]{1,0:T(8,128)(2,1)}, u32[]{:S(2)}) copy-start(bf16[128,4096]{1,0:T(8,128)(2,1)} %cot.1) | copy-start | bytes 3145732
  4.0 2.1 %collective-permute-start = (bf16[4,16,4224]{2,1,0:T(8,128)(2,1)S(1)}, bf16[4,16,4224]{2,1,0:T(8,128)(2,1)S(1)}, u32[]{:S(2)}, u32[]{:S(2)}) collective-permute-start(bf16[4,16,4224]{2,1,0:T(8,128)(2,1)S(1)} %get-tuple-element.42), channel_id=1, source_target_pairs={{0,1},{1,0},{2,3},{3,2},{4,5},{5,4},{6,7},{7,6},{8,9},{9,8},{10,11... | collective-permute-start | bytes 1622024 | tf_op jit(solution)/shard_map/route/ppermute | solution.py:34
  6.1 16.7 %collective-permute-start.2 = (bf16[2,16,4224]{2,1,0:T(8,128)(2,1)S(1)}, bf16[2,16,4224]{2,1,0:T(8,128)(2,1)S(1)}, u32[]{:S(2)}, u32[]{:S(2)}) collective-permute-start(bf16[2,16,4224]{2,1,0:T(8,128)(2,1)S(1)} %get-tuple-element.45), channel_id=1, source_target_pairs={{0,4},{1,5},{2,6},{3,7},{4,0},{5,1},{6,2},{7,3},{8,12},{9,13},{10,... | collective-permute-start | bytes 811016 | tf_op jit(solution)/shard_map/dispatch/ppermute | solution.py:34
  10.1 0.9 %copy-start.4 = (bf16[1,1,128,768]{3,2,1,0:T(8,128)(2,1)S(1)}, bf16[1,1,128,768]{3,2,1,0:T(8,128)(2,1)}, u32[]{:S(2)}) copy-start(bf16[1,1,128,768]{3,2,1,0:T(8,128)(2,1)} %param.9) | copy-start | bytes 589828
  11.5 15.6 %collective-permute-start.3 = (bf16[32,4352]{1,0:T(8,128)(2,1)S(1)}, bf16[32,4352]{1,0:T(8,128)(2,1)S(1)}, u32[]{:S(2)}, u32[]{:S(2)}) collective-permute-start(bf16[32,4352]{1,0:T(8,128)(2,1)S(1)} %get-tuple-element.46), channel_id=1, source_target_pairs={{0,24},{8,16},{16,8},{24,0},{1,25},{9,17},{17,9},{25,1},{2,26},{10... | collective-permute-start | bytes 835592 | tf_op jit(solution)/shard_map/arrive/ppermute | solution.py:34
  14.0 13.1 %collective-permute-start.4 = (bf16[32,4352]{1,0:T(8,128)(2,1)S(1)}, bf16[32,4352]{1,0:T(8,128)(2,1)S(1)}, u32[]{:S(2)}, u32[]{:S(2)}) collective-permute-start(bf16[32,4352]{1,0:T(8,128)(2,1)S(1)} %get-tuple-element.47), channel_id=1, source_target_pairs={{0,16},{8,24},{16,0},{24,8},{1,17},{9,25},{17,1},{25,9},{2,18},{10... | collective-permute-start | bytes 835592 | tf_op jit(solution)/shard_map/arrive/ppermute | solution.py:34
  14.5 12.6 %collective-permute-start.5 = (bf16[32,4352]{1,0:T(8,128)(2,1)S(1)}, bf16[32,4352]{1,0:T(8,128)(2,1)S(1)}, u32[]{:S(2)}, u32[]{:S(2)}) collective-permute-start(bf16[32,4352]{1,0:T(8,128)(2,1)S(1)} %get-tuple-element.48), channel_id=1, source_target_pairs={{0,8},{8,0},{16,24},{24,16},{1,9},{9,1},{17,25},{25,17},{2,10},{10... | collective-permute-start | bytes 835592 | tf_op jit(solution)/shard_map/arrive/ppermute | solution.py:34
  15.1 12.0 %collective-permute-start.1 = (bf16[2,16,4224]{2,1,0:T(8,128)(2,1)S(1)}, bf16[2,16,4224]{2,1,0:T(8,128)(2,1)S(1)}, u32[]{:S(2)}, u32[]{:S(2)}) collective-permute-start(bf16[2,16,4224]{2,1,0:T(8,128)(2,1)S(1)} %get-tuple-element.44), channel_id=1, source_target_pairs={{0,2},{1,3},{2,0},{3,1},{4,6},{5,7},{6,4},{7,5},{8,10},{9,11},{10,... | collective-permute-start | bytes 811016 | tf_op jit(solution)/shard_map/dispatch/ppermute | solution.py:34
  22.8 14.6 %copy-start.1 = (bf16[1,4096,768]{2,1,0:T(8,128)(2,1)S(1)}, bf16[1,4096,768]{2,1,0:T(8,128)(2,1)}, u32[]{:S(2)}) copy-start(bf16[1,4096,768]{2,1,0:T(8,128)(2,1)} %param.10) | copy-start | bytes 18874372
  22.8 14.5 %copy-start.2 = (bf16[2,128,768]{2,1,0:T(8,128)(2,1)S(1)}, bf16[2,128,768]{2,1,0:T(8,128)(2,1)}, u32[]{:S(2)}) copy-start(bf16[2,128,768]{2,1,0:T(8,128)(2,1)} %param.11) | copy-start | bytes 1179652
  22.8 14.5 %copy-start.5 = (bf16[1,1,128,768]{3,2,1,0:T(8,128)(2,1)S(1)}, bf16[1,1,128,768]{3,2,1,0:T(8,128)(2,1)}, u32[]{:S(2)}) copy-start(bf16[1,1,128,768]{3,2,1,0:T(8,128)(2,1)} %param.9) | copy-start | bytes 589828
  22.8 10.3 %collective-permute-start.6 = (bf16[2,16,4224]{2,1,0:T(8,128)(2,1)S(1)}, bf16[2,16,4224]{2,1,0:T(8,128)(2,1)S(1)}, u32[]{:S(2)}, u32[]{:S(2)}) collective-permute-start(bf16[2,16,4224]{2,1,0:T(8,128)(2,1)S(1)} %dispatch.3), channel_id=1, source_target_pairs={{0,6},{1,7},{2,4},{3,5},{4,2},{5,3},{6,0},{7,1},{8,14},{9,15},{10,... | collective-permute-start | bytes 811016 | tf_op jit(solution)/shard_map/dispatch/ppermute | solution.py:34
  27.7 9.0 %collective-permute-start.7 = (bf16[64,1280]{1,0:T(8,128)(2,1)S(1)}, bf16[64,1280]{1,0:T(8,128)(2,1)S(1)}, u32[]{:S(2)}, u32[]{:S(2)}) collective-permute-start(bf16[64,1280]{1,0:T(8,128)(2,1)S(1)} %get-tuple-element.57), channel_id=1, source_target_pairs={{0,24},{8,16},{16,8},{24,0},{1,25},{9,17},{17,9},{25,1},{2,26},{10... | collective-permute-start | bytes 491528 | tf_op jit(solution)/shard_map/arrive/ppermute | solution.py:34
  30.2 9.0 %collective-permute-start.8 = (bf16[64,1280]{1,0:T(8,128)(2,1)S(1)}, bf16[64,1280]{1,0:T(8,128)(2,1)S(1)}, u32[]{:S(2)}, u32[]{:S(2)}) collective-permute-start(bf16[64,1280]{1,0:T(8,128)(2,1)S(1)} %get-tuple-element.58), channel_id=1, source_target_pairs={{0,16},{8,24},{16,0},{24,8},{1,17},{9,25},{17,1},{25,9},{2,18},{10... | collective-permute-start | bytes 491528 | tf_op jit(solution)/shard_map/arrive/ppermute | solution.py:34
  30.7 8.7 %collective-permute-start.9 = (bf16[64,1280]{1,0:T(8,128)(2,1)S(1)}, bf16[64,1280]{1,0:T(8,128)(2,1)S(1)}, u32[]{:S(2)}, u32[]{:S(2)}) collective-permute-start(bf16[64,1280]{1,0:T(8,128)(2,1)S(1)} %get-tuple-element.59), channel_id=1, source_target_pairs={{0,8},{8,0},{16,24},{24,16},{1,9},{9,1},{17,25},{25,17},{2,10},{10... | collective-permute-start | bytes 491528 | tf_op jit(solution)/shard_map/arrive/ppermute | solution.py:34
  33.6 7.2 %collective-permute-start.10 = (bf16[32,1280]{1,0:T(8,128)(2,1)S(1)}, bf16[32,1280]{1,0:T(8,128)(2,1)S(1)}, u32[]{:S(2)}, u32[]{:S(2)}) collective-permute-start(bf16[32,1280]{1,0:T(8,128)(2,1)S(1)} %get-tuple-element.61), channel_id=1, source_target_pairs={{0,24},{8,16},{16,8},{24,0},{1,25},{9,17},{17,9},{25,1},{2,26},{10... | collective-permute-start | bytes 245768 | tf_op jit(solution)/shard_map/arrive/ppermute | solution.py:34
  36.1 5.4 %collective-permute-start.11 = (bf16[32,1280]{1,0:T(8,128)(2,1)S(1)}, bf16[32,1280]{1,0:T(8,128)(2,1)S(1)}, u32[]{:S(2)}, u32[]{:S(2)}) collective-permute-start(bf16[32,1280]{1,0:T(8,128)(2,1)S(1)} %get-tuple-element.62), channel_id=1, source_target_pairs={{0,16},{8,24},{16,0},{24,8},{1,17},{9,25},{17,1},{25,9},{2,18},{10... | collective-permute-start | bytes 245768 | tf_op jit(solution)/shard_map/arrive/ppermute | solution.py:34
  36.6 5.0 %collective-permute-start.12 = (bf16[32,1280]{1,0:T(8,128)(2,1)S(1)}, bf16[32,1280]{1,0:T(8,128)(2,1)S(1)}, u32[]{:S(2)}, u32[]{:S(2)}) collective-permute-start(bf16[32,1280]{1,0:T(8,128)(2,1)S(1)} %get-tuple-element.63), channel_id=1, source_target_pairs={{0,8},{8,0},{16,24},{24,16},{1,9},{9,1},{17,25},{25,17},{2,10},{10... | collective-permute-start | bytes 245768 | tf_op jit(solution)/shard_map/arrive/ppermute | solution.py:34
  42.5 1.7 %collective-permute-start.13 = (bf16[4,32,1280]{2,1,0:T(8,128)(2,1)S(1)}, bf16[4,32,1280]{2,1,0:T(8,128)(2,1)S(1)}, u32[]{:S(2)}, u32[]{:S(2)}) collective-permute-start(bf16[4,32,1280]{2,1,0:T(8,128)(2,1)S(1)} %get-tuple-element.69), channel_id=1, source_target_pairs={{0,1},{1,0},{2,3},{3,2},{4,5},{5,4},{6,7},{7,6},{8,9},{9,8},{10,11... | collective-permute-start | bytes 983048 | tf_op jit(solution)/shard_map/adapters/ppermute | solution.py:34
  44.2 9.2 %collective-permute-start.14 = (bf16[32,1280]{1,0:T(8,128)(2,1)S(1)}, bf16[32,1280]{1,0:T(8,128)(2,1)S(1)}, u32[]{:S(2)}, u32[]{:S(2)}) collective-permute-start(bf16[32,1280]{1,0:T(8,128)(2,1)S(1)} %get-tuple-element.71), channel_id=1, source_target_pairs={{0,4},{1,5},{2,6},{3,7},{4,0},{5,1},{6,2},{7,3},{8,12},{9,13},{10,... | collective-permute-start | bytes 245768 | tf_op jit(solution)/shard_map/adapters/ppermute | solution.py:34
  48.1 7.7 %collective-permute-start.15 = (bf16[32,1280]{1,0:T(8,128)(2,1)S(1)}, bf16[32,1280]{1,0:T(8,128)(2,1)S(1)}, u32[]{:S(2)}, u32[]{:S(2)}) collective-permute-start(bf16[32,1280]{1,0:T(8,128)(2,1)S(1)} %get-tuple-element.72), channel_id=1, source_target_pairs={{0,6},{1,7},{2,4},{3,5},{4,2},{5,3},{6,0},{7,1},{8,14},{9,15},{10,... | collective-permute-start | bytes 245768 | tf_op jit(solution)/shard_map/adapters/ppermute | solution.py:34
  50.7 5.5 %collective-permute-start.16 = (bf16[32,1280]{1,0:T(8,128)(2,1)S(1)}, bf16[32,1280]{1,0:T(8,128)(2,1)S(1)}, u32[]{:S(2)}, u32[]{:S(2)}) collective-permute-start(bf16[32,1280]{1,0:T(8,128)(2,1)S(1)} %get-tuple-element.73), channel_id=1, source_target_pairs={{0,2},{1,3},{2,0},{3,1},{4,6},{5,7},{6,4},{7,5},{8,10},{9,11},{10,... | collective-permute-start | bytes 245768 | tf_op jit(solution)/shard_map/adapters/ppermute | solution.py:34

commit v5 on v4

--- a/solution.py
+++ b/solution.py
@@ -71,7 +71,17 @@
     return route, rest - route, loop[:1]
 
 
-def route_body(chips, cap, loops, small, cot, keep, give, picks, mixed):
+def deal_rows(middle, rows, at, keep, lead, give):
+    chips = keep.shape[0]
+    keep[:, :, at] = rows[:chips]
+    lead[0, :, at], lead[1, :, at] = rows[middle], rows[chips + middle]
+    give[:middle, :, at] = rows[chips : chips + middle]
+    if middle + 1 < chips:
+        give[middle:, :, at] = rows[chips + middle + 1 :]
+
+
+def route_body(chips, cap, loops, small, cot, keep, lead, give, picks, mixed):
+    middle = chips // 2
     experts = 2 * chips
     ways = small.shape[0]
     toks, width = cot.shape
@@ -97,15 +107,12 @@
     loop_rows = lax.broadcasted_iota(jnp.int32, (LANES, toks), 0).astype(f32)
     loop_rows = jnp.where(loop_rows == loop, 1.0, 0.0).astype(bf16)
     mix = nt(mixed[...], loop_rows).astype(bf16)
-    half = chips * cap
-    keep[:, :, width:] = mix[:half].reshape(chips, cap, LANES)
-    give[:, :, width:] = mix[half:].reshape(chips, cap, LANES)
+    deal_rows(middle, mix.reshape(2 * chips, cap, LANES), slice(width, width + LANES), keep, lead, give)
     step = 1024 if width % 1024 == 0 else width
     for n in range(0, width, step):
         at = slice(n, n + step)
         got = nn(picks[...], cot[:, at]).astype(bf16)
-        keep[:, :, at] = got[:half].reshape(chips, cap, step)
-        give[:, :, at] = got[half:].reshape(chips, cap, step)
+        deal_rows(middle, got.reshape(2 * chips, cap, step), at, keep, lead, give)
 
 
 def sources(place, chips):
@@ -113,10 +120,10 @@
     return [(z ^ hop) * 2 + (c ^ half) for hop in range(chips) for half in range(2)]
 
 
-def pack_body(hops, keep, sib, *refs):
+def pack_body(hops, chips, keep, sib, *refs):
     for hop, out in zip(hops, refs[-len(hops) :]):
-        out[0] = keep[hop]
-        out[1] = sib[hop]
+        out[0, :, : keep.shape[2]] = keep[hop]
+        out[1, :, : keep.shape[2]] = sib[hop - (hop > chips // 2)]
 
 
 def arrive_body(groups, chips, cap, own, extra, adapter_out, *refs):
@@ -135,9 +142,12 @@
                 target[at : at + cap, start : start + hid_width] = block
     at = 0
     for block in blocks:
-        halves = (block[0],) if own else (block[0], block[1])
+        if len(block.shape) == 2:
+            halves = (block[...],)
+        else:
+            halves = (block[0],) if own else (block[0], block[1])
         for piece in halves:
-            rows[at : at + piece.shape[0], :] = piece
+            rows[at : at + piece.shape[0], :] = piece[:, : rows.shape[1]]
             at += piece.shape[0]
     mix_block = rows[:, width:]
     mix = mix_block.astype(f32)
@@ -324,9 +334,14 @@
 
     with jax.named_scope("route"):
         packed = shape((chips, cap, width + LANES), bf16)
-        keep, give, picks = call(
+        keep, lead, give, picks = call(
             functools.partial(route_body, chips, cap, loops),
-            (packed, packed, shape((slots, toks), bf16)),
+            (
+                packed,
+                shape((2,) + packed.shape[1:], bf16),
+                shape((chips - 1,) + packed.shape[1:], bf16),
+                shape((slots, toks), bf16),
+            ),
             (V, V),
             scratch=(pltpu.VMEM((slots, toks), bf16),),
             flops=2 * slots * toks * width,
@@ -334,20 +349,23 @@
         )(small, cotangent)
         sib = swap(give, "expert", experts, 1)
     with jax.named_scope("dispatch"):
-        far = []
-        for hops in (range(1, bounds[-2]), chunks[-1]):
+        middle = chips // 2
+        lead = swap(lead, "expert", experts, 2 * middle)
+        far = {middle: [lead[0], swap(lead[1], "expert", experts, 1)]}
+        others = [hop for hop in range(1, bounds[-2]) if hop != middle]
+        for hops, after in ((others, []), (chunks[-1], 1)):
             packs = call(
-                functools.partial(pack_body, hops),
-                (shape((2, cap, width + LANES), bf16),) * len(hops),
-                (V, V) + (A,) * len(far[-1:]),
+                functools.partial(pack_body, hops, chips),
+                tuple(shape((2, cap, width + (3 if hop == 1 else 1) * LANES), bf16) for hop in hops),
+                (V, V) + (A,) * bool(after),
                 nbytes=4 * slots * width,
-            )(keep, sib, *far[-1:])
-            far += [swap(x, "expert", experts, 2 * hop) for hop, x in zip(hops, packs)]
+            )(keep, sib, *(far[1] if after else []))
+            far.update((hop, [swap(x, "expert", experts, 2 * hop)]) for hop, x in zip(hops, packs))
     with jax.named_scope("arrive"):
         rows, masked, parts = [], [], []
         for hops in chunks:
             own, half = hops[0] == 0, 2 * len(hops) * cap
-            blocks = [natural, keep, sib] if own else far[hops[0] - 1 : hops[-1]]
+            blocks = [natural, keep, sib] if own else [x for hop in hops for x in far[hop]]
             before = parts[0][1:] if len(parts) == 1 else []
             sent = part + rank + LANES + chips * hid_width * own
             got = call(

time: 57.2 us -> 56.6 us (0.990)
  waiting for transfers between devices: 15.9 us -> 15.1 us
    ppermute x17 -> x18, waiting for transfers between devices: 15.9 us -> 15.1 us  [swap(): return lax.ppermute(x, axis, [(i, i ^ mask) for i in range(size)])]
    ppermute x17 -> x18, starting transfers between devices: 27.1 us -> 27.2 us  [swap(): return lax.ppermute(x, axis, [(i, i ^ mask) for i in range(size)])]
  transfers between devices with their start and end apart: 17 -> 18, of which waited for: 12 -> 12; matrix products, arithmetic and copies ran while one was open for 0% -> 0% of each run, Pallas kernels for 13% -> 13%
where the time goes in v5:
time: 56.6 us; the launch traced here: 56.3 us
  starting transfers between devices  27.2 us (48%)
  waiting for transfers between devices  15.1 us (27%)
  Pallas kernels  9.54 us (17%)
  local copies, waits for them, and re-layouts  2.19 us (4%)
  other arithmetic  1.51 us (3%)
  between operations  0.75 us (1%)
    ppermute x18, starting transfers between devices, swap(): return lax.ppermute(x, axis, [(i, i ^ mask) for i in range(size)])  27.2 us
    ppermute x18, waiting for transfers between devices, swap(): return lax.ppermute(x, axis, [(i, i ^ mask) for i in range(size)])  15.1 us
    pallas_call x1, Pallas kernels, on_device(): call(functools.partial(product_body, groups, chips), shape((1, part, hid_...  2.67 us
    unnamed x12, local copies, waits for them, and re-layouts  2.17 us
    pallas_call x1, Pallas kernels, on_device(): call(functools.partial(inner_body, chips, cap, len(chunks)), (shape((slot...  1.84 us
    pallas_call x3, Pallas kernels, on_device(): call(functools.partial(arrive_body, groups, chips, cap, own, len(before))...  1.47 us
    pallas_call x1, Pallas kernels, on_device(): call(functools.partial(adapter_first_body, loops, chips, cols, groups), s...  1.31 us
  transfers between devices with their start and end apart: 18, of which 12 were waited for; matrix products, arithmetic and copies ran while one was open for 0% of the time, Pallas kernels for 13%

profile of v5, /device:TPU:0, one launch (start us, length us, event | category | flops | bytes accessed | tf_op | source)
XLA Modules:
  0.0 56.3 jit_solution(8840491348309883718)
XLA Ops:
  0.6 0.8 %broadcast_multiply_fusion = s32[128]{0:T(128)S(1)} fusion(s32[128]{0:T(128)} %param.15), kind=kLoop, calls=%fused_computation.3 | loop fusion | flops 128 | bytes 1024 | tf_op jit(solution)/shard_map/mul | solution.py:329
  1.4 0.7 %add_bitcast_fusion.small = f32[8,128]{1,0:T(8,128)S(1)} fusion(bf16[128,8]{0,1:T(8,128)(2,1)} %param.13, s32[128,8]{0,1:T(8,128)} %param.14, s32[128]{0:T(128)S(1)} %broadcast_multiply_fusion), kind=kLoop, calls=%fused_computation.2 | loop fusion | flops 5120 | bytes 10752 | tf_op jit(solution)/shard_map/add | solution.py:330
  2.2 1.2 %copy-done.3 = bf16[128,4096]{1,0:T(8,128)(2,1)S(1)} copy-done((bf16[128,4096]{1,0:T(8,128)(2,1)S(1)}, bf16[128,4096]{1,0:T(8,128)(2,1)}, u32[]{:S(2)}) %copy-start.3) | copy-done | bytes 1048600
  3.4 0.6 route.1
  4.0 0.5 collective-permute-start
  4.5 3.7 %collective-permute-start.2 = (bf16[2,16,4224]{2,1,0:T(8,128)(2,1)S(1)}, bf16[2,16,4224]{2,1,0:T(8,128)(2,1)S(1)}, u32[]{:S(2)}, u32[]{:S(2)}) collective-permute-start(bf16[2,16,4224]{2,1,0:T(8,128)(2,1)S(1)} %get-tuple-element.43), channel_id=1, source_target_pairs={{0,4},{1,5},{2,6},{3,7},{4,0},{5,1},{6,2},{7,3},{8,12},{9,13},{10,... | collective-permute-start | bytes 811016 | tf_op jit(solution)/shard_map/dispatch/ppermute | solution.py:34
  8.2 1.6 %collective-permute-start.1 = (bf16[2,16,4480]{2,1,0:T(8,128)(2,1)S(1)}, bf16[2,16,4480]{2,1,0:T(8,128)(2,1)S(1)}, u32[]{:S(2)}, u32[]{:S(2)}) collective-permute-start(bf16[2,16,4480]{2,1,0:T(8,128)(2,1)S(1)} %dispatch.2), channel_id=1, source_target_pairs={{0,2},{1,3},{2,0},{3,1},{4,6},{5,7},{6,4},{7,5},{8,10},{9,11},{10,... | collective-permute-start | bytes 860168 | tf_op jit(solution)/shard_map/dispatch/ppermute | solution.py:34
  9.8 0.9 %copy-done.4 = bf16[1,1,128,768]{3,2,1,0:T(8,128)(2,1)S(1)} copy-done((bf16[1,1,128,768]{3,2,1,0:T(8,128)(2,1)S(1)}, bf16[1,1,128,768]{3,2,1,0:T(8,128)(2,1)}, u32[]{:S(2)}) %copy-start.4) | copy-done | bytes 196632
  11.2 2.5 %collective-permute-start.4 = (bf16[32,4352]{1,0:T(8,128)(2,1)S(1)}, bf16[32,4352]{1,0:T(8,128)(2,1)S(1)}, u32[]{:S(2)}, u32[]{:S(2)}) collective-permute-start(bf16[32,4352]{1,0:T(8,128)(2,1)S(1)} %get-tuple-element.44), channel_id=1, source_target_pairs={{0,24},{8,16},{16,8},{24,0},{1,25},{9,17},{17,9},{25,1},{2,26},{10... | collective-permute-start | bytes 835592 | tf_op jit(solution)/shard_map/arrive/ppermute | solution.py:34
  14.2 0.5 collective-permute-start.6
  14.8 6.3 %collective-permute-done.2 = bf16[2,16,4224]{2,1,0:T(8,128)(2,1)S(1)} collective-permute-done((bf16[2,16,4224]{2,1,0:T(8,128)(2,1)S(1)}, bf16[2,16,4224]{2,1,0:T(8,128)(2,1)S(1)}, u32[]{:S(2)}, u32[]{:S(2)}) %collective-permute-start.2) | collective-permute-done | bytes 270368 | tf_op jit(solution)/shard_map/dispatch/ppermute | solution.py:34
  21.2 0.5 collective-permute-done.1.refs_0_
  21.8 3.8 %collective-permute-start.7 = (bf16[2,16,4224]{2,1,0:T(8,128)(2,1)S(1)}, bf16[2,16,4224]{2,1,0:T(8,128)(2,1)S(1)}, u32[]{:S(2)}, u32[]{:S(2)}) collective-permute-start(bf16[2,16,4224]{2,1,0:T(8,128)(2,1)S(1)} %dispatch.3), channel_id=1, source_target_pairs={{0,6},{1,7},{2,4},{3,5},{4,2},{5,3},{6,0},{7,1},{8,14},{9,15},{10,... | collective-permute-start | bytes 811016 | tf_op jit(solution)/shard_map/dispatch/ppermute | solution.py:34
  25.6 1.0 %collective-permute-done.5.refs_4_.refs_2_ = bf16[32,4352]{1,0:T(8,128)(2,1)S(1)} collective-permute-done((bf16[32,4352]{1,0:T(8,128)(2,1)S(1)}, bf16[32,4352]{1,0:T(8,128)(2,1)S(1)}, u32[]{:S(2)}, u32[]{:S(2)}) %collective-permute-start.5) | collective-permute-done | bytes 278560 | tf_op jit(solution)/shard_map/arrive/ppermute | solution.py:34
  26.7 0.6 arrive.4
  27.3 1.7 %collective-permute-start.8 = (bf16[64,1280]{1,0:T(8,128)(2,1)S(1)}, bf16[64,1280]{1,0:T(8,128)(2,1)S(1)}, u32[]{:S(2)}, u32[]{:S(2)}) collective-permute-start(bf16[64,1280]{1,0:T(8,128)(2,1)S(1)} %get-tuple-element.55), channel_id=1, source_target_pairs={{0,24},{8,16},{16,8},{24,0},{1,25},{9,17},{17,9},{25,1},{2,26},{10... | collective-permute-start | bytes 491528 | tf_op jit(solution)/shard_map/arrive/ppermute | solution.py:34
  29.0 1.3 %collective-permute-start.9 = (bf16[64,1280]{1,0:T(8,128)(2,1)S(1)}, bf16[64,1280]{1,0:T(8,128)(2,1)S(1)}, u32[]{:S(2)}, u32[]{:S(2)}) collective-permute-start(bf16[64,1280]{1,0:T(8,128)(2,1)S(1)} %get-tuple-element.56), channel_id=1, source_target_pairs={{0,16},{8,24},{16,0},{24,8},{1,17},{9,25},{17,1},{25,9},{2,18},{10... | collective-permute-start | bytes 491528 | tf_op jit(solution)/shard_map/arrive/ppermute | solution.py:34
  30.3 0.5 collective-permute-start.10
  30.8 1.3 %collective-permute-done.7.refs_0_ = bf16[2,16,4224]{2,1,0:T(8,128)(2,1)S(1)} collective-permute-done((bf16[2,16,4224]{2,1,0:T(8,128)(2,1)S(1)}, bf16[2,16,4224]{2,1,0:T(8,128)(2,1)S(1)}, u32[]{:S(2)}, u32[]{:S(2)}) %collective-permute-start.7) | collective-permute-done | bytes 270368 | tf_op jit(solution)/shard_map/dispatch/ppermute | solution.py:34
  32.6 2.6 %collective-permute-start.11 = (bf16[32,1280]{1,0:T(8,128)(2,1)S(1)}, bf16[32,1280]{1,0:T(8,128)(2,1)S(1)}, u32[]{:S(2)}, u32[]{:S(2)}) collective-permute-start(bf16[32,1280]{1,0:T(8,128)(2,1)S(1)} %get-tuple-element.59), channel_id=1, source_target_pairs={{0,24},{8,16},{16,8},{24,0},{1,25},{9,17},{17,9},{25,1},{2,26},{10... | collective-permute-start | bytes 245768 | tf_op jit(solution)/shard_map/arrive/ppermute | solution.py:34
  35.7 1.2 %collective-permute-start.13 = (bf16[32,1280]{1,0:T(8,128)(2,1)S(1)}, bf16[32,1280]{1,0:T(8,128)(2,1)S(1)}, u32[]{:S(2)}, u32[]{:S(2)}) collective-permute-start(bf16[32,1280]{1,0:T(8,128)(2,1)S(1)} %get-tuple-element.61), channel_id=1, source_target_pairs={{0,8},{8,0},{16,24},{24,16},{1,9},{9,1},{17,25},{25,17},{2,10},{10... | collective-permute-start | bytes 245768 | tf_op jit(solution)/shard_map/arrive/ppermute | solution.py:34
  36.8 1.8 %inner.1 = (bf16[128,768]{1,0:T(8,128)(2,1)}, f32[128,128]{1,0:T(8,128)S(1)}) custom-call(bf16[4096,768]{1,0:T(8,128)(2,1)S(1)} %bitcast.12, bf16[256,768]{1,0:T(8,128)(2,1)S(1)} %bitcast.13, bf16[128,768]{1,0:T(8,128)(2,1)S(1)} %bitcast.17, bf16[32,4224]{1,0:T(8,128)(2,1)S(1)} %get-tuple-element.42.refs_0_, bf16[64,4224]{1,0:T(8,128)(2,1)S(1)} %get-tuple-element.47.refs_1_, ...), custom_call_target="tpu_custom_call" | custom-call | flops 805306368 | bytes 6291456 | tf_op jit(solution)/shard_map/inner/pallas_call | solution.py:383
  38.8 1.3 %adapters.3 = (f32[256,1024]{1,0:T(8,128)S(1)}, f32[256,256]{1,0:T(8,128)S(1)}) custom-call(bf16[256,768]{1,0:T(8,128)(2,1)S(1)} %bitcast.14, f32[128,128]{1,0:T(8,128)S(1)} %get-tuple-element.63._.mix, bf16[32,4352]{1,0:T(8,128)(2,1)S(1)} %get-tuple-element.53.refs_0_, bf16[32,4352]{1,0:T(8,128)(2,1)S(1)} %collective-permute-done.4.refs_3_.refs_1_, ...), custom_call_target="tpu_custom_call" | custom-call | flops 268435456 | bytes 524288 | tf_op jit(solution)/shard_map/adapters/pallas_call | solution.py:393
  40.5 0.7 %collective-permute-done.12.refs_10_.refs_6_ = bf16[32,1280]{1,0:T(8,128)(2,1)S(1)} collective-permute-done((bf16[32,1280]{1,0:T(8,128)(2,1)S(1)}, bf16[32,1280]{1,0:T(8,128)(2,1)S(1)}, u32[]{:S(2)}, u32[]{:S(2)}) %collective-permute-start.12) | collective-permute-done | bytes 81952 | tf_op jit(solution)/shard_map/arrive/ppermute | solution.py:34
  41.4 0.8 %adapters.4 = (f32[4,32,1280]{2,1,0:T(8,128)S(1)}, bf16[4,32,1280]{2,1,0:T(8,128)(2,1)S(1)}) custom-call(bf16[256,768]{1,0:T(8,128)(2,1)S(1)} %bitcast.15, f32[256,1024]{1,0:T(8,128)S(1)} %get-tuple-element.64.out, f32[256,256]{1,0:T(8,128)S(1)} %get-tuple-element.65.inn, f32[128,128]{1,0:T(8,128)S(1)} %get-tuple-element.63._.mix, ...), custom_call_target="tpu_custom_call" | custom-call | flops 268435456 | bytes 524288 | tf_op jit(solution)/shard_map/adapters/pallas_call | solution.py:401
  42.3 1.6 %collective-permute-done.14.got = bf16[4,32,1280]{2,1,0:T(8,128)(2,1)S(1)} collective-permute-done((bf16[4,32,1280]{2,1,0:T(8,128)(2,1)S(1)}, bf16[4,32,1280]{2,1,0:T(8,128)(2,1)S(1)}, u32[]{:S(2)}, u32[]{:S(2)}) %collective-permute-start.14) | collective-permute-done | bytes 327712 | tf_op jit(solution)/shard_map/adapters/ppermute | solution.py:34
  43.9 3.6 %collective-permute-start.15 = (bf16[32,1280]{1,0:T(8,128)(2,1)S(1)}, bf16[32,1280]{1,0:T(8,128)(2,1)S(1)}, u32[]{:S(2)}, u32[]{:S(2)}) collective-permute-start(bf16[32,1280]{1,0:T(8,128)(2,1)S(1)} %get-tuple-element.69), channel_id=1, source_target_pairs={{0,4},{1,5},{2,6},{3,7},{4,0},{5,1},{6,2},{7,3},{8,12},{9,13},{10,... | collective-permute-start | bytes 245768 | tf_op jit(solution)/shard_map/adapters/ppermute | solution.py:34
  47.6 2.5 %collective-permute-start.16 = (bf16[32,1280]{1,0:T(8,128)(2,1)S(1)}, bf16[32,1280]{1,0:T(8,128)(2,1)S(1)}, u32[]{:S(2)}, u32[]{:S(2)}) collective-permute-start(bf16[32,1280]{1,0:T(8,128)(2,1)S(1)} %get-tuple-element.70), channel_id=1, source_target_pairs={{0,6},{1,7},{2,4},{3,5},{4,2},{5,3},{6,0},{7,1},{8,14},{9,15},{10,... | collective-permute-start | bytes 245768 | tf_op jit(solution)/shard_map/adapters/ppermute | solution.py:34
  50.0 2.7 %product.1 = f32[1,1024,768]{2,1,0:T(8,128)} custom-call(bf16[32,4352]{1,0:T(8,128)(2,1)S(1)} %get-tuple-element.53.refs_0_, bf16[32,4352]{1,0:T(8,128)(2,1)S(1)} %collective-permute-done.4.refs_3_.refs_1_, bf16[32,4352]{1,0:T(8,128)(2,1)S(1)} %collective-permute-done.5.refs_4_.refs_2_, bf16[32,4352]{1,0:T(8,128)(2,1)S(1)} %collective-permute-done.6.refs_5_.refs_3_, ...), custom_call_target="tpu_custom_call" | custom-call | flops 805306368 | bytes 2097152 | tf_op jit(solution)/shard_map/product/pallas_call | solution.py:420
  52.7 2.3 %collective-permute-done.16.refs_2_ = bf16[32,1280]{1,0:T(8,128)(2,1)S(1)} collective-permute-done((bf16[32,1280]{1,0:T(8,128)(2,1)S(1)}, bf16[32,1280]{1,0:T(8,128)(2,1)S(1)}, u32[]{:S(2)}, u32[]{:S(2)}) %collective-permute-start.16) | collective-permute-done | bytes 81952 | tf_op jit(solution)/shard_map/adapters/ppermute | solution.py:34
  55.0 0.5 collective-permute-done.17.refs_3_
  55.5 0.8 %final.1 = (f32[2,16,1024]{2,1,0:T(8,128)}, f32[2,16,192]{2,1,0:T(8,128)}, f32[8,128]{1,0:T(8,128)}) custom-call(f32[8,128]{1,0:T(8,128)S(1)} %add_bitcast_fusion.small, bf16[128,128]{1,0:T(8,128)(2,1)S(1)} %get-tuple-element.62.picks, bf16[32,1280]{1,0:T(8,128)(2,1)S(1)} %get-tuple-element.68.refs_0_, bf16[32,1280]{1,0:T(8,128)(2,1)S(1)} %collective-permute-done.15.refs_1_, ...), custom_call_target="tpu_custom_call" | custom-call | bytes 1000000 | tf_op jit(solution)/shard_map/final/pallas_call | solution.py:429
  (31 shorter events, 3.0 us)
Async XLA Ops:
  0.6 9.2 %copy-start = (bf16[2,4096,128]{2,1,0:T(8,128)(2,1)S(1)}, bf16[2,4096,128]{2,1,0:T(8,128)(2,1)}, u32[]{:S(2)}) copy-start(bf16[2,4096,128]{2,1,0:T(8,128)(2,1)} %adapter_out.5) | copy-start | bytes 6291460
  2.2 1.2 %copy-start.3 = (bf16[128,4096]{1,0:T(8,128)(2,1)S(1)}, bf16[128,4096]{1,0:T(8,128)(2,1)}, u32[]{:S(2)}) copy-start(bf16[128,4096]{1,0:T(8,128)(2,1)} %cot.1) | copy-start | bytes 3145732
  4.0 4.2 %collective-permute-start = (bf16[3,16,4224]{2,1,0:T(8,128)(2,1)S(1)}, bf16[3,16,4224]{2,1,0:T(8,128)(2,1)S(1)}, u32[]{:S(2)}, u32[]{:S(2)}) collective-permute-start(bf16[3,16,4224]{2,1,0:T(8,128)(2,1)S(1)} %get-tuple-element.41), channel_id=1, source_target_pairs={{0,1},{1,0},{2,3},{3,2},{4,5},{5,4},{6,7},{7,6},{8,9},{9,8},{10,11... | collective-permute-start | bytes 1216520 | tf_op jit(solution)/shard_map/route/ppermute | solution.py:34
  4.5 16.6 %collective-permute-start.2 = (bf16[2,16,4224]{2,1,0:T(8,128)(2,1)S(1)}, bf16[2,16,4224]{2,1,0:T(8,128)(2,1)S(1)}, u32[]{:S(2)}, u32[]{:S(2)}) collective-permute-start(bf16[2,16,4224]{2,1,0:T(8,128)(2,1)S(1)} %get-tuple-element.43), channel_id=1, source_target_pairs={{0,4},{1,5},{2,6},{3,7},{4,0},{5,1},{6,2},{7,3},{8,12},{9,13},{10,... | collective-permute-start | bytes 811016 | tf_op jit(solution)/shard_map/dispatch/ppermute | solution.py:34
  8.2 13.6 %collective-permute-start.1 = (bf16[2,16,4480]{2,1,0:T(8,128)(2,1)S(1)}, bf16[2,16,4480]{2,1,0:T(8,128)(2,1)S(1)}, u32[]{:S(2)}, u32[]{:S(2)}) collective-permute-start(bf16[2,16,4480]{2,1,0:T(8,128)(2,1)S(1)} %dispatch.2), channel_id=1, source_target_pairs={{0,2},{1,3},{2,0},{3,1},{4,6},{5,7},{6,4},{7,5},{8,10},{9,11},{10,... | collective-permute-start | bytes 860168 | tf_op jit(solution)/shard_map/dispatch/ppermute | solution.py:34
  9.8 0.9 %copy-start.4 = (bf16[1,1,128,768]{3,2,1,0:T(8,128)(2,1)S(1)}, bf16[1,1,128,768]{3,2,1,0:T(8,128)(2,1)}, u32[]{:S(2)}) copy-start(bf16[1,1,128,768]{3,2,1,0:T(8,128)(2,1)} %param.9) | copy-start | bytes 589828
  11.2 14.4 %collective-permute-start.4 = (bf16[32,4352]{1,0:T(8,128)(2,1)S(1)}, bf16[32,4352]{1,0:T(8,128)(2,1)S(1)}, u32[]{:S(2)}, u32[]{:S(2)}) collective-permute-start(bf16[32,4352]{1,0:T(8,128)(2,1)S(1)} %get-tuple-element.44), channel_id=1, source_target_pairs={{0,24},{8,16},{16,8},{24,0},{1,25},{9,17},{17,9},{25,1},{2,26},{10... | collective-permute-start | bytes 835592 | tf_op jit(solution)/shard_map/arrive/ppermute | solution.py:34
  13.7 12.9 %collective-permute-start.5 = (bf16[32,4352]{1,0:T(8,128)(2,1)S(1)}, bf16[32,4352]{1,0:T(8,128)(2,1)S(1)}, u32[]{:S(2)}, u32[]{:S(2)}) collective-permute-start(bf16[32,4352]{1,0:T(8,128)(2,1)S(1)} %get-tuple-element.45), channel_id=1, source_target_pairs={{0,16},{8,24},{16,0},{24,8},{1,17},{9,25},{17,1},{25,9},{2,18},{10... | collective-permute-start | bytes 835592 | tf_op jit(solution)/shard_map/arrive/ppermute | solution.py:34
  14.2 12.5 %collective-permute-start.6 = (bf16[32,4352]{1,0:T(8,128)(2,1)S(1)}, bf16[32,4352]{1,0:T(8,128)(2,1)S(1)}, u32[]{:S(2)}, u32[]{:S(2)}) collective-permute-start(bf16[32,4352]{1,0:T(8,128)(2,1)S(1)} %get-tuple-element.46), channel_id=1, source_target_pairs={{0,8},{8,0},{16,24},{24,16},{1,9},{9,1},{17,25},{25,17},{2,10},{10... | collective-permute-start | bytes 835592 | tf_op jit(solution)/shard_map/arrive/ppermute | solution.py:34
  21.1 4.5 %collective-permute-start.3 = (bf16[16,4224]{1,0:T(8,128)(2,1)S(1)}, bf16[16,4224]{1,0:T(8,128)(2,1)S(1)}, u32[]{:S(2)}, u32[]{:S(2)}) collective-permute-start(bf16[16,4224]{1,0:T(8,128)(2,1)S(1)} %get-tuple-element.75), channel_id=1, source_target_pairs={{0,1},{1,0},{2,3},{3,2},{4,5},{5,4},{6,7},{7,6},{8,9},{9,8},{10,11... | collective-permute-start | bytes 405512 | tf_op jit(solution)/shard_map/dispatch/ppermute | solution.py:34
  21.7 15.1 %copy-start.1 = (bf16[1,4096,768]{2,1,0:T(8,128)(2,1)S(1)}, bf16[1,4096,768]{2,1,0:T(8,128)(2,1)}, u32[]{:S(2)}) copy-start(bf16[1,4096,768]{2,1,0:T(8,128)(2,1)} %param.10) | copy-start | bytes 18874372
  21.8 15.1 %copy-start.2 = (bf16[2,128,768]{2,1,0:T(8,128)(2,1)S(1)}, bf16[2,128,768]{2,1,0:T(8,128)(2,1)}, u32[]{:S(2)}) copy-start(bf16[2,128,768]{2,1,0:T(8,128)(2,1)} %param.11) | copy-start | bytes 1179652
  21.8 15.1 %copy-start.5 = (bf16[1,1,128,768]{3,2,1,0:T(8,128)(2,1)S(1)}, bf16[1,1,128,768]{3,2,1,0:T(8,128)(2,1)}, u32[]{:S(2)}) copy-start(bf16[1,1,128,768]{3,2,1,0:T(8,128)(2,1)} %param.9) | copy-start | bytes 589828
  21.8 10.3 %collective-permute-start.7 = (bf16[2,16,4224]{2,1,0:T(8,128)(2,1)S(1)}, bf16[2,16,4224]{2,1,0:T(8,128)(2,1)S(1)}, u32[]{:S(2)}, u32[]{:S(2)}) collective-permute-start(bf16[2,16,4224]{2,1,0:T(8,128)(2,1)S(1)} %dispatch.3), channel_id=1, source_target_pairs={{0,6},{1,7},{2,4},{3,5},{4,2},{5,3},{6,0},{7,1},{8,14},{9,15},{10,... | collective-permute-start | bytes 811016 | tf_op jit(solution)/shard_map/dispatch/ppermute | solution.py:34
  27.3 8.4 %collective-permute-start.8 = (bf16[64,1280]{1,0:T(8,128)(2,1)S(1)}, bf16[64,1280]{1,0:T(8,128)(2,1)S(1)}, u32[]{:S(2)}, u32[]{:S(2)}) collective-permute-start(bf16[64,1280]{1,0:T(8,128)(2,1)S(1)} %get-tuple-element.55), channel_id=1, source_target_pairs={{0,24},{8,16},{16,8},{24,0},{1,25},{9,17},{17,9},{25,1},{2,26},{10... | collective-permute-start | bytes 491528 | tf_op jit(solution)/shard_map/arrive/ppermute | solution.py:34
  29.0 9.8 %collective-permute-start.9 = (bf16[64,1280]{1,0:T(8,128)(2,1)S(1)}, bf16[64,1280]{1,0:T(8,128)(2,1)S(1)}, u32[]{:S(2)}, u32[]{:S(2)}) collective-permute-start(bf16[64,1280]{1,0:T(8,128)(2,1)S(1)} %get-tuple-element.56), channel_id=1, source_target_pairs={{0,16},{8,24},{16,0},{24,8},{1,17},{9,25},{17,1},{25,9},{2,18},{10... | collective-permute-start | bytes 491528 | tf_op jit(solution)/shard_map/arrive/ppermute | solution.py:34
  30.3 8.5 %collective-permute-start.10 = (bf16[64,1280]{1,0:T(8,128)(2,1)S(1)}, bf16[64,1280]{1,0:T(8,128)(2,1)S(1)}, u32[]{:S(2)}, u32[]{:S(2)}) collective-permute-start(bf16[64,1280]{1,0:T(8,128)(2,1)S(1)} %get-tuple-element.57), channel_id=1, source_target_pairs={{0,8},{8,0},{16,24},{24,16},{1,9},{9,1},{17,25},{25,17},{2,10},{10... | collective-permute-start | bytes 491528 | tf_op jit(solution)/shard_map/arrive/ppermute | solution.py:34
  32.6 7.9 %collective-permute-start.11 = (bf16[32,1280]{1,0:T(8,128)(2,1)S(1)}, bf16[32,1280]{1,0:T(8,128)(2,1)S(1)}, u32[]{:S(2)}, u32[]{:S(2)}) collective-permute-start(bf16[32,1280]{1,0:T(8,128)(2,1)S(1)} %get-tuple-element.59), channel_id=1, source_target_pairs={{0,24},{8,16},{16,8},{24,0},{1,25},{9,17},{17,9},{25,1},{2,26},{10... | collective-permute-start | bytes 245768 | tf_op jit(solution)/shard_map/arrive/ppermute | solution.py:34
  35.1 6.1 %collective-permute-start.12 = (bf16[32,1280]{1,0:T(8,128)(2,1)S(1)}, bf16[32,1280]{1,0:T(8,128)(2,1)S(1)}, u32[]{:S(2)}, u32[]{:S(2)}) collective-permute-start(bf16[32,1280]{1,0:T(8,128)(2,1)S(1)} %get-tuple-element.60), channel_id=1, source_target_pairs={{0,16},{8,24},{16,0},{24,8},{1,17},{9,25},{17,1},{25,9},{2,18},{10... | collective-permute-start | bytes 245768 | tf_op jit(solution)/shard_map/arrive/ppermute | solution.py:34
  35.7 5.7 %collective-permute-start.13 = (bf16[32,1280]{1,0:T(8,128)(2,1)S(1)}, bf16[32,1280]{1,0:T(8,128)(2,1)S(1)}, u32[]{:S(2)}, u32[]{:S(2)}) collective-permute-start(bf16[32,1280]{1,0:T(8,128)(2,1)S(1)} %get-tuple-element.61), channel_id=1, source_target_pairs={{0,8},{8,0},{16,24},{24,16},{1,9},{9,1},{17,25},{25,17},{2,10},{10... | collective-permute-start | bytes 245768 | tf_op jit(solution)/shard_map/arrive/ppermute | solution.py:34
  42.2 1.7 %collective-permute-start.14 = (bf16[4,32,1280]{2,1,0:T(8,128)(2,1)S(1)}, bf16[4,32,1280]{2,1,0:T(8,128)(2,1)S(1)}, u32[]{:S(2)}, u32[]{:S(2)}) collective-permute-start(bf16[4,32,1280]{2,1,0:T(8,128)(2,1)S(1)} %get-tuple-element.67), channel_id=1, source_target_pairs={{0,1},{1,0},{2,3},{3,2},{4,5},{5,4},{6,7},{7,6},{8,9},{9,8},{10,11... | collective-permute-start | bytes 983048 | tf_op jit(solution)/shard_map/adapters/ppermute | solution.py:34
  43.9 8.8 %collective-permute-start.15 = (bf16[32,1280]{1,0:T(8,128)(2,1)S(1)}, bf16[32,1280]{1,0:T(8,128)(2,1)S(1)}, u32[]{:S(2)}, u32[]{:S(2)}) collective-permute-start(bf16[32,1280]{1,0:T(8,128)(2,1)S(1)} %get-tuple-element.69), channel_id=1, source_target_pairs={{0,4},{1,5},{2,6},{3,7},{4,0},{5,1},{6,2},{7,3},{8,12},{9,13},{10,... | collective-permute-start | bytes 245768 | tf_op jit(solution)/shard_map/adapters/ppermute | solution.py:34
  47.6 7.4 %collective-permute-start.16 = (bf16[32,1280]{1,0:T(8,128)(2,1)S(1)}, bf16[32,1280]{1,0:T(8,128)(2,1)S(1)}, u32[]{:S(2)}, u32[]{:S(2)}) collective-permute-start(bf16[32,1280]{1,0:T(8,128)(2,1)S(1)} %get-tuple-element.70), channel_id=1, source_target_pairs={{0,6},{1,7},{2,4},{3,5},{4,2},{5,3},{6,0},{7,1},{8,14},{9,15},{10,... | collective-permute-start | bytes 245768 | tf_op jit(solution)/shard_map/adapters/ppermute | solution.py:34
  50.0 5.5 %collective-permute-start.17 = (bf16[32,1280]{1,0:T(8,128)(2,1)S(1)}, bf16[32,1280]{1,0:T(8,128)(2,1)S(1)}, u32[]{:S(2)}, u32[]{:S(2)}) collective-permute-start(bf16[32,1280]{1,0:T(8,128)(2,1)S(1)} %get-tuple-element.71), channel_id=1, source_target_pairs={{0,2},{1,3},{2,0},{3,1},{4,6},{5,7},{6,4},{7,5},{8,10},{9,11},{10,... | collective-permute-start | bytes 245768 | tf_op jit(solution)/shard_map/adapters/ppermute | solution.py:34

commit v6 on v5

--- a/solution.py
+++ b/solution.py
@@ -356,7 +356,7 @@
         for hops, after in ((others, []), (chunks[-1], 1)):
             packs = call(
                 functools.partial(pack_body, hops, chips),
-                tuple(shape((2, cap, width + (3 if hop == 1 else 1) * LANES), bf16) for hop in hops),
+                tuple(shape((2, cap, width + LANES), bf16) for hop in hops),
                 (V, V) + (A,) * bool(after),
                 nbytes=4 * slots * width,
             )(keep, sib, *(far[1] if after else []))

time: 56.6 us -> 56.2 us (level)
  no operation moved by 1% of the time
where the time goes in v6:
time: 56.2 us; the launch traced here: 56 us
  starting transfers between devices  26.9 us (48%)
  waiting for transfers between devices  15.1 us (27%)
  Pallas kernels  9.54 us (17%)
  local copies, waits for them, and re-layouts  2.19 us (4%)
  other arithmetic  1.51 us (3%)
  between operations  0.75 us (1%)
    ppermute x18, starting transfers between devices, swap(): return lax.ppermute(x, axis, [(i, i ^ mask) for i in range(size)])  26.9 us
    ppermute x18, waiting for transfers between devices, swap(): return lax.ppermute(x, axis, [(i, i ^ mask) for i in range(size)])  15.1 us
    pallas_call x1, Pallas kernels, on_device(): call(functools.partial(product_body, groups, chips), shape((1, part, hid_...  2.67 us
    unnamed x12, local copies, waits for them, and re-layouts  2.17 us
    pallas_call x1, Pallas kernels, on_device(): call(functools.partial(inner_body, chips, cap, len(chunks)), (shape((slot...  1.85 us
    pallas_call x3, Pallas kernels, on_device(): call(functools.partial(arrive_body, groups, chips, cap, own, len(before))...  1.47 us
    pallas_call x1, Pallas kernels, on_device(): call(functools.partial(adapter_first_body, loops, chips, cols, groups), s...  1.31 us
  transfers between devices with their start and end apart: 18, of which 12 were waited for; matrix products, arithmetic and copies ran while one was open for 0% of the time, Pallas kernels for 13%

profile of v6, /device:TPU:0, one launch (start us, length us, event | category | flops | bytes accessed | tf_op | source)
XLA Modules:
  0.0 56.0 jit_solution(18283429372929312242)
XLA Ops:
  0.6 0.8 %broadcast_multiply_fusion = s32[128]{0:T(128)S(1)} fusion(s32[128]{0:T(128)} %param.15), kind=kLoop, calls=%fused_computation.3 | loop fusion | flops 128 | bytes 1024 | tf_op jit(solution)/shard_map/mul | solution.py:329
  1.4 0.7 %add_bitcast_fusion.small = f32[8,128]{1,0:T(8,128)S(1)} fusion(bf16[128,8]{0,1:T(8,128)(2,1)} %param.13, s32[128,8]{0,1:T(8,128)} %param.14, s32[128]{0:T(128)S(1)} %broadcast_multiply_fusion), kind=kLoop, calls=%fused_computation.2 | loop fusion | flops 5120 | bytes 10752 | tf_op jit(solution)/shard_map/add | solution.py:330
  2.2 1.2 %copy-done.3 = bf16[128,4096]{1,0:T(8,128)(2,1)S(1)} copy-done((bf16[128,4096]{1,0:T(8,128)(2,1)S(1)}, bf16[128,4096]{1,0:T(8,128)(2,1)}, u32[]{:S(2)}) %copy-start.3) | copy-done | bytes 1048600
  3.4 0.6 %route.1 = (bf16[4,16,4224]{2,1,0:T(8,128)(2,1)S(1)}, bf16[2,16,4224]{2,1,0:T(8,128)(2,1)S(1)}, bf16[3,16,4224]{2,1,0:T(8,128)(2,1)S(1)}, bf16[128,128]{1,0:T(8,128)(2,1)S(1)}) custom-call(f32[8,128]{1,0:T(8,128)S(1)} %add_bitcast_fusion.small, bf16[128,4096]{1,0:T(8,128)(2,1)S(1)} %copy-done.3), custom_call_target="tpu_custom_call" | custom-call | flops 134217728 | bytes 3145728 | tf_op jit(solution)/shard_map/route/pallas_call | solution.py:337
  4.0 0.5 collective-permute-start
  4.5 3.7 %collective-permute-start.2 = (bf16[2,16,4224]{2,1,0:T(8,128)(2,1)S(1)}, bf16[2,16,4224]{2,1,0:T(8,128)(2,1)S(1)}, u32[]{:S(2)}, u32[]{:S(2)}) collective-permute-start(bf16[2,16,4224]{2,1,0:T(8,128)(2,1)S(1)} %get-tuple-element.43), channel_id=1, source_target_pairs={{0,4},{1,5},{2,6},{3,7},{4,0},{5,1},{6,2},{7,3},{8,12},{9,13},{10,... | collective-permute-start | bytes 811016 | tf_op jit(solution)/shard_map/dispatch/ppermute | solution.py:34
  8.2 1.6 %collective-permute-start.1 = (bf16[2,16,4224]{2,1,0:T(8,128)(2,1)S(1)}, bf16[2,16,4224]{2,1,0:T(8,128)(2,1)S(1)}, u32[]{:S(2)}, u32[]{:S(2)}) collective-permute-start(bf16[2,16,4224]{2,1,0:T(8,128)(2,1)S(1)} %dispatch.2), channel_id=1, source_target_pairs={{0,2},{1,3},{2,0},{3,1},{4,6},{5,7},{6,4},{7,5},{8,10},{9,11},{10,... | collective-permute-start | bytes 811016 | tf_op jit(solution)/shard_map/dispatch/ppermute | solution.py:34
  9.8 0.9 %copy-done.4 = bf16[1,1,128,768]{3,2,1,0:T(8,128)(2,1)S(1)} copy-done((bf16[1,1,128,768]{3,2,1,0:T(8,128)(2,1)S(1)}, bf16[1,1,128,768]{3,2,1,0:T(8,128)(2,1)}, u32[]{:S(2)}) %copy-start.4) | copy-done | bytes 196632
  11.2 2.5 %collective-permute-start.4 = (bf16[32,4352]{1,0:T(8,128)(2,1)S(1)}, bf16[32,4352]{1,0:T(8,128)(2,1)S(1)}, u32[]{:S(2)}, u32[]{:S(2)}) collective-permute-start(bf16[32,4352]{1,0:T(8,128)(2,1)S(1)} %get-tuple-element.44), channel_id=1, source_target_pairs={{0,24},{8,16},{16,8},{24,0},{1,25},{9,17},{17,9},{25,1},{2,26},{10... | collective-permute-start | bytes 835592 | tf_op jit(solution)/shard_map/arrive/ppermute | solution.py:34
  14.2 0.5 collective-permute-start.6
  14.8 6.3 %collective-permute-done.2 = bf16[2,16,4224]{2,1,0:T(8,128)(2,1)S(1)} collective-permute-done((bf16[2,16,4224]{2,1,0:T(8,128)(2,1)S(1)}, bf16[2,16,4224]{2,1,0:T(8,128)(2,1)S(1)}, u32[]{:S(2)}, u32[]{:S(2)}) %collective-permute-start.2) | collective-permute-done | bytes 270368 | tf_op jit(solution)/shard_map/dispatch/ppermute | solution.py:34
  21.4 3.8 %collective-permute-start.7 = (bf16[2,16,4224]{2,1,0:T(8,128)(2,1)S(1)}, bf16[2,16,4224]{2,1,0:T(8,128)(2,1)S(1)}, u32[]{:S(2)}, u32[]{:S(2)}) collective-permute-start(bf16[2,16,4224]{2,1,0:T(8,128)(2,1)S(1)} %dispatch.3), channel_id=1, source_target_pairs={{0,6},{1,7},{2,4},{3,5},{4,2},{5,3},{6,0},{7,1},{8,14},{9,15},{10,... | collective-permute-start | bytes 811016 | tf_op jit(solution)/shard_map/dispatch/ppermute | solution.py:34
  25.3 1.3 %collective-permute-done.5.refs_4_.refs_2_ = bf16[32,4352]{1,0:T(8,128)(2,1)S(1)} collective-permute-done((bf16[32,4352]{1,0:T(8,128)(2,1)S(1)}, bf16[32,4352]{1,0:T(8,128)(2,1)S(1)}, u32[]{:S(2)}, u32[]{:S(2)}) %collective-permute-start.5) | collective-permute-done | bytes 278560 | tf_op jit(solution)/shard_map/arrive/ppermute | solution.py:34
  26.7 0.6 arrive.4
  27.3 1.7 %collective-permute-start.8 = (bf16[64,1280]{1,0:T(8,128)(2,1)S(1)}, bf16[64,1280]{1,0:T(8,128)(2,1)S(1)}, u32[]{:S(2)}, u32[]{:S(2)}) collective-permute-start(bf16[64,1280]{1,0:T(8,128)(2,1)S(1)} %get-tuple-element.55), channel_id=1, source_target_pairs={{0,24},{8,16},{16,8},{24,0},{1,25},{9,17},{17,9},{25,1},{2,26},{10... | collective-permute-start | bytes 491528 | tf_op jit(solution)/shard_map/arrive/ppermute | solution.py:34
  29.0 1.3 %collective-permute-start.9 = (bf16[64,1280]{1,0:T(8,128)(2,1)S(1)}, bf16[64,1280]{1,0:T(8,128)(2,1)S(1)}, u32[]{:S(2)}, u32[]{:S(2)}) collective-permute-start(bf16[64,1280]{1,0:T(8,128)(2,1)S(1)} %get-tuple-element.56), channel_id=1, source_target_pairs={{0,16},{8,24},{16,0},{24,8},{1,17},{9,25},{17,1},{25,9},{2,18},{10... | collective-permute-start | bytes 491528 | tf_op jit(solution)/shard_map/arrive/ppermute | solution.py:34
  30.3 0.5 collective-permute-start.10
  30.8 1.3 %collective-permute-done.7.refs_0_ = bf16[2,16,4224]{2,1,0:T(8,128)(2,1)S(1)} collective-permute-done((bf16[2,16,4224]{2,1,0:T(8,128)(2,1)S(1)}, bf16[2,16,4224]{2,1,0:T(8,128)(2,1)S(1)}, u32[]{:S(2)}, u32[]{:S(2)}) %collective-permute-start.7) | collective-permute-done | bytes 270368 | tf_op jit(solution)/shard_map/dispatch/ppermute | solution.py:34
  32.6 2.6 %collective-permute-start.11 = (bf16[32,1280]{1,0:T(8,128)(2,1)S(1)}, bf16[32,1280]{1,0:T(8,128)(2,1)S(1)}, u32[]{:S(2)}, u32[]{:S(2)}) collective-permute-start(bf16[32,1280]{1,0:T(8,128)(2,1)S(1)} %get-tuple-element.59), channel_id=1, source_target_pairs={{0,24},{8,16},{16,8},{24,0},{1,25},{9,17},{17,9},{25,1},{2,26},{10... | collective-permute-start | bytes 245768 | tf_op jit(solution)/shard_map/arrive/ppermute | solution.py:34
  35.1 0.5 collective-permute-start.12
  35.7 1.2 %collective-permute-start.13 = (bf16[32,1280]{1,0:T(8,128)(2,1)S(1)}, bf16[32,1280]{1,0:T(8,128)(2,1)S(1)}, u32[]{:S(2)}, u32[]{:S(2)}) collective-permute-start(bf16[32,1280]{1,0:T(8,128)(2,1)S(1)} %get-tuple-element.61), channel_id=1, source_target_pairs={{0,8},{8,0},{16,24},{24,16},{1,9},{9,1},{17,25},{25,17},{2,10},{10... | collective-permute-start | bytes 245768 | tf_op jit(solution)/shard_map/arrive/ppermute | solution.py:34
  36.8 1.8 %inner.1 = (bf16[128,768]{1,0:T(8,128)(2,1)}, f32[128,128]{1,0:T(8,128)S(1)}) custom-call(bf16[4096,768]{1,0:T(8,128)(2,1)S(1)} %bitcast.12, bf16[256,768]{1,0:T(8,128)(2,1)S(1)} %bitcast.13, bf16[128,768]{1,0:T(8,128)(2,1)S(1)} %bitcast.17, bf16[32,4224]{1,0:T(8,128)(2,1)S(1)} %get-tuple-element.42.refs_0_, bf16[64,4224]{1,0:T(8,128)(2,1)S(1)} %get-tuple-element.47.refs_1_, ...), custom_call_target="tpu_custom_call" | custom-call | flops 805306368 | bytes 6291456 | tf_op jit(solution)/shard_map/inner/pallas_call | solution.py:383
  38.8 1.3 %adapters.3 = (f32[256,1024]{1,0:T(8,128)S(1)}, f32[256,256]{1,0:T(8,128)S(1)}) custom-call(bf16[256,768]{1,0:T(8,128)(2,1)S(1)} %bitcast.14, f32[128,128]{1,0:T(8,128)S(1)} %get-tuple-element.63._.mix, bf16[32,4352]{1,0:T(8,128)(2,1)S(1)} %get-tuple-element.53.refs_0_, bf16[32,4352]{1,0:T(8,128)(2,1)S(1)} %collective-permute-done.4.refs_3_.refs_1_, ...), custom_call_target="tpu_custom_call" | custom-call | flops 268435456 | bytes 524288 | tf_op jit(solution)/shard_map/adapters/pallas_call | solution.py:393
  40.5 0.7 %collective-permute-done.12.refs_10_.refs_6_ = bf16[32,1280]{1,0:T(8,128)(2,1)S(1)} collective-permute-done((bf16[32,1280]{1,0:T(8,128)(2,1)S(1)}, bf16[32,1280]{1,0:T(8,128)(2,1)S(1)}, u32[]{:S(2)}, u32[]{:S(2)}) %collective-permute-start.12) | collective-permute-done | bytes 81952 | tf_op jit(solution)/shard_map/arrive/ppermute | solution.py:34
  41.4 0.8 %adapters.4 = (f32[4,32,1280]{2,1,0:T(8,128)S(1)}, bf16[4,32,1280]{2,1,0:T(8,128)(2,1)S(1)}) custom-call(bf16[256,768]{1,0:T(8,128)(2,1)S(1)} %bitcast.15, f32[256,1024]{1,0:T(8,128)S(1)} %get-tuple-element.64.out, f32[256,256]{1,0:T(8,128)S(1)} %get-tuple-element.65.inn, f32[128,128]{1,0:T(8,128)S(1)} %get-tuple-element.63._.mix, ...), custom_call_target="tpu_custom_call" | custom-call | flops 268435456 | bytes 524288 | tf_op jit(solution)/shard_map/adapters/pallas_call | solution.py:401
  42.3 1.6 %collective-permute-done.14.got = bf16[4,32,1280]{2,1,0:T(8,128)(2,1)S(1)} collective-permute-done((bf16[4,32,1280]{2,1,0:T(8,128)(2,1)S(1)}, bf16[4,32,1280]{2,1,0:T(8,128)(2,1)S(1)}, u32[]{:S(2)}, u32[]{:S(2)}) %collective-permute-start.14) | collective-permute-done | bytes 327712 | tf_op jit(solution)/shard_map/adapters/ppermute | solution.py:34
  43.9 3.3 %collective-permute-start.15 = (bf16[32,1280]{1,0:T(8,128)(2,1)S(1)}, bf16[32,1280]{1,0:T(8,128)(2,1)S(1)}, u32[]{:S(2)}, u32[]{:S(2)}) collective-permute-start(bf16[32,1280]{1,0:T(8,128)(2,1)S(1)} %get-tuple-element.69), channel_id=1, source_target_pairs={{0,4},{1,5},{2,6},{3,7},{4,0},{5,1},{6,2},{7,3},{8,12},{9,13},{10,... | collective-permute-start | bytes 245768 | tf_op jit(solution)/shard_map/adapters/ppermute | solution.py:34
  47.2 2.5 %collective-permute-start.16 = (bf16[32,1280]{1,0:T(8,128)(2,1)S(1)}, bf16[32,1280]{1,0:T(8,128)(2,1)S(1)}, u32[]{:S(2)}, u32[]{:S(2)}) collective-permute-start(bf16[32,1280]{1,0:T(8,128)(2,1)S(1)} %get-tuple-element.70), channel_id=1, source_target_pairs={{0,6},{1,7},{2,4},{3,5},{4,2},{5,3},{6,0},{7,1},{8,14},{9,15},{10,... | collective-permute-start | bytes 245768 | tf_op jit(solution)/shard_map/adapters/ppermute | solution.py:34
  49.7 2.7 %product.1 = f32[1,1024,768]{2,1,0:T(8,128)} custom-call(bf16[32,4352]{1,0:T(8,128)(2,1)S(1)} %get-tuple-element.53.refs_0_, bf16[32,4352]{1,0:T(8,128)(2,1)S(1)} %collective-permute-done.4.refs_3_.refs_1_, bf16[32,4352]{1,0:T(8,128)(2,1)S(1)} %collective-permute-done.5.refs_4_.refs_2_, bf16[32,4352]{1,0:T(8,128)(2,1)S(1)} %collective-permute-done.6.refs_5_.refs_3_, ...), custom_call_target="tpu_custom_call" | custom-call | flops 805306368 | bytes 2097152 | tf_op jit(solution)/shard_map/product/pallas_call | solution.py:420
  52.4 2.3 %collective-permute-done.16.refs_2_ = bf16[32,1280]{1,0:T(8,128)(2,1)S(1)} collective-permute-done((bf16[32,1280]{1,0:T(8,128)(2,1)S(1)}, bf16[32,1280]{1,0:T(8,128)(2,1)S(1)}, u32[]{:S(2)}, u32[]{:S(2)}) %collective-permute-start.16) | collective-permute-done | bytes 81952 | tf_op jit(solution)/shard_map/adapters/ppermute | solution.py:34
  54.7 0.5 collective-permute-done.17.refs_3_
  55.2 0.8 %final.1 = (f32[2,16,1024]{2,1,0:T(8,128)}, f32[2,16,192]{2,1,0:T(8,128)}, f32[8,128]{1,0:T(8,128)}) custom-call(f32[8,128]{1,0:T(8,128)S(1)} %add_bitcast_fusion.small, bf16[128,128]{1,0:T(8,128)(2,1)S(1)} %get-tuple-element.62.picks, bf16[32,1280]{1,0:T(8,128)(2,1)S(1)} %get-tuple-element.68.refs_0_, bf16[32,1280]{1,0:T(8,128)(2,1)S(1)} %collective-permute-done.15.refs_1_, ...), custom_call_target="tpu_custom_call" | custom-call | bytes 1000000 | tf_op jit(solution)/shard_map/final/pallas_call | solution.py:429
  (31 shorter events, 2.6 us)
Async XLA Ops:
  0.6 9.2 %copy-start = (bf16[2,4096,128]{2,1,0:T(8,128)(2,1)S(1)}, bf16[2,4096,128]{2,1,0:T(8,128)(2,1)}, u32[]{:S(2)}) copy-start(bf16[2,4096,128]{2,1,0:T(8,128)(2,1)} %adapter_out.5) | copy-start | bytes 6291460
  2.2 1.2 %copy-start.3 = (bf16[128,4096]{1,0:T(8,128)(2,1)S(1)}, bf16[128,4096]{1,0:T(8,128)(2,1)}, u32[]{:S(2)}) copy-start(bf16[128,4096]{1,0:T(8,128)(2,1)} %cot.1) | copy-start | bytes 3145732
  4.0 4.2 %collective-permute-start = (bf16[3,16,4224]{2,1,0:T(8,128)(2,1)S(1)}, bf16[3,16,4224]{2,1,0:T(8,128)(2,1)S(1)}, u32[]{:S(2)}, u32[]{:S(2)}) collective-permute-start(bf16[3,16,4224]{2,1,0:T(8,128)(2,1)S(1)} %get-tuple-element.41), channel_id=1, source_target_pairs={{0,1},{1,0},{2,3},{3,2},{4,5},{5,4},{6,7},{7,6},{8,9},{9,8},{10,11... | collective-permute-start | bytes 1216520 | tf_op jit(solution)/shard_map/route/ppermute | solution.py:34
  4.5 16.6 %collective-permute-start.2 = (bf16[2,16,4224]{2,1,0:T(8,128)(2,1)S(1)}, bf16[2,16,4224]{2,1,0:T(8,128)(2,1)S(1)}, u32[]{:S(2)}, u32[]{:S(2)}) collective-permute-start(bf16[2,16,4224]{2,1,0:T(8,128)(2,1)S(1)} %get-tuple-element.43), channel_id=1, source_target_pairs={{0,4},{1,5},{2,6},{3,7},{4,0},{5,1},{6,2},{7,3},{8,12},{9,13},{10,... | collective-permute-start | bytes 811016 | tf_op jit(solution)/shard_map/dispatch/ppermute | solution.py:34
  8.2 13.2 %collective-permute-start.1 = (bf16[2,16,4224]{2,1,0:T(8,128)(2,1)S(1)}, bf16[2,16,4224]{2,1,0:T(8,128)(2,1)S(1)}, u32[]{:S(2)}, u32[]{:S(2)}) collective-permute-start(bf16[2,16,4224]{2,1,0:T(8,128)(2,1)S(1)} %dispatch.2), channel_id=1, source_target_pairs={{0,2},{1,3},{2,0},{3,1},{4,6},{5,7},{6,4},{7,5},{8,10},{9,11},{10,... | collective-permute-start | bytes 811016 | tf_op jit(solution)/shard_map/dispatch/ppermute | solution.py:34
  9.8 0.9 %copy-start.4 = (bf16[1,1,128,768]{3,2,1,0:T(8,128)(2,1)S(1)}, bf16[1,1,128,768]{3,2,1,0:T(8,128)(2,1)}, u32[]{:S(2)}) copy-start(bf16[1,1,128,768]{3,2,1,0:T(8,128)(2,1)} %param.9) | copy-start | bytes 589828
  11.2 14.1 %collective-permute-start.4 = (bf16[32,4352]{1,0:T(8,128)(2,1)S(1)}, bf16[32,4352]{1,0:T(8,128)(2,1)S(1)}, u32[]{:S(2)}, u32[]{:S(2)}) collective-permute-start(bf16[32,4352]{1,0:T(8,128)(2,1)S(1)} %get-tuple-element.44), channel_id=1, source_target_pairs={{0,24},{8,16},{16,8},{24,0},{1,25},{9,17},{17,9},{25,1},{2,26},{10... | collective-permute-start | bytes 835592 | tf_op jit(solution)/shard_map/arrive/ppermute | solution.py:34
  13.7 12.9 %collective-permute-start.5 = (bf16[32,4352]{1,0:T(8,128)(2,1)S(1)}, bf16[32,4352]{1,0:T(8,128)(2,1)S(1)}, u32[]{:S(2)}, u32[]{:S(2)}) collective-permute-start(bf16[32,4352]{1,0:T(8,128)(2,1)S(1)} %get-tuple-element.45), channel_id=1, source_target_pairs={{0,16},{8,24},{16,0},{24,8},{1,17},{9,25},{17,1},{25,9},{2,18},{10... | collective-permute-start | bytes 835592 | tf_op jit(solution)/shard_map/arrive/ppermute | solution.py:34
  14.2 12.5 %collective-permute-start.6 = (bf16[32,4352]{1,0:T(8,128)(2,1)S(1)}, bf16[32,4352]{1,0:T(8,128)(2,1)S(1)}, u32[]{:S(2)}, u32[]{:S(2)}) collective-permute-start(bf16[32,4352]{1,0:T(8,128)(2,1)S(1)} %get-tuple-element.46), channel_id=1, source_target_pairs={{0,8},{8,0},{16,24},{24,16},{1,9},{9,1},{17,25},{25,17},{2,10},{10... | collective-permute-start | bytes 835592 | tf_op jit(solution)/shard_map/arrive/ppermute | solution.py:34
  21.1 4.2 %collective-permute-start.3 = (bf16[16,4224]{1,0:T(8,128)(2,1)S(1)}, bf16[16,4224]{1,0:T(8,128)(2,1)S(1)}, u32[]{:S(2)}, u32[]{:S(2)}) collective-permute-start(bf16[16,4224]{1,0:T(8,128)(2,1)S(1)} %get-tuple-element.75), channel_id=1, source_target_pairs={{0,1},{1,0},{2,3},{3,2},{4,5},{5,4},{6,7},{7,6},{8,9},{9,8},{10,11... | collective-permute-start | bytes 405512 | tf_op jit(solution)/shard_map/dispatch/ppermute | solution.py:34
  21.4 15.4 %copy-start.1 = (bf16[1,4096,768]{2,1,0:T(8,128)(2,1)S(1)}, bf16[1,4096,768]{2,1,0:T(8,128)(2,1)}, u32[]{:S(2)}) copy-start(bf16[1,4096,768]{2,1,0:T(8,128)(2,1)} %param.10) | copy-start | bytes 18874372
  21.4 15.4 %copy-start.2 = (bf16[2,128,768]{2,1,0:T(8,128)(2,1)S(1)}, bf16[2,128,768]{2,1,0:T(8,128)(2,1)}, u32[]{:S(2)}) copy-start(bf16[2,128,768]{2,1,0:T(8,128)(2,1)} %param.11) | copy-start | bytes 1179652
  21.4 15.4 %copy-start.5 = (bf16[1,1,128,768]{3,2,1,0:T(8,128)(2,1)S(1)}, bf16[1,1,128,768]{3,2,1,0:T(8,128)(2,1)}, u32[]{:S(2)}) copy-start(bf16[1,1,128,768]{3,2,1,0:T(8,128)(2,1)} %param.9) | copy-start | bytes 589828
  21.4 10.7 %collective-permute-start.7 = (bf16[2,16,4224]{2,1,0:T(8,128)(2,1)S(1)}, bf16[2,16,4224]{2,1,0:T(8,128)(2,1)S(1)}, u32[]{:S(2)}, u32[]{:S(2)}) collective-permute-start(bf16[2,16,4224]{2,1,0:T(8,128)(2,1)S(1)} %dispatch.3), channel_id=1, source_target_pairs={{0,6},{1,7},{2,4},{3,5},{4,2},{5,3},{6,0},{7,1},{8,14},{9,15},{10,... | collective-permute-start | bytes 811016 | tf_op jit(solution)/shard_map/dispatch/ppermute | solution.py:34
  27.3 8.4 %collective-permute-start.8 = (bf16[64,1280]{1,0:T(8,128)(2,1)S(1)}, bf16[64,1280]{1,0:T(8,128)(2,1)S(1)}, u32[]{:S(2)}, u32[]{:S(2)}) collective-permute-start(bf16[64,1280]{1,0:T(8,128)(2,1)S(1)} %get-tuple-element.55), channel_id=1, source_target_pairs={{0,24},{8,16},{16,8},{24,0},{1,25},{9,17},{17,9},{25,1},{2,26},{10... | collective-permute-start | bytes 491528 | tf_op jit(solution)/shard_map/arrive/ppermute | solution.py:34
  29.0 9.8 %collective-permute-start.9 = (bf16[64,1280]{1,0:T(8,128)(2,1)S(1)}, bf16[64,1280]{1,0:T(8,128)(2,1)S(1)}, u32[]{:S(2)}, u32[]{:S(2)}) collective-permute-start(bf16[64,1280]{1,0:T(8,128)(2,1)S(1)} %get-tuple-element.56), channel_id=1, source_target_pairs={{0,16},{8,24},{16,0},{24,8},{1,17},{9,25},{17,1},{25,9},{2,18},{10... | collective-permute-start | bytes 491528 | tf_op jit(solution)/shard_map/arrive/ppermute | solution.py:34
  30.3 8.5 %collective-permute-start.10 = (bf16[64,1280]{1,0:T(8,128)(2,1)S(1)}, bf16[64,1280]{1,0:T(8,128)(2,1)S(1)}, u32[]{:S(2)}, u32[]{:S(2)}) collective-permute-start(bf16[64,1280]{1,0:T(8,128)(2,1)S(1)} %get-tuple-element.57), channel_id=1, source_target_pairs={{0,8},{8,0},{16,24},{24,16},{1,9},{9,1},{17,25},{25,17},{2,10},{10... | collective-permute-start | bytes 491528 | tf_op jit(solution)/shard_map/arrive/ppermute | solution.py:34
  32.6 7.9 %collective-permute-start.11 = (bf16[32,1280]{1,0:T(8,128)(2,1)S(1)}, bf16[32,1280]{1,0:T(8,128)(2,1)S(1)}, u32[]{:S(2)}, u32[]{:S(2)}) collective-permute-start(bf16[32,1280]{1,0:T(8,128)(2,1)S(1)} %get-tuple-element.59), channel_id=1, source_target_pairs={{0,24},{8,16},{16,8},{24,0},{1,25},{9,17},{17,9},{25,1},{2,26},{10... | collective-permute-start | bytes 245768 | tf_op jit(solution)/shard_map/arrive/ppermute | solution.py:34
  35.1 6.1 %collective-permute-start.12 = (bf16[32,1280]{1,0:T(8,128)(2,1)S(1)}, bf16[32,1280]{1,0:T(8,128)(2,1)S(1)}, u32[]{:S(2)}, u32[]{:S(2)}) collective-permute-start(bf16[32,1280]{1,0:T(8,128)(2,1)S(1)} %get-tuple-element.60), channel_id=1, source_target_pairs={{0,16},{8,24},{16,0},{24,8},{1,17},{9,25},{17,1},{25,9},{2,18},{10... | collective-permute-start | bytes 245768 | tf_op jit(solution)/shard_map/arrive/ppermute | solution.py:34
  35.7 5.7 %collective-permute-start.13 = (bf16[32,1280]{1,0:T(8,128)(2,1)S(1)}, bf16[32,1280]{1,0:T(8,128)(2,1)S(1)}, u32[]{:S(2)}, u32[]{:S(2)}) collective-permute-start(bf16[32,1280]{1,0:T(8,128)(2,1)S(1)} %get-tuple-element.61), channel_id=1, source_target_pairs={{0,8},{8,0},{16,24},{24,16},{1,9},{9,1},{17,25},{25,17},{2,10},{10... | collective-permute-start | bytes 245768 | tf_op jit(solution)/shard_map/arrive/ppermute | solution.py:34
  42.2 1.7 %collective-permute-start.14 = (bf16[4,32,1280]{2,1,0:T(8,128)(2,1)S(1)}, bf16[4,32,1280]{2,1,0:T(8,128)(2,1)S(1)}, u32[]{:S(2)}, u32[]{:S(2)}) collective-permute-start(bf16[4,32,1280]{2,1,0:T(8,128)(2,1)S(1)} %get-tuple-element.67), channel_id=1, source_target_pairs={{0,1},{1,0},{2,3},{3,2},{4,5},{5,4},{6,7},{7,6},{8,9},{9,8},{10,11... | collective-permute-start | bytes 983048 | tf_op jit(solution)/shard_map/adapters/ppermute | solution.py:34
  43.9 8.4 %collective-permute-start.15 = (bf16[32,1280]{1,0:T(8,128)(2,1)S(1)}, bf16[32,1280]{1,0:T(8,128)(2,1)S(1)}, u32[]{:S(2)}, u32[]{:S(2)}) collective-permute-start(bf16[32,1280]{1,0:T(8,128)(2,1)S(1)} %get-tuple-element.69), channel_id=1, source_target_pairs={{0,4},{1,5},{2,6},{3,7},{4,0},{5,1},{6,2},{7,3},{8,12},{9,13},{10,... | collective-permute-start | bytes 245768 | tf_op jit(solution)/shard_map/adapters/ppermute | solution.py:34
  47.2 7.5 %collective-permute-start.16 = (bf16[32,1280]{1,0:T(8,128)(2,1)S(1)}, bf16[32,1280]{1,0:T(8,128)(2,1)S(1)}, u32[]{:S(2)}, u32[]{:S(2)}) collective-permute-start(bf16[32,1280]{1,0:T(8,128)(2,1)S(1)} %get-tuple-element.70), channel_id=1, source_target_pairs={{0,6},{1,7},{2,4},{3,5},{4,2},{5,3},{6,0},{7,1},{8,14},{9,15},{10,... | collective-permute-start | bytes 245768 | tf_op jit(solution)/shard_map/adapters/ppermute | solution.py:34
  49.7 5.5 %collective-permute-start.17 = (bf16[32,1280]{1,0:T(8,128)(2,1)S(1)}, bf16[32,1280]{1,0:T(8,128)(2,1)S(1)}, u32[]{:S(2)}, u32[]{:S(2)}) collective-permute-start(bf16[32,1280]{1,0:T(8,128)(2,1)S(1)} %get-tuple-element.71), channel_id=1, source_target_pairs={{0,2},{1,3},{2,0},{3,1},{4,6},{5,7},{6,4},{7,5},{8,10},{9,11},{10,... | collective-permute-start | bytes 245768 | tf_op jit(solution)/shard_map/adapters/ppermute | solution.py:34

commit v7 on v6

--- a/solution.py
+++ b/solution.py
@@ -196,23 +196,24 @@
     return [holder[:, at : at + hid_width] for at in blocks]
 
 
-def adapter_sums(loops, chips, cols, part, start, adapter_in, rows, holders):
-    rank = adapter_in.shape[0] // loops
+def from_hidden(chips, cols, wide, start, stop, adapter_in, holders):
     hid_width = adapter_in.shape[1]
-    stop = start + rows[0].shape[0]
-    side = part + rank + LANES
-    wide = wide_of(cols)
     row = lax.broadcasted_iota(jnp.int32, (hid_width, wide), 0)
     lane = lax.broadcasted_iota(jnp.int32, (hid_width, wide), 1)
     pick = (row == lane + here()[1] * cols) & (lane < cols)
     pick = jnp.where(pick, 1.0, 0.0).astype(bf16)
     hid = [x for h in holders for x in hidden_rows(h, hid_width, chips, start, stop)]
     hid = jnp.concatenate(hid, axis=0)
+    return nt(hid, adapter_in[...]).astype(bf16), nn(hid, pick).astype(bf16)
+
+
+def adapter_sums(loops, part, rows, down, picked):
+    rank = down.shape[1] // loops
+    side = part + rank + LANES
     tail = jnp.concatenate([r[:, part:side] for r in rows], axis=0).astype(f32)
     body = jnp.concatenate([r[:, :part] for r in rows], axis=0)
-    down = nt(hid, adapter_in[...])
-    picked = nn(hid, pick).astype(bf16)
     masks = [tail[:, rank + l : rank + l + 1] > 0.0 for l in range(loops)]
+    down = down.astype(f32)
     left = [jnp.where(masks[l], down[:, l * rank : (l + 1) * rank], 0.0) for l in range(loops)]
     out = tn(jnp.concatenate(left, axis=1).astype(bf16), body)
     left = [jnp.where(masks[l], tail[:, :rank], 0.0) for l in range(loops)]
@@ -224,25 +225,28 @@
 
 
 def adapter_first_body(loops, chips, cols, groups, adapter_in, _, *refs):
-    rows, (out, inn) = refs[:-2], refs[-2:]
+    rows, (out, inn, down_last, picked_last) = refs[:-4], refs[-4:]
+    part, wide = out.shape[1], inn.shape[1]
     start = 0
     for at in range(0, len(rows), groups):
         chunk = rows[at : at + groups]
-        terms = adapter_sums(
-            loops, chips, cols, out.shape[1], start, adapter_in, chunk, rows[:groups]
-        )
+        stop = start + chunk[0].shape[0]
+        parts = from_hidden(chips, cols, wide, start, stop, adapter_in, rows[:groups])
+        terms = adapter_sums(loops, part, chunk, *parts)
         for target, term in zip((out, inn), terms):
             target[...] = target[...] + term if start else term
-        start += chunk[0].shape[0]
-
-
-def adapter_last_body(loops, chips, cap, cols, groups, adapter_in, out, inn, mix, *refs):
-    holders, rows, (keep, give, sums, narrow) = refs[:groups], refs[groups:-4], refs[-4:]
-    rank = adapter_in.shape[0] // loops
+        start = stop
+    stop = chips * rows[0].shape[0]
+    parts = from_hidden(chips, cols, wide, start, stop, adapter_in, rows[:groups])
+    down_last[...], picked_last[...] = parts
+
+
+def adapter_last_body(loops, chips, cap, cols, out, inn, mix, down, picked, *refs):
+    rows, (keep, give, sums, narrow) = refs[:-4], refs[-4:]
+    rank = out.shape[0] // loops
     part = out.shape[1]
     share = rank // (2 * chips)
-    start = mix.shape[0] - rows[0].shape[0]
-    more = adapter_sums(loops, chips, cols, part, start, adapter_in, rows, holders)
+    more = adapter_sums(loops, part, rows, down[...], picked[...])
     sums[...] = out[...] + more[0]
     narrow[...] = inn[...] + more[1]
     owners = sources(here(), chips)
@@ -390,22 +394,23 @@
     with jax.named_scope("adapters"):
         work = groups * slots * loops * rank * (part + hid_width + wide)
         sums = (shape((loops * rank, part), f32), shape((loops * rank, wide), f32))
-        out, inn = call(
+        size = groups * 2 * len(chunks[-1]) * cap
+        out, inn, down, picked = call(
             functools.partial(adapter_first_body, loops, chips, cols, groups),
-            sums,
+            sums + (shape((size, loops * rank), bf16), shape((size, wide), bf16)),
             (V, A) + (V,) * (groups * (len(chunks) - 1)),
             flops=work,
             nbytes=groups * slots * part,
         )(flat_in, mix, *(p for chunk in parts[:-1] for p in chunk))
         block = (chips, loops * share, part + wide)
         keep3, give3 = call(
-            functools.partial(adapter_last_body, loops, chips, cap, cols, groups),
+            functools.partial(adapter_last_body, loops, chips, cap, cols),
             (shape(block, f32), shape(block, bf16)),
-            (V,) * (4 + 2 * groups),
+            (V,) * (5 + groups),
             scratch=[pltpu.VMEM(s.shape, f32) for s in sums],
             flops=work,
             nbytes=groups * slots * part,
-        )(flat_in, out, inn, mix, *parts[0], *parts[-1])
+        )(out, inn, mix, down, picked, *parts[-1])
         got3 = swap(give3, "expert", experts, 1)
         ready = call(
             functools.partial(pair_body, chips),

time: 56.2 us -> 55.9 us (level)
  no operation moved by 1% of the time
where the time goes in v7:
time: 55.9 us; the launch traced here: 55.7 us
  starting transfers between devices  26.9 us (48%)
  waiting for transfers between devices  14.9 us (27%)
  Pallas kernels  9.36 us (17%)
  local copies, waits for them, and re-layouts  2.19 us (4%)
  other arithmetic  1.51 us (3%)
  between operations  0.76 us (1%)
    ppermute x18, starting transfers between devices, swap(): return lax.ppermute(x, axis, [(i, i ^ mask) for i in range(size)])  26.9 us
    ppermute x18, waiting for transfers between devices, swap(): return lax.ppermute(x, axis, [(i, i ^ mask) for i in range(size)])  14.9 us
    pallas_call x1, Pallas kernels, on_device(): call(functools.partial(product_body, groups, chips), shape((1, part, hid_...  2.67 us
    unnamed x12, local copies, waits for them, and re-layouts  2.17 us
    pallas_call x1, Pallas kernels, on_device(): call(functools.partial(inner_body, chips, cap, len(chunks)), (shape((slot...  1.85 us
    pallas_call x3, Pallas kernels, on_device(): call(functools.partial(arrive_body, groups, chips, cap, own, len(before))...  1.47 us
    pallas_call x1, Pallas kernels, on_device(): call(functools.partial(adapter_first_body, loops, chips, cols, groups), s...  1.44 us
  transfers between devices with their start and end apart: 18, of which 12 were waited for; matrix products, arithmetic and copies ran while one was open for 0% of the time, Pallas kernels for 13%

profile of v7, /device:TPU:0, one launch (start us, length us, event | category | flops | bytes accessed | tf_op | source)
XLA Modules:
  0.0 55.7 jit_solution(14420632735424838944)
XLA Ops:
  0.6 0.8 %broadcast_multiply_fusion = s32[128]{0:T(128)S(1)} fusion(s32[128]{0:T(128)} %param.15), kind=kLoop, calls=%fused_computation.3 | loop fusion | flops 128 | bytes 1024 | tf_op jit(solution)/shard_map/mul | solution.py:333
  1.4 0.7 %add_bitcast_fusion.small = f32[8,128]{1,0:T(8,128)S(1)} fusion(bf16[128,8]{0,1:T(8,128)(2,1)} %param.13, s32[128,8]{0,1:T(8,128)} %param.14, s32[128]{0:T(128)S(1)} %broadcast_multiply_fusion), kind=kLoop, calls=%fused_computation.2 | loop fusion | flops 5120 | bytes 10752 | tf_op jit(solution)/shard_map/add | solution.py:334
  2.2 1.2 %copy-done.3 = bf16[128,4096]{1,0:T(8,128)(2,1)S(1)} copy-done((bf16[128,4096]{1,0:T(8,128)(2,1)S(1)}, bf16[128,4096]{1,0:T(8,128)(2,1)}, u32[]{:S(2)}) %copy-start.3) | copy-done | bytes 1048600
  3.4 0.6 %route.1 = (bf16[4,16,4224]{2,1,0:T(8,128)(2,1)S(1)}, bf16[2,16,4224]{2,1,0:T(8,128)(2,1)S(1)}, bf16[3,16,4224]{2,1,0:T(8,128)(2,1)S(1)}, bf16[128,128]{1,0:T(8,128)(2,1)S(1)}) custom-call(f32[8,128]{1,0:T(8,128)S(1)} %add_bitcast_fusion.small, bf16[128,4096]{1,0:T(8,128)(2,1)S(1)} %copy-done.3), custom_call_target="tpu_custom_call" | custom-call | flops 134217728 | bytes 3145728 | tf_op jit(solution)/shard_map/route/pallas_call | solution.py:341
  4.0 0.5 collective-permute-start
  4.5 3.7 %collective-permute-start.2 = (bf16[2,16,4224]{2,1,0:T(8,128)(2,1)S(1)}, bf16[2,16,4224]{2,1,0:T(8,128)(2,1)S(1)}, u32[]{:S(2)}, u32[]{:S(2)}) collective-permute-start(bf16[2,16,4224]{2,1,0:T(8,128)(2,1)S(1)} %get-tuple-element.45), channel_id=1, source_target_pairs={{0,4},{1,5},{2,6},{3,7},{4,0},{5,1},{6,2},{7,3},{8,12},{9,13},{10,... | collective-permute-start | bytes 811016 | tf_op jit(solution)/shard_map/dispatch/ppermute | solution.py:34
  8.2 1.6 %collective-permute-start.1 = (bf16[2,16,4224]{2,1,0:T(8,128)(2,1)S(1)}, bf16[2,16,4224]{2,1,0:T(8,128)(2,1)S(1)}, u32[]{:S(2)}, u32[]{:S(2)}) collective-permute-start(bf16[2,16,4224]{2,1,0:T(8,128)(2,1)S(1)} %dispatch.2), channel_id=1, source_target_pairs={{0,2},{1,3},{2,0},{3,1},{4,6},{5,7},{6,4},{7,5},{8,10},{9,11},{10,... | collective-permute-start | bytes 811016 | tf_op jit(solution)/shard_map/dispatch/ppermute | solution.py:34
  9.8 0.9 %copy-done.4 = bf16[1,1,128,768]{3,2,1,0:T(8,128)(2,1)S(1)} copy-done((bf16[1,1,128,768]{3,2,1,0:T(8,128)(2,1)S(1)}, bf16[1,1,128,768]{3,2,1,0:T(8,128)(2,1)}, u32[]{:S(2)}) %copy-start.4) | copy-done | bytes 196632
  11.2 2.5 %collective-permute-start.4 = (bf16[32,4352]{1,0:T(8,128)(2,1)S(1)}, bf16[32,4352]{1,0:T(8,128)(2,1)S(1)}, u32[]{:S(2)}, u32[]{:S(2)}) collective-permute-start(bf16[32,4352]{1,0:T(8,128)(2,1)S(1)} %get-tuple-element.46), channel_id=1, source_target_pairs={{0,24},{8,16},{16,8},{24,0},{1,25},{9,17},{17,9},{25,1},{2,26},{10... | collective-permute-start | bytes 835592 | tf_op jit(solution)/shard_map/arrive/ppermute | solution.py:34
  13.7 0.5 collective-permute-start.5
  14.2 0.5 collective-permute-start.6
  14.8 6.3 %collective-permute-done.2 = bf16[2,16,4224]{2,1,0:T(8,128)(2,1)S(1)} collective-permute-done((bf16[2,16,4224]{2,1,0:T(8,128)(2,1)S(1)}, bf16[2,16,4224]{2,1,0:T(8,128)(2,1)S(1)}, u32[]{:S(2)}, u32[]{:S(2)}) %collective-permute-start.2) | collective-permute-done | bytes 270368 | tf_op jit(solution)/shard_map/dispatch/ppermute | solution.py:34
  21.4 3.8 %collective-permute-start.7 = (bf16[2,16,4224]{2,1,0:T(8,128)(2,1)S(1)}, bf16[2,16,4224]{2,1,0:T(8,128)(2,1)S(1)}, u32[]{:S(2)}, u32[]{:S(2)}) collective-permute-start(bf16[2,16,4224]{2,1,0:T(8,128)(2,1)S(1)} %dispatch.3), channel_id=1, source_target_pairs={{0,6},{1,7},{2,4},{3,5},{4,2},{5,3},{6,0},{7,1},{8,14},{9,15},{10,... | collective-permute-start | bytes 811016 | tf_op jit(solution)/shard_map/dispatch/ppermute | solution.py:34
  25.3 1.3 %collective-permute-done.5.refs_4_.refs_2_ = bf16[32,4352]{1,0:T(8,128)(2,1)S(1)} collective-permute-done((bf16[32,4352]{1,0:T(8,128)(2,1)S(1)}, bf16[32,4352]{1,0:T(8,128)(2,1)S(1)}, u32[]{:S(2)}, u32[]{:S(2)}) %collective-permute-start.5) | collective-permute-done | bytes 278560 | tf_op jit(solution)/shard_map/arrive/ppermute | solution.py:34
  26.7 0.6 arrive.4
  27.3 1.7 %collective-permute-start.8 = (bf16[64,1280]{1,0:T(8,128)(2,1)S(1)}, bf16[64,1280]{1,0:T(8,128)(2,1)S(1)}, u32[]{:S(2)}, u32[]{:S(2)}) collective-permute-start(bf16[64,1280]{1,0:T(8,128)(2,1)S(1)} %get-tuple-element.57), channel_id=1, source_target_pairs={{0,24},{8,16},{16,8},{24,0},{1,25},{9,17},{17,9},{25,1},{2,26},{10... | collective-permute-start | bytes 491528 | tf_op jit(solution)/shard_map/arrive/ppermute | solution.py:34
  29.0 1.3 %collective-permute-start.9 = (bf16[64,1280]{1,0:T(8,128)(2,1)S(1)}, bf16[64,1280]{1,0:T(8,128)(2,1)S(1)}, u32[]{:S(2)}, u32[]{:S(2)}) collective-permute-start(bf16[64,1280]{1,0:T(8,128)(2,1)S(1)} %get-tuple-element.58), channel_id=1, source_target_pairs={{0,16},{8,24},{16,0},{24,8},{1,17},{9,25},{17,1},{25,9},{2,18},{10... | collective-permute-start | bytes 491528 | tf_op jit(solution)/shard_map/arrive/ppermute | solution.py:34
  30.3 0.5 collective-permute-start.10
  30.8 1.3 %collective-permute-done.7.refs_0_ = bf16[2,16,4224]{2,1,0:T(8,128)(2,1)S(1)} collective-permute-done((bf16[2,16,4224]{2,1,0:T(8,128)(2,1)S(1)}, bf16[2,16,4224]{2,1,0:T(8,128)(2,1)S(1)}, u32[]{:S(2)}, u32[]{:S(2)}) %collective-permute-start.7) | collective-permute-done | bytes 270368 | tf_op jit(solution)/shard_map/dispatch/ppermute | solution.py:34
  32.6 2.6 %collective-permute-start.11 = (bf16[32,1280]{1,0:T(8,128)(2,1)S(1)}, bf16[32,1280]{1,0:T(8,128)(2,1)S(1)}, u32[]{:S(2)}, u32[]{:S(2)}) collective-permute-start(bf16[32,1280]{1,0:T(8,128)(2,1)S(1)} %get-tuple-element.61), channel_id=1, source_target_pairs={{0,24},{8,16},{16,8},{24,0},{1,25},{9,17},{17,9},{25,1},{2,26},{10... | collective-permute-start | bytes 245768 | tf_op jit(solution)/shard_map/arrive/ppermute | solution.py:34
  35.1 0.5 collective-permute-start.12
  35.7 1.2 %collective-permute-start.13 = (bf16[32,1280]{1,0:T(8,128)(2,1)S(1)}, bf16[32,1280]{1,0:T(8,128)(2,1)S(1)}, u32[]{:S(2)}, u32[]{:S(2)}) collective-permute-start(bf16[32,1280]{1,0:T(8,128)(2,1)S(1)} %get-tuple-element.63), channel_id=1, source_target_pairs={{0,8},{8,0},{16,24},{24,16},{1,9},{9,1},{17,25},{25,17},{2,10},{10... | collective-permute-start | bytes 245768 | tf_op jit(solution)/shard_map/arrive/ppermute | solution.py:34
  36.8 1.8 %inner.1 = (bf16[128,768]{1,0:T(8,128)(2,1)}, f32[128,128]{1,0:T(8,128)S(1)}) custom-call(bf16[4096,768]{1,0:T(8,128)(2,1)S(1)} %bitcast.12, bf16[256,768]{1,0:T(8,128)(2,1)S(1)} %bitcast.13, bf16[128,768]{1,0:T(8,128)(2,1)S(1)} %bitcast.16, bf16[32,4224]{1,0:T(8,128)(2,1)S(1)} %get-tuple-element.44.refs_0_, bf16[64,4224]{1,0:T(8,128)(2,1)S(1)} %get-tuple-element.49.refs_1_, ...), custom_call_target="tpu_custom_call" | custom-call | flops 805306368 | bytes 6291456 | tf_op jit(solution)/shard_map/inner/pallas_call | solution.py:387
  38.8 1.4 %adapters.3 = (f32[256,1024]{1,0:T(8,128)S(1)}, f32[256,256]{1,0:T(8,128)S(1)}, bf16[128,256]{1,0:T(8,128)(2,1)S(1)}, bf16[128,256]{1,0:T(8,128)(2,1)S(1)}) custom-call(bf16[256,768]{1,0:T(8,128)(2,1)S(1)} %bitcast.14, f32[128,128]{1,0:T(8,128)S(1)} %get-tuple-element.65._.mix, bf16[32,4352]{1,0:T(8,128)(2,1)S(1)} %get-tuple-element.55.refs_0_, ...), custom_call_target="tpu_custom_call" | custom-call | flops 268435456 | bytes 524288 | tf_op jit(solution)/shard_map/adapters/pallas_call | solution.py:398
  40.5 0.7 %collective-permute-done.12.refs_10_.refs_2_ = bf16[32,1280]{1,0:T(8,128)(2,1)S(1)} collective-permute-done((bf16[32,1280]{1,0:T(8,128)(2,1)S(1)}, bf16[32,1280]{1,0:T(8,128)(2,1)S(1)}, u32[]{:S(2)}, u32[]{:S(2)}) %collective-permute-start.12) | collective-permute-done | bytes 81952 | tf_op jit(solution)/shard_map/arrive/ppermute | solution.py:34
  41.9 1.6 %collective-permute-done.14.got = bf16[4,32,1280]{2,1,0:T(8,128)(2,1)S(1)} collective-permute-done((bf16[4,32,1280]{2,1,0:T(8,128)(2,1)S(1)}, bf16[4,32,1280]{2,1,0:T(8,128)(2,1)S(1)}, u32[]{:S(2)}, u32[]{:S(2)}) %collective-permute-start.14) | collective-permute-done | bytes 327712 | tf_op jit(solution)/shard_map/adapters/ppermute | solution.py:34
  43.6 3.3 %collective-permute-start.15 = (bf16[32,1280]{1,0:T(8,128)(2,1)S(1)}, bf16[32,1280]{1,0:T(8,128)(2,1)S(1)}, u32[]{:S(2)}, u32[]{:S(2)}) collective-permute-start(bf16[32,1280]{1,0:T(8,128)(2,1)S(1)} %get-tuple-element.73), channel_id=1, source_target_pairs={{0,4},{1,5},{2,6},{3,7},{4,0},{5,1},{6,2},{7,3},{8,12},{9,13},{10,... | collective-permute-start | bytes 245768 | tf_op jit(solution)/shard_map/adapters/ppermute | solution.py:34
  46.9 2.5 %collective-permute-start.16 = (bf16[32,1280]{1,0:T(8,128)(2,1)S(1)}, bf16[32,1280]{1,0:T(8,128)(2,1)S(1)}, u32[]{:S(2)}, u32[]{:S(2)}) collective-permute-start(bf16[32,1280]{1,0:T(8,128)(2,1)S(1)} %get-tuple-element.74), channel_id=1, source_target_pairs={{0,6},{1,7},{2,4},{3,5},{4,2},{5,3},{6,0},{7,1},{8,14},{9,15},{10,... | collective-permute-start | bytes 245768 | tf_op jit(solution)/shard_map/adapters/ppermute | solution.py:34
  49.4 2.7 %product.1 = f32[1,1024,768]{2,1,0:T(8,128)} custom-call(bf16[32,4352]{1,0:T(8,128)(2,1)S(1)} %get-tuple-element.55.refs_0_, bf16[32,4352]{1,0:T(8,128)(2,1)S(1)} %collective-permute-done.4.refs_3_.refs_1_, bf16[32,4352]{1,0:T(8,128)(2,1)S(1)} %collective-permute-done.5.refs_4_.refs_2_, bf16[32,4352]{1,0:T(8,128)(2,1)S(1)} %collective-permute-done.6.refs_5_.refs_3_, ...), custom_call_target="tpu_custom_call" | custom-call | flops 805306368 | bytes 2097152 | tf_op jit(solution)/shard_map/product/pallas_call | solution.py:425
  52.0 2.3 %collective-permute-done.16.refs_2_ = bf16[32,1280]{1,0:T(8,128)(2,1)S(1)} collective-permute-done((bf16[32,1280]{1,0:T(8,128)(2,1)S(1)}, bf16[32,1280]{1,0:T(8,128)(2,1)S(1)}, u32[]{:S(2)}, u32[]{:S(2)}) %collective-permute-start.16) | collective-permute-done | bytes 81952 | tf_op jit(solution)/shard_map/adapters/ppermute | solution.py:34
  54.4 0.5 collective-permute-done.17.refs_3_
  54.9 0.8 %final.1 = (f32[2,16,1024]{2,1,0:T(8,128)}, f32[2,16,192]{2,1,0:T(8,128)}, f32[8,128]{1,0:T(8,128)}) custom-call(f32[8,128]{1,0:T(8,128)S(1)} %add_bitcast_fusion.small, bf16[128,128]{1,0:T(8,128)(2,1)S(1)} %get-tuple-element.64.picks, bf16[32,1280]{1,0:T(8,128)(2,1)S(1)} %get-tuple-element.72.refs_0_, bf16[32,1280]{1,0:T(8,128)(2,1)S(1)} %collective-permute-done.15.refs_1_, ...), custom_call_target="tpu_custom_call" | custom-call | bytes 1000000 | tf_op jit(solution)/shard_map/final/pallas_call | solution.py:434
  (31 shorter events, 2.5 us)
Async XLA Ops:
  0.6 9.2 %copy-start = (bf16[2,4096,128]{2,1,0:T(8,128)(2,1)S(1)}, bf16[2,4096,128]{2,1,0:T(8,128)(2,1)}, u32[]{:S(2)}) copy-start(bf16[2,4096,128]{2,1,0:T(8,128)(2,1)} %adapter_out.5) | copy-start | bytes 6291460
  2.2 1.2 %copy-start.3 = (bf16[128,4096]{1,0:T(8,128)(2,1)S(1)}, bf16[128,4096]{1,0:T(8,128)(2,1)}, u32[]{:S(2)}) copy-start(bf16[128,4096]{1,0:T(8,128)(2,1)} %cot.1) | copy-start | bytes 3145732
  4.0 4.2 %collective-permute-start = (bf16[3,16,4224]{2,1,0:T(8,128)(2,1)S(1)}, bf16[3,16,4224]{2,1,0:T(8,128)(2,1)S(1)}, u32[]{:S(2)}, u32[]{:S(2)}) collective-permute-start(bf16[3,16,4224]{2,1,0:T(8,128)(2,1)S(1)} %get-tuple-element.43), channel_id=1, source_target_pairs={{0,1},{1,0},{2,3},{3,2},{4,5},{5,4},{6,7},{7,6},{8,9},{9,8},{10,11... | collective-permute-start | bytes 1216520 | tf_op jit(solution)/shard_map/route/ppermute | solution.py:34
  4.5 16.6 %collective-permute-start.2 = (bf16[2,16,4224]{2,1,0:T(8,128)(2,1)S(1)}, bf16[2,16,4224]{2,1,0:T(8,128)(2,1)S(1)}, u32[]{:S(2)}, u32[]{:S(2)}) collective-permute-start(bf16[2,16,4224]{2,1,0:T(8,128)(2,1)S(1)} %get-tuple-element.45), channel_id=1, source_target_pairs={{0,4},{1,5},{2,6},{3,7},{4,0},{5,1},{6,2},{7,3},{8,12},{9,13},{10,... | collective-permute-start | bytes 811016 | tf_op jit(solution)/shard_map/dispatch/ppermute | solution.py:34
  8.2 13.2 %collective-permute-start.1 = (bf16[2,16,4224]{2,1,0:T(8,128)(2,1)S(1)}, bf16[2,16,4224]{2,1,0:T(8,128)(2,1)S(1)}, u32[]{:S(2)}, u32[]{:S(2)}) collective-permute-start(bf16[2,16,4224]{2,1,0:T(8,128)(2,1)S(1)} %dispatch.2), channel_id=1, source_target_pairs={{0,2},{1,3},{2,0},{3,1},{4,6},{5,7},{6,4},{7,5},{8,10},{9,11},{10,... | collective-permute-start | bytes 811016 | tf_op jit(solution)/shard_map/dispatch/ppermute | solution.py:34
  9.8 0.9 %copy-start.4 = (bf16[1,1,128,768]{3,2,1,0:T(8,128)(2,1)S(1)}, bf16[1,1,128,768]{3,2,1,0:T(8,128)(2,1)}, u32[]{:S(2)}) copy-start(bf16[1,1,128,768]{3,2,1,0:T(8,128)(2,1)} %param.9) | copy-start | bytes 589828
  11.2 14.1 %collective-permute-start.4 = (bf16[32,4352]{1,0:T(8,128)(2,1)S(1)}, bf16[32,4352]{1,0:T(8,128)(2,1)S(1)}, u32[]{:S(2)}, u32[]{:S(2)}) collective-permute-start(bf16[32,4352]{1,0:T(8,128)(2,1)S(1)} %get-tuple-element.46), channel_id=1, source_target_pairs={{0,24},{8,16},{16,8},{24,0},{1,25},{9,17},{17,9},{25,1},{2,26},{10... | collective-permute-start | bytes 835592 | tf_op jit(solution)/shard_map/arrive/ppermute | solution.py:34
  13.7 12.9 %collective-permute-start.5 = (bf16[32,4352]{1,0:T(8,128)(2,1)S(1)}, bf16[32,4352]{1,0:T(8,128)(2,1)S(1)}, u32[]{:S(2)}, u32[]{:S(2)}) collective-permute-start(bf16[32,4352]{1,0:T(8,128)(2,1)S(1)} %get-tuple-element.47), channel_id=1, source_target_pairs={{0,16},{8,24},{16,0},{24,8},{1,17},{9,25},{17,1},{25,9},{2,18},{10... | collective-permute-start | bytes 835592 | tf_op jit(solution)/shard_map/arrive/ppermute | solution.py:34
  14.2 12.5 %collective-permute-start.6 = (bf16[32,4352]{1,0:T(8,128)(2,1)S(1)}, bf16[32,4352]{1,0:T(8,128)(2,1)S(1)}, u32[]{:S(2)}, u32[]{:S(2)}) collective-permute-start(bf16[32,4352]{1,0:T(8,128)(2,1)S(1)} %get-tuple-element.48), channel_id=1, source_target_pairs={{0,8},{8,0},{16,24},{24,16},{1,9},{9,1},{17,25},{25,17},{2,10},{10... | collective-permute-start | bytes 835592 | tf_op jit(solution)/shard_map/arrive/ppermute | solution.py:34
  21.1 4.2 %collective-permute-start.3 = (bf16[16,4224]{1,0:T(8,128)(2,1)S(1)}, bf16[16,4224]{1,0:T(8,128)(2,1)S(1)}, u32[]{:S(2)}, u32[]{:S(2)}) collective-permute-start(bf16[16,4224]{1,0:T(8,128)(2,1)S(1)} %get-tuple-element.79), channel_id=1, source_target_pairs={{0,1},{1,0},{2,3},{3,2},{4,5},{5,4},{6,7},{7,6},{8,9},{9,8},{10,11... | collective-permute-start | bytes 405512 | tf_op jit(solution)/shard_map/dispatch/ppermute | solution.py:34
  21.4 15.4 %copy-start.1 = (bf16[1,4096,768]{2,1,0:T(8,128)(2,1)S(1)}, bf16[1,4096,768]{2,1,0:T(8,128)(2,1)}, u32[]{:S(2)}) copy-start(bf16[1,4096,768]{2,1,0:T(8,128)(2,1)} %param.10) | copy-start | bytes 18874372
  21.4 15.4 %copy-start.2 = (bf16[2,128,768]{2,1,0:T(8,128)(2,1)S(1)}, bf16[2,128,768]{2,1,0:T(8,128)(2,1)}, u32[]{:S(2)}) copy-start(bf16[2,128,768]{2,1,0:T(8,128)(2,1)} %param.11) | copy-start | bytes 1179652
  21.4 15.4 %copy-start.5 = (bf16[1,1,128,768]{3,2,1,0:T(8,128)(2,1)S(1)}, bf16[1,1,128,768]{3,2,1,0:T(8,128)(2,1)}, u32[]{:S(2)}) copy-start(bf16[1,1,128,768]{3,2,1,0:T(8,128)(2,1)} %param.9) | copy-start | bytes 589828
  21.4 10.7 %collective-permute-start.7 = (bf16[2,16,4224]{2,1,0:T(8,128)(2,1)S(1)}, bf16[2,16,4224]{2,1,0:T(8,128)(2,1)S(1)}, u32[]{:S(2)}, u32[]{:S(2)}) collective-permute-start(bf16[2,16,4224]{2,1,0:T(8,128)(2,1)S(1)} %dispatch.3), channel_id=1, source_target_pairs={{0,6},{1,7},{2,4},{3,5},{4,2},{5,3},{6,0},{7,1},{8,14},{9,15},{10,... | collective-permute-start | bytes 811016 | tf_op jit(solution)/shard_map/dispatch/ppermute | solution.py:34
  27.3 8.4 %collective-permute-start.8 = (bf16[64,1280]{1,0:T(8,128)(2,1)S(1)}, bf16[64,1280]{1,0:T(8,128)(2,1)S(1)}, u32[]{:S(2)}, u32[]{:S(2)}) collective-permute-start(bf16[64,1280]{1,0:T(8,128)(2,1)S(1)} %get-tuple-element.57), channel_id=1, source_target_pairs={{0,24},{8,16},{16,8},{24,0},{1,25},{9,17},{17,9},{25,1},{2,26},{10... | collective-permute-start | bytes 491528 | tf_op jit(solution)/shard_map/arrive/ppermute | solution.py:34
  29.0 9.8 %collective-permute-start.9 = (bf16[64,1280]{1,0:T(8,128)(2,1)S(1)}, bf16[64,1280]{1,0:T(8,128)(2,1)S(1)}, u32[]{:S(2)}, u32[]{:S(2)}) collective-permute-start(bf16[64,1280]{1,0:T(8,128)(2,1)S(1)} %get-tuple-element.58), channel_id=1, source_target_pairs={{0,16},{8,24},{16,0},{24,8},{1,17},{9,25},{17,1},{25,9},{2,18},{10... | collective-permute-start | bytes 491528 | tf_op jit(solution)/shard_map/arrive/ppermute | solution.py:34
  30.3 8.5 %collective-permute-start.10 = (bf16[64,1280]{1,0:T(8,128)(2,1)S(1)}, bf16[64,1280]{1,0:T(8,128)(2,1)S(1)}, u32[]{:S(2)}, u32[]{:S(2)}) collective-permute-start(bf16[64,1280]{1,0:T(8,128)(2,1)S(1)} %get-tuple-element.59), channel_id=1, source_target_pairs={{0,8},{8,0},{16,24},{24,16},{1,9},{9,1},{17,25},{25,17},{2,10},{10... | collective-permute-start | bytes 491528 | tf_op jit(solution)/shard_map/arrive/ppermute | solution.py:34
  32.6 7.9 %collective-permute-start.11 = (bf16[32,1280]{1,0:T(8,128)(2,1)S(1)}, bf16[32,1280]{1,0:T(8,128)(2,1)S(1)}, u32[]{:S(2)}, u32[]{:S(2)}) collective-permute-start(bf16[32,1280]{1,0:T(8,128)(2,1)S(1)} %get-tuple-element.61), channel_id=1, source_target_pairs={{0,24},{8,16},{16,8},{24,0},{1,25},{9,17},{17,9},{25,1},{2,26},{10... | collective-permute-start | bytes 245768 | tf_op jit(solution)/shard_map/arrive/ppermute | solution.py:34
  35.1 6.1 %collective-permute-start.12 = (bf16[32,1280]{1,0:T(8,128)(2,1)S(1)}, bf16[32,1280]{1,0:T(8,128)(2,1)S(1)}, u32[]{:S(2)}, u32[]{:S(2)}) collective-permute-start(bf16[32,1280]{1,0:T(8,128)(2,1)S(1)} %get-tuple-element.62), channel_id=1, source_target_pairs={{0,16},{8,24},{16,0},{24,8},{1,17},{9,25},{17,1},{25,9},{2,18},{10... | collective-permute-start | bytes 245768 | tf_op jit(solution)/shard_map/arrive/ppermute | solution.py:34
  35.7 5.7 %collective-permute-start.13 = (bf16[32,1280]{1,0:T(8,128)(2,1)S(1)}, bf16[32,1280]{1,0:T(8,128)(2,1)S(1)}, u32[]{:S(2)}, u32[]{:S(2)}) collective-permute-start(bf16[32,1280]{1,0:T(8,128)(2,1)S(1)} %get-tuple-element.63), channel_id=1, source_target_pairs={{0,8},{8,0},{16,24},{24,16},{1,9},{9,1},{17,25},{25,17},{2,10},{10... | collective-permute-start | bytes 245768 | tf_op jit(solution)/shard_map/arrive/ppermute | solution.py:34
  41.9 1.7 %collective-permute-start.14 = (bf16[4,32,1280]{2,1,0:T(8,128)(2,1)S(1)}, bf16[4,32,1280]{2,1,0:T(8,128)(2,1)S(1)}, u32[]{:S(2)}, u32[]{:S(2)}) collective-permute-start(bf16[4,32,1280]{2,1,0:T(8,128)(2,1)S(1)} %get-tuple-element.71), channel_id=1, source_target_pairs={{0,1},{1,0},{2,3},{3,2},{4,5},{5,4},{6,7},{7,6},{8,9},{9,8},{10,11... | collective-permute-start | bytes 983048 | tf_op jit(solution)/shard_map/adapters/ppermute | solution.py:34
  43.6 8.4 %collective-permute-start.15 = (bf16[32,1280]{1,0:T(8,128)(2,1)S(1)}, bf16[32,1280]{1,0:T(8,128)(2,1)S(1)}, u32[]{:S(2)}, u32[]{:S(2)}) collective-permute-start(bf16[32,1280]{1,0:T(8,128)(2,1)S(1)} %get-tuple-element.73), channel_id=1, source_target_pairs={{0,4},{1,5},{2,6},{3,7},{4,0},{5,1},{6,2},{7,3},{8,12},{9,13},{10,... | collective-permute-start | bytes 245768 | tf_op jit(solution)/shard_map/adapters/ppermute | solution.py:34
  46.9 7.5 %collective-permute-start.16 = (bf16[32,1280]{1,0:T(8,128)(2,1)S(1)}, bf16[32,1280]{1,0:T(8,128)(2,1)S(1)}, u32[]{:S(2)}, u32[]{:S(2)}) collective-permute-start(bf16[32,1280]{1,0:T(8,128)(2,1)S(1)} %get-tuple-element.74), channel_id=1, source_target_pairs={{0,6},{1,7},{2,4},{3,5},{4,2},{5,3},{6,0},{7,1},{8,14},{9,15},{10,... | collective-permute-start | bytes 245768 | tf_op jit(solution)/shard_map/adapters/ppermute | solution.py:34
  49.4 5.5 %collective-permute-start.17 = (bf16[32,1280]{1,0:T(8,128)(2,1)S(1)}, bf16[32,1280]{1,0:T(8,128)(2,1)S(1)}, u32[]{:S(2)}, u32[]{:S(2)}) collective-permute-start(bf16[32,1280]{1,0:T(8,128)(2,1)S(1)} %get-tuple-element.75), channel_id=1, source_target_pairs={{0,2},{1,3},{2,0},{3,1},{4,6},{5,7},{6,4},{7,5},{8,10},{9,11},{10,... | collective-permute-start | bytes 245768 | tf_op jit(solution)/shard_map/adapters/ppermute | solution.py:34

commit v8 on v7

--- a/solution.py
+++ b/solution.py
@@ -62,13 +62,10 @@
     return ((place[0] // 2) ^ hop) * 2 + ((place[0] % 2) ^ half)
 
 
-def decode(small, experts, loops):
-    loop = jnp.zeros_like(small)
-    for l in range(1, loops):
-        loop = loop + jnp.where(small >= l * (experts + 1.0), 1.0, 0.0)
-    rest = small - loop * (experts + 1.0)
-    route = jnp.floor(rest)
-    return route, rest - route, loop[:1]
+def decode(small, loops):
+    whole = jnp.floor(small)
+    route = jnp.floor((whole + 0.5) * (1.0 / loops))
+    return route, small - whole, (whole - route * loops)[:1]
 
 
 def deal_rows(middle, rows, at, keep, lead, give):
@@ -86,7 +83,7 @@
     ways = small.shape[0]
     toks, width = cot.shape
     owner = owner_column(here(), chips, experts).astype(f32)
-    route, chance, loop = decode(small[...], experts, loops)
+    route, chance, loop = decode(small[...], loops)
     named = jnp.zeros((experts, toks), f32)
     weight = jnp.zeros((experts, toks), f32)
     for k in range(ways):
@@ -289,7 +286,7 @@
         in_grad[l] = total[rows, part : part + cols]
     experts = 2 * chips
     owner = owner_column(here(), chips, experts).astype(f32)
-    routes = decode(small[...], experts, loops)[0]
+    routes = decode(small[...], loops)[0]
     sums = jnp.zeros(combine.shape, f32)
     for j in range(experts):
         half, hop = j // chips, j % chips
@@ -330,7 +327,7 @@
     bounds = [0, 1, max(2, 3 * chips // 4), chips]
     chunks = [range(a, b) for a, b in zip(bounds[:-1], bounds[1:])]
     flat_in = adapter_in.reshape(loops * rank, hid_width)
-    small = token_loop.reshape(1, toks) * (experts + 1) + jnp.minimum(routes.T, experts)
+    small = jnp.minimum(routes.T, experts) * loops + token_loop.reshape(1, toks)
     small = small.astype(f32) + probs.T.astype(f32)
 
     turns = range(groups - 1, 0, -1)

time: 55.9 us -> 55.2 us (0.987)
  other arithmetic: 1.51 us -> 0.85 us
    mul x1 -> x0, other arithmetic: 0.81 us -> none  [on_device(): token_loop.reshape(1, toks) * (experts + 1) + jnp.minimum(routes.T, experts)]
  transfers between devices with their start and end apart: 18 -> 18, of which waited for: 12 -> 12; matrix products, arithmetic and copies ran while one was open for 0% -> 0% of each run, Pallas kernels for 13% -> 14%
where the time goes in v8:
time: 55.2 us; the launch traced here: 55 us
  starting transfers between devices  26.9 us (49%)
  waiting for transfers between devices  15 us (27%)
  Pallas kernels  9.36 us (17%)
  local copies, waits for them, and re-layouts  2.19 us (4%)
  other arithmetic  0.85 us (2%)
  between operations  0.76 us (1%)
    ppermute x18, starting transfers between devices, swap(): return lax.ppermute(x, axis, [(i, i ^ mask) for i in range(size)])  26.9 us
    ppermute x18, waiting for transfers between devices, swap(): return lax.ppermute(x, axis, [(i, i ^ mask) for i in range(size)])  15 us
    pallas_call x1, Pallas kernels, on_device(): call(functools.partial(product_body, groups, chips), shape((1, part, hid_...  2.67 us
    unnamed x12, local copies, waits for them, and re-layouts  2.17 us
    pallas_call x1, Pallas kernels, on_device(): call(functools.partial(inner_body, chips, cap, len(chunks)), (shape((slot...  1.84 us
    pallas_call x3, Pallas kernels, on_device(): call(functools.partial(arrive_body, groups, chips, cap, own, len(before))...  1.46 us
    pallas_call x1, Pallas kernels, on_device(): call(functools.partial(adapter_first_body, loops, chips, cols, groups), s...  1.44 us
  transfers between devices with their start and end apart: 18, of which 12 were waited for; matrix products, arithmetic and copies ran while one was open for 0% of the time, Pallas kernels for 14%

profile of v8, /device:TPU:0, one launch (start us, length us, event | category | flops | bytes accessed | tf_op | source)
XLA Modules:
  0.0 55.0 jit_solution(17198402692507215156)
XLA Ops:
  0.6 0.9 %add_bitcast_fusion.small = f32[8,128]{1,0:T(8,128)S(1)} fusion(bf16[128,8]{0,1:T(8,128)(2,1)} %param.13, s32[128,8]{0,1:T(8,128)} %param.14, s32[128]{0:T(128)} %param.15), kind=kLoop, calls=%fused_computation.2 | loop fusion | flops 6144 | bytes 10752 | tf_op jit(solution)/shard_map/add | solution.py:331
  1.5 1.2 %copy-done.3 = bf16[128,4096]{1,0:T(8,128)(2,1)S(1)} copy-done((bf16[128,4096]{1,0:T(8,128)(2,1)S(1)}, bf16[128,4096]{1,0:T(8,128)(2,1)}, u32[]{:S(2)}) %copy-start.3) | copy-done | bytes 1048600
  2.7 0.6 %route.1 = (bf16[4,16,4224]{2,1,0:T(8,128)(2,1)S(1)}, bf16[2,16,4224]{2,1,0:T(8,128)(2,1)S(1)}, bf16[3,16,4224]{2,1,0:T(8,128)(2,1)S(1)}, bf16[128,128]{1,0:T(8,128)(2,1)S(1)}) custom-call(f32[8,128]{1,0:T(8,128)S(1)} %add_bitcast_fusion.small, bf16[128,4096]{1,0:T(8,128)(2,1)S(1)} %copy-done.3), custom_call_target="tpu_custom_call" | custom-call | flops 134217728 | bytes 3145728 | tf_op jit(solution)/shard_map/route/pallas_call | solution.py:338
  3.3 0.5 collective-permute-start
  3.8 3.7 %collective-permute-start.2 = (bf16[2,16,4224]{2,1,0:T(8,128)(2,1)S(1)}, bf16[2,16,4224]{2,1,0:T(8,128)(2,1)S(1)}, u32[]{:S(2)}, u32[]{:S(2)}) collective-permute-start(bf16[2,16,4224]{2,1,0:T(8,128)(2,1)S(1)} %get-tuple-element.45), channel_id=1, source_target_pairs={{0,4},{1,5},{2,6},{3,7},{4,0},{5,1},{6,2},{7,3},{8,12},{9,13},{10,... | collective-permute-start | bytes 811016 | tf_op jit(solution)/shard_map/dispatch/ppermute | solution.py:34
  7.5 1.6 %collective-permute-start.1 = (bf16[2,16,4224]{2,1,0:T(8,128)(2,1)S(1)}, bf16[2,16,4224]{2,1,0:T(8,128)(2,1)S(1)}, u32[]{:S(2)}, u32[]{:S(2)}) collective-permute-start(bf16[2,16,4224]{2,1,0:T(8,128)(2,1)S(1)} %dispatch.2), channel_id=1, source_target_pairs={{0,2},{1,3},{2,0},{3,1},{4,6},{5,7},{6,4},{7,5},{8,10},{9,11},{10,... | collective-permute-start | bytes 811016 | tf_op jit(solution)/shard_map/dispatch/ppermute | solution.py:34
  9.1 0.9 %copy-done.4 = bf16[1,1,128,768]{3,2,1,0:T(8,128)(2,1)S(1)} copy-done((bf16[1,1,128,768]{3,2,1,0:T(8,128)(2,1)S(1)}, bf16[1,1,128,768]{3,2,1,0:T(8,128)(2,1)}, u32[]{:S(2)}) %copy-start.4) | copy-done | bytes 196632
  10.6 2.5 %collective-permute-start.4 = (bf16[32,4352]{1,0:T(8,128)(2,1)S(1)}, bf16[32,4352]{1,0:T(8,128)(2,1)S(1)}, u32[]{:S(2)}, u32[]{:S(2)}) collective-permute-start(bf16[32,4352]{1,0:T(8,128)(2,1)S(1)} %get-tuple-element.46), channel_id=1, source_target_pairs={{0,24},{8,16},{16,8},{24,0},{1,25},{9,17},{17,9},{25,1},{2,26},{10... | collective-permute-start | bytes 835592 | tf_op jit(solution)/shard_map/arrive/ppermute | solution.py:34
  13.1 0.5 collective-permute-start.5
  13.6 0.5 collective-permute-start.6
  14.1 6.3 %collective-permute-done.2 = bf16[2,16,4224]{2,1,0:T(8,128)(2,1)S(1)} collective-permute-done((bf16[2,16,4224]{2,1,0:T(8,128)(2,1)S(1)}, bf16[2,16,4224]{2,1,0:T(8,128)(2,1)S(1)}, u32[]{:S(2)}, u32[]{:S(2)}) %collective-permute-start.2) | collective-permute-done | bytes 270368 | tf_op jit(solution)/shard_map/dispatch/ppermute | solution.py:34
  20.8 3.8 %collective-permute-start.7 = (bf16[2,16,4224]{2,1,0:T(8,128)(2,1)S(1)}, bf16[2,16,4224]{2,1,0:T(8,128)(2,1)S(1)}, u32[]{:S(2)}, u32[]{:S(2)}) collective-permute-start(bf16[2,16,4224]{2,1,0:T(8,128)(2,1)S(1)} %dispatch.3), channel_id=1, source_target_pairs={{0,6},{1,7},{2,4},{3,5},{4,2},{5,3},{6,0},{7,1},{8,14},{9,15},{10,... | collective-permute-start | bytes 811016 | tf_op jit(solution)/shard_map/dispatch/ppermute | solution.py:34
  24.6 1.3 %collective-permute-done.5.refs_4_.refs_2_ = bf16[32,4352]{1,0:T(8,128)(2,1)S(1)} collective-permute-done((bf16[32,4352]{1,0:T(8,128)(2,1)S(1)}, bf16[32,4352]{1,0:T(8,128)(2,1)S(1)}, u32[]{:S(2)}, u32[]{:S(2)}) %collective-permute-start.5) | collective-permute-done | bytes 278560 | tf_op jit(solution)/shard_map/arrive/ppermute | solution.py:34
  26.0 0.6 %arrive.4 = (bf16[64,4224]{1,0:T(8,128)(2,1)S(1)}, bf16[64,256]{1,0:T(8,128)(2,1)S(1)}, bf16[64,1280]{1,0:T(8,128)(2,1)S(1)}, bf16[64,1280]{1,0:T(8,128)(2,1)S(1...) custom-call(bf16[2,4096,128]{2,1,0:T(8,128)(2,1)S(1)} %copy-done, ...), custom_call_target="tpu_custom_call" | custom-call | flops 134217728 | bytes 1048576 | tf_op jit(solution)/shard_map/arrive/pallas_call | solution.py:372
  26.6 1.7 %collective-permute-start.8 = (bf16[64,1280]{1,0:T(8,128)(2,1)S(1)}, bf16[64,1280]{1,0:T(8,128)(2,1)S(1)}, u32[]{:S(2)}, u32[]{:S(2)}) collective-permute-start(bf16[64,1280]{1,0:T(8,128)(2,1)S(1)} %get-tuple-element.57), channel_id=1, source_target_pairs={{0,24},{8,16},{16,8},{24,0},{1,25},{9,17},{17,9},{25,1},{2,26},{10... | collective-permute-start | bytes 491528 | tf_op jit(solution)/shard_map/arrive/ppermute | solution.py:34
  28.3 1.3 %collective-permute-start.9 = (bf16[64,1280]{1,0:T(8,128)(2,1)S(1)}, bf16[64,1280]{1,0:T(8,128)(2,1)S(1)}, u32[]{:S(2)}, u32[]{:S(2)}) collective-permute-start(bf16[64,1280]{1,0:T(8,128)(2,1)S(1)} %get-tuple-element.58), channel_id=1, source_target_pairs={{0,16},{8,24},{16,0},{24,8},{1,17},{9,25},{17,1},{25,9},{2,18},{10... | collective-permute-start | bytes 491528 | tf_op jit(solution)/shard_map/arrive/ppermute | solution.py:34
  29.6 0.5 collective-permute-start.10
  30.2 1.3 %collective-permute-done.7.refs_0_ = bf16[2,16,4224]{2,1,0:T(8,128)(2,1)S(1)} collective-permute-done((bf16[2,16,4224]{2,1,0:T(8,128)(2,1)S(1)}, bf16[2,16,4224]{2,1,0:T(8,128)(2,1)S(1)}, u32[]{:S(2)}, u32[]{:S(2)}) %collective-permute-start.7) | collective-permute-done | bytes 270368 | tf_op jit(solution)/shard_map/dispatch/ppermute | solution.py:34
  31.9 2.6 %collective-permute-start.11 = (bf16[32,1280]{1,0:T(8,128)(2,1)S(1)}, bf16[32,1280]{1,0:T(8,128)(2,1)S(1)}, u32[]{:S(2)}, u32[]{:S(2)}) collective-permute-start(bf16[32,1280]{1,0:T(8,128)(2,1)S(1)} %get-tuple-element.61), channel_id=1, source_target_pairs={{0,24},{8,16},{16,8},{24,0},{1,25},{9,17},{17,9},{25,1},{2,26},{10... | collective-permute-start | bytes 245768 | tf_op jit(solution)/shard_map/arrive/ppermute | solution.py:34
  34.5 0.5 collective-permute-start.12
  35.0 1.2 %collective-permute-start.13 = (bf16[32,1280]{1,0:T(8,128)(2,1)S(1)}, bf16[32,1280]{1,0:T(8,128)(2,1)S(1)}, u32[]{:S(2)}, u32[]{:S(2)}) collective-permute-start(bf16[32,1280]{1,0:T(8,128)(2,1)S(1)} %get-tuple-element.63), channel_id=1, source_target_pairs={{0,8},{8,0},{16,24},{24,16},{1,9},{9,1},{17,25},{25,17},{2,10},{10... | collective-permute-start | bytes 245768 | tf_op jit(solution)/shard_map/arrive/ppermute | solution.py:34
  36.2 1.8 %inner.1 = (bf16[128,768]{1,0:T(8,128)(2,1)}, f32[128,128]{1,0:T(8,128)S(1)}) custom-call(bf16[4096,768]{1,0:T(8,128)(2,1)S(1)} %bitcast.12, bf16[256,768]{1,0:T(8,128)(2,1)S(1)} %bitcast.13, bf16[128,768]{1,0:T(8,128)(2,1)S(1)} %bitcast.16, bf16[32,4224]{1,0:T(8,128)(2,1)S(1)} %get-tuple-element.44.refs_0_, bf16[64,4224]{1,0:T(8,128)(2,1)S(1)} %get-tuple-element.49.refs_1_, ...), custom_call_target="tpu_custom_call" | custom-call | flops 805306368 | bytes 6291456 | tf_op jit(solution)/shard_map/inner/pallas_call | solution.py:384
  38.1 1.4 %adapters.3 = (f32[256,1024]{1,0:T(8,128)S(1)}, f32[256,256]{1,0:T(8,128)S(1)}, bf16[128,256]{1,0:T(8,128)(2,1)S(1)}, bf16[128,256]{1,0:T(8,128)(2,1)S(1)}) custom-call(bf16[256,768]{1,0:T(8,128)(2,1)S(1)} %bitcast.14, f32[128,128]{1,0:T(8,128)S(1)} %get-tuple-element.65._.mix, bf16[32,4352]{1,0:T(8,128)(2,1)S(1)} %get-tuple-element.55.refs_0_, ...), custom_call_target="tpu_custom_call" | custom-call | flops 268435456 | bytes 524288 | tf_op jit(solution)/shard_map/adapters/pallas_call | solution.py:395
  39.9 0.7 %collective-permute-done.12.refs_10_.refs_2_ = bf16[32,1280]{1,0:T(8,128)(2,1)S(1)} collective-permute-done((bf16[32,1280]{1,0:T(8,128)(2,1)S(1)}, bf16[32,1280]{1,0:T(8,128)(2,1)S(1)}, u32[]{:S(2)}, u32[]{:S(2)}) %collective-permute-start.12) | collective-permute-done | bytes 81952 | tf_op jit(solution)/shard_map/arrive/ppermute | solution.py:34
  40.7 0.5 adapters.4
  41.3 1.6 %collective-permute-done.14.got = bf16[4,32,1280]{2,1,0:T(8,128)(2,1)S(1)} collective-permute-done((bf16[4,32,1280]{2,1,0:T(8,128)(2,1)S(1)}, bf16[4,32,1280]{2,1,0:T(8,128)(2,1)S(1)}, u32[]{:S(2)}, u32[]{:S(2)}) %collective-permute-start.14) | collective-permute-done | bytes 327712 | tf_op jit(solution)/shard_map/adapters/ppermute | solution.py:34
  43.0 3.3 %collective-permute-start.15 = (bf16[32,1280]{1,0:T(8,128)(2,1)S(1)}, bf16[32,1280]{1,0:T(8,128)(2,1)S(1)}, u32[]{:S(2)}, u32[]{:S(2)}) collective-permute-start(bf16[32,1280]{1,0:T(8,128)(2,1)S(1)} %get-tuple-element.73), channel_id=1, source_target_pairs={{0,4},{1,5},{2,6},{3,7},{4,0},{5,1},{6,2},{7,3},{8,12},{9,13},{10,... | collective-permute-start | bytes 245768 | tf_op jit(solution)/shard_map/adapters/ppermute | solution.py:34
  46.2 2.5 %collective-permute-start.16 = (bf16[32,1280]{1,0:T(8,128)(2,1)S(1)}, bf16[32,1280]{1,0:T(8,128)(2,1)S(1)}, u32[]{:S(2)}, u32[]{:S(2)}) collective-permute-start(bf16[32,1280]{1,0:T(8,128)(2,1)S(1)} %get-tuple-element.74), channel_id=1, source_target_pairs={{0,6},{1,7},{2,4},{3,5},{4,2},{5,3},{6,0},{7,1},{8,14},{9,15},{10,... | collective-permute-start | bytes 245768 | tf_op jit(solution)/shard_map/adapters/ppermute | solution.py:34
  48.7 2.7 %product.1 = f32[1,1024,768]{2,1,0:T(8,128)} custom-call(bf16[32,4352]{1,0:T(8,128)(2,1)S(1)} %get-tuple-element.55.refs_0_, bf16[32,4352]{1,0:T(8,128)(2,1)S(1)} %collective-permute-done.4.refs_3_.refs_1_, bf16[32,4352]{1,0:T(8,128)(2,1)S(1)} %collective-permute-done.5.refs_4_.refs_2_, bf16[32,4352]{1,0:T(8,128)(2,1)S(1)} %collective-permute-done.6.refs_5_.refs_3_, ...), custom_call_target="tpu_custom_call" | custom-call | flops 805306368 | bytes 2097152 | tf_op jit(solution)/shard_map/product/pallas_call | solution.py:422
  51.4 2.3 %collective-permute-done.16.refs_2_ = bf16[32,1280]{1,0:T(8,128)(2,1)S(1)} collective-permute-done((bf16[32,1280]{1,0:T(8,128)(2,1)S(1)}, bf16[32,1280]{1,0:T(8,128)(2,1)S(1)}, u32[]{:S(2)}, u32[]{:S(2)}) %collective-permute-start.16) | collective-permute-done | bytes 81952 | tf_op jit(solution)/shard_map/adapters/ppermute | solution.py:34
  53.7 0.5 collective-permute-done.17.refs_3_
  54.2 0.8 %final.1 = (f32[2,16,1024]{2,1,0:T(8,128)}, f32[2,16,192]{2,1,0:T(8,128)}, f32[8,128]{1,0:T(8,128)}) custom-call(f32[8,128]{1,0:T(8,128)S(1)} %add_bitcast_fusion.small, bf16[128,128]{1,0:T(8,128)(2,1)S(1)} %get-tuple-element.64.picks, bf16[32,1280]{1,0:T(8,128)(2,1)S(1)} %get-tuple-element.72.refs_0_, bf16[32,1280]{1,0:T(8,128)(2,1)S(1)} %collective-permute-done.15.refs_1_, ...), custom_call_target="tpu_custom_call" | custom-call | bytes 1000000 | tf_op jit(solution)/shard_map/final/pallas_call | solution.py:431
  (30 shorter events, 2.0 us)
Async XLA Ops:
  0.6 8.5 %copy-start = (bf16[2,4096,128]{2,1,0:T(8,128)(2,1)S(1)}, bf16[2,4096,128]{2,1,0:T(8,128)(2,1)}, u32[]{:S(2)}) copy-start(bf16[2,4096,128]{2,1,0:T(8,128)(2,1)} %adapter_out.5) | copy-start | bytes 6291460
  1.5 1.2 %copy-start.3 = (bf16[128,4096]{1,0:T(8,128)(2,1)S(1)}, bf16[128,4096]{1,0:T(8,128)(2,1)}, u32[]{:S(2)}) copy-start(bf16[128,4096]{1,0:T(8,128)(2,1)} %cot.1) | copy-start | bytes 3145732
  3.3 4.2 %collective-permute-start = (bf16[3,16,4224]{2,1,0:T(8,128)(2,1)S(1)}, bf16[3,16,4224]{2,1,0:T(8,128)(2,1)S(1)}, u32[]{:S(2)}, u32[]{:S(2)}) collective-permute-start(bf16[3,16,4224]{2,1,0:T(8,128)(2,1)S(1)} %get-tuple-element.43), channel_id=1, source_target_pairs={{0,1},{1,0},{2,3},{3,2},{4,5},{5,4},{6,7},{7,6},{8,9},{9,8},{10,11... | collective-permute-start | bytes 1216520 | tf_op jit(solution)/shard_map/route/ppermute | solution.py:34
  3.8 16.6 %collective-permute-start.2 = (bf16[2,16,4224]{2,1,0:T(8,128)(2,1)S(1)}, bf16[2,16,4224]{2,1,0:T(8,128)(2,1)S(1)}, u32[]{:S(2)}, u32[]{:S(2)}) collective-permute-start(bf16[2,16,4224]{2,1,0:T(8,128)(2,1)S(1)} %get-tuple-element.45), channel_id=1, source_target_pairs={{0,4},{1,5},{2,6},{3,7},{4,0},{5,1},{6,2},{7,3},{8,12},{9,13},{10,... | collective-permute-start | bytes 811016 | tf_op jit(solution)/shard_map/dispatch/ppermute | solution.py:34
  7.5 13.2 %collective-permute-start.1 = (bf16[2,16,4224]{2,1,0:T(8,128)(2,1)S(1)}, bf16[2,16,4224]{2,1,0:T(8,128)(2,1)S(1)}, u32[]{:S(2)}, u32[]{:S(2)}) collective-permute-start(bf16[2,16,4224]{2,1,0:T(8,128)(2,1)S(1)} %dispatch.2), channel_id=1, source_target_pairs={{0,2},{1,3},{2,0},{3,1},{4,6},{5,7},{6,4},{7,5},{8,10},{9,11},{10,... | collective-permute-start | bytes 811016 | tf_op jit(solution)/shard_map/dispatch/ppermute | solution.py:34
  9.1 0.9 %copy-start.4 = (bf16[1,1,128,768]{3,2,1,0:T(8,128)(2,1)S(1)}, bf16[1,1,128,768]{3,2,1,0:T(8,128)(2,1)}, u32[]{:S(2)}) copy-start(bf16[1,1,128,768]{3,2,1,0:T(8,128)(2,1)} %param.9) | copy-start | bytes 589828
  10.6 14.1 %collective-permute-start.4 = (bf16[32,4352]{1,0:T(8,128)(2,1)S(1)}, bf16[32,4352]{1,0:T(8,128)(2,1)S(1)}, u32[]{:S(2)}, u32[]{:S(2)}) collective-permute-start(bf16[32,4352]{1,0:T(8,128)(2,1)S(1)} %get-tuple-element.46), channel_id=1, source_target_pairs={{0,24},{8,16},{16,8},{24,0},{1,25},{9,17},{17,9},{25,1},{2,26},{10... | collective-permute-start | bytes 835592 | tf_op jit(solution)/shard_map/arrive/ppermute | solution.py:34
  13.1 12.9 %collective-permute-start.5 = (bf16[32,4352]{1,0:T(8,128)(2,1)S(1)}, bf16[32,4352]{1,0:T(8,128)(2,1)S(1)}, u32[]{:S(2)}, u32[]{:S(2)}) collective-permute-start(bf16[32,4352]{1,0:T(8,128)(2,1)S(1)} %get-tuple-element.47), channel_id=1, source_target_pairs={{0,16},{8,24},{16,0},{24,8},{1,17},{9,25},{17,1},{25,9},{2,18},{10... | collective-permute-start | bytes 835592 | tf_op jit(solution)/shard_map/arrive/ppermute | solution.py:34
  13.6 12.5 %collective-permute-start.6 = (bf16[32,4352]{1,0:T(8,128)(2,1)S(1)}, bf16[32,4352]{1,0:T(8,128)(2,1)S(1)}, u32[]{:S(2)}, u32[]{:S(2)}) collective-permute-start(bf16[32,4352]{1,0:T(8,128)(2,1)S(1)} %get-tuple-element.48), channel_id=1, source_target_pairs={{0,8},{8,0},{16,24},{24,16},{1,9},{9,1},{17,25},{25,17},{2,10},{10... | collective-permute-start | bytes 835592 | tf_op jit(solution)/shard_map/arrive/ppermute | solution.py:34
  20.5 4.1 %collective-permute-start.3 = (bf16[16,4224]{1,0:T(8,128)(2,1)S(1)}, bf16[16,4224]{1,0:T(8,128)(2,1)S(1)}, u32[]{:S(2)}, u32[]{:S(2)}) collective-permute-start(bf16[16,4224]{1,0:T(8,128)(2,1)S(1)} %get-tuple-element.79), channel_id=1, source_target_pairs={{0,1},{1,0},{2,3},{3,2},{4,5},{5,4},{6,7},{7,6},{8,9},{9,8},{10,11... | collective-permute-start | bytes 405512 | tf_op jit(solution)/shard_map/dispatch/ppermute | solution.py:34
  20.7 15.4 %copy-start.1 = (bf16[1,4096,768]{2,1,0:T(8,128)(2,1)S(1)}, bf16[1,4096,768]{2,1,0:T(8,128)(2,1)}, u32[]{:S(2)}) copy-start(bf16[1,4096,768]{2,1,0:T(8,128)(2,1)} %param.10) | copy-start | bytes 18874372
  20.8 15.4 %copy-start.2 = (bf16[2,128,768]{2,1,0:T(8,128)(2,1)S(1)}, bf16[2,128,768]{2,1,0:T(8,128)(2,1)}, u32[]{:S(2)}) copy-start(bf16[2,128,768]{2,1,0:T(8,128)(2,1)} %param.11) | copy-start | bytes 1179652
  20.8 15.4 %copy-start.5 = (bf16[1,1,128,768]{3,2,1,0:T(8,128)(2,1)S(1)}, bf16[1,1,128,768]{3,2,1,0:T(8,128)(2,1)}, u32[]{:S(2)}) copy-start(bf16[1,1,128,768]{3,2,1,0:T(8,128)(2,1)} %param.9) | copy-start | bytes 589828
  20.8 10.7 %collective-permute-start.7 = (bf16[2,16,4224]{2,1,0:T(8,128)(2,1)S(1)}, bf16[2,16,4224]{2,1,0:T(8,128)(2,1)S(1)}, u32[]{:S(2)}, u32[]{:S(2)}) collective-permute-start(bf16[2,16,4224]{2,1,0:T(8,128)(2,1)S(1)} %dispatch.3), channel_id=1, source_target_pairs={{0,6},{1,7},{2,4},{3,5},{4,2},{5,3},{6,0},{7,1},{8,14},{9,15},{10,... | collective-permute-start | bytes 811016 | tf_op jit(solution)/shard_map/dispatch/ppermute | solution.py:34
  26.6 8.4 %collective-permute-start.8 = (bf16[64,1280]{1,0:T(8,128)(2,1)S(1)}, bf16[64,1280]{1,0:T(8,128)(2,1)S(1)}, u32[]{:S(2)}, u32[]{:S(2)}) collective-permute-start(bf16[64,1280]{1,0:T(8,128)(2,1)S(1)} %get-tuple-element.57), channel_id=1, source_target_pairs={{0,24},{8,16},{16,8},{24,0},{1,25},{9,17},{17,9},{25,1},{2,26},{10... | collective-permute-start | bytes 491528 | tf_op jit(solution)/shard_map/arrive/ppermute | solution.py:34
  28.3 9.8 %collective-permute-start.9 = (bf16[64,1280]{1,0:T(8,128)(2,1)S(1)}, bf16[64,1280]{1,0:T(8,128)(2,1)S(1)}, u32[]{:S(2)}, u32[]{:S(2)}) collective-permute-start(bf16[64,1280]{1,0:T(8,128)(2,1)S(1)} %get-tuple-element.58), channel_id=1, source_target_pairs={{0,16},{8,24},{16,0},{24,8},{1,17},{9,25},{17,1},{25,9},{2,18},{10... | collective-permute-start | bytes 491528 | tf_op jit(solution)/shard_map/arrive/ppermute | solution.py:34
  29.6 8.5 %collective-permute-start.10 = (bf16[64,1280]{1,0:T(8,128)(2,1)S(1)}, bf16[64,1280]{1,0:T(8,128)(2,1)S(1)}, u32[]{:S(2)}, u32[]{:S(2)}) collective-permute-start(bf16[64,1280]{1,0:T(8,128)(2,1)S(1)} %get-tuple-element.59), channel_id=1, source_target_pairs={{0,8},{8,0},{16,24},{24,16},{1,9},{9,1},{17,25},{25,17},{2,10},{10... | collective-permute-start | bytes 491528 | tf_op jit(solution)/shard_map/arrive/ppermute | solution.py:34
  31.9 7.9 %collective-permute-start.11 = (bf16[32,1280]{1,0:T(8,128)(2,1)S(1)}, bf16[32,1280]{1,0:T(8,128)(2,1)S(1)}, u32[]{:S(2)}, u32[]{:S(2)}) collective-permute-start(bf16[32,1280]{1,0:T(8,128)(2,1)S(1)} %get-tuple-element.61), channel_id=1, source_target_pairs={{0,24},{8,16},{16,8},{24,0},{1,25},{9,17},{17,9},{25,1},{2,26},{10... | collective-permute-start | bytes 245768 | tf_op jit(solution)/shard_map/arrive/ppermute | solution.py:34
  34.5 6.1 %collective-permute-start.12 = (bf16[32,1280]{1,0:T(8,128)(2,1)S(1)}, bf16[32,1280]{1,0:T(8,128)(2,1)S(1)}, u32[]{:S(2)}, u32[]{:S(2)}) collective-permute-start(bf16[32,1280]{1,0:T(8,128)(2,1)S(1)} %get-tuple-element.62), channel_id=1, source_target_pairs={{0,16},{8,24},{16,0},{24,8},{1,17},{9,25},{17,1},{25,9},{2,18},{10... | collective-permute-start | bytes 245768 | tf_op jit(solution)/shard_map/arrive/ppermute | solution.py:34
  35.0 5.7 %collective-permute-start.13 = (bf16[32,1280]{1,0:T(8,128)(2,1)S(1)}, bf16[32,1280]{1,0:T(8,128)(2,1)S(1)}, u32[]{:S(2)}, u32[]{:S(2)}) collective-permute-start(bf16[32,1280]{1,0:T(8,128)(2,1)S(1)} %get-tuple-element.63), channel_id=1, source_target_pairs={{0,8},{8,0},{16,24},{24,16},{1,9},{9,1},{17,25},{25,17},{2,10},{10... | collective-permute-start | bytes 245768 | tf_op jit(solution)/shard_map/arrive/ppermute | solution.py:34
  41.2 1.7 %collective-permute-start.14 = (bf16[4,32,1280]{2,1,0:T(8,128)(2,1)S(1)}, bf16[4,32,1280]{2,1,0:T(8,128)(2,1)S(1)}, u32[]{:S(2)}, u32[]{:S(2)}) collective-permute-start(bf16[4,32,1280]{2,1,0:T(8,128)(2,1)S(1)} %get-tuple-element.71), channel_id=1, source_target_pairs={{0,1},{1,0},{2,3},{3,2},{4,5},{5,4},{6,7},{7,6},{8,9},{9,8},{10,11... | collective-permute-start | bytes 983048 | tf_op jit(solution)/shard_map/adapters/ppermute | solution.py:34
  43.0 8.4 %collective-permute-start.15 = (bf16[32,1280]{1,0:T(8,128)(2,1)S(1)}, bf16[32,1280]{1,0:T(8,128)(2,1)S(1)}, u32[]{:S(2)}, u32[]{:S(2)}) collective-permute-start(bf16[32,1280]{1,0:T(8,128)(2,1)S(1)} %get-tuple-element.73), channel_id=1, source_target_pairs={{0,4},{1,5},{2,6},{3,7},{4,0},{5,1},{6,2},{7,3},{8,12},{9,13},{10,... | collective-permute-start | bytes 245768 | tf_op jit(solution)/shard_map/adapters/ppermute | solution.py:34
  46.2 7.4 %collective-permute-start.16 = (bf16[32,1280]{1,0:T(8,128)(2,1)S(1)}, bf16[32,1280]{1,0:T(8,128)(2,1)S(1)}, u32[]{:S(2)}, u32[]{:S(2)}) collective-permute-start(bf16[32,1280]{1,0:T(8,128)(2,1)S(1)} %get-tuple-element.74), channel_id=1, source_target_pairs={{0,6},{1,7},{2,4},{3,5},{4,2},{5,3},{6,0},{7,1},{8,14},{9,15},{10,... | collective-permute-start | bytes 245768 | tf_op jit(solution)/shard_map/adapters/ppermute | solution.py:34
  48.7 5.5 %collective-permute-start.17 = (bf16[32,1280]{1,0:T(8,128)(2,1)S(1)}, bf16[32,1280]{1,0:T(8,128)(2,1)S(1)}, u32[]{:S(2)}, u32[]{:S(2)}) collective-permute-start(bf16[32,1280]{1,0:T(8,128)(2,1)S(1)} %get-tuple-element.75), channel_id=1, source_target_pairs={{0,2},{1,3},{2,0},{3,1},{4,6},{5,7},{6,4},{7,5},{8,10},{9,11},{10,... | collective-permute-start | bytes 245768 | tf_op jit(solution)/shard_map/adapters/ppermute | solution.py:34

commit v9 on v8

--- a/solution.py
+++ b/solution.py
@@ -77,7 +77,16 @@
         give[middle:, :, at] = rows[chips + middle + 1 :]
 
 
-def route_body(chips, cap, loops, small, cot, keep, lead, give, picks, mixed):
+def route_body(chips, cap, loops, small, cot_h, keep, lead, give, picks, cot, mixed, sems):
+    step = cot.shape[1] // sems.shape[0]
+    columns = [
+        pltpu.make_async_copy(
+            cot_h.at[:, pl.ds(n, step)], cot.at[:, pl.ds(n, step)], sems.at[n // step]
+        )
+        for n in range(0, cot.shape[1], step)
+    ]
+    for column in columns:
+        column.start()
     middle = chips // 2
     experts = 2 * chips
     ways = small.shape[0]
@@ -105,8 +114,8 @@
     loop_rows = jnp.where(loop_rows == loop, 1.0, 0.0).astype(bf16)
     mix = nt(mixed[...], loop_rows).astype(bf16)
     deal_rows(middle, mix.reshape(2 * chips, cap, LANES), slice(width, width + LANES), keep, lead, give)
-    step = 1024 if width % 1024 == 0 else width
     for n in range(0, width, step):
+        columns[n // step].wait()
         at = slice(n, n + step)
         got = nn(picks[...], cot[:, at]).astype(bf16)
         deal_rows(middle, got.reshape(2 * chips, cap, step), at, keep, lead, give)
@@ -343,8 +352,13 @@
                 shape((chips - 1,) + packed.shape[1:], bf16),
                 shape((slots, toks), bf16),
             ),
-            (V, V),
-            scratch=(pltpu.VMEM((slots, toks), bf16),),
+            (V, pltpu.HBM),
+            scratch=(
+                pltpu.VMEM((toks, width), bf16),
+                pltpu.VMEM((slots, toks), bf16),
+                pltpu.SemaphoreType.DMA((2,)),
+            ),
+            limit=52,
             flops=2 * slots * toks * width,
             nbytes=6 * toks * width,
         )(small, cotangent)

time: 55.2 us -> 55 us (level)
  local copies, waits for them, and re-layouts: 2.19 us -> 0.97 us
  Pallas kernels: 9.36 us -> 10.5 us
    unnamed x12 -> x10, local copies, waits for them, and re-layouts: 2.17 us -> 0.95 us
    pallas_call x1, Pallas kernels: 0.56 us -> 1.66 us  [on_device(): call(functools.partial(route_body, chips, cap, loops), (packed, shape((2,...]
where the time goes in v9:
time: 55 us; the launch traced here: 54.9 us
  starting transfers between devices  26.9 us (49%)
  waiting for transfers between devices  14.9 us (27%)
  Pallas kernels  10.5 us (19%)
  local copies, waits for them, and re-layouts  0.97 us (2%)
  other arithmetic  0.85 us (2%)
  between operations  0.76 us (1%)
    ppermute x18, starting transfers between devices, swap(): return lax.ppermute(x, axis, [(i, i ^ mask) for i in range(size)])  26.9 us
    ppermute x18, waiting for transfers between devices, swap(): return lax.ppermute(x, axis, [(i, i ^ mask) for i in range(size)])  14.9 us
    pallas_call x1, Pallas kernels, on_device(): call(functools.partial(product_body, groups, chips), shape((1, part, hid_...  2.67 us
    pallas_call x1, Pallas kernels, on_device(): call(functools.partial(inner_body, chips, cap, len(chunks)), (shape((slot...  1.85 us
    pallas_call x1, Pallas kernels, on_device(): call(functools.partial(route_body, chips, cap, loops), (packed, shape((2,...  1.66 us
    pallas_call x3, Pallas kernels, on_device(): call(functools.partial(arrive_body, groups, chips, cap, own, len(before))...  1.48 us
    pallas_call x1, Pallas kernels, on_device(): call(functools.partial(adapter_first_body, loops, chips, cols, groups), s...  1.45 us
  transfers between devices with their start and end apart: 18, of which 12 were waited for; matrix products, arithmetic and copies ran while one was open for 0% of the time, Pallas kernels for 14%

profile of v9, /device:TPU:0, one launch (start us, length us, event | category | flops | bytes accessed | tf_op | source)
XLA Modules:
  0.0 54.9 jit_solution(17978989910501893505)
XLA Ops:
  0.6 0.9 %add_bitcast_fusion.small = f32[8,128]{1,0:T(8,128)S(1)} fusion(bf16[128,8]{0,1:T(8,128)(2,1)} %param.13, s32[128,8]{0,1:T(8,128)} %param.14, s32[128]{0:T(128)} %param.15), kind=kLoop, calls=%fused_computation.2 | loop fusion | flops 6144 | bytes 10752 | tf_op jit(solution)/shard_map/add | solution.py:340
  1.5 1.7 %route.1 = (bf16[4,16,4224]{2,1,0:T(8,128)(2,1)S(1)}, bf16[2,16,4224]{2,1,0:T(8,128)(2,1)S(1)}, bf16[3,16,4224]{2,1,0:T(8,128)(2,1)S(1)}, bf16[128,128]{1,0:T(8,128)(2,1)S(1)}) custom-call(f32[8,128]{1,0:T(8,128)S(1)} %add_bitcast_fusion.small, bf16[128,4096]{1,0:T(8,128)(2,1)} %cot_h.1), custom_call_target="tpu_custom_call" | custom-call | flops 134217728 | bytes 3145728 | tf_op jit(solution)/shard_map/route/pallas_call | solution.py:347
  3.2 0.5 collective-permute-start
  3.7 3.6 %collective-permute-start.2 = (bf16[2,16,4224]{2,1,0:T(8,128)(2,1)S(1)}, bf16[2,16,4224]{2,1,0:T(8,128)(2,1)S(1)}, u32[]{:S(2)}, u32[]{:S(2)}) collective-permute-start(bf16[2,16,4224]{2,1,0:T(8,128)(2,1)S(1)} %get-tuple-element.45), channel_id=1, source_target_pairs={{0,4},{1,5},{2,6},{3,7},{4,0},{5,1},{6,2},{7,3},{8,12},{9,13},{10,... | collective-permute-start | bytes 811016 | tf_op jit(solution)/shard_map/dispatch/ppermute | solution.py:34
  7.4 1.6 %collective-permute-start.1 = (bf16[2,16,4224]{2,1,0:T(8,128)(2,1)S(1)}, bf16[2,16,4224]{2,1,0:T(8,128)(2,1)S(1)}, u32[]{:S(2)}, u32[]{:S(2)}) collective-permute-start(bf16[2,16,4224]{2,1,0:T(8,128)(2,1)S(1)} %dispatch.2), channel_id=1, source_target_pairs={{0,2},{1,3},{2,0},{3,1},{4,6},{5,7},{6,4},{7,5},{8,10},{9,11},{10,... | collective-permute-start | bytes 811016 | tf_op jit(solution)/shard_map/dispatch/ppermute | solution.py:34
  9.0 0.9 %copy-done.3 = bf16[1,1,128,768]{3,2,1,0:T(8,128)(2,1)S(1)} copy-done((bf16[1,1,128,768]{3,2,1,0:T(8,128)(2,1)S(1)}, bf16[1,1,128,768]{3,2,1,0:T(8,128)(2,1)}, u32[]{:S(2)}) %copy-start.3) | copy-done | bytes 196632
  9.9 0.5 arrive.3
  10.4 2.5 %collective-permute-start.4 = (bf16[32,4352]{1,0:T(8,128)(2,1)S(1)}, bf16[32,4352]{1,0:T(8,128)(2,1)S(1)}, u32[]{:S(2)}, u32[]{:S(2)}) collective-permute-start(bf16[32,4352]{1,0:T(8,128)(2,1)S(1)} %get-tuple-element.46), channel_id=1, source_target_pairs={{0,24},{8,16},{16,8},{24,0},{1,25},{9,17},{17,9},{25,1},{2,26},{10... | collective-permute-start | bytes 835592 | tf_op jit(solution)/shard_map/arrive/ppermute | solution.py:34
  12.9 0.5 collective-permute-start.5
  13.5 0.5 collective-permute-start.6
  14.0 6.3 %collective-permute-done.2 = bf16[2,16,4224]{2,1,0:T(8,128)(2,1)S(1)} collective-permute-done((bf16[2,16,4224]{2,1,0:T(8,128)(2,1)S(1)}, bf16[2,16,4224]{2,1,0:T(8,128)(2,1)S(1)}, u32[]{:S(2)}, u32[]{:S(2)}) %collective-permute-start.2) | collective-permute-done | bytes 270368 | tf_op jit(solution)/shard_map/dispatch/ppermute | solution.py:34
  20.6 3.8 %collective-permute-start.7 = (bf16[2,16,4224]{2,1,0:T(8,128)(2,1)S(1)}, bf16[2,16,4224]{2,1,0:T(8,128)(2,1)S(1)}, u32[]{:S(2)}, u32[]{:S(2)}) collective-permute-start(bf16[2,16,4224]{2,1,0:T(8,128)(2,1)S(1)} %dispatch.3), channel_id=1, source_target_pairs={{0,6},{1,7},{2,4},{3,5},{4,2},{5,3},{6,0},{7,1},{8,14},{9,15},{10,... | collective-permute-start | bytes 811016 | tf_op jit(solution)/shard_map/dispatch/ppermute | solution.py:34
  24.5 1.3 %collective-permute-done.5.refs_4_.refs_2_ = bf16[32,4352]{1,0:T(8,128)(2,1)S(1)} collective-permute-done((bf16[32,4352]{1,0:T(8,128)(2,1)S(1)}, bf16[32,4352]{1,0:T(8,128)(2,1)S(1)}, u32[]{:S(2)}, u32[]{:S(2)}) %collective-permute-start.5) | collective-permute-done | bytes 278560 | tf_op jit(solution)/shard_map/arrive/ppermute | solution.py:34
  25.9 0.5 arrive.4
  26.5 1.7 %collective-permute-start.8 = (bf16[64,1280]{1,0:T(8,128)(2,1)S(1)}, bf16[64,1280]{1,0:T(8,128)(2,1)S(1)}, u32[]{:S(2)}, u32[]{:S(2)}) collective-permute-start(bf16[64,1280]{1,0:T(8,128)(2,1)S(1)} %get-tuple-element.57), channel_id=1, source_target_pairs={{0,24},{8,16},{16,8},{24,0},{1,25},{9,17},{17,9},{25,1},{2,26},{10... | collective-permute-start | bytes 491528 | tf_op jit(solution)/shard_map/arrive/ppermute | solution.py:34
  28.2 1.3 %collective-permute-start.9 = (bf16[64,1280]{1,0:T(8,128)(2,1)S(1)}, bf16[64,1280]{1,0:T(8,128)(2,1)S(1)}, u32[]{:S(2)}, u32[]{:S(2)}) collective-permute-start(bf16[64,1280]{1,0:T(8,128)(2,1)S(1)} %get-tuple-element.58), channel_id=1, source_target_pairs={{0,16},{8,24},{16,0},{24,8},{1,17},{9,25},{17,1},{25,9},{2,18},{10... | collective-permute-start | bytes 491528 | tf_op jit(solution)/shard_map/arrive/ppermute | solution.py:34
  29.5 0.5 collective-permute-start.10
  30.0 1.3 %collective-permute-done.7.refs_0_ = bf16[2,16,4224]{2,1,0:T(8,128)(2,1)S(1)} collective-permute-done((bf16[2,16,4224]{2,1,0:T(8,128)(2,1)S(1)}, bf16[2,16,4224]{2,1,0:T(8,128)(2,1)S(1)}, u32[]{:S(2)}, u32[]{:S(2)}) %collective-permute-start.7) | collective-permute-done | bytes 270368 | tf_op jit(solution)/shard_map/dispatch/ppermute | solution.py:34
  31.8 2.6 %collective-permute-start.11 = (bf16[32,1280]{1,0:T(8,128)(2,1)S(1)}, bf16[32,1280]{1,0:T(8,128)(2,1)S(1)}, u32[]{:S(2)}, u32[]{:S(2)}) collective-permute-start(bf16[32,1280]{1,0:T(8,128)(2,1)S(1)} %get-tuple-element.61), channel_id=1, source_target_pairs={{0,24},{8,16},{16,8},{24,0},{1,25},{9,17},{17,9},{25,1},{2,26},{10... | collective-permute-start | bytes 245768 | tf_op jit(solution)/shard_map/arrive/ppermute | solution.py:34
  34.4 0.5 collective-permute-start.12
  34.9 1.2 %collective-permute-start.13 = (bf16[32,1280]{1,0:T(8,128)(2,1)S(1)}, bf16[32,1280]{1,0:T(8,128)(2,1)S(1)}, u32[]{:S(2)}, u32[]{:S(2)}) collective-permute-start(bf16[32,1280]{1,0:T(8,128)(2,1)S(1)} %get-tuple-element.63), channel_id=1, source_target_pairs={{0,8},{8,0},{16,24},{24,16},{1,9},{9,1},{17,25},{25,17},{2,10},{10... | collective-permute-start | bytes 245768 | tf_op jit(solution)/shard_map/arrive/ppermute | solution.py:34
  36.1 1.8 %inner.1 = (bf16[128,768]{1,0:T(8,128)(2,1)}, f32[128,128]{1,0:T(8,128)S(1)}) custom-call(bf16[4096,768]{1,0:T(8,128)(2,1)S(1)} %bitcast.12, bf16[256,768]{1,0:T(8,128)(2,1)S(1)} %bitcast.13, bf16[128,768]{1,0:T(8,128)(2,1)S(1)} %bitcast.16, bf16[32,4224]{1,0:T(8,128)(2,1)S(1)} %get-tuple-element.44.refs_0_, bf16[64,4224]{1,0:T(8,128)(2,1)S(1)} %get-tuple-element.49.refs_1_, ...), custom_call_target="tpu_custom_call" | custom-call | flops 805306368 | bytes 6291456 | tf_op jit(solution)/shard_map/inner/pallas_call | solution.py:398
  38.0 1.5 %adapters.3 = (f32[256,1024]{1,0:T(8,128)S(1)}, f32[256,256]{1,0:T(8,128)S(1)}, bf16[128,256]{1,0:T(8,128)(2,1)S(1)}, bf16[128,256]{1,0:T(8,128)(2,1)S(1)}) custom-call(bf16[256,768]{1,0:T(8,128)(2,1)S(1)} %bitcast.14, f32[128,128]{1,0:T(8,128)S(1)} %get-tuple-element.65._.mix, bf16[32,4352]{1,0:T(8,128)(2,1)S(1)} %get-tuple-element.55.refs_0_, ...), custom_call_target="tpu_custom_call" | custom-call | flops 268435456 | bytes 524288 | tf_op jit(solution)/shard_map/adapters/pallas_call | solution.py:409
  39.8 0.7 %collective-permute-done.12.refs_10_.refs_2_ = bf16[32,1280]{1,0:T(8,128)(2,1)S(1)} collective-permute-done((bf16[32,1280]{1,0:T(8,128)(2,1)S(1)}, bf16[32,1280]{1,0:T(8,128)(2,1)S(1)}, u32[]{:S(2)}, u32[]{:S(2)}) %collective-permute-start.12) | collective-permute-done | bytes 81952 | tf_op jit(solution)/shard_map/arrive/ppermute | solution.py:34
  40.6 0.5 adapters.4
  41.2 1.6 %collective-permute-done.14.got = bf16[4,32,1280]{2,1,0:T(8,128)(2,1)S(1)} collective-permute-done((bf16[4,32,1280]{2,1,0:T(8,128)(2,1)S(1)}, bf16[4,32,1280]{2,1,0:T(8,128)(2,1)S(1)}, u32[]{:S(2)}, u32[]{:S(2)}) %collective-permute-start.14) | collective-permute-done | bytes 327712 | tf_op jit(solution)/shard_map/adapters/ppermute | solution.py:34
  42.8 3.3 %collective-permute-start.15 = (bf16[32,1280]{1,0:T(8,128)(2,1)S(1)}, bf16[32,1280]{1,0:T(8,128)(2,1)S(1)}, u32[]{:S(2)}, u32[]{:S(2)}) collective-permute-start(bf16[32,1280]{1,0:T(8,128)(2,1)S(1)} %get-tuple-element.73), channel_id=1, source_target_pairs={{0,4},{1,5},{2,6},{3,7},{4,0},{5,1},{6,2},{7,3},{8,12},{9,13},{10,... | collective-permute-start | bytes 245768 | tf_op jit(solution)/shard_map/adapters/ppermute | solution.py:34
  46.1 2.5 %collective-permute-start.16 = (bf16[32,1280]{1,0:T(8,128)(2,1)S(1)}, bf16[32,1280]{1,0:T(8,128)(2,1)S(1)}, u32[]{:S(2)}, u32[]{:S(2)}) collective-permute-start(bf16[32,1280]{1,0:T(8,128)(2,1)S(1)} %get-tuple-element.74), channel_id=1, source_target_pairs={{0,6},{1,7},{2,4},{3,5},{4,2},{5,3},{6,0},{7,1},{8,14},{9,15},{10,... | collective-permute-start | bytes 245768 | tf_op jit(solution)/shard_map/adapters/ppermute | solution.py:34
  48.6 2.7 %product.1 = f32[1,1024,768]{2,1,0:T(8,128)} custom-call(bf16[32,4352]{1,0:T(8,128)(2,1)S(1)} %get-tuple-element.55.refs_0_, bf16[32,4352]{1,0:T(8,128)(2,1)S(1)} %collective-permute-done.4.refs_3_.refs_1_, bf16[32,4352]{1,0:T(8,128)(2,1)S(1)} %collective-permute-done.5.refs_4_.refs_2_, bf16[32,4352]{1,0:T(8,128)(2,1)S(1)} %collective-permute-done.6.refs_5_.refs_3_, ...), custom_call_target="tpu_custom_call" | custom-call | flops 805306368 | bytes 2097152 | tf_op jit(solution)/shard_map/product/pallas_call | solution.py:436
  51.3 2.3 %collective-permute-done.16.refs_2_ = bf16[32,1280]{1,0:T(8,128)(2,1)S(1)} collective-permute-done((bf16[32,1280]{1,0:T(8,128)(2,1)S(1)}, bf16[32,1280]{1,0:T(8,128)(2,1)S(1)}, u32[]{:S(2)}, u32[]{:S(2)}) %collective-permute-start.16) | collective-permute-done | bytes 81952 | tf_op jit(solution)/shard_map/adapters/ppermute | solution.py:34
  53.6 0.5 collective-permute-done.17.refs_3_
  54.1 0.8 %final.1 = (f32[2,16,1024]{2,1,0:T(8,128)}, f32[2,16,192]{2,1,0:T(8,128)}, f32[8,128]{1,0:T(8,128)}) custom-call(f32[8,128]{1,0:T(8,128)S(1)} %add_bitcast_fusion.small, bf16[128,128]{1,0:T(8,128)(2,1)S(1)} %get-tuple-element.64.picks, bf16[32,1280]{1,0:T(8,128)(2,1)S(1)} %get-tuple-element.72.refs_0_, bf16[32,1280]{1,0:T(8,128)(2,1)S(1)} %collective-permute-done.15.refs_1_, ...), custom_call_target="tpu_custom_call" | custom-call | bytes 1000000 | tf_op jit(solution)/shard_map/final/pallas_call | solution.py:445
  (28 shorter events, 1.5 us)
Async XLA Ops:
  0.6 8.4 %copy-start = (bf16[2,4096,128]{2,1,0:T(8,128)(2,1)S(1)}, bf16[2,4096,128]{2,1,0:T(8,128)(2,1)}, u32[]{:S(2)}) copy-start(bf16[2,4096,128]{2,1,0:T(8,128)(2,1)} %adapter_out.5) | copy-start | bytes 6291460
  3.2 4.2 %collective-permute-start = (bf16[3,16,4224]{2,1,0:T(8,128)(2,1)S(1)}, bf16[3,16,4224]{2,1,0:T(8,128)(2,1)S(1)}, u32[]{:S(2)}, u32[]{:S(2)}) collective-permute-start(bf16[3,16,4224]{2,1,0:T(8,128)(2,1)S(1)} %get-tuple-element.43), channel_id=1, source_target_pairs={{0,1},{1,0},{2,3},{3,2},{4,5},{5,4},{6,7},{7,6},{8,9},{9,8},{10,11... | collective-permute-start | bytes 1216520 | tf_op jit(solution)/shard_map/route/ppermute | solution.py:34
  3.7 16.6 %collective-permute-start.2 = (bf16[2,16,4224]{2,1,0:T(8,128)(2,1)S(1)}, bf16[2,16,4224]{2,1,0:T(8,128)(2,1)S(1)}, u32[]{:S(2)}, u32[]{:S(2)}) collective-permute-start(bf16[2,16,4224]{2,1,0:T(8,128)(2,1)S(1)} %get-tuple-element.45), channel_id=1, source_target_pairs={{0,4},{1,5},{2,6},{3,7},{4,0},{5,1},{6,2},{7,3},{8,12},{9,13},{10,... | collective-permute-start | bytes 811016 | tf_op jit(solution)/shard_map/dispatch/ppermute | solution.py:34
  7.4 13.2 %collective-permute-start.1 = (bf16[2,16,4224]{2,1,0:T(8,128)(2,1)S(1)}, bf16[2,16,4224]{2,1,0:T(8,128)(2,1)S(1)}, u32[]{:S(2)}, u32[]{:S(2)}) collective-permute-start(bf16[2,16,4224]{2,1,0:T(8,128)(2,1)S(1)} %dispatch.2), channel_id=1, source_target_pairs={{0,2},{1,3},{2,0},{3,1},{4,6},{5,7},{6,4},{7,5},{8,10},{9,11},{10,... | collective-permute-start | bytes 811016 | tf_op jit(solution)/shard_map/dispatch/ppermute | solution.py:34
  9.0 0.9 %copy-start.3 = (bf16[1,1,128,768]{3,2,1,0:T(8,128)(2,1)S(1)}, bf16[1,1,128,768]{3,2,1,0:T(8,128)(2,1)}, u32[]{:S(2)}) copy-start(bf16[1,1,128,768]{3,2,1,0:T(8,128)(2,1)} %param.9) | copy-start | bytes 589828
  10.4 14.1 %collective-permute-start.4 = (bf16[32,4352]{1,0:T(8,128)(2,1)S(1)}, bf16[32,4352]{1,0:T(8,128)(2,1)S(1)}, u32[]{:S(2)}, u32[]{:S(2)}) collective-permute-start(bf16[32,4352]{1,0:T(8,128)(2,1)S(1)} %get-tuple-element.46), channel_id=1, source_target_pairs={{0,24},{8,16},{16,8},{24,0},{1,25},{9,17},{17,9},{25,1},{2,26},{10... | collective-permute-start | bytes 835592 | tf_op jit(solution)/shard_map/arrive/ppermute | solution.py:34
  12.9 12.9 %collective-permute-start.5 = (bf16[32,4352]{1,0:T(8,128)(2,1)S(1)}, bf16[32,4352]{1,0:T(8,128)(2,1)S(1)}, u32[]{:S(2)}, u32[]{:S(2)}) collective-permute-start(bf16[32,4352]{1,0:T(8,128)(2,1)S(1)} %get-tuple-element.47), channel_id=1, source_target_pairs={{0,16},{8,24},{16,0},{24,8},{1,17},{9,25},{17,1},{25,9},{2,18},{10... | collective-permute-start | bytes 835592 | tf_op jit(solution)/shard_map/arrive/ppermute | solution.py:34
  13.5 12.5 %collective-permute-start.6 = (bf16[32,4352]{1,0:T(8,128)(2,1)S(1)}, bf16[32,4352]{1,0:T(8,128)(2,1)S(1)}, u32[]{:S(2)}, u32[]{:S(2)}) collective-permute-start(bf16[32,4352]{1,0:T(8,128)(2,1)S(1)} %get-tuple-element.48), channel_id=1, source_target_pairs={{0,8},{8,0},{16,24},{24,16},{1,9},{9,1},{17,25},{25,17},{2,10},{10... | collective-permute-start | bytes 835592 | tf_op jit(solution)/shard_map/arrive/ppermute | solution.py:34
  20.3 4.2 %collective-permute-start.3 = (bf16[16,4224]{1,0:T(8,128)(2,1)S(1)}, bf16[16,4224]{1,0:T(8,128)(2,1)S(1)}, u32[]{:S(2)}, u32[]{:S(2)}) collective-permute-start(bf16[16,4224]{1,0:T(8,128)(2,1)S(1)} %get-tuple-element.79), channel_id=1, source_target_pairs={{0,1},{1,0},{2,3},{3,2},{4,5},{5,4},{6,7},{7,6},{8,9},{9,8},{10,11... | collective-permute-start | bytes 405512 | tf_op jit(solution)/shard_map/dispatch/ppermute | solution.py:34
  20.6 15.5 %copy-start.1 = (bf16[1,4096,768]{2,1,0:T(8,128)(2,1)S(1)}, bf16[1,4096,768]{2,1,0:T(8,128)(2,1)}, u32[]{:S(2)}) copy-start(bf16[1,4096,768]{2,1,0:T(8,128)(2,1)} %param.10) | copy-start | bytes 18874372
  20.6 15.4 %copy-start.2 = (bf16[2,128,768]{2,1,0:T(8,128)(2,1)S(1)}, bf16[2,128,768]{2,1,0:T(8,128)(2,1)}, u32[]{:S(2)}) copy-start(bf16[2,128,768]{2,1,0:T(8,128)(2,1)} %param.11) | copy-start | bytes 1179652
  20.6 15.4 %copy-start.4 = (bf16[1,1,128,768]{3,2,1,0:T(8,128)(2,1)S(1)}, bf16[1,1,128,768]{3,2,1,0:T(8,128)(2,1)}, u32[]{:S(2)}) copy-start(bf16[1,1,128,768]{3,2,1,0:T(8,128)(2,1)} %param.9) | copy-start | bytes 589828
  20.6 10.7 %collective-permute-start.7 = (bf16[2,16,4224]{2,1,0:T(8,128)(2,1)S(1)}, bf16[2,16,4224]{2,1,0:T(8,128)(2,1)S(1)}, u32[]{:S(2)}, u32[]{:S(2)}) collective-permute-start(bf16[2,16,4224]{2,1,0:T(8,128)(2,1)S(1)} %dispatch.3), channel_id=1, source_target_pairs={{0,6},{1,7},{2,4},{3,5},{4,2},{5,3},{6,0},{7,1},{8,14},{9,15},{10,... | collective-permute-start | bytes 811016 | tf_op jit(solution)/shard_map/dispatch/ppermute | solution.py:34
  26.5 8.4 %collective-permute-start.8 = (bf16[64,1280]{1,0:T(8,128)(2,1)S(1)}, bf16[64,1280]{1,0:T(8,128)(2,1)S(1)}, u32[]{:S(2)}, u32[]{:S(2)}) collective-permute-start(bf16[64,1280]{1,0:T(8,128)(2,1)S(1)} %get-tuple-element.57), channel_id=1, source_target_pairs={{0,24},{8,16},{16,8},{24,0},{1,25},{9,17},{17,9},{25,1},{2,26},{10... | collective-permute-start | bytes 491528 | tf_op jit(solution)/shard_map/arrive/ppermute | solution.py:34
  28.2 9.8 %collective-permute-start.9 = (bf16[64,1280]{1,0:T(8,128)(2,1)S(1)}, bf16[64,1280]{1,0:T(8,128)(2,1)S(1)}, u32[]{:S(2)}, u32[]{:S(2)}) collective-permute-start(bf16[64,1280]{1,0:T(8,128)(2,1)S(1)} %get-tuple-element.58), channel_id=1, source_target_pairs={{0,16},{8,24},{16,0},{24,8},{1,17},{9,25},{17,1},{25,9},{2,18},{10... | collective-permute-start | bytes 491528 | tf_op jit(solution)/shard_map/arrive/ppermute | solution.py:34
  29.5 8.5 %collective-permute-start.10 = (bf16[64,1280]{1,0:T(8,128)(2,1)S(1)}, bf16[64,1280]{1,0:T(8,128)(2,1)S(1)}, u32[]{:S(2)}, u32[]{:S(2)}) collective-permute-start(bf16[64,1280]{1,0:T(8,128)(2,1)S(1)} %get-tuple-element.59), channel_id=1, source_target_pairs={{0,8},{8,0},{16,24},{24,16},{1,9},{9,1},{17,25},{25,17},{2,10},{10... | collective-permute-start | bytes 491528 | tf_op jit(solution)/shard_map/arrive/ppermute | solution.py:34
  31.8 7.9 %collective-permute-start.11 = (bf16[32,1280]{1,0:T(8,128)(2,1)S(1)}, bf16[32,1280]{1,0:T(8,128)(2,1)S(1)}, u32[]{:S(2)}, u32[]{:S(2)}) collective-permute-start(bf16[32,1280]{1,0:T(8,128)(2,1)S(1)} %get-tuple-element.61), channel_id=1, source_target_pairs={{0,24},{8,16},{16,8},{24,0},{1,25},{9,17},{17,9},{25,1},{2,26},{10... | collective-permute-start | bytes 245768 | tf_op jit(solution)/shard_map/arrive/ppermute | solution.py:34
  34.4 6.1 %collective-permute-start.12 = (bf16[32,1280]{1,0:T(8,128)(2,1)S(1)}, bf16[32,1280]{1,0:T(8,128)(2,1)S(1)}, u32[]{:S(2)}, u32[]{:S(2)}) collective-permute-start(bf16[32,1280]{1,0:T(8,128)(2,1)S(1)} %get-tuple-element.62), channel_id=1, source_target_pairs={{0,16},{8,24},{16,0},{24,8},{1,17},{9,25},{17,1},{25,9},{2,18},{10... | collective-permute-start | bytes 245768 | tf_op jit(solution)/shard_map/arrive/ppermute | solution.py:34
  34.9 5.7 %collective-permute-start.13 = (bf16[32,1280]{1,0:T(8,128)(2,1)S(1)}, bf16[32,1280]{1,0:T(8,128)(2,1)S(1)}, u32[]{:S(2)}, u32[]{:S(2)}) collective-permute-start(bf16[32,1280]{1,0:T(8,128)(2,1)S(1)} %get-tuple-element.63), channel_id=1, source_target_pairs={{0,8},{8,0},{16,24},{24,16},{1,9},{9,1},{17,25},{25,17},{2,10},{10... | collective-permute-start | bytes 245768 | tf_op jit(solution)/shard_map/arrive/ppermute | solution.py:34
  41.1 1.7 %collective-permute-start.14 = (bf16[4,32,1280]{2,1,0:T(8,128)(2,1)S(1)}, bf16[4,32,1280]{2,1,0:T(8,128)(2,1)S(1)}, u32[]{:S(2)}, u32[]{:S(2)}) collective-permute-start(bf16[4,32,1280]{2,1,0:T(8,128)(2,1)S(1)} %get-tuple-element.71), channel_id=1, source_target_pairs={{0,1},{1,0},{2,3},{3,2},{4,5},{5,4},{6,7},{7,6},{8,9},{9,8},{10,11... | collective-permute-start | bytes 983048 | tf_op jit(solution)/shard_map/adapters/ppermute | solution.py:34
  42.8 8.4 %collective-permute-start.15 = (bf16[32,1280]{1,0:T(8,128)(2,1)S(1)}, bf16[32,1280]{1,0:T(8,128)(2,1)S(1)}, u32[]{:S(2)}, u32[]{:S(2)}) collective-permute-start(bf16[32,1280]{1,0:T(8,128)(2,1)S(1)} %get-tuple-element.73), channel_id=1, source_target_pairs={{0,4},{1,5},{2,6},{3,7},{4,0},{5,1},{6,2},{7,3},{8,12},{9,13},{10,... | collective-permute-start | bytes 245768 | tf_op jit(solution)/shard_map/adapters/ppermute | solution.py:34
  46.1 7.5 %collective-permute-start.16 = (bf16[32,1280]{1,0:T(8,128)(2,1)S(1)}, bf16[32,1280]{1,0:T(8,128)(2,1)S(1)}, u32[]{:S(2)}, u32[]{:S(2)}) collective-permute-start(bf16[32,1280]{1,0:T(8,128)(2,1)S(1)} %get-tuple-element.74), channel_id=1, source_target_pairs={{0,6},{1,7},{2,4},{3,5},{4,2},{5,3},{6,0},{7,1},{8,14},{9,15},{10,... | collective-permute-start | bytes 245768 | tf_op jit(solution)/shard_map/adapters/ppermute | solution.py:34
  48.6 5.5 %collective-permute-start.17 = (bf16[32,1280]{1,0:T(8,128)(2,1)S(1)}, bf16[32,1280]{1,0:T(8,128)(2,1)S(1)}, u32[]{:S(2)}, u32[]{:S(2)}) collective-permute-start(bf16[32,1280]{1,0:T(8,128)(2,1)S(1)} %get-tuple-element.75), channel_id=1, source_target_pairs={{0,2},{1,3},{2,0},{3,1},{4,6},{5,7},{6,4},{7,5},{8,10},{9,11},{10,... | collective-permute-start | bytes 245768 | tf_op jit(solution)/shard_map/adapters/ppermute | solution.py:34

commit v10 on v8

--- a/solution.py
+++ b/solution.py
@@ -105,7 +105,7 @@
     loop_rows = jnp.where(loop_rows == loop, 1.0, 0.0).astype(bf16)
     mix = nt(mixed[...], loop_rows).astype(bf16)
     deal_rows(middle, mix.reshape(2 * chips, cap, LANES), slice(width, width + LANES), keep, lead, give)
-    step = 1024 if width % 1024 == 0 else width
+    step = 2048 if width % 2048 == 0 else width
     for n in range(0, width, step):
         at = slice(n, n + step)
         got = nn(picks[...], cot[:, at]).astype(bf16)

time: 55.2 us -> 55.2 us (level)
  no operation moved by 1% of the time
where the time goes in v10:
time: 55.2 us; the launch traced here: 55 us
  starting transfers between devices  26.9 us (49%)
  waiting for transfers between devices  15 us (27%)
  Pallas kernels  9.37 us (17%)
  local copies, waits for them, and re-layouts  2.19 us (4%)
  other arithmetic  0.85 us (2%)
  between operations  0.76 us (1%)
    ppermute x18, starting transfers between devices, swap(): return lax.ppermute(x, axis, [(i, i ^ mask) for i in range(size)])  26.9 us
    ppermute x18, waiting for transfers between devices, swap(): return lax.ppermute(x, axis, [(i, i ^ mask) for i in range(size)])  15 us
    pallas_call x1, Pallas kernels, on_device(): call(functools.partial(product_body, groups, chips), shape((1, part, hid_...  2.67 us
    unnamed x12, local copies, waits for them, and re-layouts  2.17 us
    pallas_call x1, Pallas kernels, on_device(): call(functools.partial(inner_body, chips, cap, len(chunks)), (shape((slot...  1.85 us
    pallas_call x3, Pallas kernels, on_device(): call(functools.partial(arrive_body, groups, chips, cap, own, len(before))...  1.46 us
    pallas_call x1, Pallas kernels, on_device(): call(functools.partial(adapter_first_body, loops, chips, cols, groups), s...  1.44 us
  transfers between devices with their start and end apart: 18, of which 12 were waited for; matrix products, arithmetic and copies ran while one was open for 0% of the time, Pallas kernels for 14%

profile of v10, /device:TPU:0, one launch (start us, length us, event | category | flops | bytes accessed | tf_op | source)
XLA Modules:
  0.0 55.0 jit_solution(18347913266023258369)
XLA Ops:
  0.6 0.9 %add_bitcast_fusion.small = f32[8,128]{1,0:T(8,128)S(1)} fusion(bf16[128,8]{0,1:T(8,128)(2,1)} %param.13, s32[128,8]{0,1:T(8,128)} %param.14, s32[128]{0:T(128)} %param.15), kind=kLoop, calls=%fused_computation.2 | loop fusion | flops 6144 | bytes 10752 | tf_op jit(solution)/shard_map/add | solution.py:331
  1.5 1.2 %copy-done.3 = bf16[128,4096]{1,0:T(8,128)(2,1)S(1)} copy-done((bf16[128,4096]{1,0:T(8,128)(2,1)S(1)}, bf16[128,4096]{1,0:T(8,128)(2,1)}, u32[]{:S(2)}) %copy-start.3) | copy-done | bytes 1048600
  2.7 0.6 %route.1 = (bf16[4,16,4224]{2,1,0:T(8,128)(2,1)S(1)}, bf16[2,16,4224]{2,1,0:T(8,128)(2,1)S(1)}, bf16[3,16,4224]{2,1,0:T(8,128)(2,1)S(1)}, bf16[128,128]{1,0:T(8,128)(2,1)S(1)}) custom-call(f32[8,128]{1,0:T(8,128)S(1)} %add_bitcast_fusion.small, bf16[128,4096]{1,0:T(8,128)(2,1)S(1)} %copy-done.3), custom_call_target="tpu_custom_call" | custom-call | flops 134217728 | bytes 3145728 | tf_op jit(solution)/shard_map/route/pallas_call | solution.py:338
  3.3 0.5 collective-permute-start
  3.8 3.7 %collective-permute-start.2 = (bf16[2,16,4224]{2,1,0:T(8,128)(2,1)S(1)}, bf16[2,16,4224]{2,1,0:T(8,128)(2,1)S(1)}, u32[]{:S(2)}, u32[]{:S(2)}) collective-permute-start(bf16[2,16,4224]{2,1,0:T(8,128)(2,1)S(1)} %get-tuple-element.45), channel_id=1, source_target_pairs={{0,4},{1,5},{2,6},{3,7},{4,0},{5,1},{6,2},{7,3},{8,12},{9,13},{10,... | collective-permute-start | bytes 811016 | tf_op jit(solution)/shard_map/dispatch/ppermute | solution.py:34
  7.5 1.6 %collective-permute-start.1 = (bf16[2,16,4224]{2,1,0:T(8,128)(2,1)S(1)}, bf16[2,16,4224]{2,1,0:T(8,128)(2,1)S(1)}, u32[]{:S(2)}, u32[]{:S(2)}) collective-permute-start(bf16[2,16,4224]{2,1,0:T(8,128)(2,1)S(1)} %dispatch.2), channel_id=1, source_target_pairs={{0,2},{1,3},{2,0},{3,1},{4,6},{5,7},{6,4},{7,5},{8,10},{9,11},{10,... | collective-permute-start | bytes 811016 | tf_op jit(solution)/shard_map/dispatch/ppermute | solution.py:34
  9.1 0.9 %copy-done.4 = bf16[1,1,128,768]{3,2,1,0:T(8,128)(2,1)S(1)} copy-done((bf16[1,1,128,768]{3,2,1,0:T(8,128)(2,1)S(1)}, bf16[1,1,128,768]{3,2,1,0:T(8,128)(2,1)}, u32[]{:S(2)}) %copy-start.4) | copy-done | bytes 196632
  10.6 2.5 %collective-permute-start.4 = (bf16[32,4352]{1,0:T(8,128)(2,1)S(1)}, bf16[32,4352]{1,0:T(8,128)(2,1)S(1)}, u32[]{:S(2)}, u32[]{:S(2)}) collective-permute-start(bf16[32,4352]{1,0:T(8,128)(2,1)S(1)} %get-tuple-element.46), channel_id=1, source_target_pairs={{0,24},{8,16},{16,8},{24,0},{1,25},{9,17},{17,9},{25,1},{2,26},{10... | collective-permute-start | bytes 835592 | tf_op jit(solution)/shard_map/arrive/ppermute | solution.py:34
  13.1 0.5 collective-permute-start.5
  13.6 0.5 collective-permute-start.6
  14.1 6.3 %collective-permute-done.2 = bf16[2,16,4224]{2,1,0:T(8,128)(2,1)S(1)} collective-permute-done((bf16[2,16,4224]{2,1,0:T(8,128)(2,1)S(1)}, bf16[2,16,4224]{2,1,0:T(8,128)(2,1)S(1)}, u32[]{:S(2)}, u32[]{:S(2)}) %collective-permute-start.2) | collective-permute-done | bytes 270368 | tf_op jit(solution)/shard_map/dispatch/ppermute | solution.py:34
  20.8 3.8 %collective-permute-start.7 = (bf16[2,16,4224]{2,1,0:T(8,128)(2,1)S(1)}, bf16[2,16,4224]{2,1,0:T(8,128)(2,1)S(1)}, u32[]{:S(2)}, u32[]{:S(2)}) collective-permute-start(bf16[2,16,4224]{2,1,0:T(8,128)(2,1)S(1)} %dispatch.3), channel_id=1, source_target_pairs={{0,6},{1,7},{2,4},{3,5},{4,2},{5,3},{6,0},{7,1},{8,14},{9,15},{10,... | collective-permute-start | bytes 811016 | tf_op jit(solution)/shard_map/dispatch/ppermute | solution.py:34
  24.6 1.3 %collective-permute-done.5.refs_4_.refs_2_ = bf16[32,4352]{1,0:T(8,128)(2,1)S(1)} collective-permute-done((bf16[32,4352]{1,0:T(8,128)(2,1)S(1)}, bf16[32,4352]{1,0:T(8,128)(2,1)S(1)}, u32[]{:S(2)}, u32[]{:S(2)}) %collective-permute-start.5) | collective-permute-done | bytes 278560 | tf_op jit(solution)/shard_map/arrive/ppermute | solution.py:34
  26.0 0.5 arrive.4
  26.6 1.7 %collective-permute-start.8 = (bf16[64,1280]{1,0:T(8,128)(2,1)S(1)}, bf16[64,1280]{1,0:T(8,128)(2,1)S(1)}, u32[]{:S(2)}, u32[]{:S(2)}) collective-permute-start(bf16[64,1280]{1,0:T(8,128)(2,1)S(1)} %get-tuple-element.57), channel_id=1, source_target_pairs={{0,24},{8,16},{16,8},{24,0},{1,25},{9,17},{17,9},{25,1},{2,26},{10... | collective-permute-start | bytes 491528 | tf_op jit(solution)/shard_map/arrive/ppermute | solution.py:34
  28.3 1.3 %collective-permute-start.9 = (bf16[64,1280]{1,0:T(8,128)(2,1)S(1)}, bf16[64,1280]{1,0:T(8,128)(2,1)S(1)}, u32[]{:S(2)}, u32[]{:S(2)}) collective-permute-start(bf16[64,1280]{1,0:T(8,128)(2,1)S(1)} %get-tuple-element.58), channel_id=1, source_target_pairs={{0,16},{8,24},{16,0},{24,8},{1,17},{9,25},{17,1},{25,9},{2,18},{10... | collective-permute-start | bytes 491528 | tf_op jit(solution)/shard_map/arrive/ppermute | solution.py:34
  29.6 0.5 collective-permute-start.10
  30.1 1.3 %collective-permute-done.7.refs_0_ = bf16[2,16,4224]{2,1,0:T(8,128)(2,1)S(1)} collective-permute-done((bf16[2,16,4224]{2,1,0:T(8,128)(2,1)S(1)}, bf16[2,16,4224]{2,1,0:T(8,128)(2,1)S(1)}, u32[]{:S(2)}, u32[]{:S(2)}) %collective-permute-start.7) | collective-permute-done | bytes 270368 | tf_op jit(solution)/shard_map/dispatch/ppermute | solution.py:34
  31.9 2.6 %collective-permute-start.11 = (bf16[32,1280]{1,0:T(8,128)(2,1)S(1)}, bf16[32,1280]{1,0:T(8,128)(2,1)S(1)}, u32[]{:S(2)}, u32[]{:S(2)}) collective-permute-start(bf16[32,1280]{1,0:T(8,128)(2,1)S(1)} %get-tuple-element.61), channel_id=1, source_target_pairs={{0,24},{8,16},{16,8},{24,0},{1,25},{9,17},{17,9},{25,1},{2,26},{10... | collective-permute-start | bytes 245768 | tf_op jit(solution)/shard_map/arrive/ppermute | solution.py:34
  34.5 0.5 collective-permute-start.12
  35.0 1.2 %collective-permute-start.13 = (bf16[32,1280]{1,0:T(8,128)(2,1)S(1)}, bf16[32,1280]{1,0:T(8,128)(2,1)S(1)}, u32[]{:S(2)}, u32[]{:S(2)}) collective-permute-start(bf16[32,1280]{1,0:T(8,128)(2,1)S(1)} %get-tuple-element.63), channel_id=1, source_target_pairs={{0,8},{8,0},{16,24},{24,16},{1,9},{9,1},{17,25},{25,17},{2,10},{10... | collective-permute-start | bytes 245768 | tf_op jit(solution)/shard_map/arrive/ppermute | solution.py:34
  36.2 1.8 %inner.1 = (bf16[128,768]{1,0:T(8,128)(2,1)}, f32[128,128]{1,0:T(8,128)S(1)}) custom-call(bf16[4096,768]{1,0:T(8,128)(2,1)S(1)} %bitcast.12, bf16[256,768]{1,0:T(8,128)(2,1)S(1)} %bitcast.13, bf16[128,768]{1,0:T(8,128)(2,1)S(1)} %bitcast.16, bf16[32,4224]{1,0:T(8,128)(2,1)S(1)} %get-tuple-element.44.refs_0_, bf16[64,4224]{1,0:T(8,128)(2,1)S(1)} %get-tuple-element.49.refs_1_, ...), custom_call_target="tpu_custom_call" | custom-call | flops 805306368 | bytes 6291456 | tf_op jit(solution)/shard_map/inner/pallas_call | solution.py:384
  38.1 1.4 %adapters.3 = (f32[256,1024]{1,0:T(8,128)S(1)}, f32[256,256]{1,0:T(8,128)S(1)}, bf16[128,256]{1,0:T(8,128)(2,1)S(1)}, bf16[128,256]{1,0:T(8,128)(2,1)S(1)}) custom-call(bf16[256,768]{1,0:T(8,128)(2,1)S(1)} %bitcast.14, f32[128,128]{1,0:T(8,128)S(1)} %get-tuple-element.65._.mix, bf16[32,4352]{1,0:T(8,128)(2,1)S(1)} %get-tuple-element.55.refs_0_, ...), custom_call_target="tpu_custom_call" | custom-call | flops 268435456 | bytes 524288 | tf_op jit(solution)/shard_map/adapters/pallas_call | solution.py:395
  39.9 0.7 %collective-permute-done.12.refs_10_.refs_2_ = bf16[32,1280]{1,0:T(8,128)(2,1)S(1)} collective-permute-done((bf16[32,1280]{1,0:T(8,128)(2,1)S(1)}, bf16[32,1280]{1,0:T(8,128)(2,1)S(1)}, u32[]{:S(2)}, u32[]{:S(2)}) %collective-permute-start.12) | collective-permute-done | bytes 81952 | tf_op jit(solution)/shard_map/arrive/ppermute | solution.py:34
  40.7 0.5 adapters.4
  41.3 1.6 %collective-permute-done.14.got = bf16[4,32,1280]{2,1,0:T(8,128)(2,1)S(1)} collective-permute-done((bf16[4,32,1280]{2,1,0:T(8,128)(2,1)S(1)}, bf16[4,32,1280]{2,1,0:T(8,128)(2,1)S(1)}, u32[]{:S(2)}, u32[]{:S(2)}) %collective-permute-start.14) | collective-permute-done | bytes 327712 | tf_op jit(solution)/shard_map/adapters/ppermute | solution.py:34
  43.0 3.3 %collective-permute-start.15 = (bf16[32,1280]{1,0:T(8,128)(2,1)S(1)}, bf16[32,1280]{1,0:T(8,128)(2,1)S(1)}, u32[]{:S(2)}, u32[]{:S(2)}) collective-permute-start(bf16[32,1280]{1,0:T(8,128)(2,1)S(1)} %get-tuple-element.73), channel_id=1, source_target_pairs={{0,4},{1,5},{2,6},{3,7},{4,0},{5,1},{6,2},{7,3},{8,12},{9,13},{10,... | collective-permute-start | bytes 245768 | tf_op jit(solution)/shard_map/adapters/ppermute | solution.py:34
  46.2 2.5 %collective-permute-start.16 = (bf16[32,1280]{1,0:T(8,128)(2,1)S(1)}, bf16[32,1280]{1,0:T(8,128)(2,1)S(1)}, u32[]{:S(2)}, u32[]{:S(2)}) collective-permute-start(bf16[32,1280]{1,0:T(8,128)(2,1)S(1)} %get-tuple-element.74), channel_id=1, source_target_pairs={{0,6},{1,7},{2,4},{3,5},{4,2},{5,3},{6,0},{7,1},{8,14},{9,15},{10,... | collective-permute-start | bytes 245768 | tf_op jit(solution)/shard_map/adapters/ppermute | solution.py:34
  48.7 2.7 %product.1 = f32[1,1024,768]{2,1,0:T(8,128)} custom-call(bf16[32,4352]{1,0:T(8,128)(2,1)S(1)} %get-tuple-element.55.refs_0_, bf16[32,4352]{1,0:T(8,128)(2,1)S(1)} %collective-permute-done.4.refs_3_.refs_1_, bf16[32,4352]{1,0:T(8,128)(2,1)S(1)} %collective-permute-done.5.refs_4_.refs_2_, bf16[32,4352]{1,0:T(8,128)(2,1)S(1)} %collective-permute-done.6.refs_5_.refs_3_, ...), custom_call_target="tpu_custom_call" | custom-call | flops 805306368 | bytes 2097152 | tf_op jit(solution)/shard_map/product/pallas_call | solution.py:422
  51.4 2.3 %collective-permute-done.16.refs_2_ = bf16[32,1280]{1,0:T(8,128)(2,1)S(1)} collective-permute-done((bf16[32,1280]{1,0:T(8,128)(2,1)S(1)}, bf16[32,1280]{1,0:T(8,128)(2,1)S(1)}, u32[]{:S(2)}, u32[]{:S(2)}) %collective-permute-start.16) | collective-permute-done | bytes 81952 | tf_op jit(solution)/shard_map/adapters/ppermute | solution.py:34
  53.7 0.5 collective-permute-done.17.refs_3_
  54.2 0.8 %final.1 = (f32[2,16,1024]{2,1,0:T(8,128)}, f32[2,16,192]{2,1,0:T(8,128)}, f32[8,128]{1,0:T(8,128)}) custom-call(f32[8,128]{1,0:T(8,128)S(1)} %add_bitcast_fusion.small, bf16[128,128]{1,0:T(8,128)(2,1)S(1)} %get-tuple-element.64.picks, bf16[32,1280]{1,0:T(8,128)(2,1)S(1)} %get-tuple-element.72.refs_0_, bf16[32,1280]{1,0:T(8,128)(2,1)S(1)} %collective-permute-done.15.refs_1_, ...), custom_call_target="tpu_custom_call" | custom-call | bytes 1000000 | tf_op jit(solution)/shard_map/final/pallas_call | solution.py:431
  (30 shorter events, 2.0 us)
Async XLA Ops:
  0.6 8.5 %copy-start = (bf16[2,4096,128]{2,1,0:T(8,128)(2,1)S(1)}, bf16[2,4096,128]{2,1,0:T(8,128)(2,1)}, u32[]{:S(2)}) copy-start(bf16[2,4096,128]{2,1,0:T(8,128)(2,1)} %adapter_out.5) | copy-start | bytes 6291460
  1.5 1.2 %copy-start.3 = (bf16[128,4096]{1,0:T(8,128)(2,1)S(1)}, bf16[128,4096]{1,0:T(8,128)(2,1)}, u32[]{:S(2)}) copy-start(bf16[128,4096]{1,0:T(8,128)(2,1)} %cot.1) | copy-start | bytes 3145732
  3.3 4.2 %collective-permute-start = (bf16[3,16,4224]{2,1,0:T(8,128)(2,1)S(1)}, bf16[3,16,4224]{2,1,0:T(8,128)(2,1)S(1)}, u32[]{:S(2)}, u32[]{:S(2)}) collective-permute-start(bf16[3,16,4224]{2,1,0:T(8,128)(2,1)S(1)} %get-tuple-element.43), channel_id=1, source_target_pairs={{0,1},{1,0},{2,3},{3,2},{4,5},{5,4},{6,7},{7,6},{8,9},{9,8},{10,11... | collective-permute-start | bytes 1216520 | tf_op jit(solution)/shard_map/route/ppermute | solution.py:34
  3.8 16.6 %collective-permute-start.2 = (bf16[2,16,4224]{2,1,0:T(8,128)(2,1)S(1)}, bf16[2,16,4224]{2,1,0:T(8,128)(2,1)S(1)}, u32[]{:S(2)}, u32[]{:S(2)}) collective-permute-start(bf16[2,16,4224]{2,1,0:T(8,128)(2,1)S(1)} %get-tuple-element.45), channel_id=1, source_target_pairs={{0,4},{1,5},{2,6},{3,7},{4,0},{5,1},{6,2},{7,3},{8,12},{9,13},{10,... | collective-permute-start | bytes 811016 | tf_op jit(solution)/shard_map/dispatch/ppermute | solution.py:34
  7.5 13.2 %collective-permute-start.1 = (bf16[2,16,4224]{2,1,0:T(8,128)(2,1)S(1)}, bf16[2,16,4224]{2,1,0:T(8,128)(2,1)S(1)}, u32[]{:S(2)}, u32[]{:S(2)}) collective-permute-start(bf16[2,16,4224]{2,1,0:T(8,128)(2,1)S(1)} %dispatch.2), channel_id=1, source_target_pairs={{0,2},{1,3},{2,0},{3,1},{4,6},{5,7},{6,4},{7,5},{8,10},{9,11},{10,... | collective-permute-start | bytes 811016 | tf_op jit(solution)/shard_map/dispatch/ppermute | solution.py:34
  9.1 0.9 %copy-start.4 = (bf16[1,1,128,768]{3,2,1,0:T(8,128)(2,1)S(1)}, bf16[1,1,128,768]{3,2,1,0:T(8,128)(2,1)}, u32[]{:S(2)}) copy-start(bf16[1,1,128,768]{3,2,1,0:T(8,128)(2,1)} %param.9) | copy-start | bytes 589828
  10.6 14.1 %collective-permute-start.4 = (bf16[32,4352]{1,0:T(8,128)(2,1)S(1)}, bf16[32,4352]{1,0:T(8,128)(2,1)S(1)}, u32[]{:S(2)}, u32[]{:S(2)}) collective-permute-start(bf16[32,4352]{1,0:T(8,128)(2,1)S(1)} %get-tuple-element.46), channel_id=1, source_target_pairs={{0,24},{8,16},{16,8},{24,0},{1,25},{9,17},{17,9},{25,1},{2,26},{10... | collective-permute-start | bytes 835592 | tf_op jit(solution)/shard_map/arrive/ppermute | solution.py:34
  13.1 12.9 %collective-permute-start.5 = (bf16[32,4352]{1,0:T(8,128)(2,1)S(1)}, bf16[32,4352]{1,0:T(8,128)(2,1)S(1)}, u32[]{:S(2)}, u32[]{:S(2)}) collective-permute-start(bf16[32,4352]{1,0:T(8,128)(2,1)S(1)} %get-tuple-element.47), channel_id=1, source_target_pairs={{0,16},{8,24},{16,0},{24,8},{1,17},{9,25},{17,1},{25,9},{2,18},{10... | collective-permute-start | bytes 835592 | tf_op jit(solution)/shard_map/arrive/ppermute | solution.py:34
  13.6 12.5 %collective-permute-start.6 = (bf16[32,4352]{1,0:T(8,128)(2,1)S(1)}, bf16[32,4352]{1,0:T(8,128)(2,1)S(1)}, u32[]{:S(2)}, u32[]{:S(2)}) collective-permute-start(bf16[32,4352]{1,0:T(8,128)(2,1)S(1)} %get-tuple-element.48), channel_id=1, source_target_pairs={{0,8},{8,0},{16,24},{24,16},{1,9},{9,1},{17,25},{25,17},{2,10},{10... | collective-permute-start | bytes 835592 | tf_op jit(solution)/shard_map/arrive/ppermute | solution.py:34
  20.5 4.1 %collective-permute-start.3 = (bf16[16,4224]{1,0:T(8,128)(2,1)S(1)}, bf16[16,4224]{1,0:T(8,128)(2,1)S(1)}, u32[]{:S(2)}, u32[]{:S(2)}) collective-permute-start(bf16[16,4224]{1,0:T(8,128)(2,1)S(1)} %get-tuple-element.79), channel_id=1, source_target_pairs={{0,1},{1,0},{2,3},{3,2},{4,5},{5,4},{6,7},{7,6},{8,9},{9,8},{10,11... | collective-permute-start | bytes 405512 | tf_op jit(solution)/shard_map/dispatch/ppermute | solution.py:34
  20.7 15.4 %copy-start.1 = (bf16[1,4096,768]{2,1,0:T(8,128)(2,1)S(1)}, bf16[1,4096,768]{2,1,0:T(8,128)(2,1)}, u32[]{:S(2)}) copy-start(bf16[1,4096,768]{2,1,0:T(8,128)(2,1)} %param.10) | copy-start | bytes 18874372
  20.8 15.4 %copy-start.2 = (bf16[2,128,768]{2,1,0:T(8,128)(2,1)S(1)}, bf16[2,128,768]{2,1,0:T(8,128)(2,1)}, u32[]{:S(2)}) copy-start(bf16[2,128,768]{2,1,0:T(8,128)(2,1)} %param.11) | copy-start | bytes 1179652
  20.8 15.4 %copy-start.5 = (bf16[1,1,128,768]{3,2,1,0:T(8,128)(2,1)S(1)}, bf16[1,1,128,768]{3,2,1,0:T(8,128)(2,1)}, u32[]{:S(2)}) copy-start(bf16[1,1,128,768]{3,2,1,0:T(8,128)(2,1)} %param.9) | copy-start | bytes 589828
  20.8 10.7 %collective-permute-start.7 = (bf16[2,16,4224]{2,1,0:T(8,128)(2,1)S(1)}, bf16[2,16,4224]{2,1,0:T(8,128)(2,1)S(1)}, u32[]{:S(2)}, u32[]{:S(2)}) collective-permute-start(bf16[2,16,4224]{2,1,0:T(8,128)(2,1)S(1)} %dispatch.3), channel_id=1, source_target_pairs={{0,6},{1,7},{2,4},{3,5},{4,2},{5,3},{6,0},{7,1},{8,14},{9,15},{10,... | collective-permute-start | bytes 811016 | tf_op jit(solution)/shard_map/dispatch/ppermute | solution.py:34
  26.6 8.4 %collective-permute-start.8 = (bf16[64,1280]{1,0:T(8,128)(2,1)S(1)}, bf16[64,1280]{1,0:T(8,128)(2,1)S(1)}, u32[]{:S(2)}, u32[]{:S(2)}) collective-permute-start(bf16[64,1280]{1,0:T(8,128)(2,1)S(1)} %get-tuple-element.57), channel_id=1, source_target_pairs={{0,24},{8,16},{16,8},{24,0},{1,25},{9,17},{17,9},{25,1},{2,26},{10... | collective-permute-start | bytes 491528 | tf_op jit(solution)/shard_map/arrive/ppermute | solution.py:34
  28.3 9.8 %collective-permute-start.9 = (bf16[64,1280]{1,0:T(8,128)(2,1)S(1)}, bf16[64,1280]{1,0:T(8,128)(2,1)S(1)}, u32[]{:S(2)}, u32[]{:S(2)}) collective-permute-start(bf16[64,1280]{1,0:T(8,128)(2,1)S(1)} %get-tuple-element.58), channel_id=1, source_target_pairs={{0,16},{8,24},{16,0},{24,8},{1,17},{9,25},{17,1},{25,9},{2,18},{10... | collective-permute-start | bytes 491528 | tf_op jit(solution)/shard_map/arrive/ppermute | solution.py:34
  29.6 8.5 %collective-permute-start.10 = (bf16[64,1280]{1,0:T(8,128)(2,1)S(1)}, bf16[64,1280]{1,0:T(8,128)(2,1)S(1)}, u32[]{:S(2)}, u32[]{:S(2)}) collective-permute-start(bf16[64,1280]{1,0:T(8,128)(2,1)S(1)} %get-tuple-element.59), channel_id=1, source_target_pairs={{0,8},{8,0},{16,24},{24,16},{1,9},{9,1},{17,25},{25,17},{2,10},{10... | collective-permute-start | bytes 491528 | tf_op jit(solution)/shard_map/arrive/ppermute | solution.py:34
  31.9 7.9 %collective-permute-start.11 = (bf16[32,1280]{1,0:T(8,128)(2,1)S(1)}, bf16[32,1280]{1,0:T(8,128)(2,1)S(1)}, u32[]{:S(2)}, u32[]{:S(2)}) collective-permute-start(bf16[32,1280]{1,0:T(8,128)(2,1)S(1)} %get-tuple-element.61), channel_id=1, source_target_pairs={{0,24},{8,16},{16,8},{24,0},{1,25},{9,17},{17,9},{25,1},{2,26},{10... | collective-permute-start | bytes 245768 | tf_op jit(solution)/shard_map/arrive/ppermute | solution.py:34
  34.5 6.1 %collective-permute-start.12 = (bf16[32,1280]{1,0:T(8,128)(2,1)S(1)}, bf16[32,1280]{1,0:T(8,128)(2,1)S(1)}, u32[]{:S(2)}, u32[]{:S(2)}) collective-permute-start(bf16[32,1280]{1,0:T(8,128)(2,1)S(1)} %get-tuple-element.62), channel_id=1, source_target_pairs={{0,16},{8,24},{16,0},{24,8},{1,17},{9,25},{17,1},{25,9},{2,18},{10... | collective-permute-start | bytes 245768 | tf_op jit(solution)/shard_map/arrive/ppermute | solution.py:34
  35.0 5.7 %collective-permute-start.13 = (bf16[32,1280]{1,0:T(8,128)(2,1)S(1)}, bf16[32,1280]{1,0:T(8,128)(2,1)S(1)}, u32[]{:S(2)}, u32[]{:S(2)}) collective-permute-start(bf16[32,1280]{1,0:T(8,128)(2,1)S(1)} %get-tuple-element.63), channel_id=1, source_target_pairs={{0,8},{8,0},{16,24},{24,16},{1,9},{9,1},{17,25},{25,17},{2,10},{10... | collective-permute-start | bytes 245768 | tf_op jit(solution)/shard_map/arrive/ppermute | solution.py:34
  41.2 1.7 %collective-permute-start.14 = (bf16[4,32,1280]{2,1,0:T(8,128)(2,1)S(1)}, bf16[4,32,1280]{2,1,0:T(8,128)(2,1)S(1)}, u32[]{:S(2)}, u32[]{:S(2)}) collective-permute-start(bf16[4,32,1280]{2,1,0:T(8,128)(2,1)S(1)} %get-tuple-element.71), channel_id=1, source_target_pairs={{0,1},{1,0},{2,3},{3,2},{4,5},{5,4},{6,7},{7,6},{8,9},{9,8},{10,11... | collective-permute-start | bytes 983048 | tf_op jit(solution)/shard_map/adapters/ppermute | solution.py:34
  43.0 8.4 %collective-permute-start.15 = (bf16[32,1280]{1,0:T(8,128)(2,1)S(1)}, bf16[32,1280]{1,0:T(8,128)(2,1)S(1)}, u32[]{:S(2)}, u32[]{:S(2)}) collective-permute-start(bf16[32,1280]{1,0:T(8,128)(2,1)S(1)} %get-tuple-element.73), channel_id=1, source_target_pairs={{0,4},{1,5},{2,6},{3,7},{4,0},{5,1},{6,2},{7,3},{8,12},{9,13},{10,... | collective-permute-start | bytes 245768 | tf_op jit(solution)/shard_map/adapters/ppermute | solution.py:34
  46.2 7.5 %collective-permute-start.16 = (bf16[32,1280]{1,0:T(8,128)(2,1)S(1)}, bf16[32,1280]{1,0:T(8,128)(2,1)S(1)}, u32[]{:S(2)}, u32[]{:S(2)}) collective-permute-start(bf16[32,1280]{1,0:T(8,128)(2,1)S(1)} %get-tuple-element.74), channel_id=1, source_target_pairs={{0,6},{1,7},{2,4},{3,5},{4,2},{5,3},{6,0},{7,1},{8,14},{9,15},{10,... | collective-permute-start | bytes 245768 | tf_op jit(solution)/shard_map/adapters/ppermute | solution.py:34
  48.7 5.5 %collective-permute-start.17 = (bf16[32,1280]{1,0:T(8,128)(2,1)S(1)}, bf16[32,1280]{1,0:T(8,128)(2,1)S(1)}, u32[]{:S(2)}, u32[]{:S(2)}) collective-permute-start(bf16[32,1280]{1,0:T(8,128)(2,1)S(1)} %get-tuple-element.75), channel_id=1, source_target_pairs={{0,2},{1,3},{2,0},{3,1},{4,6},{5,7},{6,4},{7,5},{8,10},{9,11},{10,... | collective-permute-start | bytes 245768 | tf_op jit(solution)/shard_map/adapters/ppermute | solution.py:34
